TPU v7x, 32 devices: a whole 2x2x4 slice. The times are simulated.
32 devices in a mesh: dp: 4 (over z), row: 4 (over y, x), col: 2 (over core).
Axes of the slice: x: 2, y: 2, z: 4, core: 2. Of those that a mesh axis runs over, the one named last changes fastest.
Arguments:
- layer_input: bfloat16 [8192, 1536], P(('dp', 'col'), 'row'), may hold values from -12 to 12
- first_gain: float32 [1536], P('row'), may hold values from 0.25 to 1.75
- query_weight: bfloat16 [1536, 1536], P('row', 'col'), may hold values from -0.15625 to 0.15625
- key_projection_weight: bfloat16 [1536, 768], P('row', 'col'), may hold values from -0.15625 to 0.15625
- value_projection_weight: bfloat16 [1536, 768], P('row', 'col'), may hold values from -0.15625 to 0.15625
- output_weight: bfloat16 [1536, 1536], P('col', 'row'), may hold values from -0.875 to 0.875
- second_gain: float32 [1536], P('row'), may hold values from 0.25 to 1.75
- gate_weight: bfloat16 [1536, 4096], P('row', 'col'), may hold values from -0.15625 to 0.15625
- up_weight: bfloat16 [1536, 4096], P('row', 'col'), may hold values from -0.15625 to 0.15625
- down_weight: bfloat16 [4096, 1536], P('col', 'row'), may hold values from -0.09375 to 0.09375
- sequence_lengths: int32 [4, 3], P('dp'), may hold values from 1 to 1536, 2048 in all within a row
- cotangent: bfloat16 [8192, 1536], P(('dp', 'col'), 'row'), may hold values from -6 to 6
Outputs:
- layer_output: bfloat16 [8192, 1536], P(('dp', 'col'), 'row')
- input_gradient: float32 [8192, 1536], P(('dp', 'col'), 'row')
- query_gradient: float32 [1536, 1536], P('row', 'col')
- key_gradient: float32 [1536, 768], P('row', 'col')
- value_gradient: float32 [1536, 768], P('row', 'col')
- output_gradient: float32 [1536, 1536], P('col', 'row')
- gate_gradient: float32 [1536, 4096], P('row', 'col')
- up_gradient: float32 [1536, 4096], P('row', 'col')
- down_gradient: float32 [4096, 1536], P('col', 'row')
- first_gain_gradient: float32 [1536], P('row')
- second_gain_gradient: float32 [1536], P('row')
Inputs may be any that keep to these rules, and one draw needn't show every extreme that they name: `sequence_lengths`: row b gives, in order, the lengths of the 3 sequences that fill token block b; their sum is 2048.
All inputs are finite; a program needn't handle non-finite values.
Results may differ from a plain program's by a relative error of at most 0.039.
Values may be sent and summed in bfloat16 or wider, within the bound.
No kernel may reach another device: no remote copies, remote signals or barrier semaphores. Data moves between devices by JAX's collectives and lax.ppermute only.
A program may use at most 192 MiB of HBM per device.

v0:
```python
import jax
import jax.numpy as jnp
from jax import lax
from jax.sharding import PartitionSpec as P

MODEL_WIDTH = 1536
QUERY_HEADS = 16
KEY_VALUE_HEADS = 8
HEAD_SIZE = 96
QBLOCK = 512


EPSILON = 1e-05
THETA = 100000.0
CONTRACT_LAST = (((1,), (1,)), ((), ()))
CONTRACT_FIRST = (((0,), (0,)), ((), ()))


def product(left, right):
    return jnp.dot(left, right, preferred_element_type=jnp.float32)


def times_transposed(left, right):
    return lax.dot_general(left, right, CONTRACT_LAST, preferred_element_type=jnp.float32)


def transposed_times(left, right):
    return lax.dot_general(left, right, CONTRACT_FIRST, preferred_element_type=jnp.float32)


def layout(length_row, token_total_count):
    end_points = jnp.cumsum(length_row)
    starts = end_points - length_row
    places = jnp.arange(token_total_count, dtype=jnp.int32)
    member = jnp.sum((places[:, None] >= end_points[None, :]).astype(jnp.int32), axis=1)
    chosen = member[:, None] == jnp.arange(length_row.shape[0], dtype=jnp.int32)[None, :]
    offset = jnp.sum(jnp.where(chosen, starts[None, :], 0), axis=1)
    return (member, places - offset)


def tables(places, head_size):
    half_width = head_size // 2
    frequency = THETA ** (-2.0 * jnp.arange(half_width, dtype=jnp.float32) / head_size)
    angles = places.astype(jnp.float32)[:, None] * frequency[None, :]
    return (jnp.cos(angles), jnp.sin(angles))


def rotate(values, cosine, sine_part):
    half_width = values.shape[-1] // 2
    first_half = values[..., :half_width]
    second_half = values[..., half_width:]
    cos_heads = cosine[:, None, :]
    sin_heads = sine_part[:, None, :]
    return jnp.concatenate(
        [
            first_half * cos_heads - second_half * sin_heads,
            second_half * cos_heads + first_half * sin_heads,
        ],
        axis=-1,
    )


def row_totals(partial_sums):
    return lax.psum(partial_sums, "row")


def norm_forward(values, norm_gain):
    inverse = lax.rsqrt(row_totals(jnp.sum(values * values, axis=1)) / MODEL_WIDTH + EPSILON)
    return (inverse, values * inverse[:, None] * norm_gain)


def norm_backward(values, inverse, norm_gain, gradient):
    scaled = gradient * norm_gain
    inner = row_totals(jnp.sum(scaled * values, axis=1))
    values_grad = (
        inverse[:, None] * scaled
        - values * (inverse * inverse * inverse * inner / MODEL_WIDTH)[:, None]
    )
    gain_grad = jnp.sum(gradient * values * inverse[:, None], axis=0)
    return (values_grad, gain_grad)


def gather_block(rows_low):
    return lax.all_gather(rows_low, "col", axis=0, tiled=True)


def gather_mixer(columns_low):
    return lax.all_gather(columns_low, "row", axis=1, tiled=True)


def sum_branch(partial_value):
    return lax.psum_scatter(
        partial_value.astype(jnp.bfloat16), "col", scatter_dimension=0, tiled=True
    ).astype(jnp.float32)


def gather_gradient(rows_low):
    return lax.all_gather(rows_low, "col", axis=0, tiled=True)


def return_rows(columns_low):
    return lax.all_gather(columns_low, "row", axis=1, tiled=True)


def sum_input(partial_value):
    return lax.psum_scatter(
        partial_value.astype(jnp.bfloat16), "col", scatter_dimension=0, tiled=True
    ).astype(jnp.float32)


def arrange(matrices, splits):
    pieces = [
        matrix.reshape(matrix.shape[0], splits, matrix.shape[1] // splits) for matrix in matrices
    ]
    joined = jnp.concatenate(pieces, axis=2)
    return joined.reshape(joined.shape[0], joined.shape[1] * joined.shape[2])


def unarrange(joined, column_counts, splits):
    shaped = joined.reshape(joined.shape[0], splits, joined.shape[1] // splits)
    result = []
    offset = 0
    for columns in column_counts:
        portion = columns // splits
        result.append(shaped[:, :, offset : offset + portion].reshape(joined.shape[0], columns))
        offset = offset + portion
    return result


def widen(gathered, joined):
    partial_value = product(gathered, joined)
    return lax.psum_scatter(
        partial_value.astype(jnp.bfloat16), "row", scatter_dimension=1, tiled=True
    ).astype(jnp.float32)


def narrow(gradient_rows, matrix):
    partial_value = times_transposed(gradient_rows, matrix)
    return lax.psum_scatter(
        partial_value.astype(jnp.bfloat16), "row", scatter_dimension=1, tiled=True
    ).astype(jnp.float32)


def block_mask(member, anchor, row_count):
    key_index = jnp.arange(member.shape[0], dtype=jnp.int32)
    query_index = anchor + jnp.arange(row_count, dtype=jnp.int32)
    query_member = lax.dynamic_slice_in_dim(member, anchor, row_count, 0)
    return (query_member[:, None] == member[None, :]) & (query_index[:, None] >= key_index[None, :])


def attend(turned_q, turned_k, value_low, member):
    blocks = turned_q.shape[0] // QBLOCK
    factor = HEAD_SIZE ** (-0.5)

    def one_block(number):
        anchor = number * QBLOCK
        query_part = lax.dynamic_slice_in_dim(turned_q, anchor, QBLOCK, 0)
        scores = jnp.einsum(
            "qkgd,tkd->kgqt", query_part, turned_k, preferred_element_type=jnp.float32
        )
        logits = jnp.where(block_mask(member, anchor, QBLOCK), scores * factor, -1e30)
        maximum = jnp.max(logits, axis=-1, keepdims=True)
        exponent = jnp.exp(logits - maximum)
        totals = jnp.sum(exponent, axis=-1, keepdims=True)
        probability = (exponent / totals).astype(jnp.bfloat16)
        attended = jnp.einsum(
            "kgqt,tkd->qkgd", probability, value_low, preferred_element_type=jnp.float32
        )
        return (attended, maximum[..., 0] + jnp.log(totals[..., 0]))

    attended, log_totals = lax.map(one_block, jnp.arange(blocks, dtype=jnp.int32))
    return (attended.reshape(turned_q.shape), log_totals)


def attend_back(turned_q, turned_k, value_low, member, attended, log_totals, heads_grad):
    blocks = turned_q.shape[0] // QBLOCK
    factor = HEAD_SIZE ** (-0.5)
    delta_rows = jnp.sum(heads_grad.astype(jnp.float32) * attended, axis=-1)

    def one_block(carried, number):
        key_total, value_total = carried
        anchor = number * QBLOCK
        query_part = lax.dynamic_slice_in_dim(turned_q, anchor, QBLOCK, 0)
        grad_part = lax.dynamic_slice_in_dim(heads_grad, anchor, QBLOCK, 0)
        delta_part = jnp.transpose(
            lax.dynamic_slice_in_dim(delta_rows, anchor, QBLOCK, 0), (1, 2, 0)
        )
        scores = jnp.einsum(
            "qkgd,tkd->kgqt", query_part, turned_k, preferred_element_type=jnp.float32
        )
        probability = jnp.where(
            block_mask(member, anchor, QBLOCK),
            jnp.exp(scores * factor - log_totals[number][..., None]),
            0.0,
        )
        prob_low = probability.astype(jnp.bfloat16)
        pressure = jnp.einsum(
            "qkgd,tkd->kgqt", grad_part, value_low, preferred_element_type=jnp.float32
        )
        score_grad = (probability * (pressure - delta_part[..., None]) * factor).astype(
            jnp.bfloat16
        )
        query_grad = jnp.einsum(
            "kgqt,tkd->qkgd", score_grad, turned_k, preferred_element_type=jnp.float32
        )
        key_total = key_total + jnp.einsum(
            "kgqt,qkgd->tkd", score_grad, query_part, preferred_element_type=jnp.float32
        )
        value_total = value_total + jnp.einsum(
            "kgqt,qkgd->tkd", prob_low, grad_part, preferred_element_type=jnp.float32
        )
        return ((key_total, value_total), query_grad)

    zeros_kv = jnp.zeros(turned_k.shape, jnp.float32)
    (key_grad, value_grad), query_grads = lax.scan(
        one_block, (zeros_kv, zeros_kv), jnp.arange(blocks, dtype=jnp.int32)
    )
    return (query_grads.reshape(turned_q.shape), key_grad, value_grad)


def on_device(
    layer_input,
    first_gain,
    query_weight,
    key_projection_weight,
    value_projection_weight,
    output_weight,
    second_gain,
    gate_weight,
    up_weight,
    down_weight,
    sequence_lengths,
    cotangent,
):
    splits = lax.axis_size("row")
    group_width = QUERY_HEADS // KEY_VALUE_HEADS
    inputs = layer_input.astype(jnp.float32)
    first_inverse, first_norm_output = norm_forward(inputs, first_gain)
    first_rows = gather_block(first_norm_output.astype(jnp.bfloat16))
    token_total_count = first_rows.shape[0]
    member, places = layout(sequence_lengths[0], token_total_count)
    cosine, sine_part = tables(places, HEAD_SIZE)
    attention_joined = arrange(
        (query_weight, key_projection_weight, value_projection_weight), splits
    )
    projected = widen(first_rows, attention_joined)
    query_cols = query_weight.shape[1] // splits
    key_cols = key_projection_weight.shape[1] // splits
    kv_heads = key_cols // HEAD_SIZE
    queries = projected[:, :query_cols].reshape(
        token_total_count, kv_heads * group_width, HEAD_SIZE
    )
    key_head_rows = projected[:, query_cols : query_cols + key_cols].reshape(
        token_total_count, kv_heads, HEAD_SIZE
    )
    value_head_rows = projected[:, query_cols + key_cols :].reshape(
        token_total_count, kv_heads, HEAD_SIZE
    )
    turned_q = (
        rotate(queries, cosine, sine_part)
        .astype(jnp.bfloat16)
        .reshape(token_total_count, kv_heads, group_width, HEAD_SIZE)
    )
    turned_k = rotate(key_head_rows, cosine, sine_part).astype(jnp.bfloat16)
    value_low = value_head_rows.astype(jnp.bfloat16)
    attended, log_totals = attend(turned_q, turned_k, value_low, member)
    heads_out = attended.astype(jnp.bfloat16).reshape(token_total_count, query_cols)
    heads_rows = gather_mixer(heads_out)
    middle = inputs + sum_branch(product(heads_rows, output_weight))
    second_inverse, second_normed = norm_forward(middle, second_gain)
    second_rows = gather_block(second_normed.astype(jnp.bfloat16))
    feed_joined = arrange((gate_weight, up_weight), splits)
    gate_up = widen(second_rows, feed_joined)
    unit_count = gate_weight.shape[1] // splits
    gate_values = gate_up[:, :unit_count]
    up_values = gate_up[:, unit_count:]
    gate_sigmoid = jax.nn.sigmoid(gate_values)
    hidden = (gate_values * gate_sigmoid * up_values).astype(jnp.bfloat16)
    hidden_rows = gather_mixer(hidden)
    layer_output = (middle + sum_branch(product(hidden_rows, down_weight))).astype(jnp.bfloat16)
    upstream = gather_gradient(cotangent)
    down_total = transposed_times(hidden_rows, upstream)
    hidden_grad = narrow(upstream, down_weight)
    gate_grad = (
        hidden_grad * up_values * gate_sigmoid * (1.0 + gate_values * (1.0 - gate_sigmoid))
    ).astype(jnp.bfloat16)
    up_grad = (hidden_grad * gate_values * gate_sigmoid).astype(jnp.bfloat16)
    feed_back = return_rows(jnp.concatenate([gate_grad, up_grad], axis=1))
    gate_total, up_total = unarrange(
        transposed_times(second_rows, feed_back), (gate_weight.shape[1], up_weight.shape[1]), splits
    )
    second_grad = sum_input(times_transposed(feed_back, feed_joined))
    middle_back, second_gain_grad = norm_backward(middle, second_inverse, second_gain, second_grad)
    middle_grad = cotangent.astype(jnp.float32) + middle_back
    branch_rows = gather_gradient(middle_grad.astype(jnp.bfloat16))
    output_total = transposed_times(heads_rows, branch_rows)
    heads_grad = (
        narrow(branch_rows, output_weight)
        .astype(jnp.bfloat16)
        .reshape(token_total_count, kv_heads, group_width, HEAD_SIZE)
    )
    query_back, key_back, value_back = attend_back(
        turned_q, turned_k, value_low, member, attended, log_totals, heads_grad
    )
    query_flat = (
        rotate(
            query_back.reshape(token_total_count, kv_heads * group_width, HEAD_SIZE),
            cosine,
            -sine_part,
        )
        .astype(jnp.bfloat16)
        .reshape(token_total_count, query_cols)
    )
    key_flat = (
        rotate(key_back, cosine, -sine_part)
        .astype(jnp.bfloat16)
        .reshape(token_total_count, key_cols)
    )
    value_flat = value_back.astype(jnp.bfloat16).reshape(token_total_count, key_cols)
    attention_back = return_rows(jnp.concatenate([query_flat, key_flat, value_flat], axis=1))
    query_total, key_total, value_total = unarrange(
        transposed_times(first_rows, attention_back),
        (query_weight.shape[1], key_projection_weight.shape[1], value_projection_weight.shape[1]),
        splits,
    )
    first_grad = sum_input(times_transposed(attention_back, attention_joined))
    input_back, first_gain_grad = norm_backward(inputs, first_inverse, first_gain, first_grad)
    input_gradient = middle_grad + input_back
    summed = (
        lax.psum(query_total.astype(jnp.bfloat16), "dp").astype(jnp.float32),
        lax.psum(key_total.astype(jnp.bfloat16), "dp").astype(jnp.float32),
        lax.psum(value_total.astype(jnp.bfloat16), "dp").astype(jnp.float32),
        lax.psum(output_total.astype(jnp.bfloat16), "dp").astype(jnp.float32),
        lax.psum(gate_total.astype(jnp.bfloat16), "dp").astype(jnp.float32),
        lax.psum(up_total.astype(jnp.bfloat16), "dp").astype(jnp.float32),
        lax.psum(down_total.astype(jnp.bfloat16), "dp").astype(jnp.float32),
        lax.psum(first_gain_grad.astype(jnp.bfloat16), "dp").astype(jnp.float32),
        lax.psum(second_gain_grad.astype(jnp.bfloat16), "dp").astype(jnp.float32),
    )
    first_gain_total, second_gain_total = lax.psum((summed[7], summed[8]), "col")
    return (
        layer_output,
        input_gradient,
        summed[0],
        summed[1],
        summed[2],
        summed[3],
        summed[4],
        summed[5],
        summed[6],
        first_gain_total,
        second_gain_total,
    )


def solution(mesh):
    return jax.shard_map(
        on_device,
        mesh=mesh,
        in_specs=(
            P(("dp", "col"), "row"),
            P("row"),
            P("row", "col"),
            P("row", "col"),
            P("row", "col"),
            P("col", "row"),
            P("row"),
            P("row", "col"),
            P("row", "col"),
            P("col", "row"),
            P("dp", None),
            P(("dp", "col"), "row"),
        ),
        out_specs=(
            P(("dp", "col"), "row"),
            P(("dp", "col"), "row"),
            P("row", "col"),
            P("row", "col"),
            P("row", "col"),
            P("col", "row"),
            P("row", "col"),
            P("row", "col"),
            P("col", "row"),
            P("row"),
            P("row"),
        ),
        check_vma=False,
    )
```

profile of v0, /device:TPU:0, one launch (start us, length us, event | category | flops | bytes accessed | tf_op | source)
XLA Modules:
  0.0 1402.3 jit_solution(10952253037149926772)
XLA Ops:
  8.8 11.4 psum.105
  24.4 7.4 all-gather.9.cloned.1.call-done
  31.8 7.8 convolution_convert_fusion.2
  39.6 8.7 copy.85
  51.7 68.1 %reduce-scatter.25.cloned.1.call-done = bf16[384,2048]{1,0:T(8,128)(2,1)} async-done(((bf16[1536,2048]{1,0:T(8,128)(2,1)}), bf16[384,2048]{1,0:T(8,128)(2,1)}) %reduce-scatter.25.cloned.1.call-update) | async-done | bytes 1572880
  131.4 47.8 %while.27 = (s32[]{:T(128)}, f32[4,512,1,2,96]{1,4,3,2,0:T(8,128)}, f32[4,1,2,512]{3,2,1,0:T(2,128)}, s32[4]{0:T(128)S(1)}, s32[2048]{0:T(1024)S(1)}, /*index=5*...) while((s32[]{:T(128)}, f32[4,512,1,2,96]{1,4,3,2,0:T(8,128)}, ...), condition=%wide.region_9.10_spmd, body=%wide.region_6.9_spmd.sunk | while | flops 833617408 | bytes 30787788 | solution.py:171
  139.3 3.4 fusion.170
  151.3 3.4 fusion.170
  163.2 3.4 fusion.170
  175.2 3.4 fusion.170
  182.5 44.1 %all-gather.11.cloned.1.call-done = bf16[2048,768]{0,1:T(8,128)(2,1)} async-done(((bf16[2048,192]{0,1:T(8,128)(2,1)}), bf16[2048,768]{0,1:T(8,128)(2,1)}) %all-gather.11.cloned.1.call-update) | async-done | bytes 3145744 | tf_op jit(solution)/shard_map/all_gather | solution.py:88
  226.6 4.9 convolution_convert_fusion.7
  231.5 9.2 reduce-scatter.11.cloned.1.call-done
  242.2 10.1 psum.106
  255.1 3.9 reshape.450
  259.0 3.9 reshape.451
  262.9 3.3 pad_maximum_fusion.1
  266.2 3.1 copy.99
  269.3 14.1 %convolution_convert_fusion = bf16[2048,4096]{1,0:T(8,128)(2,1)} fusion(bf16[2048,384]{1,0:T(8,128)(2,1)} %all-gather.13.cloned.1.call-done, bf16[384,4096]{1,0:T(8,128)(2,1)} %bitcast.296), kind=kOutput, calls=%fused_computation.64 | convolution fusion | flops 6450839552 | bytes 21495808 | tf_op jit(solution)/shard_map/dot_general | solution.py:20
  283.5 8.3 convolution_convert_fusion.1
  292.3 144.4 %reduce-scatter.13.cloned.1.call-done = bf16[2048,1024]{1,0:T(8,128)(2,1)} async-done(((bf16[2048,4096]{1,0:T(8,128)(2,1)}), bf16[2048,1024]{1,0:T(8,128)(2,1)}) %reduce-scatter.13.cloned.1.call-update) | async-done | bytes 4194320 | tf_op jit(solution)/shard_map/reduce_scatter | solution.py:132
  436.7 6.5 convert_element_type.222
  443.2 83.2 %reduce-scatter.17.cloned.1.call-done = bf16[2048,512]{1,0:T(8,128)(2,1)} async-done(((bf16[2048,2048]{1,0:T(8,128)(2,1)}), bf16[2048,512]{1,0:T(8,128)(2,1)}) %reduce-scatter.17.cloned.1.call-update) | async-done | bytes 2097168 | tf_op jit(solution)/shard_map/reduce_scatter | solution.py:139
  526.5 6.2 fusion.69
  535.4 157.5 %all-gather.19.cloned.1.call-done = bf16[2048,4096]{1,0:T(8,128)(2,1)} async-done(((bf16[2048,1024]{1,0:T(8,128)(2,1)}), bf16[2048,4096]{1,0:T(8,128)(2,1)}) %all-gather.19.cloned.1.call-update) | async-done | bytes 16777232 | tf_op jit(solution)/shard_map/all_gather | solution.py:102
  692.9 14.2 %convolution_convert_fusion.10 = bf16[2048,384]{1,0:T(8,128)(2,1)} fusion(bf16[2048,4096]{1,0:T(8,128)(2,1)} %all-gather.19.cloned.1.call-done, bf16[384,4096]{1,0:T(8,128)(2,1)} %bitcast.297), kind=kOutput, calls=%fused_computation.91 | convolution fusion | flops 6443237376 | bytes 21495808 | tf_op jit(solution)/shard_map/dot_general | solution.py:24
  707.1 9.2 reduce-scatter.19.cloned.1.call-done
  718.7 10.8 psum.107
  733.2 9.0 all-gather.21.cloned.1.call-done
  742.2 5.0 convolution_convert_fusion.4
  747.5 45.0 %reduce-scatter.21.cloned.1.call-done = bf16[2048,192]{0,1:T(8,128)(2,1)} async-done(((bf16[2048,768]{0,1:T(8,128)(2,1)}), bf16[2048,192]{0,1:T(8,128)(2,1)}) %reduce-scatter.21.cloned.1.call-update) | async-done | bytes 786448 | tf_op jit(solution)/shard_map/reduce_scatter | solution.py:139
  792.5 3.1 reshape.457
  795.6 3.1 fusion.88
  799.2 124.4 %while.28 = (s32[]{:T(128)}, f32[2048,1,96]{0,2,1:T(8,128)}, f32[2048,1,96]{0,2,1:T(8,128)}, f32[4,512,1,2,96]{1,0,4,3,2:T(4,128)}, s32[4]{0:T(128)}, /*index=5*...) while((s32[]{:T(128)}, f32[2048,1,96]{0,2,1:T(8,128)}, ...), condition=%wide.region_22.23_spmd.clone, body=%wide.region_21.22_spmd.clone.sunk | while | flops 2040267264 | bytes 48019756 | solution.py:215
  807.9 4.3 fusion.185
  812.2 4.5 fusion.183
  821.2 8.6 dynamic_update_slice.19
  838.5 4.6 fusion.185
  843.2 4.5 fusion.183
  849.1 3.0 fusion.184
  852.5 8.6 dynamic_update_slice.19
  869.8 4.6 fusion.185
  874.4 4.5 fusion.183
  883.8 8.6 dynamic_update_slice.19
  901.1 4.6 fusion.185
  905.7 4.5 fusion.183
  911.6 3.0 fusion.184
  915.0 8.6 dynamic_update_slice.19
  923.7 3.2 reshape_reshape.3
  926.9 3.1 fusion.109
  933.5 69.7 %all-gather.23.cloned.1.call-done = bf16[2048,1536]{0,1:T(8,128)(2,1)} async-done(((bf16[2048,384]{0,1:T(8,128)(2,1)}), bf16[2048,1536]{0,1:T(8,128)(2,1)}) %all-gather.23.cloned.1.call-update) | async-done | bytes 6291472 | tf_op jit(solution)/shard_map/all_gather | solution.py:102
  1003.2 7.7 convolution_convert_fusion.9
  1011.0 82.1 %all-gather.15.cloned.1.call-done = bf16[2048,2048]{1,0:T(8,128)(2,1)} async-done(((bf16[2048,512]{1,0:T(8,128)(2,1)}), bf16[2048,2048]{1,0:T(8,128)(2,1)}) %all-gather.15.cloned.1.call-update) | async-done | bytes 8388624 | tf_op jit(solution)/shard_map/all_gather | solution.py:88
  1093.1 9.1 convolution_convert_fusion.6
  1102.2 9.9 convolution_convert_fusion.5
  1112.1 12.3 convolution_convert_fusion.3
  1124.4 6.2 reshape.459
  1140.2 3.7 convolution_convert_fusion.8
  1152.7 12.1 all-reduce.1
  1164.8 3.0 all-reduce
  1167.8 8.8 psum.108
  1176.7 3.6 fusion.76
  1180.3 201.4 %all-reduce.5.cloned.1.call-done = (bf16[384,768]{0,1:T(8,128)(2,1)}, bf16[384,384]{0,1:T(8,128)(2,1)}, bf16[384,384]{0,1:T(8,128)(2,1)}, bf16[768,384]{1,0:T(8,...) async-done(((bf16[384,768]{0,1:T(8,128)(2,1)}, bf16[384,384]{0,1:T(8,128)(2,1)}, bf16[384,384]{0,1:T(8,128)(2,1)}, ...) | async-done | bytes 6488080 | tf_op jit(solution)/shard_map/psum | solution.py:330
  1388.1 3.6 convert_element_type.251
  (243 shorter events, 139.2 us)
Async XLA Ops:
  7.2 276.3 %copy-start = (bf16[2048,384]{1,0:T(8,128)(2,1)S(1)}, bf16[2048,384]{1,0:T(8,128)(2,1)}, u32[]{:S(2)}) copy-start(bf16[2048,384]{1,0:T(8,128)(2,1)} %param.25) | copy-start | bytes 4718596
  7.2 15.3 %copy-start.16 = (bf16[384,384]{1,0:T(8,128)(2,1)S(1)}, bf16[384,384]{1,0:T(8,128)(2,1)}, u32[]{:S(2)}) copy-start(bf16[384,384]{1,0:T(8,128)(2,1)} %param.19) | copy-start | bytes 884740
  7.2 15.6 %copy-start.17 = (bf16[384,384]{1,0:T(8,128)(2,1)S(1)}, bf16[384,384]{1,0:T(8,128)(2,1)}, u32[]{:S(2)}) copy-start(bf16[384,384]{1,0:T(8,128)(2,1)} %param.20) | copy-start | bytes 884740
  7.2 15.8 %copy-start.12 = (bf16[384,768]{1,0:T(8,128)(2,1)S(1)}, bf16[384,768]{1,0:T(8,128)(2,1)}, u32[]{:S(2)}) copy-start(bf16[384,768]{1,0:T(8,128)(2,1)} %param.18) | copy-start | bytes 1769476
  7.2 24.6 %all-gather.9.cloned.1.call-start = ((), (), s32[]{:S(2)}) async-start(), calls=%async_computation.8 | async-start | bytes 2359296 | tf_op jit(solution)/shard_map/all_gather | solution.py:84
  20.1 2.6 copy-start.22
  20.2 2.6 copy-start.20
  22.5 97.4 %reduce-scatter.25.cloned.1.call-start = ((), (), s32[]{:S(2)}) async-start(), calls=%async_computation.23 | async-start | bytes 7864320
  48.3 0.7 copy-start.36
  48.3 178.2 %all-gather.11.cloned.1.call-start = ((), (), s32[]{:S(2)}) async-start(), calls=%async_computation.9 | async-start | bytes 3932160 | tf_op jit(solution)/shard_map/all_gather | solution.py:88
  49.2 77.8 %copy-start.28 = (f32[48]{0:T(128)}, f32[48]{0:T(128)S(1)}, u32[]{:S(2)}) copy-start(f32[48]{0:T(128)S(1)} %multiply_power_fusion) | copy-start | bytes 580
  49.4 77.6 %copy-start.18 = (f32[2048]{0:T(1024)}, f32[2048]{0:T(1024)S(1)}, u32[]{:S(2)}) copy-start(f32[2048]{0:T(1024)S(1)} %subtract_convert_fusion.2) | copy-start | bytes 24580
  51.7 77.0 %copy-start.5 = (f32[2048,48]{0,1:T(8,128)}, f32[2048,48]{0,1:T(8,128)S(1)}, u32[]{:S(2)}) copy-start(f32[2048,48]{0,1:T(8,128)S(1)} %get-tuple-element.351) | copy-start | bytes 1179652
  126.9 1.8 copy-start.8
  128.7 2.7 copy-start.13
  180.7 45.8 %copy-start.35 = (bf16[768,384]{1,0:T(8,128)(2,1)S(1)}, bf16[768,384]{1,0:T(8,128)(2,1)}, u32[]{:S(2)}) copy-start(bf16[768,384]{1,0:T(8,128)(2,1)} %param.21) | copy-start | bytes 1769476
  182.4 58.2 %reduce-scatter.11.cloned.1.call-start = ((), (), s32[]{:S(2)}) async-start(), calls=%async_computation.10 | async-start | bytes 2359296 | tf_op jit(solution)/shard_map/reduce_scatter | solution.py:92
  231.4 9.2 copy-start.1
  231.5 37.8 %all-gather.13.cloned.1.call-start = ((), (), s32[]{:S(2)}) async-start(), calls=%async_computation.11 | async-start | bytes 2359296 | tf_op jit(solution)/shard_map/all_gather | solution.py:84
  240.7 11.7 copy-start.2
  252.4 6.6 copy-start.24
  254.3 29.2 %all-gather.17.cloned.1.call-start = ((), (), s32[]{:S(2)}) async-start(), calls=%async_computation.15 | async-start | bytes 2359296 | tf_op jit(solution)/shard_map/all_gather | solution.py:98
  254.8 181.9 %reduce-scatter.13.cloned.1.call-start = ((), (), s32[]{:S(2)}) async-start(), calls=%async_computation.12 | async-start | bytes 20971520 | tf_op jit(solution)/shard_map/reduce_scatter | solution.py:132
  283.4 243.0 %reduce-scatter.17.cloned.1.call-start = ((), (), s32[]{:S(2)}) async-start(), calls=%async_computation.16 | async-start | bytes 10485760 | tf_op jit(solution)/shard_map/reduce_scatter | solution.py:139
  291.9 401.0 %all-gather.19.cloned.1.call-start = ((), (), s32[]{:S(2)}) async-start(), calls=%async_computation.17 | async-start | bytes 20971520 | tf_op jit(solution)/shard_map/all_gather | solution.py:102
  535.3 181.0 %copy-start.25 = (f32[384]{0:T(512)S(1)}, f32[384]{0:T(512)}, u32[]{:S(2)}) copy-start(f32[384]{0:T(512)} %param.22) | copy-start | bytes 4612
  535.3 181.0 %reduce-scatter.19.cloned.1.call-start = ((), (), s32[]{:S(2)}) async-start(), calls=%async_computation.18 | async-start | bytes 2359296 | tf_op jit(solution)/shard_map/reduce_scatter | solution.py:106
  707.1 35.1 %all-gather.21.cloned.1.call-start = ((), (), s32[]{:S(2)}) async-start(), calls=%async_computation.19 | async-start | bytes 2359296 | tf_op jit(solution)/shard_map/all_gather | solution.py:98
  733.1 59.4 %reduce-scatter.21.cloned.1.call-start = ((), (), s32[]{:S(2)}) async-start(), calls=%async_computation.20 | async-start | bytes 3932160 | tf_op jit(solution)/shard_map/reduce_scatter | solution.py:139
  747.2 256.0 %all-gather.23.cloned.1.call-start = ((), (), s32[]{:S(2)}) async-start(), calls=%async_computation.21 | async-start | bytes 7864320 | tf_op jit(solution)/shard_map/all_gather | solution.py:102
  795.6 3.6 copy-start.14
  923.6 3.2 copy-start.19
  923.6 3.2 copy-start.29
  923.6 7.6 copy-start.6
  923.6 7.6 copy-start.7
  926.9 4.3 copy-start.4
  932.9 160.2 %all-gather.15.cloned.1.call-start = ((), (), s32[]{:S(2)}) async-start(), calls=%async_computation.13 | async-start | bytes 10485760 | tf_op jit(solution)/shard_map/all_gather | solution.py:88
  933.5 216.7 %reduce-scatter.23.cloned.1.call-start = ((), (), s32[]{:S(2)}) async-start(), calls=%async_computation.22 | async-start | bytes 2359296 | tf_op jit(solution)/shard_map/reduce_scatter | solution.py:106
  1010.9 165.7 %reduce-scatter.15.cloned.1.call-start = ((), (), s32[]{:S(2)}) async-start(), calls=%async_computation.14 | async-start | bytes 2359296 | tf_op jit(solution)/shard_map/reduce_scatter | solution.py:92
  1102.2 279.5 %all-reduce.5.cloned.1.call-start = ((), (), s32[]{:S(2)}) async-start(), calls=%async_computation.24 | async-start | bytes 12976128 | tf_op jit(solution)/shard_map/psum | solution.py:330
  1102.2 9.9 copy-start.33
  1133.5 3.2 copy-start.34
  1135.1 2.5 copy-start.31
  1135.1 5.1 slice-start
  1137.6 2.6 slice-start.1
  1137.6 2.6 copy-start.32
  1150.1 0.7 copy-start.21
  1150.1 0.7 copy-start.27
  1150.1 2.6 copy-start.30
  1150.1 26.5 %copy-start.23 = (f32[1024]{0:T(1024)S(1)}, f32[1024]{0:T(1024)}, u32[]{:S(2)}) copy-start(f32[1024]{0:T(1024)} %copy-done.22) | copy-start | bytes 12292
  1150.1 26.6 %copy-start.26 = (f32[384]{0:T(512)S(1)}, f32[384]{0:T(512)}, u32[]{:S(2)}) copy-start(f32[384]{0:T(512)} %param.22) | copy-start | bytes 4612
  1150.2 26.5 %copy-start.3 = (bf16[1024,384]{1,0:T(8,128)(2,1)S(1)}, bf16[1024,384]{1,0:T(8,128)(2,1)}, u32[]{:S(2)}) copy-start(bf16[1024,384]{1,0:T(8,128)(2,1)} %reduce-scatter.11.cloned.1.call-done) | copy-start | bytes 2359300
  1381.7 4.3 copy-start.15
  1381.7 5.3 copy-start.11
  1388.1 3.6 copy-start.10
  1391.7 2.0 copy-start.9
Sparse Core Ops, SparseCore 0:
  22.6 9.1 all-gather.8
  48.5 71.3 reduce-scatter.24
  182.6 43.9 all-gather.10
  231.6 9.0 reduce-scatter.10
  254.4 8.8 all-gather.12
  264.8 10.9 all-gather.16
  283.6 153.0 reduce-scatter.12
  440.1 86.3 reduce-scatter.16
  535.4 157.4 all-gather.18
  707.2 9.0 reduce-scatter.18
  733.2 8.8 all-gather.20
  747.4 45.1 reduce-scatter.20
  933.0 70.1 all-gather.22
  1005.6 87.4 all-gather.14
  1095.9 9.0 reduce-scatter.22
  1107.6 10.2 reduce-scatter.14
  1150.3 231.3 all-reduce.4
where the time goes:
time: 1410 us; the launch traced here: 1400 us
  waiting for transfers between devices  932 us (66%)
  matrix products  187 us (13%)
  local copies, waits for them, and re-layouts  109 us (8%)
  other arithmetic  88.6 us (6%)
  blocking collectives  56.2 us (4%)
  between operations  14.7 us (1%)
    all_gather x2, waiting for transfers between devices, return_rows(): return lax.all_gather(columns_low, 'row', axis=1, tiled=True)  227 us
    psum x1, waiting for transfers between devices, on_device(): lax.psum(query_total.astype(jnp.bfloat16), 'dp').astype(jnp.float32)  201 us
    reduce_scatter x1, waiting for transfers between devices, widen(): lax.psum_scatter(partial_value.astype(jnp.bfloat16), 'row', scatter_dimen...  144 us
    reduce_scatter x2, waiting for transfers between devices, narrow(): lax.psum_scatter(partial_value.astype(jnp.bfloat16), 'row', scatter_dimen...  128 us
    all_gather x2, waiting for transfers between devices, gather_mixer(): return lax.all_gather(columns_low, 'row', axis=1, tiled=True)  126 us
    unnamed x18, waiting for transfers between devices  69.4 us
    psum x4, blocking collectives, row_totals(): return lax.psum(partial_sums, 'row')  41.1 us
    dynamic_update_slice x8, local copies, waits for them, and re-layouts, attend(): lax.map(one_block, jnp.arange(blocks, dtype=jnp.int32))  36.1 us
  transfers between devices with their start and end apart: 17, of which 13 were waited for; matrix products, arithmetic and copies ran while one was open for 8% of the time, Pallas kernels for 0%

commit v1 on v0

v1 whole, which is shorter than its diff:
```python
import functools

import jax
import jax.numpy as jnp
from jax import lax
from jax.experimental import pallas as pl
from jax.experimental.pallas import tpu as pltpu
from jax.sharding import PartitionSpec as P

HEAD = 96
LANES = 128
SIDE = 48
TILE = 256
EPSILON = 1e-05
THETA = 100000.0
LOG2E = 1.4426950408889634
FACTOR = HEAD**-0.5
LOW = jnp.bfloat16
F32 = jnp.float32
NN = (((1,), (0,)), ((), ()))
NT = (((1,), (1,)), ((), ()))
TN = (((0,), (0,)), ((), ()))
VMEM_LIMIT = 48 * 1024 * 1024


def dot(left, right, dims=NN):
    return lax.dot_general(left, right, dims, preferred_element_type=F32)


def swap(value, step):
    return lax.ppermute(value, "row", [(i, i ^ step) for i in range(4)])


def other(value):
    return lax.ppermute(value, "col", [(0, 1), (1, 0)])


def gather_row(value):
    half = value.shape[0] // 2
    along_x = swap(value, 1)
    along_y = swap(value, 2)
    top = swap(along_x[:half], 2)
    bottom = swap(along_y[half:], 1)
    return [value, along_x, along_y, jnp.concatenate([top, bottom], axis=0)]


def exchange_row(pieces):
    return [pieces[0]] + [swap(pieces[i], i) for i in (1, 2, 3)]


def total_row(value):
    return value + swap(value, 1) + swap(value, 2) + swap(value, 3)


def scatter_row(parts):
    own_a, a_xd, a_y, own_b, b_yd, b_x = parts
    width = own_a.shape[1]
    got_a = swap(a_xd, 1)
    got_b = swap(b_yd, 2)
    send_a = (a_y.astype(F32) + got_a[:, width:].astype(F32)).astype(LOW)
    send_b = (b_x.astype(F32) + got_b[:, width:].astype(F32)).astype(LOW)
    last_a = swap(send_a, 2)
    last_b = swap(send_b, 1)
    total_a = own_a.astype(F32) + got_a[:, :width].astype(F32) + last_a.astype(F32)
    total_b = own_b.astype(F32) + got_b[:, :width].astype(F32) + last_b.astype(F32)
    return jnp.concatenate([total_a, total_b], axis=0)


def chain_scatter(take, count):
    place = lax.axis_index("dp")
    own = take(place)
    if count == 1:
        return own
    right = left = None
    for step in range(1, count):
        up = take(jnp.clip(count - step + place, 0, count - 1))
        down = take(jnp.clip(place - (count - step), 0, count - 1))
        if right is not None:
            up = (up.astype(F32) + right.astype(F32)).astype(LOW)
            down = (down.astype(F32) + left.astype(F32)).astype(LOW)
        ups = [(i, i + 1) for i in range(min(step, count - 1))]
        right = lax.ppermute(up, "dp", ups)
        left = lax.ppermute(down, "dp", [(count - 1 - i, count - 1 - j) for i, j in ups])
    return (own.astype(F32) + right.astype(F32) + left.astype(F32)).astype(LOW)


def chain_gather(shard, count):
    place = lax.axis_index("dp")
    shape = (shard.shape[0], count) + shard.shape[1:]
    result = jnp.zeros(shape, shard.dtype)
    zero = jnp.zeros((), jnp.int32)

    def put(result, piece, at):
        start = (zero, at) + (zero,) * (len(shape) - 2)
        return lax.dynamic_update_slice(result, piece[:, None], start)

    right = left = shard
    for step in range(1, count):
        ups = [(i, i + 1) for i in range(step - 1, count - 1)]
        right = lax.ppermute(right, "dp", ups)
        left = lax.ppermute(left, "dp", [(count - 1 - i, count - 1 - j) for i, j in ups])
        result = put(result, right, jnp.where(place - step >= 0, place - step, place))
        result = put(result, left, jnp.where(place + step < count, place + step, place))
    return put(result, shard, place)


def call(kernel, out_shape, in_specs, out_specs, grid=(), scratch=(), prefetch=0, flops=0, moved=0):
    return pl.pallas_call(
        kernel,
        out_shape=out_shape,
        grid_spec=pltpu.PrefetchScalarGridSpec(
            num_scalar_prefetch=prefetch,
            grid=grid,
            in_specs=in_specs,
            out_specs=out_specs,
            scratch_shapes=list(scratch),
        ),
        compiler_params=pltpu.CompilerParams(vmem_limit_bytes=VMEM_LIMIT),
        cost_estimate=pl.CostEstimate(flops=int(flops), bytes_accessed=int(moved), transcendentals=0),
    )


def shape(dims, kind=LOW):
    return jax.ShapeDtypeStruct(tuple(dims), kind)


def whole(array):
    rank = len(array.shape)
    return pl.BlockSpec(tuple(array.shape), lambda *_: (0,) * rank)


def bytes_of(*arrays):
    return sum(int(a.size) * a.dtype.itemsize for a in arrays)


def pack_kernel(row_ref, q_ref, k_ref, v_ref, out_ref):
    row = row_ref[0]
    query, key = q_ref.shape[1] // 4, k_ref.shape[1] // 4
    for j in range(4):
        at = jnp.bitwise_xor(row, j)
        out_ref[at, :, :query] = q_ref[:, j * query : (j + 1) * query]
        out_ref[at, :, query : query + key] = k_ref[:, j * key : (j + 1) * key]
        out_ref[at, :, query + key :] = v_ref[:, j * key : (j + 1) * key]


def pack(row, query_weight, key_weight, value_weight):
    depth = query_weight.shape[0]
    width = (query_weight.shape[1] + 2 * key_weight.shape[1]) // 4
    out = shape((4, depth, width))
    arrays = (query_weight, key_weight, value_weight)
    return call(
        pack_kernel,
        out,
        [whole(a) for a in arrays],
        whole(out),
        grid=(1,),
        prefetch=1,
        moved=2 * bytes_of(out),
    )(row, *arrays)


def project_kernel(x0, x1, x2, x3, gain, w_own, w_oth, cos, sin, first, r1, own, oth):
    x = jnp.concatenate([x0[...], x1[...], x2[...], x3[...]], axis=1).astype(F32)
    inverse = lax.rsqrt(jnp.mean(x * x, axis=1, keepdims=True) + EPSILON)
    normed = (x * inverse * gain[...]).astype(LOW)
    first[...] = normed
    r1[...] = jnp.broadcast_to(inverse, r1.shape)
    for weight, out in ((w_own, own), (w_oth, oth)):
        heads = dot(normed, weight[...])
        for h in range(3):
            part = heads[:, h * LANES : (h + 1) * LANES]
            turned = part * cos[...] + pltpu.roll(part, LANES // 2, 1) * sin[...]
            out[:, h * LANES : (h + 1) * LANES] = turned.astype(LOW)
        out[:, 3 * LANES :] = heads[:, 3 * LANES :].astype(LOW)


def project(xs, gain, w_own, w_oth, cos, sin):
    tokens, width = xs[0].shape
    rows = lambda n: pl.BlockSpec((TILE, n), lambda b: (b, 0))
    outs = (shape((tokens, 4 * width)), shape((tokens, LANES), F32), shape((tokens, 512)), shape((tokens, 512)))
    return call(
        project_kernel,
        outs,
        [rows(width)] * 4 + [whole(gain), whole(w_own), whole(w_oth), rows(LANES), rows(LANES)],
        tuple(rows(o.shape[1]) for o in outs),
        grid=(tokens // TILE,),
        flops=2 * tokens * 4 * width * 1024,
        moved=bytes_of(*xs, w_own, w_oth, *outs),
    )(*xs, gain, w_own, w_oth, cos, sin)


def stack_heads(ref, rows):
    return jnp.concatenate([ref[rows, :LANES], ref[rows, LANES : 2 * LANES]], axis=0)


def block_limits(start_ref, block):
    rows = pl.ds(pl.multiple_of(block * TILE, TILE), TILE)
    start = start_ref[:, rows]
    query = block * TILE + lax.broadcasted_iota(jnp.int32, (1, TILE), 1)
    return jnp.concatenate([start, start], axis=1), jnp.concatenate([query, query], axis=1)


def allowed_keys(number, start, query):
    key = number * TILE + lax.broadcasted_iota(jnp.int32, (TILE, 2 * TILE), 0)
    return (key >= start) & (key <= query)


def attend_kernel(info, own, oth, start_ref, keep, send, out, lse, full, values, top, total, acc):
    block = pl.program_id(0)
    core = info[0]
    half = own.shape[0]

    @pl.when(block == 0)
    def _():
        full[pl.ds(pl.multiple_of(core * half, half), half), :] = own[...]
        full[pl.ds(pl.multiple_of((1 - core) * half, half), half), :] = oth[...]
        values[...] = full[:, 3 * LANES :].T

    rows = pl.ds(pl.multiple_of(block * TILE, TILE), TILE)
    query = stack_heads(full, rows)
    start, place = block_limits(start_ref, block)
    top[...] = jnp.full(top.shape, -1e30, F32)
    total[...] = jnp.zeros(total.shape, F32)
    acc[...] = jnp.zeros(acc.shape, F32)

    def step(number, _):
        keys = pl.ds(pl.multiple_of(number * TILE, TILE), TILE)
        scores = dot(full[keys, 2 * LANES : 3 * LANES], query, NT) * (FACTOR * LOG2E)
        scores = jnp.where(allowed_keys(number, start, place), scores, -1e30)
        before = top[...]
        now = jnp.maximum(before, jnp.max(scores, axis=0, keepdims=True))
        weight = jnp.exp2(scores - now)
        scale = jnp.exp2(before - now)
        top[...] = now
        total[...] = total[...] * scale + jnp.sum(weight, axis=0, keepdims=True)
        acc[...] = acc[...] * scale + dot(values[:, keys], weight.astype(LOW))
        return 0

    lax.fori_loop(info[1 + block], block + 1, step, 0)
    lse[...] = top[...] + jnp.log2(total[...])
    result = (acc[...] / total[...]).T.astype(LOW)
    out[:, :LANES] = result[:TILE]
    out[:, LANES:] = result[TILE:]
    mine = (block // (half // TILE)) == core
    for target, wanted in ((keep, mine), (send, jnp.logical_not(mine))):

        @pl.when(wanted)
        def _(target=target):
            target[:, :HEAD] = result[:TILE, :HEAD]
            target[:, HEAD:] = result[TILE:, :HEAD]


def attend(info, own, oth, start):
    half = own.shape[0]
    tokens = 2 * half
    per_half = half // TILE
    outs = (
        shape((half, 2 * HEAD)),
        shape((half, 2 * HEAD)),
        shape((tokens, 2 * LANES)),
        shape((1, 2 * tokens), F32),
    )
    return call(
        attend_kernel,
        outs,
        [whole(own), whole(oth), whole(start)],
        (
            pl.BlockSpec((TILE, 2 * HEAD), lambda b, s: (jnp.clip(b - s[0] * per_half, 0, per_half - 1), 0)),
            pl.BlockSpec((TILE, 2 * HEAD), lambda b, s: (jnp.clip(b - (1 - s[0]) * per_half, 0, per_half - 1), 0)),
            pl.BlockSpec((TILE, 2 * LANES), lambda b, s: (b, 0)),
            pl.BlockSpec((1, 2 * TILE), lambda b, s: (0, b)),
        ),
        grid=(tokens // TILE,),
        scratch=(
            pltpu.VMEM((tokens, 4 * LANES), LOW),
            pltpu.VMEM((LANES, tokens), LOW),
            pltpu.VMEM((1, 2 * TILE), F32),
            pltpu.VMEM((1, 2 * TILE), F32),
            pltpu.VMEM((LANES, 2 * TILE), F32),
        ),
        prefetch=1,
        flops=4 * tokens * tokens * LANES * 2,
        moved=bytes_of(own, oth, *outs),
    )(info, own, oth, start)


def turn_back(part, cos, sin):
    return part * cos - pltpu.roll(part, LANES // 2, 1) * sin


def attend_back_kernel(
    info, own, oth, g_own, g_oth, out, lse, start_ref, cos, sin,
    keep, send, full, grads, keys_t, d_keys, d_values, d_query, result,
):
    block = pl.program_id(0)
    core = info[0]
    half = own.shape[0]

    @pl.when(block == 0)
    def _():
        mine = pl.ds(pl.multiple_of(core * half, half), half)
        theirs = pl.ds(pl.multiple_of((1 - core) * half, half), half)
        full[mine, :] = own[...]
        full[theirs, :] = oth[...]
        grads[mine, :] = g_own[...]
        grads[theirs, :] = g_oth[...]
        keys_t[...] = full[:, 2 * LANES : 3 * LANES].T
        d_keys[...] = jnp.zeros(d_keys.shape, F32)
        d_values[...] = jnp.zeros(d_values.shape, F32)

    rows = pl.ds(pl.multiple_of(block * TILE, TILE), TILE)
    query = stack_heads(full, rows)
    grad = stack_heads(grads, rows)
    reply = stack_heads(out, slice(None))
    start, place = block_limits(start_ref, block)
    level = lse[...]
    delta = jnp.sum((grad.astype(F32) * reply.astype(F32)).T, axis=0, keepdims=True)
    d_query[...] = jnp.zeros(d_query.shape, F32)

    def step(number, _):
        keys = pl.ds(pl.multiple_of(number * TILE, TILE), TILE)
        scores = dot(full[keys, 2 * LANES : 3 * LANES], query, NT) * (FACTOR * LOG2E)
        scores = jnp.where(allowed_keys(number, start, place), scores, -1e30)
        weight = jnp.exp2(scores - level)
        pressure = dot(full[keys, 3 * LANES :], grad, NT)
        slope = (weight * (pressure - delta) * FACTOR).astype(LOW)
        d_values[keys, :] += dot(weight.astype(LOW), grad)
        d_keys[keys, :] += dot(slope, query)
        d_query[...] += dot(keys_t[:, keys], slope)
        return 0

    lax.fori_loop(info[1 + block], block + 1, step, 0)
    turned = d_query[...].T
    for h in range(2):
        part = turned[h * TILE : (h + 1) * TILE]
        result[rows, h * LANES : (h + 1) * LANES] = turn_back(part, cos[rows, :], sin[rows, :]).astype(LOW)

    @pl.when(block == pl.num_programs(0) - 1)
    def _():
        mine = pl.ds(pl.multiple_of(core * half, half), half)
        theirs = pl.ds(pl.multiple_of((1 - core) * half, half), half)
        for target, which in ((keep, mine), (send, theirs)):
            target[:, : 2 * LANES] = result[which, :]
            target[:, 2 * LANES : 3 * LANES] = turn_back(
                d_keys[which, :], cos[which, :], sin[which, :]
            ).astype(LOW)
            target[:, 3 * LANES :] = d_values[which, :].astype(LOW)


def attend_back(info, own, oth, g_own, g_oth, out, lse, start, cos, sin):
    half = own.shape[0]
    tokens = 2 * half
    outs = (shape((half, 4 * LANES)), shape((half, 4 * LANES)))
    return call(
        attend_back_kernel,
        outs,
        [
            whole(own),
            whole(oth),
            whole(g_own),
            whole(g_oth),
            pl.BlockSpec((TILE, 2 * LANES), lambda b, s: (b, 0)),
            pl.BlockSpec((1, 2 * TILE), lambda b, s: (0, b)),
            whole(start),
            whole(cos),
            whole(sin),
        ],
        tuple(whole(o) for o in outs),
        grid=(tokens // TILE,),
        scratch=(
            pltpu.VMEM((tokens, 4 * LANES), LOW),
            pltpu.VMEM((tokens, 2 * LANES), LOW),
            pltpu.VMEM((LANES, tokens), LOW),
            pltpu.VMEM((tokens, LANES), F32),
            pltpu.VMEM((tokens, LANES), F32),
            pltpu.VMEM((LANES, 2 * TILE), F32),
            pltpu.VMEM((tokens, 2 * LANES), LOW),
        ),
        prefetch=1,
        flops=10 * tokens * tokens * LANES * 2,
        moved=bytes_of(own, oth, g_own, g_oth, out, *outs),
    )(info, own, oth, g_own, g_oth, out, lse, start, cos, sin)


def middle_kernel(h0, h1, h2, h3, x0, x1, x2, x3, weight, gain, second, middle, r2):
    heads = jnp.concatenate([h0[...], h1[...], h2[...], h3[...]], axis=1)
    x = jnp.concatenate([x0[...], x1[...], x2[...], x3[...]], axis=1).astype(F32)
    value = x + dot(heads, weight[...])
    inverse = lax.rsqrt(jnp.mean(value * value, axis=1, keepdims=True) + EPSILON)
    second[...] = (value * inverse * gain[...]).astype(LOW)
    middle[...] = value[:, : middle.shape[1]]
    r2[...] = jnp.broadcast_to(inverse, r2.shape)


def middle_of(heads, xs, weight, gain):
    tokens, width = xs[0].shape
    rows = lambda n: pl.BlockSpec((TILE, n), lambda b: (b, 0))
    outs = (shape((tokens, 4 * width)), shape((tokens, width), F32), shape((tokens, LANES), F32))
    return call(
        middle_kernel,
        outs,
        [rows(width)] * 8 + [whole(weight), whole(gain)],
        tuple(rows(o.shape[1]) for o in outs),
        grid=(tokens // TILE,),
        flops=2 * tokens * 16 * width * width,
        moved=bytes_of(*heads, *xs, weight, *outs),
    )(*heads, *xs, weight, gain)


def feed_kernel(second, cot, g_own, u_own, g_oth, u_oth, d_own, d_oth, hidden_own, hidden_oth, back_own, back_oth):
    block = pl.program_id(0)
    per = pl.num_programs(0) // 2
    units = hidden_own.shape[1]

    def body(gate_w, up_w, down_w, hidden, back, at):
        gate = dot(second[...], gate_w[...])
        up = dot(second[...], up_w[...])
        hidden_grad = dot(cot[...], down_w[...], NT)
        share = 1.0 / (1.0 + jnp.exp(-gate))
        silu = gate * share
        hidden[:, pl.ds(pl.multiple_of(at, TILE), TILE)] = (silu * up).astype(LOW)
        back[:, pl.ds(pl.multiple_of(at, TILE), TILE)] = (
            hidden_grad * up * share * (1.0 + gate * (1.0 - share))
        ).astype(LOW)
        back[:, pl.ds(pl.multiple_of(units + at, TILE), TILE)] = (hidden_grad * silu).astype(LOW)

    @pl.when(block < per)
    def _():
        body(g_own, u_own, d_own, hidden_own, back_own, block * TILE)

    @pl.when(block >= per)
    def _():
        body(g_oth, u_oth, d_oth, hidden_oth, back_oth, (block - per) * TILE)


def feed(second, cot, gu_own, gu_oth, d_own, d_oth):
    tokens, model = second.shape
    units = gu_own.shape[1] // 2
    per = units // TILE
    early = lambda b: jnp.minimum(b, per - 1)
    late = lambda b: jnp.maximum(b - per, 0)
    column = lambda at: pl.BlockSpec((model, TILE), lambda b: (0, at(b)))
    down = lambda at: pl.BlockSpec((TILE, model), lambda b: (at(b), 0))
    outs = (shape((tokens, units)), shape((tokens, units)), shape((tokens, 2 * units)), shape((tokens, 2 * units)))
    return call(
        feed_kernel,
        outs,
        [
            whole(second),
            whole(cot),
            column(early),
            column(lambda b: per + early(b)),
            column(late),
            column(lambda b: per + late(b)),
            down(early),
            down(late),
        ],
        tuple(whole(o) for o in outs),
        grid=(2 * per,),
        flops=12 * tokens * model * units,
        moved=bytes_of(second, cot, gu_own, gu_oth, d_own, d_oth, *outs),
    )(second, cot, gu_own, gu_own, gu_oth, gu_oth, d_own, d_oth)


def back_kernel(dims, a_own, a_oth, w_own, w_oth, *rest):
    value = dot(a_own[...], w_own[...], dims) + dot(a_oth[...], w_oth[...], dims)
    if len(rest) == 5:
        against, own, far, near, sums = rest
        sums[...] = jnp.broadcast_to(
            jnp.sum(value * against[...].astype(F32), axis=1, keepdims=True), sums.shape
        )
    else:
        own, far, near = rest
    width = own.shape[1]
    low = value.astype(LOW)
    own[...] = low[:, :width]
    return low, far, near, width


def back_first(dims, *refs):
    low, far, near, width = back_kernel(dims, *refs)
    far[:, :width] = low[:, width : 2 * width]
    far[:, width:] = low[:, 3 * width :]
    near[...] = low[:, 2 * width : 3 * width]


def back_second(dims, *refs):
    low, far, near, width = back_kernel(dims, *refs)
    far[...] = low[:, 2 * width :]
    near[...] = low[:, width : 2 * width]


def partial_half(which, dims, a_own, a_oth, w_own, w_oth, against):
    tokens, depth = a_own.shape
    model = w_own.shape[0] if dims == NT else w_own.shape[1]
    half, width = tokens // 2, model // 4
    blocks = half // TILE
    read = lambda n: pl.BlockSpec((TILE, n), lambda b: (which * blocks + b, 0))
    write = lambda n: pl.BlockSpec((TILE, n), lambda b: (b, 0))
    outs = [shape((half, width)), shape((half, 2 * width)), shape((half, width))]
    args = [a_own, a_oth, w_own, w_oth]
    specs = [read(depth), read(depth), whole(w_own), whole(w_oth)]
    if against is not None:
        outs.append(shape((half, LANES), F32))
        args.append(against)
        specs.append(read(model))
    return call(
        functools.partial(back_second if which else back_first, dims),
        tuple(outs),
        specs,
        tuple(write(o.shape[1]) for o in outs),
        grid=(blocks,),
        flops=4 * half * depth * model,
        moved=bytes_of(w_own, w_oth, *outs) + half * 4 * depth,
    )(*args)


def partial_sums(dims, a_own, a_oth, w_own, w_oth, against=None):
    first = partial_half(0, dims, a_own, a_oth, w_own, w_oth, against)
    second = partial_half(1, dims, a_own, a_oth, w_own, w_oth, against)
    sums = None if against is None else jnp.concatenate([first[3][:, 0], second[3][:, 0]])
    return (first[0], first[1], first[2], second[0], second[1], second[2]), sums


def feed_place_kernel(row_ref, piece, gate, up, down):
    units = gate.shape[1]
    gate[...] = piece[0, :, :units].astype(F32)
    up[...] = piece[0, :, units : 2 * units].astype(F32)
    down[...] = piece[0, :, 2 * units :].astype(F32).T


def feed_place(row, pieces):
    _, depth, triple = pieces.shape
    units = triple // 3
    outs = (shape((depth, 4 * units), F32), shape((depth, 4 * units), F32), shape((4 * units, depth), F32))
    return call(
        feed_place_kernel,
        outs,
        [pl.BlockSpec((1, depth, triple), lambda j, s: (jnp.bitwise_xor(s[0], j), 0, 0))],
        (
            pl.BlockSpec((depth, units), lambda j, s: (0, j)),
            pl.BlockSpec((depth, units), lambda j, s: (0, j)),
            pl.BlockSpec((units, depth), lambda j, s: (j, 0)),
        ),
        grid=(4,),
        prefetch=1,
        moved=bytes_of(pieces, *outs),
    )(row, pieces)


def mix_place_kernel(row_ref, pieces, heads, query, key, value, output):
    row = row_ref[0]
    wide, narrow = query.shape[1] // 4, key.shape[1] // 4
    for j in range(4):
        piece = pieces[jnp.bitwise_xor(row, j)].astype(F32)
        query[:, j * wide : (j + 1) * wide] = piece[:, :wide]
        key[:, j * narrow : (j + 1) * narrow] = piece[:, wide : wide + narrow]
        value[:, j * narrow : (j + 1) * narrow] = piece[:, wide + narrow :]
        output[j * wide : (j + 1) * wide, :] = heads[jnp.bitwise_xor(row, j)].astype(F32)


def mix_place(row, pieces, heads):
    _, depth, width = pieces.shape
    wide, narrow = width // 2, width // 4
    outs = (
        shape((depth, 4 * wide), F32),
        shape((depth, 4 * narrow), F32),
        shape((depth, 4 * narrow), F32),
        shape((4 * wide, depth), F32),
    )
    return call(
        mix_place_kernel,
        outs,
        [whole(pieces), whole(heads)],
        tuple(whole(o) for o in outs),
        grid=(1,),
        prefetch=1,
        moved=bytes_of(pieces, heads, *outs),
    )(row, pieces, heads)


def sequence_starts(lengths, tokens):
    places = jnp.arange(tokens, dtype=jnp.int32)
    starts = jnp.zeros((tokens,), jnp.int32)
    end = jnp.zeros((), jnp.int32)
    for k in range(lengths.shape[0]):
        end = end + lengths[k]
        starts = jnp.where(places >= end, end, starts)
    return places, starts


def tables(places):
    lane = jnp.arange(LANES, dtype=jnp.int32)
    entry = lane % (LANES // 2)
    frequency = THETA ** (-2.0 * entry.astype(F32) / HEAD)
    real = entry < SIDE
    angles = places.astype(F32)[:, None] * frequency[None, :]
    cosine = jnp.where(real[None, :], jnp.cos(angles), 0.0)
    sign = jnp.where(lane < LANES // 2, -1.0, 1.0)
    sine = jnp.where(real[None, :], jnp.sin(angles) * sign[None, :], 0.0)
    return cosine, sine


def spread_matrix():
    source = jnp.arange(4 * HEAD, dtype=jnp.int32)
    head, entry = source // HEAD, source % HEAD
    inside = jnp.where((head < 3) & (entry >= SIDE), entry - SIDE + LANES // 2, entry)
    target = head * LANES + inside
    return (target[:, None] == jnp.arange(4 * LANES, dtype=jnp.int32)[None, :]).astype(LOW)


def pad_heads(rows):
    heads = rows.shape[0] // HEAD
    split = rows.reshape(heads, HEAD, rows.shape[1])
    return jnp.pad(split, ((0, 0), (0, LANES - HEAD), (0, 0))).reshape(heads * LANES, rows.shape[1])


def on_device(
    layer_input,
    first_gain,
    query_weight,
    key_projection_weight,
    value_projection_weight,
    output_weight,
    second_gain,
    gate_weight,
    up_weight,
    down_weight,
    sequence_lengths,
    cotangent,
):
    row = lax.axis_index("row")
    core = lax.axis_index("col")
    blocks = lax.axis_size("dp")
    row_info = row.reshape(1).astype(jnp.int32)
    half, width = layer_input.shape
    tokens, model = 2 * half, 4 * width
    units = gate_weight.shape[1] // 4
    relative = [jnp.bitwise_xor(row, i) for i in range(4)]

    packed = pack(row_info, query_weight, key_projection_weight, value_projection_weight)
    xs = gather_row(layer_input)
    gains = jnp.stack([first_gain, second_gain])
    gains = jnp.concatenate(exchange_row([gains] * 4), axis=1)
    mixer = jnp.concatenate(exchange_row([packed[i] for i in range(4)]), axis=0)
    w_own = dot(mixer, spread_matrix()).astype(LOW)
    w_oth = other(w_own)

    places, starts = sequence_starts(sequence_lengths[0], tokens)
    cosine, sine = tables(places - starts)
    start_row = starts[None, :]
    first_blocks = starts[::TILE] // TILE
    info = jnp.concatenate([core.reshape(1), first_blocks]).astype(jnp.int32)
    cos_own = lax.dynamic_slice_in_dim(cosine, core * half, half, 0)
    sin_own = lax.dynamic_slice_in_dim(sine, core * half, half, 0)

    first, r1, qkv_own, qkv_oth = project(xs, gains[:1], w_own, w_oth, cos_own, sin_own)
    qkv_got = other(qkv_oth)
    keep, send, attended, lse = attend(info, qkv_own, qkv_got, start_row)
    heads = gather_row(jnp.concatenate([keep, other(send)], axis=1))

    out_w = jnp.concatenate(gather_row(output_weight), axis=1)
    out_w_oth = other(out_w)
    chunk = out_w.shape[0] // 4
    ordered = []
    for i in range(4):
        for matrix in (out_w, out_w_oth):
            ordered.append(lax.dynamic_slice_in_dim(matrix, relative[i] * chunk, chunk, 0))
    out_full = jnp.concatenate(ordered, axis=0)
    out_mine = pad_heads(out_full[: 2 * chunk])

    gate_up = [
        jnp.concatenate(
            [lax.dynamic_slice_in_dim(w, relative[i] * units, units, 1) for w in (gate_weight, up_weight)], axis=1
        )
        for i in range(4)
    ]
    gu_own = jnp.concatenate(exchange_row(gate_up), axis=0)
    gu_oth = other(gu_own)
    down = [lax.dynamic_slice_in_dim(down_weight, relative[i] * units, units, 0) for i in range(4)]
    d_own = jnp.concatenate(exchange_row(down), axis=1)
    d_oth = other(d_own)
    cot = jnp.concatenate(gather_row(cotangent), axis=1)

    second, middle, r2 = middle_of(heads, xs, out_full, gains[1:])
    hidden_own, hidden_oth, back_own, back_oth = feed(second, cot, gu_own, gu_oth, d_own, d_oth)

    parts, sums = partial_sums(NT, back_own, back_oth, gu_own, gu_oth, second)
    second_grad = scatter_row(parts)
    inner = total_row(sums.reshape(8, half // 8)).reshape(half)
    parts, _ = partial_sums(NN, hidden_own, hidden_oth, d_own, d_oth)
    layer_output = (middle + scatter_row(parts)).astype(LOW)

    def both(own, oth):
        return own.astype(LOW), oth.astype(LOW)

    g_own, g_oth = both(dot(second, back_own, TN), dot(second, back_oth, TN))
    c_own, c_oth = both(dot(cot, hidden_own, TN), dot(cot, hidden_oth, TN))
    feed_own = jnp.concatenate([g_own, c_own], axis=1)
    feed_oth = jnp.concatenate([g_oth, c_oth], axis=1)
    feed_sum = (feed_own.astype(F32) + other(feed_oth).astype(F32)).astype(LOW)
    feed_sum = feed_sum.reshape(4, width, 3 * units)
    share = width // blocks

    def finish(take):
        shard = chain_scatter(take, blocks)
        return shard

    feed_shard = finish(lambda s: lax.dynamic_slice_in_dim(feed_sum, s * share, share, 1))
    feed_shard = jnp.stack(exchange_row([feed_shard[i] for i in range(4)]))
    feed_all = chain_gather(feed_shard, blocks).reshape(4, width, 3 * units)
    gate_total, up_total, down_total = feed_place(row_info, feed_all)

    r2 = r2[:, :1]
    middle_grad = (
        cotangent.astype(F32)
        + r2 * second_gain[None, :] * second_grad
        - middle * (r2 * r2 * inner[:, None] / model)
    )
    second_gain_part = jnp.sum(second_grad * middle * r2, axis=0)
    branch = middle_grad.astype(LOW)
    branch_all = jnp.concatenate(gather_row(branch), axis=1)
    heads_grad = dot(branch_all, out_mine, NT).astype(LOW)
    grad_own = heads_grad[:, : 2 * LANES]
    grad_got = other(heads_grad[:, 2 * LANES :])
    back_keep, back_send = attend_back(
        info, qkv_own, qkv_got, grad_own, grad_got, attended, lse, start_row, cosine, sine
    )
    back_got = other(back_send)
    parts, sums = partial_sums(NT, back_keep, back_got, w_own, w_oth, first)
    first_grad = scatter_row(parts)
    inner = total_row(sums.reshape(8, half // 8)).reshape(half)
    r1 = r1[:, :1]
    inputs = layer_input.astype(F32)
    input_gradient = (
        middle_grad + r1 * first_gain[None, :] * first_grad - inputs * (r1 * r1 * inner[:, None] / model)
    )
    first_gain_part = jnp.sum(first_grad * inputs * r1, axis=0)

    spread = spread_matrix()
    flat_own = dot(back_keep, spread, NT).astype(LOW)
    flat_got = dot(back_got, spread, NT).astype(LOW)
    q_own, q_oth = both(dot(first, flat_own, TN), dot(first, flat_got, TN))
    heads_all = jnp.concatenate(heads, axis=1)
    o_all = dot(heads_all, branch, TN).astype(LOW).reshape(4, 2, chunk, width)
    mix_own = jnp.concatenate([q_own.reshape(4, width, 2 * chunk), o_all[:, 0]], axis=1)
    mix_oth = jnp.concatenate([q_oth.reshape(4, width, 2 * chunk), o_all[:, 1]], axis=1)
    mix_sum = (mix_own.astype(F32) + other(mix_oth).astype(F32)).astype(LOW)
    small = chunk // blocks

    def take(s):
        return jnp.concatenate(
            [
                lax.dynamic_slice_in_dim(mix_sum, s * share, share, 1),
                lax.dynamic_slice_in_dim(mix_sum, width + s * small, small, 1),
            ],
            axis=1,
        )

    mix_shard = finish(take)
    mix_shard = jnp.concatenate(
        [jnp.stack(exchange_row([mix_shard[i, :share] for i in range(4)])), mix_shard[:, share:]], axis=1
    )
    mix_all = chain_gather(mix_shard, blocks)
    query_total, key_total, value_total, output_total = mix_place(
        row_info,
        mix_all[:, :, :share].reshape(4, width, 2 * chunk),
        mix_all[:, :, share:].reshape(4, chunk, width),
    )

    gain_parts = jnp.stack([first_gain_part, second_gain_part])
    gain_parts = gain_parts + other(gain_parts)
    gain_total = gain_parts
    for step in range(1, blocks):
        gain_total = gain_total + lax.ppermute(
            gain_parts, "dp", [(i, (i + step) % blocks) for i in range(blocks)]
        )
    return (
        layer_output,
        input_gradient,
        query_total,
        key_total,
        value_total,
        output_total,
        gate_total,
        up_total,
        down_total,
        gain_total[0],
        gain_total[1],
    )


def solution(mesh):
    return jax.shard_map(
        on_device,
        mesh=mesh,
        in_specs=(
            P(("dp", "col"), "row"),
            P("row"),
            P("row", "col"),
            P("row", "col"),
            P("row", "col"),
            P("col", "row"),
            P("row"),
            P("row", "col"),
            P("row", "col"),
            P("col", "row"),
            P("dp", None),
            P(("dp", "col"), "row"),
        ),
        out_specs=(
            P(("dp", "col"), "row"),
            P(("dp", "col"), "row"),
            P("row", "col"),
            P("row", "col"),
            P("row", "col"),
            P("col", "row"),
            P("row", "col"),
            P("row", "col"),
            P("col", "row"),
            P("row"),
            P("row"),
        ),
        check_vma=False,
    )
```

time: 1410 us -> 752 us (0.53)
  waiting for transfers between devices: 932 us -> 287 us
  matrix products: 187 us -> 35.1 us
  starting transfers between devices: 1.67 us -> 149 us
  Pallas kernels: 0 us -> 113 us
  blocking collectives: 56.2 us -> 0 us
  local copies, waits for them, and re-layouts: 109 us -> 72.9 us
    all_gather x8 -> x0, waiting for transfers between devices: 370 us -> none  [the longest x2 227 us: return_rows(): return lax.all_gather(columns_low, 'row', axis=1, tiled=True)]
    reduce_scatter x7 -> x0, waiting for transfers between devices: 291 us -> none  [the longest x1 144 us: widen(): lax.psum_scatter(partial_value.astype(jnp.bfloat16), 'row', scatter_dimen...]
    ppermute x0 -> x94, waiting for transfers between devices: none -> 287 us  [the longest x56 115 us: swap(): return lax.ppermute(value, 'row', [(i, i ^ step) for i in range(4)])]
    psum x1 -> x0, waiting for transfers between devices: 201 us -> none  [on_device(): lax.psum(query_total.astype(jnp.bfloat16), 'dp').astype(jnp.float32)]
    dot_general x40 -> x9, matrix products: 187 us -> 35.1 us  [dot(): return lax.dot_general(left, right, dims, preferred_element_type=F32)]
    ppermute x0 -> x94, starting transfers between devices: none -> 149 us  [the longest x56 76.4 us: swap(): return lax.ppermute(value, 'row', [(i, i ^ step) for i in range(4)])]
    pallas_call x0 -> x14, Pallas kernels: none -> 113 us  [the longest x6 31.3 us: partial_half(): call(functools.partial(back_second if which else back_first, dims), tuple...]
    unnamed x18 -> x0, waiting for transfers between devices: 69.4 us -> none
  transfers between devices with their start and end apart: 17 -> 94, of which waited for: 13 -> 29; matrix products, arithmetic and copies ran while one was open for 8% -> 23% of each run, Pallas kernels for 0% -> 10%
where the time goes in v1:
time: 752 us; the launch traced here: 741 us
  waiting for transfers between devices  287 us (38%)
  starting transfers between devices  149 us (20%)
  Pallas kernels  113 us (15%)
  other arithmetic  79.5 us (11%)
  local copies, waits for them, and re-layouts  72.9 us (10%)
  matrix products  35.1 us (5%)
    ppermute x56, waiting for transfers between devices, swap(): return lax.ppermute(value, 'row', [(i, i ^ step) for i in range(4)])  115 us
    ppermute x6, waiting for transfers between devices, chain_gather(): lax.ppermute(left, 'dp', [(count - 1 - i, count - 1 - j) for i, j in ups])  88.9 us
    ppermute x56, starting transfers between devices, swap(): return lax.ppermute(value, 'row', [(i, i ^ step) for i in range(4)])  76.4 us
    ppermute x6, starting transfers between devices, chain_scatter(): right = lax.ppermute(up, 'dp', ups)  42 us
    dot_general x9, matrix products, dot(): return lax.dot_general(left, right, dims, preferred_element_type=F32)  35.1 us
    ppermute x6, waiting for transfers between devices, chain_scatter(): lax.ppermute(down, 'dp', [(count - 1 - i, count - 1 - j) for i, j in ups])  33.3 us
    unnamed x185, local copies, waits for them, and re-layouts  31.5 us
    pallas_call x6, Pallas kernels, partial_half(): call(functools.partial(back_second if which else back_first, dims), tuple...  31.3 us
  transfers between devices with their start and end apart: 94, of which 29 were waited for; matrix products, arithmetic and copies ran while one was open for 23% of the time, Pallas kernels for 10%

profile of v1, /device:TPU:0, one launch (start us, length us, event | category | flops | bytes accessed | tf_op | source)
XLA Modules:
  0.0 741.2 jit_solution(1998313701793631790)
XLA Ops:
  2.0 3.0 collective-permute-start.4
  21.2 5.0 fusion.26
  34.0 31.2 %collective-permute-done.9 = bf16[384,384]{1,0:T(8,128)(2,1)S(1)} collective-permute-done((bf16[384,384]{1,0:T(8,128)(2,1)S(1)}, bf16[384,384]{1,0:T(8,128)(2,1)S(1)}, u32[]{:S(2)}, u32[]{:S(2)}) %collective-permute-start.9) | collective-permute-done | bytes 294944 | tf_op jit(solution)/shard_map/ppermute | solution.py:31
  82.1 3.8 collective-permute-done.31
  96.8 3.3 maximum_maximum_fusion.1
  100.1 6.6 collective-permute-done.22
  111.2 6.3 collective-permute-done.2
  117.5 3.8 collective-permute-start.28
  124.9 7.8 %shard_map.204 = (bf16[1024,1536]{1,0:T(8,128)(2,1)}, f32[1024,128]{1,0:T(8,128)S(1)}, bf16[1024,512]{1,0:T(8,128)(2,1)S(1)}, bf16[1024,512]{1,0:T(8,128)(2,1)}) custom-call(bf16[1024,384]{1,0:T(8,128)(2,1)S(1)} %copy-done.4, bf16[1024,384]{1,0:T(8,128)(2,1)S(1)} %copy-done.30, bf16[1024,384]{1,0:T(8,128)(2,1)S(1)} %copy-done.32, ...), custom_call_target="tpu_custom_call" | custom-call | flops 3221225472 | bytes 12058624 | tf_op jit(solution)/shard_map/pallas_call | solution.py:181
  134.3 16.7 %collective-permute-done.27 = bf16[384,1024]{1,0:T(8,128)(2,1)S(1)} collective-permute-done((bf16[384,1024]{1,0:T(8,128)(2,1)S(1)}, bf16[384,1024]{1,0:T(8,128)(2,1)S(1)}, u32[]{:S(2)}, u32[]{:S(2)}) %collective-permute-start.27) | collective-permute-done | bytes 786464 | tf_op jit(solution)/shard_map/ppermute | solution.py:31
  154.1 6.3 pad_maximum_fusion.1.g_own.u_own.refs_2_
  160.5 2.6 constant_dynamic-update-slice_fusion.5
  163.1 11.3 %maximum_maximum_fusion.cot = bf16[1024,1536]{1,0:T(8,128)(2,1)} fusion(bf16[512,384]{1,0:T(8,128)(2,1)S(1)} %collective-permute-done.25, bf16[512,384]{1,0:T(8,128)(2,1)S(1)} %collective-permute-done.24, bf16[1024,384]{1,0:T(8,128)(2,1)S(1)} %collective-permute-done.23, bf16[1024,384]{1,0:T(8,128)(2,1)S(1)} %collective-permute-done.22, ...), kind=kLoop, calls=%fused_computation.5 | loop fusion | flops 15728640 | bytes 6291456 | tf_op jit(solution)/shard_map/concatenate | solution.py:683
  174.5 17.2 %shard_map.205 = (bf16[1024,192]{1,0:T(8,128)(2,1)S(1)}, bf16[1024,192]{1,0:T(8,128)(2,1)S(1)}, bf16[2048,256]{1,0:T(8,128)(2,1)S(1)}, f32[1,4096]{1,0:T(1,128)S(1)}) custom-call(s32[9]{0:T(128)S(1)} %pad_add_fusion.info, bf16[1024,512]{1,0:T(8,128)(2,1)S(1)} %get-tuple-element.57.own, bf16[1024,512]{1,0:T(8,128)(2,1)S(1)} %collective-permute-done.11.oth, ...), custom_call_target="tpu_custom_call" | custom-call | flops 4294967296 | bytes 3948544 | tf_op jit(solution)/shard_map/pallas_call | solution.py:263
  205.1 11.3 %collective-permute-done.13.h1 = bf16[1024,384]{1,0:T(8,128)(2,1)S(1)} collective-permute-done((bf16[1024,384]{1,0:T(8,128)(2,1)S(1)}, bf16[1024,384]{1,0:T(8,128)(2,1)S(1)}, u32[]{:S(2)}, u32[]{:S(2)}) %collective-permute-start.13) | collective-permute-done | bytes 786464 | tf_op jit(solution)/shard_map/ppermute | solution.py:31
  216.4 2.4 collective-permute-start.15
  224.3 3.3 collective-permute-done.15
  229.2 9.8 %shard_map.206 = (bf16[1024,1536]{1,0:T(8,128)(2,1)}, f32[1024,384]{1,0:T(8,128)}, f32[1024,128]{1,0:T(8,128)S(1)}) custom-call(bf16[1024,384]{1,0:T(8,128)(2,1)S(1)} %pad_maximum_fusion.8.h0, bf16[1024,384]{1,0:T(8,128)(2,1)S(1)} %collective-permute-done.13.h1, bf16[1024,384]{1,0:T(8,128)(2,1)S(1)} %collective-permute-done.14.h2, ...), custom_call_target="tpu_custom_call" | custom-call | flops 4831838208 | bytes 16252928 | tf_op jit(solution)/shard_map/pallas_call | solution.py:399
  239.9 17.7 %shard_map.207 = (bf16[1024,512]{1,0:T(8,128)(2,1)S(1)}, bf16[1024,512]{1,0:T(8,128)(2,1)S(1)}, bf16[1024,1024]{1,0:T(8,128)(2,1)}, bf16[1024,1024]{1,0:T(8,128)(2,1)}) custom-call(bf16[1024,1536]{1,0:T(8,128)(2,1)} %get-tuple-element.62.second.refs_4_, bf16[1024,1536]{1,0:T(8,128)(2,1)} %maximum_maximum_fusion.cot, bf16[1536,1024]{1,0:T(8,128)(2,1)} %copy-done.45, ...), custom_call_target="tpu_custom_call" | custom-call | flops 9663676416 | bytes 22020096 | tf_op jit(solution)/shard_map/pallas_call | solution.py:445
  261.1 7.6 %shard_map.210 = (bf16[512,384]{1,0:T(8,128)(2,1)S(1)}, bf16[512,768]{1,0:T(8,128)(2,1)}, bf16[512,384]{1,0:T(8,128)(2,1)S(1)}, f32[512,128]{1,0:T(8,128)S(1)}) custom-call(bf16[1024,1024]{1,0:T(8,128)(2,1)S(1)} %copy-done, bf16[1024,1024]{1,0:T(8,128)(2,1)S(1)} %copy-done.1, bf16[1536,1024]{1,0:T(8,128)(2,1)} %copy-done.45, ...), custom_call_target="tpu_custom_call" | custom-call | flops 3221225472 | bytes 10223616 | tf_op jit(solution)/shard_map/pallas_call | solution.py:507
  270.3 7.6 %shard_map.211 = (bf16[512,384]{1,0:T(8,128)(2,1)S(1)}, bf16[512,768]{1,0:T(8,128)(2,1)}, bf16[512,384]{1,0:T(8,128)(2,1)S(1)}, f32[512,128]{1,0:T(8,128)S(1)}) custom-call(bf16[1024,1024]{1,0:T(8,128)(2,1)S(1)} %copy-done, bf16[1024,1024]{1,0:T(8,128)(2,1)S(1)} %copy-done.1, bf16[1536,1024]{1,0:T(8,128)(2,1)} %copy-done.45, ...), custom_call_target="tpu_custom_call" | custom-call | flops 3221225472 | bytes 10223616 | tf_op jit(solution)/shard_map/pallas_call | solution.py:507
  281.7 5.6 convolution_convert_fusion
  287.3 5.1 convolution_convert_fusion.1
  296.0 2.5 pad_maximum_fusion
  298.5 4.1 shard_map.208
  304.1 4.2 shard_map.209
  319.0 11.6 %collective-permute-done.34 = bf16[512,768]{1,0:T(8,128)(2,1)} collective-permute-done((bf16[512,768]{1,0:T(8,128)(2,1)}, bf16[512,768]{1,0:T(8,128)(2,1)}, u32[]{:S(2)}, u32[]{:S(2)}) %collective-permute-start.34) | collective-permute-done | bytes 786464 | tf_op jit(solution)/shard_map/ppermute | solution.py:31
  333.3 6.3 collective-permute-done.39
  345.7 3.0 convolution_convert_fusion.3
  348.7 5.3 concatenate.154
  367.4 3.0 convolution_convert_fusion.6
  370.4 3.6 collective-permute-done.48
  374.0 3.4 fusion.14
  380.8 22.7 %shard_map.212 = (bf16[1024,512]{1,0:T(8,128)(2,1)S(1)}, bf16[1024,512]{1,0:T(8,128)(2,1)}) custom-call(s32[9]{0:T(128)S(1)} %pad_add_fusion.info, bf16[1024,512]{1,0:T(8,128)(2,1)S(1)} %copy-done.43, bf16[1024,512]{1,0:T(8,128)(2,1)S(1)} %copy-done.36, bf16[1024,256]{1,0:T(8,128)(2,1)S(1)} %get-tuple-element.158.g_own, ...), custom_call_target="tpu_custom_call" | custom-call | flops 10737418240 | bytes 6291456 | tf_op jit(solution)/shard_map/pallas_call | solution.py:354
  404.1 5.7 add_convert_fusion
  409.8 6.6 copy.90
  416.4 3.2 constant_dynamic-slice_fusion.1
  421.9 5.4 convolution_convert_fusion.5
  427.3 2.8 pad_maximum_fusion.2
  430.1 3.9 shard_map.213
  435.8 3.9 shard_map.214
  448.6 2.9 add_convert_fusion.6
  451.5 5.7 collective-permute-start.76
  457.2 5.4 convolution_convert_fusion.7
  465.0 2.4 add_convert_fusion.1
  469.5 13.2 %collective-permute-done.76 = bf16[4,96,1536]{2,1,0:T(8,128)(2,1)} collective-permute-done((bf16[4,96,1536]{2,1,0:T(8,128)(2,1)}, bf16[4,96,1536]{2,1,0:T(8,128)(2,1)}, u32[]{:S(2)}, u32[]{:S(2)}) %collective-permute-start.76) | collective-permute-done | bytes 1179680 | tf_op jit(solution)/shard_map/ppermute | solution.py:82
  482.7 3.0 add_convert_fusion.5
  490.7 4.4 collective-permute-start.60
  498.3 4.9 collective-permute-done.60
  503.3 4.4 collective-permute-start.61
  507.8 23.5 %collective-permute-start.77 = (bf16[4,96,1536]{2,1,0:T(8,128)(2,1)S(1)}, bf16[4,96,1536]{2,1,0:T(8,128)(2,1)S(1)}, u32[]{:S(2)}, u32[]{:S(2)}) collective-permute-start(bf16[4,96,1536]{2,1,0:T(8,128)(2,1)S(1)} %get-tuple-element.113), channel_id=1, source_target_pairs={{0,8},{8,16},{16,24},{1,9},{9,17},{17,25},{2,10},{10,18},{18,26},{... | collective-permute-start | bytes 3538952 | tf_op jit(solution)/shard_map/ppermute | solution.py:82
  536.9 33.3 %collective-permute-done.64 = bf16[4,144,384]{2,1,0:T(8,128)(2,1)S(1)} collective-permute-done((bf16[4,144,384]{2,1,0:T(8,128)(2,1)S(1)}, bf16[4,144,384]{2,1,0:T(8,128)(2,1)S(1)}, u32[]{:S(2)}, u32[]{:S(2)}) %collective-permute-start.64) | collective-permute-done | bytes 442400 | tf_op jit(solution)/shard_map/ppermute | solution.py:83
  575.9 2.9 multiply_reduce_fusion
  581.2 6.9 collective-permute-done.66
  589.0 3.3 collective-permute-start.68
  594.8 4.6 collective-permute-start.84
  601.0 27.0 %collective-permute-done.91 = f32[2,384]{1,0:T(2,128)S(1)} collective-permute-done((f32[2,384]{1,0:T(2,128)}, f32[2,384]{1,0:T(2,128)S(1)}, u32[]{:S(2)}, u32[]{:S(2)}) %collective-permute-start.91) | collective-permute-done | bytes 3104 | tf_op jit(solution)/shard_map/ppermute | solution.py:775
  628.0 2.6 collective-permute-start.93
  638.0 13.7 %collective-permute-done.71 = bf16[4,144,384]{2,1,0:T(8,128)(2,1)S(1)} collective-permute-done((bf16[4,144,384]{2,1,0:T(8,128)(2,1)S(1)}, bf16[4,144,384]{2,1,0:T(8,128)(2,1)S(1)}, u32[]{:S(2)}, u32[]{:S(2)}) %collective-permute-start.71) | collective-permute-done | bytes 442400 | tf_op jit(solution)/shard_map/ppermute | solution.py:101
  654.2 22.7 %collective-permute-done.85 = bf16[4,96,1536]{2,1,0:T(8,128)(2,1)S(1)} collective-permute-done((bf16[4,96,1536]{2,1,0:T(8,128)(2,1)}, bf16[4,96,1536]{2,1,0:T(8,128)(2,1)S(1)}, u32[]{:S(2)}, u32[]{:S(2)}) %collective-permute-start.85) | collective-permute-done | bytes 1179680 | tf_op jit(solution)/shard_map/ppermute | solution.py:101
  678.2 8.2 %collective-permute-done.73 = bf16[4,144,384]{2,1,0:T(8,128)(2,1)S(1)} collective-permute-done((bf16[4,144,384]{2,1,0:T(8,128)(2,1)S(1)}, bf16[4,144,384]{2,1,0:T(8,128)(2,1)S(1)}, u32[]{:S(2)}, u32[]{:S(2)}) %collective-permute-start.73) | collective-permute-done | bytes 442400 | tf_op jit(solution)/shard_map/ppermute | solution.py:101
  690.4 18.7 %collective-permute-done.87 = bf16[4,96,1536]{2,1,0:T(8,128)(2,1)S(1)} collective-permute-done((bf16[4,96,1536]{2,1,0:T(8,128)(2,1)S(1)}, bf16[4,96,1536]{2,1,0:T(8,128)(2,1)S(1)}, u32[]{:S(2)}, u32[]{:S(2)}) %collective-permute-start.87) | collective-permute-done | bytes 1179680 | tf_op jit(solution)/shard_map/ppermute | solution.py:101
  710.8 25.7 %collective-permute-done.89 = bf16[4,96,1536]{2,1,0:T(8,128)(2,1)S(1)} collective-permute-done((bf16[4,96,1536]{2,1,0:T(8,128)(2,1)S(1)}, bf16[4,96,1536]{2,1,0:T(8,128)(2,1)S(1)}, u32[]{:S(2)}, u32[]{:S(2)}) %collective-permute-start.89) | collective-permute-done | bytes 1179680 | tf_op jit(solution)/shard_map/ppermute | solution.py:101
  736.8 3.9 shard_map.216
  (453 shorter events, 196.4 us)
Async XLA Ops:
  2.0 26.1 %collective-permute-start.4 = (f32[2,384]{1,0:T(2,128)S(1)}, f32[2,384]{1,0:T(2,128)S(1)}, u32[]{:S(2)}, u32[]{:S(2)}) collective-permute-start(f32[2,384]{1,0:T(2,128)S(1)} %pad_maximum_fusion.18), channel_id=1, source_target_pairs={{0,2},{2,0},{4,6},{6,4},{1,3},{3,1},{5,7},{7,5},{8,10},{10,8},{12,... | collective-permute-start | bytes 9224 | tf_op jit(solution)/shard_map/ppermute | solution.py:31
  5.0 23.7 %collective-permute-start.5 = (f32[2,384]{1,0:T(2,128)S(1)}, f32[2,384]{1,0:T(2,128)S(1)}, u32[]{:S(2)}, u32[]{:S(2)}) collective-permute-start(f32[2,384]{1,0:T(2,128)S(1)} %pad_maximum_fusion.18), channel_id=1, source_target_pairs={{0,4},{2,6},{4,0},{6,2},{1,5},{3,7},{5,1},{7,3},{8,12},{10,14},{12... | collective-permute-start | bytes 9224 | tf_op jit(solution)/shard_map/ppermute | solution.py:31
  6.5 23.2 %collective-permute-start.6 = (f32[2,384]{1,0:T(2,128)S(1)}, f32[2,384]{1,0:T(2,128)S(1)}, u32[]{:S(2)}, u32[]{:S(2)}) collective-permute-start(f32[2,384]{1,0:T(2,128)S(1)} %pad_maximum_fusion.18), channel_id=1, source_target_pairs={{0,6},{2,4},{4,2},{6,0},{1,7},{3,5},{5,3},{7,1},{8,14},{10,12},{12... | collective-permute-start | bytes 9224 | tf_op jit(solution)/shard_map/ppermute | solution.py:31
  11.1 20.6 %collective-permute-start.7 = (bf16[384,384]{1,0:T(8,128)(2,1)}, bf16[384,384]{1,0:T(8,128)(2,1)}, u32[]{:S(2)}, u32[]{:S(2)}) collective-permute-start(bf16[384,384]{1,0:T(8,128)(2,1)} %get-tuple-element.156), channel_id=1, source_target_pairs={{0,2},{2,0},{4,6},{6,4},{1,3},{3,1},{5,7},{7,5},{8,10},{10,8},{12,... | collective-permute-start | bytes 884744 | tf_op jit(solution)/shard_map/ppermute | solution.py:31
  28.2 39.3 %collective-permute-start.17 = (bf16[768,384]{1,0:T(8,128)(2,1)}, bf16[768,384]{1,0:T(8,128)(2,1)}, u32[]{:S(2)}, u32[]{:S(2)}) collective-permute-start(bf16[768,384]{1,0:T(8,128)(2,1)} %param.17), channel_id=1, source_target_pairs={{0,2},{2,0},{4,6},{6,4},{1,3},{3,1},{5,7},{7,5},{8,10},{10,8},{12,... | collective-permute-start | bytes 1769480 | tf_op jit(solution)/shard_map/ppermute | solution.py:31
  28.7 40.5 %collective-permute-start.18 = (bf16[768,384]{1,0:T(8,128)(2,1)}, bf16[768,384]{1,0:T(8,128)(2,1)}, u32[]{:S(2)}, u32[]{:S(2)}) collective-permute-start(bf16[768,384]{1,0:T(8,128)(2,1)} %param.17), channel_id=1, source_target_pairs={{0,4},{2,6},{4,0},{6,2},{1,5},{3,7},{5,1},{7,3},{8,12},{10,14},{12... | collective-permute-start | bytes 1769480 | tf_op jit(solution)/shard_map/ppermute | solution.py:31
  29.7 47.8 %collective-permute-start = (bf16[1024,384]{1,0:T(8,128)(2,1)S(1)}, bf16[1024,384]{1,0:T(8,128)(2,1)S(1)}, u32[]{:S(2)}, u32[]{:S(2)}) collective-permute-start(bf16[1024,384]{1,0:T(8,128)(2,1)S(1)} %copy-done.4), channel_id=1, source_target_pairs={{0,2},{2,0},{4,6},{6,4},{1,3},{3,1},{5,7},{7,5},{8,10},{10,8},{12,... | collective-permute-start | bytes 2359304 | tf_op jit(solution)/shard_map/ppermute | solution.py:31
  31.7 47.3 %collective-permute-start.1 = (bf16[1024,384]{1,0:T(8,128)(2,1)S(1)}, bf16[1024,384]{1,0:T(8,128)(2,1)S(1)}, u32[]{:S(2)}, u32[]{:S(2)}) collective-permute-start(bf16[1024,384]{1,0:T(8,128)(2,1)S(1)} %copy-done.4), channel_id=1, source_target_pairs={{0,4},{2,6},{4,0},{6,2},{1,5},{3,7},{5,1},{7,3},{8,12},{10,14},{12... | collective-permute-start | bytes 2359304 | tf_op jit(solution)/shard_map/ppermute | solution.py:31
  33.3 32.0 %collective-permute-start.9 = (bf16[384,384]{1,0:T(8,128)(2,1)S(1)}, bf16[384,384]{1,0:T(8,128)(2,1)S(1)}, u32[]{:S(2)}, u32[]{:S(2)}) collective-permute-start(bf16[384,384]{1,0:T(8,128)(2,1)S(1)} %copy-done.78), channel_id=1, source_target_pairs={{0,6},{2,4},{4,2},{6,0},{1,7},{3,5},{5,3},{7,1},{8,14},{10,12},{12... | collective-permute-start | bytes 884744 | tf_op jit(solution)/shard_map/ppermute | solution.py:31
  77.5 46.8 %collective-permute-start.10 = (bf16[1536,512]{1,0:T(8,128)(2,1)S(1)}, bf16[1536,512]{1,0:T(8,128)(2,1)}, u32[]{:S(2)}, u32[]{:S(2)}) collective-permute-start(bf16[1536,512]{1,0:T(8,128)(2,1)S(1)} %convolution_convert_fusion.4.w_own.refs_2_), channel_id=1, source_target_pairs={{0,1},{1,0},{2,3},{3,2},{4,5},{5,4},{6,7},{7,6},{8,9},{9,8},{10,11... | collective-permute-start | bytes 4718600 | tf_op jit(solution)/shard_map/ppermute | solution.py:35
  85.9 20.9 %collective-permute-start.22 = (bf16[1024,384]{1,0:T(8,128)(2,1)}, bf16[1024,384]{1,0:T(8,128)(2,1)S(1)}, u32[]{:S(2)}, u32[]{:S(2)}) collective-permute-start(bf16[1024,384]{1,0:T(8,128)(2,1)} %param.23), channel_id=1, source_target_pairs={{0,2},{2,0},{4,6},{6,4},{1,3},{3,1},{5,7},{7,5},{8,10},{10,8},{12,... | collective-permute-start | bytes 2359304 | tf_op jit(solution)/shard_map/ppermute | solution.py:31
  88.1 21.0 %collective-permute-start.23 = (bf16[1024,384]{1,0:T(8,128)(2,1)}, bf16[1024,384]{1,0:T(8,128)(2,1)S(1)}, u32[]{:S(2)}, u32[]{:S(2)}) collective-permute-start(bf16[1024,384]{1,0:T(8,128)(2,1)} %param.23), channel_id=1, source_target_pairs={{0,4},{2,6},{4,0},{6,2},{1,5},{3,7},{5,1},{7,3},{8,12},{10,14},{12... | collective-permute-start | bytes 2359304 | tf_op jit(solution)/shard_map/ppermute | solution.py:31
  92.2 25.3 %collective-permute-start.2 = (bf16[512,384]{1,0:T(8,128)(2,1)S(1)}, bf16[512,384]{1,0:T(8,128)(2,1)S(1)}, u32[]{:S(2)}, u32[]{:S(2)}) collective-permute-start(bf16[512,384]{1,0:T(8,128)(2,1)S(1)} %slice.225), channel_id=1, source_target_pairs={{0,4},{2,6},{4,0},{6,2},{1,5},{3,7},{5,1},{7,3},{8,12},{10,14},{12... | collective-permute-start | bytes 1179656 | tf_op jit(solution)/shard_map/ppermute | solution.py:31
  94.5 26.9 %collective-permute-start.3 = (bf16[512,384]{1,0:T(8,128)(2,1)S(1)}, bf16[512,384]{1,0:T(8,128)(2,1)S(1)}, u32[]{:S(2)}, u32[]{:S(2)}) collective-permute-start(bf16[512,384]{1,0:T(8,128)(2,1)S(1)} %slice.226), channel_id=1, source_target_pairs={{0,2},{2,0},{4,6},{6,4},{1,3},{3,1},{5,7},{7,5},{8,10},{10,8},{12,... | collective-permute-start | bytes 1179656 | tf_op jit(solution)/shard_map/ppermute | solution.py:31
  106.7 26.0 %collective-permute-start.26 = (bf16[384,1024]{1,0:T(8,128)(2,1)S(1)}, bf16[384,1024]{1,0:T(8,128)(2,1)S(1)}, u32[]{:S(2)}, u32[]{:S(2)}) collective-permute-start(bf16[384,1024]{1,0:T(8,128)(2,1)S(1)} %copy-done.77), channel_id=1, source_target_pairs={{0,2},{2,0},{4,6},{6,4},{1,3},{3,1},{5,7},{7,5},{8,10},{10,8},{12,... | collective-permute-start | bytes 2359304 | tf_op jit(solution)/shard_map/ppermute | solution.py:31
  109.1 41.9 %collective-permute-start.27 = (bf16[384,1024]{1,0:T(8,128)(2,1)S(1)}, bf16[384,1024]{1,0:T(8,128)(2,1)S(1)}, u32[]{:S(2)}, u32[]{:S(2)}) collective-permute-start(bf16[384,1024]{1,0:T(8,128)(2,1)S(1)} %copy-done.76), channel_id=1, source_target_pairs={{0,4},{2,6},{4,0},{6,2},{1,5},{3,7},{5,1},{7,3},{8,12},{10,14},{12... | collective-permute-start | bytes 2359304 | tf_op jit(solution)/shard_map/ppermute | solution.py:31
  117.5 35.7 %collective-permute-start.28 = (bf16[384,1024]{1,0:T(8,128)(2,1)}, bf16[384,1024]{1,0:T(8,128)(2,1)S(1)}, u32[]{:S(2)}, u32[]{:S(2)}) collective-permute-start(bf16[384,1024]{1,0:T(8,128)(2,1)} %pad_maximum_fusion.11), channel_id=1, source_target_pairs={{0,6},{2,4},{4,2},{6,0},{1,7},{3,5},{5,3},{7,1},{8,14},{10,12},{12... | collective-permute-start | bytes 2359304 | tf_op jit(solution)/shard_map/ppermute | solution.py:31
  121.3 71.0 %collective-permute-start.21 = (bf16[768,1536]{1,0:T(8,128)(2,1)}, bf16[768,1536]{1,0:T(8,128)(2,1)}, u32[]{:S(2)}, u32[]{:S(2)}) collective-permute-start(bf16[768,1536]{1,0:T(8,128)(2,1)} %maximum_maximum_fusion.1), channel_id=1, source_target_pairs={{0,1},{1,0},{2,3},{3,2},{4,5},{5,4},{6,7},{7,6},{8,9},{9,8},{10,11... | collective-permute-start | bytes 7077896 | tf_op jit(solution)/shard_map/ppermute | solution.py:35
  124.3 115.5 %collective-permute-start.33 = (bf16[512,1536]{1,0:T(8,128)(2,1)S(1)}, bf16[512,1536]{1,0:T(8,128)(2,1)S(1)}, u32[]{:S(2)}, u32[]{:S(2)}) collective-permute-start(bf16[512,1536]{1,0:T(8,128)(2,1)S(1)} %pad_maximum_fusion.3.d_own.refs_2_), channel_id=1, source_target_pairs={{0,1},{1,0},{2,3},{3,2},{4,5},{5,4},{6,7},{7,6},{8,9},{9,8},{10,11... | collective-permute-start | bytes 4718600 | tf_op jit(solution)/shard_map/ppermute | solution.py:35
  132.7 30.4 %collective-permute-start.24 = (bf16[512,384]{1,0:T(8,128)(2,1)}, bf16[512,384]{1,0:T(8,128)(2,1)S(1)}, u32[]{:S(2)}, u32[]{:S(2)}) collective-permute-start(bf16[512,384]{1,0:T(8,128)(2,1)} %slice.237), channel_id=1, source_target_pairs={{0,4},{2,6},{4,0},{6,2},{1,5},{3,7},{5,1},{7,3},{8,12},{10,14},{12... | collective-permute-start | bytes 1179656 | tf_op jit(solution)/shard_map/ppermute | solution.py:31
  153.3 21.2 %collective-permute-start.11 = (bf16[1024,512]{1,0:T(8,128)(2,1)}, bf16[1024,512]{1,0:T(8,128)(2,1)S(1)}, u32[]{:S(2)}, u32[]{:S(2)}) collective-permute-start(bf16[1024,512]{1,0:T(8,128)(2,1)} %get-tuple-element.58), channel_id=1, source_target_pairs={{0,1},{1,0},{2,3},{3,2},{4,5},{5,4},{6,7},{7,6},{8,9},{9,8},{10,11... | collective-permute-start | bytes 3145736 | tf_op jit(solution)/shard_map/ppermute | solution.py:35
  163.1 76.7 %collective-permute-start.29 = (bf16[1536,1024]{1,0:T(8,128)(2,1)S(1)}, bf16[1536,1024]{1,0:T(8,128)(2,1)}, u32[]{:S(2)}, u32[]{:S(2)}) collective-permute-start(bf16[1536,1024]{1,0:T(8,128)(2,1)S(1)} %pad_maximum_fusion.1.g_own.u_own.refs_2_), channel_id=1, source_target_pairs={{0,1},{1,0},{2,3},{3,2},{4,5},{5,4},{6,7},{7,6},{8,9},{9,8},{10,11... | collective-permute-start | bytes 9437192 | tf_op jit(solution)/shard_map/ppermute | solution.py:35
  196.8 22.0 %collective-permute-start.14 = (bf16[1024,384]{1,0:T(8,128)(2,1)S(1)}, bf16[1024,384]{1,0:T(8,128)(2,1)S(1)}, u32[]{:S(2)}, u32[]{:S(2)}) collective-permute-start(bf16[1024,384]{1,0:T(8,128)(2,1)S(1)} %pad_maximum_fusion.8.h0), channel_id=1, source_target_pairs={{0,4},{2,6},{4,0},{6,2},{1,5},{3,7},{5,1},{7,3},{8,12},{10,14},{12... | collective-permute-start | bytes 2359304 | tf_op jit(solution)/shard_map/ppermute | solution.py:31
  278.1 31.6 %collective-permute-start.42 = (f32[8,128]{1,0:T(8,128)S(1)}, f32[8,128]{1,0:T(8,128)S(1)}, u32[]{:S(2)}, u32[]{:S(2)}) collective-permute-start(f32[8,128]{1,0:T(8,128)S(1)} %pad_maximum_fusion.16), channel_id=1, source_target_pairs={{0,2},{2,0},{4,6},{6,4},{1,3},{3,1},{5,7},{7,5},{8,10},{10,8},{12,... | collective-permute-start | bytes 12296 | tf_op jit(solution)/shard_map/ppermute | solution.py:31
  278.5 32.0 %collective-permute-start.43 = (f32[8,128]{1,0:T(8,128)S(1)}, f32[8,128]{1,0:T(8,128)S(1)}, u32[]{:S(2)}, u32[]{:S(2)}) collective-permute-start(f32[8,128]{1,0:T(8,128)S(1)} %pad_maximum_fusion.16), channel_id=1, source_target_pairs={{0,4},{2,6},{4,0},{6,2},{1,5},{3,7},{5,1},{7,3},{8,12},{10,14},{12... | collective-permute-start | bytes 12296 | tf_op jit(solution)/shard_map/ppermute | solution.py:31
  279.8 32.5 %collective-permute-start.44 = (f32[8,128]{1,0:T(8,128)S(1)}, f32[8,128]{1,0:T(8,128)S(1)}, u32[]{:S(2)}, u32[]{:S(2)}) collective-permute-start(f32[8,128]{1,0:T(8,128)S(1)} %pad_maximum_fusion.16), channel_id=1, source_target_pairs={{0,6},{2,4},{4,2},{6,0},{1,7},{3,5},{5,3},{7,1},{8,14},{10,12},{12... | collective-permute-start | bytes 12296 | tf_op jit(solution)/shard_map/ppermute | solution.py:31
  292.5 22.4 %collective-permute-start.38 = (bf16[512,768]{1,0:T(8,128)(2,1)}, bf16[512,768]{1,0:T(8,128)(2,1)}, u32[]{:S(2)}, u32[]{:S(2)}) collective-permute-start(bf16[512,768]{1,0:T(8,128)(2,1)} %get-tuple-element.75), channel_id=1, source_target_pairs={{0,2},{2,0},{4,6},{6,4},{1,3},{3,1},{5,7},{7,5},{8,10},{10,8},{12,... | collective-permute-start | bytes 2359304 | tf_op jit(solution)/shard_map/ppermute | solution.py:31
  292.9 23.7 %collective-permute-start.40 = (bf16[512,768]{1,0:T(8,128)(2,1)}, bf16[512,768]{1,0:T(8,128)(2,1)}, u32[]{:S(2)}, u32[]{:S(2)}) collective-permute-start(bf16[512,768]{1,0:T(8,128)(2,1)} %get-tuple-element.78), channel_id=1, source_target_pairs={{0,4},{2,6},{4,0},{6,2},{1,5},{3,7},{5,1},{7,3},{8,12},{10,14},{12... | collective-permute-start | bytes 2359304 | tf_op jit(solution)/shard_map/ppermute | solution.py:31
  309.8 20.8 %collective-permute-start.34 = (bf16[512,768]{1,0:T(8,128)(2,1)}, bf16[512,768]{1,0:T(8,128)(2,1)}, u32[]{:S(2)}, u32[]{:S(2)}) collective-permute-start(bf16[512,768]{1,0:T(8,128)(2,1)} %get-tuple-element.66), channel_id=1, source_target_pairs={{0,2},{2,0},{4,6},{6,4},{1,3},{3,1},{5,7},{7,5},{8,10},{10,8},{12,... | collective-permute-start | bytes 2359304 | tf_op jit(solution)/shard_map/ppermute | solution.py:31
  310.5 43.4 %collective-permute-start.36 = (bf16[512,768]{1,0:T(8,128)(2,1)}, bf16[512,768]{1,0:T(8,128)(2,1)}, u32[]{:S(2)}, u32[]{:S(2)}) collective-permute-start(bf16[512,768]{1,0:T(8,128)(2,1)} %get-tuple-element.69), channel_id=1, source_target_pairs={{0,4},{2,6},{4,0},{6,2},{1,5},{3,7},{5,1},{7,3},{8,12},{10,14},{12... | collective-permute-start | bytes 2359304 | tf_op jit(solution)/shard_map/ppermute | solution.py:31
  312.2 91.8 %collective-permute-start.74 = (bf16[1536,1536]{0,1:T(8,128)(2,1)}, bf16[1536,1536]{0,1:T(8,128)(2,1)}, u32[]{:S(2)}, u32[]{:S(2)}) collective-permute-start(bf16[1536,1536]{0,1:T(8,128)(2,1)} %pad_maximum_fusion), channel_id=1, source_target_pairs={{0,1},{1,0},{2,3},{3,2},{4,5},{5,4},{6,7},{7,6},{8,9},{9,8},{10,11... | collective-permute-start | bytes 14155784 | tf_op jit(solution)/shard_map/ppermute | solution.py:35
  316.2 23.5 %collective-permute-start.39 = (bf16[512,384]{1,0:T(8,128)(2,1)S(1)}, bf16[512,384]{1,0:T(8,128)(2,1)S(1)}, u32[]{:S(2)}, u32[]{:S(2)}) collective-permute-start(bf16[512,384]{1,0:T(8,128)(2,1)S(1)} %add_convert_fusion.15), channel_id=1, source_target_pairs={{0,4},{2,6},{4,0},{6,2},{1,5},{3,7},{5,1},{7,3},{8,12},{10,14},{12... | collective-permute-start | bytes 1179656 | tf_op jit(solution)/shard_map/ppermute | solution.py:31
  317.6 23.1 %collective-permute-start.41 = (bf16[512,384]{1,0:T(8,128)(2,1)S(1)}, bf16[512,384]{1,0:T(8,128)(2,1)S(1)}, u32[]{:S(2)}, u32[]{:S(2)}) collective-permute-start(bf16[512,384]{1,0:T(8,128)(2,1)S(1)} %add_convert_fusion.14), channel_id=1, source_target_pairs={{0,2},{2,0},{4,6},{6,4},{1,3},{3,1},{5,7},{7,5},{8,10},{10,8},{12,... | collective-permute-start | bytes 1179656 | tf_op jit(solution)/shard_map/ppermute | solution.py:31
  332.6 24.5 %collective-permute-start.35 = (bf16[512,384]{1,0:T(8,128)(2,1)}, bf16[512,384]{1,0:T(8,128)(2,1)}, u32[]{:S(2)}, u32[]{:S(2)}) collective-permute-start(bf16[512,384]{1,0:T(8,128)(2,1)} %add_convert_fusion.17), channel_id=1, source_target_pairs={{0,4},{2,6},{4,0},{6,2},{1,5},{3,7},{5,1},{7,3},{8,12},{10,14},{12... | collective-permute-start | bytes 1179656 | tf_op jit(solution)/shard_map/ppermute | solution.py:31
  344.9 20.2 %collective-permute-start.46 = (bf16[1024,384]{1,0:T(8,128)(2,1)}, bf16[1024,384]{1,0:T(8,128)(2,1)}, u32[]{:S(2)}, u32[]{:S(2)}) collective-permute-start(bf16[1024,384]{1,0:T(8,128)(2,1)} %fusion.43), channel_id=1, source_target_pairs={{0,4},{2,6},{4,0},{6,2},{1,5},{3,7},{5,1},{7,3},{8,12},{10,14},{12... | collective-permute-start | bytes 2359304 | tf_op jit(solution)/shard_map/ppermute | solution.py:31
  355.3 23.4 %collective-permute-start.37 = (bf16[512,384]{1,0:T(8,128)(2,1)S(1)}, bf16[512,384]{1,0:T(8,128)(2,1)S(1)}, u32[]{:S(2)}, u32[]{:S(2)}) collective-permute-start(bf16[512,384]{1,0:T(8,128)(2,1)S(1)} %add_convert_fusion.16), channel_id=1, source_target_pairs={{0,2},{2,0},{4,6},{6,4},{1,3},{3,1},{5,7},{7,5},{8,10},{10,8},{12,... | collective-permute-start | bytes 1179656 | tf_op jit(solution)/shard_map/ppermute | solution.py:31
  419.6 27.3 %collective-permute-start.75 = (bf16[4,96,1536]{2,1,0:T(8,128)(2,1)}, bf16[4,96,1536]{2,1,0:T(8,128)(2,1)}, u32[]{:S(2)}, u32[]{:S(2)}) collective-permute-start(bf16[4,96,1536]{2,1,0:T(8,128)(2,1)} %get-tuple-element.115), channel_id=1, source_target_pairs={{0,8},{1,9},{2,10},{3,11},{4,12},{5,13},{6,14},{7,15}} | collective-permute-start | bytes 3538952 | tf_op jit(solution)/shard_map/ppermute | solution.py:82
  430.1 34.9 %collective-permute-start.58 = (bf16[4,576,384]{2,1,0:T(8,128)(2,1)}, bf16[4,576,384]{2,1,0:T(8,128)(2,1)}, u32[]{:S(2)}, u32[]{:S(2)}) collective-permute-start(bf16[4,576,384]{2,1,0:T(8,128)(2,1)} %pad_maximum_fusion.2), channel_id=1, source_target_pairs={{0,1},{1,0},{2,3},{3,2},{4,5},{5,4},{6,7},{7,6},{8,9},{9,8},{10,11... | collective-permute-start | bytes 5308424 | tf_op jit(solution)/shard_map/ppermute | solution.py:35
  443.3 20.5 %collective-permute-start.57 = (f32[8,128]{1,0:T(8,128)S(1)}, f32[8,128]{1,0:T(8,128)S(1)}, u32[]{:S(2)}, u32[]{:S(2)}) collective-permute-start(f32[8,128]{1,0:T(8,128)S(1)} %pad_maximum_fusion.17), channel_id=1, source_target_pairs={{0,6},{2,4},{4,2},{6,0},{1,7},{3,5},{5,3},{7,1},{8,14},{10,12},{12... | collective-permute-start | bytes 12296 | tf_op jit(solution)/shard_map/ppermute | solution.py:31
  446.9 22.6 %collective-permute-start.78 = (bf16[4,96,1536]{2,1,0:T(8,128)(2,1)}, bf16[4,96,1536]{2,1,0:T(8,128)(2,1)}, u32[]{:S(2)}, u32[]{:S(2)}) collective-permute-start(bf16[4,96,1536]{2,1,0:T(8,128)(2,1)} %get-tuple-element.116), channel_id=1, source_target_pairs={{24,16},{25,17},{26,18},{27,19},{28,20},{29,21},{30,22},{31,23}} | collective-permute-start | bytes 3538952 | tf_op jit(solution)/shard_map/ppermute | solution.py:83
  451.5 31.2 %collective-permute-start.76 = (bf16[4,96,1536]{2,1,0:T(8,128)(2,1)}, bf16[4,96,1536]{2,1,0:T(8,128)(2,1)}, u32[]{:S(2)}, u32[]{:S(2)}) collective-permute-start(bf16[4,96,1536]{2,1,0:T(8,128)(2,1)} %add_convert_fusion.6), channel_id=1, source_target_pairs={{0,8},{8,16},{1,9},{9,17},{2,10},{10,18},{3,11},{11,19},{4,12},{12... | collective-permute-start | bytes 3538952 | tf_op jit(solution)/shard_map/ppermute | solution.py:82
  462.6 23.9 %collective-permute-start.51 = (bf16[512,768]{1,0:T(8,128)(2,1)}, bf16[512,768]{1,0:T(8,128)(2,1)}, u32[]{:S(2)}, u32[]{:S(2)}) collective-permute-start(bf16[512,768]{1,0:T(8,128)(2,1)} %copy-done.39), channel_id=1, source_target_pairs={{0,2},{2,0},{4,6},{6,4},{1,3},{3,1},{5,7},{7,5},{8,10},{10,8},{12,... | collective-permute-start | bytes 2359304 | tf_op jit(solution)/shard_map/ppermute | solution.py:31
  463.8 31.3 %collective-permute-start.53 = (bf16[512,768]{1,0:T(8,128)(2,1)S(1)}, bf16[512,768]{1,0:T(8,128)(2,1)}, u32[]{:S(2)}, u32[]{:S(2)}) collective-permute-start(bf16[512,768]{1,0:T(8,128)(2,1)S(1)} %copy-done.38), channel_id=1, source_target_pairs={{0,4},{2,6},{4,0},{6,2},{1,5},{3,7},{5,1},{7,3},{8,12},{10,14},{12... | collective-permute-start | bytes 2359304 | tf_op jit(solution)/shard_map/ppermute | solution.py:31
  467.9 22.6 %collective-permute-start.59 = (bf16[4,144,384]{2,1,0:T(8,128)(2,1)S(1)}, bf16[4,144,384]{2,1,0:T(8,128)(2,1)S(1)}, u32[]{:S(2)}, u32[]{:S(2)}) collective-permute-start(bf16[4,144,384]{2,1,0:T(8,128)(2,1)S(1)} %pad_maximum_fusion.12), channel_id=1, source_target_pairs={{0,8},{1,9},{2,10},{3,11},{4,12},{5,13},{6,14},{7,15}} | collective-permute-start | bytes 1327112 | tf_op jit(solution)/shard_map/ppermute | solution.py:82
  485.7 22.0 %collective-permute-start.79 = (bf16[4,96,1536]{2,1,0:T(8,128)(2,1)S(1)}, bf16[4,96,1536]{2,1,0:T(8,128)(2,1)S(1)}, u32[]{:S(2)}, u32[]{:S(2)}) collective-permute-start(bf16[4,96,1536]{2,1,0:T(8,128)(2,1)S(1)} %get-tuple-element.114), channel_id=1, source_target_pairs={{24,16},{16,8},{25,17},{17,9},{26,18},{18,10},{27,19},{19,11},{28,... | collective-permute-start | bytes 3538952 | tf_op jit(solution)/shard_map/ppermute | solution.py:83
  487.6 45.7 %collective-permute-start.52 = (bf16[512,384]{1,0:T(8,128)(2,1)S(1)}, bf16[512,384]{1,0:T(8,128)(2,1)S(1)}, u32[]{:S(2)}, u32[]{:S(2)}) collective-permute-start(bf16[512,384]{1,0:T(8,128)(2,1)S(1)} %add_convert_fusion.13), channel_id=1, source_target_pairs={{0,4},{2,6},{4,0},{6,2},{1,5},{3,7},{5,1},{7,3},{8,12},{10,14},{12... | collective-permute-start | bytes 1179656 | tf_op jit(solution)/shard_map/ppermute | solution.py:31
  496.2 39.5 %collective-permute-start.54 = (bf16[512,384]{1,0:T(8,128)(2,1)S(1)}, bf16[512,384]{1,0:T(8,128)(2,1)S(1)}, u32[]{:S(2)}, u32[]{:S(2)}) collective-permute-start(bf16[512,384]{1,0:T(8,128)(2,1)S(1)} %add_convert_fusion.12), channel_id=1, source_target_pairs={{0,2},{2,0},{4,6},{6,4},{1,3},{3,1},{5,7},{7,5},{8,10},{10,8},{12,... | collective-permute-start | bytes 1179656 | tf_op jit(solution)/shard_map/ppermute | solution.py:31
  497.6 34.1 %collective-permute-start.63 = (bf16[4,144,384]{2,1,0:T(8,128)(2,1)S(1)}, bf16[4,144,384]{2,1,0:T(8,128)(2,1)S(1)}, u32[]{:S(2)}, u32[]{:S(2)}) collective-permute-start(bf16[4,144,384]{2,1,0:T(8,128)(2,1)S(1)} %add_convert_fusion.9), channel_id=1, source_target_pairs={{24,16},{16,8},{25,17},{17,9},{26,18},{18,10},{27,19},{19,11},{28,... | collective-permute-start | bytes 1327112 | tf_op jit(solution)/shard_map/ppermute | solution.py:83
  503.3 33.6 %collective-permute-start.61 = (bf16[4,144,384]{2,1,0:T(8,128)(2,1)S(1)}, bf16[4,144,384]{2,1,0:T(8,128)(2,1)S(1)}, u32[]{:S(2)}, u32[]{:S(2)}) collective-permute-start(bf16[4,144,384]{2,1,0:T(8,128)(2,1)S(1)} %add_convert_fusion.10), channel_id=1, source_target_pairs={{0,8},{8,16},{16,24},{1,9},{9,17},{17,25},{2,10},{10,18},{18,26},{... | collective-permute-start | bytes 1327112 | tf_op jit(solution)/shard_map/ppermute | solution.py:82
  507.8 63.9 %collective-permute-start.77 = (bf16[4,96,1536]{2,1,0:T(8,128)(2,1)S(1)}, bf16[4,96,1536]{2,1,0:T(8,128)(2,1)S(1)}, u32[]{:S(2)}, u32[]{:S(2)}) collective-permute-start(bf16[4,96,1536]{2,1,0:T(8,128)(2,1)S(1)} %get-tuple-element.113), channel_id=1, source_target_pairs={{0,8},{8,16},{16,24},{1,9},{9,17},{17,25},{2,10},{10,18},{18,26},{... | collective-permute-start | bytes 3538952 | tf_op jit(solution)/shard_map/ppermute | solution.py:82
  531.7 40.0 %collective-permute-start.80 = (bf16[4,96,1536]{2,1,0:T(8,128)(2,1)S(1)}, bf16[4,96,1536]{2,1,0:T(8,128)(2,1)S(1)}, u32[]{:S(2)}, u32[]{:S(2)}) collective-permute-start(bf16[4,96,1536]{2,1,0:T(8,128)(2,1)S(1)} %add_convert_fusion.3), channel_id=1, source_target_pairs={{24,16},{16,8},{8,0},{25,17},{17,9},{9,1},{26,18},{18,10},{10,2},{... | collective-permute-start | bytes 3538952 | tf_op jit(solution)/shard_map/ppermute | solution.py:83
  533.2 37.0 %collective-permute-start.64 = (bf16[4,144,384]{2,1,0:T(8,128)(2,1)S(1)}, bf16[4,144,384]{2,1,0:T(8,128)(2,1)S(1)}, u32[]{:S(2)}, u32[]{:S(2)}) collective-permute-start(bf16[4,144,384]{2,1,0:T(8,128)(2,1)S(1)} %add_convert_fusion.8), channel_id=1, source_target_pairs={{24,16},{16,8},{8,0},{25,17},{17,9},{9,1},{26,18},{18,10},{10,2},{... | collective-permute-start | bytes 1327112 | tf_op jit(solution)/shard_map/ppermute | solution.py:83
  573.2 20.4 %collective-permute-start.82 = (bf16[96,1536]{1,0:T(8,128)(2,1)S(1)}, bf16[96,1536]{1,0:T(8,128)(2,1)S(1)}, u32[]{:S(2)}, u32[]{:S(2)}) collective-permute-start(bf16[96,1536]{1,0:T(8,128)(2,1)S(1)} %get-tuple-element.149), channel_id=1, source_target_pairs={{0,4},{2,6},{4,0},{6,2},{1,5},{3,7},{5,1},{7,3},{8,12},{10,14},{12... | collective-permute-start | bytes 884744 | tf_op jit(solution)/shard_map/ppermute | solution.py:31
  589.0 44.7 %collective-permute-start.68 = (bf16[4,144,384]{2,1,0:T(8,128)(2,1)}, bf16[4,144,384]{2,1,0:T(8,128)(2,1)S(1)}, u32[]{:S(2)}, u32[]{:S(2)}) collective-permute-start(bf16[4,144,384]{2,1,0:T(8,128)(2,1)} %pad_maximum_fusion.14), channel_id=1, source_target_pairs={{0,8},{8,16},{16,24},{1,9},{9,17},{17,25},{2,10},{10,18},{18,26},{... | collective-permute-start | bytes 1327112 | tf_op jit(solution)/shard_map/ppermute | solution.py:100
  592.3 42.0 %collective-permute-start.69 = (bf16[4,144,384]{2,1,0:T(8,128)(2,1)}, bf16[4,144,384]{2,1,0:T(8,128)(2,1)S(1)}, u32[]{:S(2)}, u32[]{:S(2)}) collective-permute-start(bf16[4,144,384]{2,1,0:T(8,128)(2,1)} %pad_maximum_fusion.14), channel_id=1, source_target_pairs={{24,16},{16,8},{8,0},{25,17},{17,9},{9,1},{26,18},{18,10},{10,2},{... | collective-permute-start | bytes 1327112 | tf_op jit(solution)/shard_map/ppermute | solution.py:101
  594.8 58.2 %collective-permute-start.84 = (bf16[4,96,1536]{2,1,0:T(8,128)(2,1)}, bf16[4,96,1536]{2,1,0:T(8,128)(2,1)S(1)}, u32[]{:S(2)}, u32[]{:S(2)}) collective-permute-start(bf16[4,96,1536]{2,1,0:T(8,128)(2,1)} %pad_maximum_fusion.7), channel_id=1, source_target_pairs={{0,8},{8,16},{16,24},{1,9},{9,17},{17,25},{2,10},{10,18},{18,26},{... | collective-permute-start | bytes 3538952 | tf_op jit(solution)/shard_map/ppermute | solution.py:100
  600.1 28.0 %collective-permute-start.91 = (f32[2,384]{1,0:T(2,128)}, f32[2,384]{1,0:T(2,128)S(1)}, u32[]{:S(2)}, u32[]{:S(2)}) collective-permute-start(f32[2,384]{1,0:T(2,128)} %fusion.42), channel_id=1, source_target_pairs={{0,8},{8,16},{16,24},{24,0},{1,9},{9,17},{17,25},{25,1},{2,10},{10... | collective-permute-start | bytes 9224 | tf_op jit(solution)/shard_map/ppermute | solution.py:775
  601.0 29.6 %collective-permute-start.92 = (f32[2,384]{1,0:T(2,128)}, f32[2,384]{1,0:T(2,128)}, u32[]{:S(2)}, u32[]{:S(2)}) collective-permute-start(f32[2,384]{1,0:T(2,128)} %fusion.42), channel_id=1, source_target_pairs={{0,16},{8,24},{16,0},{24,8},{1,17},{9,25},{17,1},{25,9},{2,18},{10... | collective-permute-start | bytes 9224 | tf_op jit(solution)/shard_map/ppermute | solution.py:775
  635.6 41.3 %collective-permute-start.85 = (bf16[4,96,1536]{2,1,0:T(8,128)(2,1)}, bf16[4,96,1536]{2,1,0:T(8,128)(2,1)S(1)}, u32[]{:S(2)}, u32[]{:S(2)}) collective-permute-start(bf16[4,96,1536]{2,1,0:T(8,128)(2,1)} %pad_maximum_fusion.7), channel_id=1, source_target_pairs={{24,16},{16,8},{8,0},{25,17},{17,9},{9,1},{26,18},{18,10},{10,2},{... | collective-permute-start | bytes 3538952 | tf_op jit(solution)/shard_map/ppermute | solution.py:101
  651.6 34.8 %collective-permute-start.73 = (bf16[4,144,384]{2,1,0:T(8,128)(2,1)S(1)}, bf16[4,144,384]{2,1,0:T(8,128)(2,1)S(1)}, u32[]{:S(2)}, u32[]{:S(2)}) collective-permute-start(bf16[4,144,384]{2,1,0:T(8,128)(2,1)S(1)} %collective-permute-done.71), channel_id=1, source_target_pairs={{8,0},{9,1},{10,2},{11,3},{12,4},{13,5},{14,6},{15,7}} | collective-permute-start | bytes 1327112 | tf_op jit(solution)/shard_map/ppermute | solution.py:101
  653.0 36.5 %collective-permute-start.86 = (bf16[4,96,1536]{2,1,0:T(8,128)(2,1)S(1)}, bf16[4,96,1536]{2,1,0:T(8,128)(2,1)S(1)}, u32[]{:S(2)}, u32[]{:S(2)}) collective-permute-start(bf16[4,96,1536]{2,1,0:T(8,128)(2,1)S(1)} %collective-permute-done.84), channel_id=1, source_target_pairs={{8,16},{16,24},{9,17},{17,25},{10,18},{18,26},{11,19},{19,27},{12,... | collective-permute-start | bytes 3538952 | tf_op jit(solution)/shard_map/ppermute | solution.py:100
  676.9 32.2 %collective-permute-start.87 = (bf16[4,96,1536]{2,1,0:T(8,128)(2,1)S(1)}, bf16[4,96,1536]{2,1,0:T(8,128)(2,1)S(1)}, u32[]{:S(2)}, u32[]{:S(2)}) collective-permute-start(bf16[4,96,1536]{2,1,0:T(8,128)(2,1)S(1)} %collective-permute-done.85), channel_id=1, source_target_pairs={{16,8},{8,0},{17,9},{9,1},{18,10},{10,2},{19,11},{11,3},{20,12},{1... | collective-permute-start | bytes 3538952 | tf_op jit(solution)/shard_map/ppermute | solution.py:101
  689.6 21.1 %collective-permute-start.88 = (bf16[4,96,1536]{2,1,0:T(8,128)(2,1)S(1)}, bf16[4,96,1536]{2,1,0:T(8,128)(2,1)S(1)}, u32[]{:S(2)}, u32[]{:S(2)}) collective-permute-start(bf16[4,96,1536]{2,1,0:T(8,128)(2,1)S(1)} %collective-permute-done.86), channel_id=1, source_target_pairs={{16,24},{17,25},{18,26},{19,27},{20,28},{21,29},{22,30},{23,31}} | collective-permute-start | bytes 3538952 | tf_op jit(solution)/shard_map/ppermute | solution.py:100
  709.2 27.3 %collective-permute-start.89 = (bf16[4,96,1536]{2,1,0:T(8,128)(2,1)S(1)}, bf16[4,96,1536]{2,1,0:T(8,128)(2,1)S(1)}, u32[]{:S(2)}, u32[]{:S(2)}) collective-permute-start(bf16[4,96,1536]{2,1,0:T(8,128)(2,1)S(1)} %collective-permute-done.87), channel_id=1, source_target_pairs={{8,0},{9,1},{10,2},{11,3},{12,4},{13,5},{14,6},{15,7}} | collective-permute-start | bytes 3538952 | tf_op jit(solution)/shard_map/ppermute | solution.py:101
  (118 other events, 1315.1 us)

commit v2 on v1

--- a/solution.py
+++ b/solution.py
@@ -21,6 +21,7 @@
 NT = (((1,), (1,)), ((), ()))
 TN = (((0,), (0,)), ((), ()))
 VMEM_LIMIT = 48 * 1024 * 1024
+WEIGHT = 1 / 64
 
 
 def dot(left, right, dims=NN):
@@ -35,73 +36,196 @@
     return lax.ppermute(value, "col", [(0, 1), (1, 0)])
 
 
-def gather_row(value):
-    half = value.shape[0] // 2
-    along_x = swap(value, 1)
-    along_y = swap(value, 2)
-    top = swap(along_x[:half], 2)
-    bottom = swap(along_y[half:], 1)
-    return [value, along_x, along_y, jnp.concatenate([top, bottom], axis=0)]
-
-
-def exchange_row(pieces):
-    return [pieces[0]] + [swap(pieces[i], i) for i in (1, 2, 3)]
-
-
-def total_row(value):
-    return value + swap(value, 1) + swap(value, 2) + swap(value, 3)
-
-
-def scatter_row(parts):
-    own_a, a_xd, a_y, own_b, b_yd, b_x = parts
-    width = own_a.shape[1]
-    got_a = swap(a_xd, 1)
-    got_b = swap(b_yd, 2)
-    send_a = (a_y.astype(F32) + got_a[:, width:].astype(F32)).astype(LOW)
-    send_b = (b_x.astype(F32) + got_b[:, width:].astype(F32)).astype(LOW)
-    last_a = swap(send_a, 2)
-    last_b = swap(send_b, 1)
-    total_a = own_a.astype(F32) + got_a[:, :width].astype(F32) + last_a.astype(F32)
-    total_b = own_b.astype(F32) + got_b[:, :width].astype(F32) + last_b.astype(F32)
-    return jnp.concatenate([total_a, total_b], axis=0)
-
-
-def chain_scatter(take, count):
-    place = lax.axis_index("dp")
-    own = take(place)
-    if count == 1:
+def pair(value, count):
+    return lax.ppermute(value, "dp", [(i, i ^ 1) for i in range(count)])
+
+
+def spread_row(shard):
+    return jnp.stack([shard[0]] + [swap(shard[i], i) for i in (1, 2, 3)])
+
+
+class Live:
+    def __init__(self, **values):
+        self.values = values
+
+    def __getitem__(self, name):
+        return self.values[name]
+
+    def __setitem__(self, name, value):
+        self.values[name] = value
+
+    def take(self, *names):
+        found = [self.values.pop(name) for name in names]
+        return found if len(found) > 1 else found[0]
+
+    def sync(self, *chains, late=()):
+        left_out = {name: self.values.pop(name) for name in late}
+        moving = [chain.moving() for chain in chains]
+        self.values, moving = lax.optimization_barrier((self.values, moving))
+        self.values.update(left_out)
+        for chain, values in zip(chains, moving):
+            chain.landed(values)
+
+
+def gather_one(live, name):
+    live[name + "x"] = swap(live[name], 1)
+    live[name + "y"] = swap(live[name], 2)
+
+
+def gather_two(live, name):
+    half = live[name].shape[0] // 2
+    live[name + "t"] = swap(live[name + "x"][:half], 2)
+    live[name + "b"] = swap(live[name + "y"][half:], 1)
+
+
+def gathered(live, name):
+    return [live[name + end] for end in ("", "x", "y", "t", "b")]
+
+
+def fetch_one(live, name, pieces, place, count):
+    parts = 2 if count % 2 == 0 else 1
+    rows = pieces[0].shape[0] // parts
+    at = (place % parts) * rows
+    live[name] = pieces[0]
+    for i in (1, 2, 3):
+        live[f"{name}{i}"] = swap(lax.dynamic_slice_in_dim(pieces[i], at, rows, 0), i)
+
+
+def fetch_two(live, name, count):
+    live[name + "m"] = jnp.stack(live.take(*[f"{name}{i}" for i in (1, 2, 3)]))
+    if count % 2 == 0:
+        live[name + "p"] = pair(live[name + "m"], count)
+
+
+def fetched(live, name, place, count):
+    own, mine = live.take(name, name + "m")
+    if count % 2:
+        return jnp.concatenate([own[None], mine])
+    theirs = live.take(name + "p")
+    rows = mine.shape[1]
+    bit = place % 2
+    zero = jnp.zeros((), jnp.int32)
+    result = jnp.zeros((4,) + own.shape, own.dtype)
+    result = lax.dynamic_update_slice(result, own[None], (0, 0, 0))
+    result = lax.dynamic_update_slice(result, mine, (zero + 1, bit * rows, zero))
+    return lax.dynamic_update_slice(result, theirs, (zero + 1, (1 - bit) * rows, zero))
+
+
+SUMS = ("own_a", "far_a", "near_a", "own_b", "far_b", "near_b")
+
+
+def scatter_put(live, name, parts):
+    for end, part in zip(SUMS, parts):
+        live[name + end] = part
+
+
+def scatter_one(live, name):
+    live[name + "got_a"] = swap(live.take(name + "far_a"), 1)
+    live[name + "got_b"] = swap(live.take(name + "far_b"), 2)
+
+
+def scatter_two(live, name):
+    got_a, got_b = live[name + "got_a"], live[name + "got_b"]
+    width = got_a.shape[1] // 2
+    send_a = (live.take(name + "near_a").astype(F32) + got_a[:, width:].astype(F32)).astype(LOW)
+    send_b = (live.take(name + "near_b").astype(F32) + got_b[:, width:].astype(F32)).astype(LOW)
+    live[name + "last_a"] = swap(send_a, 2)
+    live[name + "last_b"] = swap(send_b, 1)
+
+
+def scattered(live, name):
+    halves = []
+    for end in ("a", "b"):
+        own, got, last = live.take(name + "own_" + end, name + "got_" + end, name + "last_" + end)
+        halves.append(own.astype(F32) + got[:, : own.shape[1]].astype(F32) + last.astype(F32))
+    return jnp.concatenate(halves, axis=0)
+
+
+class Scatter:
+    def __init__(self, live, name, count, rows=()):
+        self.live, self.name, self.count, self.at, self.rows = live, name, count, 1, rows
+        self.place = lax.axis_index("dp")
+
+    def part(self, number):
+        total = self.live[self.name]
+        rows = self.rows if self.rows else (total.shape[1],)
+        found, at = [], 0
+        for count in rows:
+            size = count // self.count
+            found.append(lax.dynamic_slice_in_dim(total, at + number * size, size, 1))
+            at = at + count
+        return found[0] if len(found) == 1 else jnp.concatenate(found, axis=1)
+
+    def step(self):
+        count, at, place = self.count, self.at, self.place
+        if at >= count:
+            return
+        up = self.part(jnp.clip(count - at + place, 0, count - 1))
+        down = self.part(jnp.clip(place - (count - at), 0, count - 1))
+        if at > 1:
+            up = (up.astype(F32) + self.up.astype(F32)).astype(LOW)
+            down = (down.astype(F32) + self.down.astype(F32)).astype(LOW)
+        ups = [(i, i + 1) for i in range(min(at, count - 1))]
+        self.up = lax.ppermute(up, "dp", ups)
+        self.down = lax.ppermute(down, "dp", [(count - 1 - i, count - 1 - j) for i, j in ups])
+        self.at = at + 1
+
+    def moving(self):
+        return (self.up, self.down) if self.at > 1 else ()
+
+    def landed(self, values):
+        if values:
+            self.up, self.down = values
+
+    def finish(self):
+        while self.at < self.count:
+            self.step()
+        own = self.part(self.place)
+        if self.count > 1:
+            own = (own.astype(F32) + self.up.astype(F32) + self.down.astype(F32)).astype(LOW)
+        self.live.take(self.name)
         return own
-    right = left = None
-    for step in range(1, count):
-        up = take(jnp.clip(count - step + place, 0, count - 1))
-        down = take(jnp.clip(place - (count - step), 0, count - 1))
-        if right is not None:
-            up = (up.astype(F32) + right.astype(F32)).astype(LOW)
-            down = (down.astype(F32) + left.astype(F32)).astype(LOW)
-        ups = [(i, i + 1) for i in range(min(step, count - 1))]
-        right = lax.ppermute(up, "dp", ups)
-        left = lax.ppermute(down, "dp", [(count - 1 - i, count - 1 - j) for i, j in ups])
-    return (own.astype(F32) + right.astype(F32) + left.astype(F32)).astype(LOW)
-
-
-def chain_gather(shard, count):
-    place = lax.axis_index("dp")
-    shape = (shard.shape[0], count) + shard.shape[1:]
-    result = jnp.zeros(shape, shard.dtype)
-    zero = jnp.zeros((), jnp.int32)
-
-    def put(result, piece, at):
-        start = (zero, at) + (zero,) * (len(shape) - 2)
-        return lax.dynamic_update_slice(result, piece[:, None], start)
-
-    right = left = shard
-    for step in range(1, count):
-        ups = [(i, i + 1) for i in range(step - 1, count - 1)]
-        right = lax.ppermute(right, "dp", ups)
-        left = lax.ppermute(left, "dp", [(count - 1 - i, count - 1 - j) for i, j in ups])
-        result = put(result, right, jnp.where(place - step >= 0, place - step, place))
-        result = put(result, left, jnp.where(place + step < count, place + step, place))
-    return put(result, shard, place)
+
+
+class Gather:
+    def __init__(self, live, name, count):
+        self.live, self.name, self.count = live, name, count
+        self.place = lax.axis_index("dp")
+        self.ups, self.downs = [], []
+
+    def step(self):
+        count, at = self.count, len(self.ups) + 1
+        if at >= count:
+            return
+        own = self.live[self.name]
+        up, down = self.ups[-1] if self.ups else own, self.downs[-1] if self.downs else own
+        ups = [(i, i + 1) for i in range(at - 1, count - 1)]
+        self.ups.append(lax.ppermute(up, "dp", ups))
+        self.downs.append(lax.ppermute(down, "dp", [(count - 1 - i, count - 1 - j) for i, j in ups]))
+
+    def moving(self):
+        return (self.ups, self.downs)
+
+    def landed(self, values):
+        self.ups, self.downs = values
+
+    def finish(self):
+        while len(self.ups) + 1 < self.count:
+            self.step()
+        count, place = self.count, self.place
+        shard = self.live.take(self.name)
+        dims = (shard.shape[0], count) + shard.shape[1:]
+        zero = jnp.zeros((), jnp.int32)
+        result = jnp.zeros(dims, shard.dtype)
+
+        def put(result, piece, at):
+            return lax.dynamic_update_slice(result, piece[:, None], (zero, at) + (zero,) * (len(dims) - 2))
+
+        for at, (up, down) in enumerate(zip(self.ups, self.downs), 1):
+            result = put(result, up, jnp.where(place - at >= 0, place - at, place))
+            result = put(result, down, jnp.where(place + at < count, place + at, place))
+        result = put(result, shard, place)
+        return result.reshape(dims[0], count * dims[2], dims[3])
 
 
 def call(kernel, out_shape, in_specs, out_specs, grid=(), scratch=(), prefetch=0, flops=0, moved=0):
@@ -116,7 +240,9 @@
             scratch_shapes=list(scratch),
         ),
         compiler_params=pltpu.CompilerParams(vmem_limit_bytes=VMEM_LIMIT),
-        cost_estimate=pl.CostEstimate(flops=int(flops), bytes_accessed=int(moved), transcendentals=0),
+        cost_estimate=pl.CostEstimate(
+            flops=int(flops * WEIGHT), bytes_accessed=int(moved * WEIGHT), transcendentals=0
+        ),
     )
 
 
@@ -131,6 +257,87 @@
 
 def bytes_of(*arrays):
     return sum(int(a.size) * a.dtype.itemsize for a in arrays)
+
+
+def read_pieces(refs, upper):
+    x0, x1, x2, top, bottom = refs
+    return jnp.concatenate([x0[...], x1[...], x2[...], jnp.where(upper, top[...], bottom[...])], axis=1)
+
+
+def piece_specs(width, tile, blocks, shift=0):
+    halfway = blocks // 2
+    plain = pl.BlockSpec((tile, width), lambda b, *_: (b + shift, 0))
+    top = pl.BlockSpec((tile, width), lambda b, *_: (jnp.minimum(b + shift, halfway - 1), 0))
+    bottom = pl.BlockSpec((tile, width), lambda b, *_: (jnp.maximum(b + shift - halfway, 0), 0))
+    return [plain, plain, plain, top, bottom]
+
+
+def join_kernel(x0, x1, x2, top, bottom, out):
+    width, half = x0.shape[1], top.shape[0]
+    for i, ref in enumerate((x0, x1, x2)):
+        out[:, i * width : (i + 1) * width] = ref[...]
+    out[:half, 3 * width :] = top[...]
+    out[half:, 3 * width :] = bottom[...]
+
+
+def join(pieces):
+    tokens, width = pieces[0].shape
+    out = shape((tokens, 4 * width))
+    return call(
+        join_kernel, out, [whole(p) for p in pieces], whole(out), grid=(1,), moved=2 * bytes_of(out)
+    )(*pieces)
+
+
+def order_kernel(row_ref, own, oth, full, mine):
+    row = row_ref[0]
+    features, chunk = own.shape[2], own.shape[1] // 4
+    for k in range(4):
+        columns = slice(k * features, (k + 1) * features)
+        for i in range(4):
+            rows = pl.ds(pl.multiple_of(jnp.bitwise_xor(row, i) * chunk, chunk), chunk)
+            for s, weight in enumerate((own, oth)):
+                at = (2 * i + s) * chunk
+                full[at : at + chunk, columns] = weight[k, rows, :]
+    mine[...] = jnp.zeros(mine.shape, mine.dtype)
+    for h in range(2 * chunk // HEAD):
+        mine[h * LANES : h * LANES + HEAD, :] = full[h * HEAD : (h + 1) * HEAD, :]
+
+
+def order(row, own, oth):
+    _, rows, features = own.shape
+    full, mine = shape((2 * rows, 4 * features)), shape((2 * rows // 4 // HEAD * LANES, 4 * features))
+    return call(
+        order_kernel,
+        (full, mine),
+        [whole(own), whole(oth)],
+        (whole(full), whole(mine)),
+        grid=(1,),
+        prefetch=1,
+        moved=2 * bytes_of(full) + bytes_of(mine),
+    )(row, own, oth)
+
+
+def heads_grad_kernel(x0, x1, x2, top, bottom, weight, own, oth):
+    upper = pl.program_id(0) < pl.num_programs(0) // 2
+    grad = dot(read_pieces((x0, x1, x2, top, bottom), upper), weight[...], NT).astype(LOW)
+    own[...] = grad[:, : own.shape[1]]
+    oth[...] = grad[:, own.shape[1] :]
+
+
+def heads_grad_of(pieces, weight):
+    tokens, width = pieces[0].shape
+    columns = weight.shape[0] // 2
+    outs = (shape((tokens, columns)), shape((tokens, columns)))
+    rows = pl.BlockSpec((TILE, columns), lambda b: (b, 0))
+    return call(
+        heads_grad_kernel,
+        outs,
+        piece_specs(width, TILE, tokens // TILE) + [whole(weight)],
+        (rows, rows),
+        grid=(tokens // TILE,),
+        flops=2 * tokens * 4 * width * weight.shape[0],
+        moved=bytes_of(*pieces, weight, *outs),
+    )(*pieces, weight)
 
 
 def pack_kernel(row_ref, q_ref, k_ref, v_ref, out_ref):
@@ -159,8 +366,9 @@
     )(row, *arrays)
 
 
-def project_kernel(x0, x1, x2, x3, gain, w_own, w_oth, cos, sin, first, r1, own, oth):
-    x = jnp.concatenate([x0[...], x1[...], x2[...], x3[...]], axis=1).astype(F32)
+def project_kernel(x0, x1, x2, top, bottom, gain, w_own, w_oth, cos, sin, first, r1, own, oth):
+    upper = pl.program_id(0) < pl.num_programs(0) // 2
+    x = read_pieces((x0, x1, x2, top, bottom), upper).astype(F32)
     inverse = lax.rsqrt(jnp.mean(x * x, axis=1, keepdims=True) + EPSILON)
     normed = (x * inverse * gain[...]).astype(LOW)
     first[...] = normed
@@ -181,7 +389,8 @@
     return call(
         project_kernel,
         outs,
-        [rows(width)] * 4 + [whole(gain), whole(w_own), whole(w_oth), rows(LANES), rows(LANES)],
+        piece_specs(width, TILE, tokens // TILE)
+        + [whole(gain), whole(w_own), whole(w_oth), rows(LANES), rows(LANES)],
         tuple(rows(o.shape[1]) for o in outs),
         grid=(tokens // TILE,),
         flops=2 * tokens * 4 * width * 1024,
@@ -382,9 +591,12 @@
     )(info, own, oth, g_own, g_oth, out, lse, start, cos, sin)
 
 
-def middle_kernel(h0, h1, h2, h3, x0, x1, x2, x3, weight, gain, second, middle, r2):
-    heads = jnp.concatenate([h0[...], h1[...], h2[...], h3[...]], axis=1)
-    x = jnp.concatenate([x0[...], x1[...], x2[...], x3[...]], axis=1).astype(F32)
+def middle_kernel(*refs):
+    weight, gain, second, middle, r2, joined = refs[10:]
+    upper = pl.program_id(0) < pl.num_programs(0) // 2
+    heads = read_pieces(refs[:5], upper)
+    joined[...] = heads
+    x = read_pieces(refs[5:10], upper).astype(F32)
     value = x + dot(heads, weight[...])
     inverse = lax.rsqrt(jnp.mean(value * value, axis=1, keepdims=True) + EPSILON)
     second[...] = (value * inverse * gain[...]).astype(LOW)
@@ -395,11 +607,16 @@
 def middle_of(heads, xs, weight, gain):
     tokens, width = xs[0].shape
     rows = lambda n: pl.BlockSpec((TILE, n), lambda b: (b, 0))
-    outs = (shape((tokens, 4 * width)), shape((tokens, width), F32), shape((tokens, LANES), F32))
+    outs = (
+        shape((tokens, 4 * width)),
+        shape((tokens, width), F32),
+        shape((tokens, LANES), F32),
+        shape((tokens, 4 * width)),
+    )
     return call(
         middle_kernel,
         outs,
-        [rows(width)] * 8 + [whole(weight), whole(gain)],
+        piece_specs(width, TILE, tokens // TILE) * 2 + [whole(weight), whole(gain)],
         tuple(rows(o.shape[1]) for o in outs),
         grid=(tokens // TILE,),
         flops=2 * tokens * 16 * width * width,
@@ -410,19 +627,23 @@
 def feed_kernel(second, cot, g_own, u_own, g_oth, u_oth, d_own, d_oth, hidden_own, hidden_oth, back_own, back_oth):
     block = pl.program_id(0)
     per = pl.num_programs(0) // 2
-    units = hidden_own.shape[1]
+    tokens, units = hidden_own.shape
+    width = d_own.shape[2]
 
     def body(gate_w, up_w, down_w, hidden, back, at):
-        gate = dot(second[...], gate_w[...])
-        up = dot(second[...], up_w[...])
-        hidden_grad = dot(cot[...], down_w[...], NT)
-        share = 1.0 / (1.0 + jnp.exp(-gate))
-        silu = gate * share
-        hidden[:, pl.ds(pl.multiple_of(at, TILE), TILE)] = (silu * up).astype(LOW)
-        back[:, pl.ds(pl.multiple_of(at, TILE), TILE)] = (
-            hidden_grad * up * share * (1.0 + gate * (1.0 - share))
-        ).astype(LOW)
-        back[:, pl.ds(pl.multiple_of(units + at, TILE), TILE)] = (hidden_grad * silu).astype(LOW)
+        down = jnp.concatenate([down_w[i] for i in range(4)], axis=1)
+        near = pl.ds(pl.multiple_of(at, TILE), TILE)
+        far = pl.ds(pl.multiple_of(units + at, TILE), TILE)
+        for m in range(0, tokens, TILE):
+            rows = slice(m, m + TILE)
+            gate = dot(second[rows, :], gate_w[...])
+            up = dot(second[rows, :], up_w[...])
+            hidden_grad = dot(cot[rows, :], down, NT)
+            share = 1.0 / (1.0 + jnp.exp(-gate))
+            silu = gate * share
+            hidden[rows, near] = (silu * up).astype(LOW)
+            back[rows, near] = (hidden_grad * up * share * (1.0 + gate * (1.0 - share))).astype(LOW)
+            back[rows, far] = (hidden_grad * silu).astype(LOW)
 
     @pl.when(block < per)
     def _():
@@ -440,7 +661,7 @@
     early = lambda b: jnp.minimum(b, per - 1)
     late = lambda b: jnp.maximum(b - per, 0)
     column = lambda at: pl.BlockSpec((model, TILE), lambda b: (0, at(b)))
-    down = lambda at: pl.BlockSpec((TILE, model), lambda b: (at(b), 0))
+    down = lambda at: pl.BlockSpec((4, TILE, model // 4), lambda b: (0, at(b), 0))
     outs = (shape((tokens, units)), shape((tokens, units)), shape((tokens, 2 * units)), shape((tokens, 2 * units)))
     return call(
         feed_kernel,
@@ -462,37 +683,34 @@
     )(second, cot, gu_own, gu_own, gu_oth, gu_oth, d_own, d_oth)
 
 
-def back_kernel(dims, a_own, a_oth, w_own, w_oth, *rest):
-    value = dot(a_own[...], w_own[...], dims) + dot(a_oth[...], w_oth[...], dims)
+def partial_kernel(which, blocked, a_own, a_oth, w_own, w_oth, *rest):
     if len(rest) == 5:
         against, own, far, near, sums = rest
-        sums[...] = jnp.broadcast_to(
-            jnp.sum(value * against[...].astype(F32), axis=1, keepdims=True), sums.shape
-        )
     else:
         own, far, near = rest
     width = own.shape[1]
-    low = value.astype(LOW)
-    own[...] = low[:, :width]
-    return low, far, near, width
-
-
-def back_first(dims, *refs):
-    low, far, near, width = back_kernel(dims, *refs)
-    far[:, :width] = low[:, width : 2 * width]
-    far[:, width:] = low[:, 3 * width :]
-    near[...] = low[:, 2 * width : 3 * width]
-
-
-def back_second(dims, *refs):
-    low, far, near, width = back_kernel(dims, *refs)
-    far[...] = low[:, 2 * width :]
-    near[...] = low[:, width : 2 * width]
-
-
-def partial_half(which, dims, a_own, a_oth, w_own, w_oth, against):
+    total = 0.0
+    left, right = a_own[...], a_oth[...]
+    for k, target in enumerate((own, far if not which else near, near if not which else far, far)):
+        columns = slice(k * width, (k + 1) * width)
+        if blocked:
+            value = dot(left, w_own[k]) + dot(right, w_oth[k])
+        else:
+            value = dot(left, w_own[columns, :], NT) + dot(right, w_oth[columns, :], NT)
+        if len(rest) == 5:
+            total = total + jnp.sum(value * against[:, columns].astype(F32), axis=1, keepdims=True)
+        if target is far:
+            place = width if k == 3 else 0
+            far[:, place : place + width] = value.astype(LOW)
+        else:
+            target[...] = value.astype(LOW)
+    if len(rest) == 5:
+        sums[...] = jnp.broadcast_to(total, sums.shape)
+
+
+def partial_half(which, blocked, a_own, a_oth, w_own, w_oth, against):
     tokens, depth = a_own.shape
-    model = w_own.shape[0] if dims == NT else w_own.shape[1]
+    model = 4 * w_own.shape[2] if blocked else w_own.shape[0]
     half, width = tokens // 2, model // 4
     blocks = half // TILE
     read = lambda n: pl.BlockSpec((TILE, n), lambda b: (which * blocks + b, 0))
@@ -505,7 +723,7 @@
         args.append(against)
         specs.append(read(model))
     return call(
-        functools.partial(back_second if which else back_first, dims),
+        functools.partial(partial_kernel, which, blocked),
         tuple(outs),
         specs,
         tuple(write(o.shape[1]) for o in outs),
@@ -515,28 +733,83 @@
     )(*args)
 
 
-def partial_sums(dims, a_own, a_oth, w_own, w_oth, against=None):
-    first = partial_half(0, dims, a_own, a_oth, w_own, w_oth, against)
-    second = partial_half(1, dims, a_own, a_oth, w_own, w_oth, against)
+def partial_sums(blocked, a_own, a_oth, w_own, w_oth, against=None):
+    first = partial_half(0, blocked, a_own, a_oth, w_own, w_oth, against)
+    second = partial_half(1, blocked, a_own, a_oth, w_own, w_oth, against)
     sums = None if against is None else jnp.concatenate([first[3][:, 0], second[3][:, 0]])
     return (first[0], first[1], first[2], second[0], second[1], second[2]), sums
 
 
+def feed_grads_kernel(second, cot, back, hidden, out):
+    double, share = back.shape[1], out.shape[2]
+    for columns, left, right in ((slice(0, double), second, back), (slice(double, None), cot, hidden)):
+        value = dot(left[...], right[...], TN).astype(LOW)
+        for k in range(out.shape[0]):
+            out[k, 0, :, columns] = value[k * share : (k + 1) * share]
+
+
+def feed_grads(second, cot, back, hidden, count):
+    tokens, model = second.shape
+    width = model // 4
+    out = shape((count, 4, width // count, back.shape[1] + hidden.shape[1]))
+    block = pl.BlockSpec((tokens, width), lambda i: (0, i))
+    return call(
+        feed_grads_kernel,
+        out,
+        [block, block, whole(back), whole(hidden)],
+        pl.BlockSpec((count, 1) + out.shape[2:], lambda i: (0, i, 0, 0)),
+        grid=(4,),
+        flops=2 * tokens * model * out.shape[3],
+        moved=bytes_of(second, cot, back, hidden, out),
+    )(second, cot, back, hidden)
+
+
+def mix_grads_kernel(which, first, heads, back, branch, spread, out, flat):
+    @pl.when(pl.program_id(0) == 0)
+    def _():
+        flat[...] = dot(back[...], spread[...], NT).astype(LOW)
+
+    width, chunk = first.shape[1], heads.shape[1] // 2
+    out[0, :width, :] = dot(first[...], flat[...], TN).astype(LOW)
+    out[0, width:, :] = dot(heads[:, which * chunk : (which + 1) * chunk], branch[...], TN).astype(LOW)
+
+
+def mix_grads(which, first, heads, back, branch, spread):
+    tokens, model = first.shape
+    width = model // 4
+    out = shape((4, width + width // 2, width))
+    block = pl.BlockSpec((tokens, width), lambda i: (0, i))
+    return call(
+        functools.partial(mix_grads_kernel, which),
+        out,
+        [block, block, whole(back), whole(branch), whole(spread)],
+        pl.BlockSpec((1,) + out.shape[1:], lambda i: (i, 0, 0)),
+        grid=(4,),
+        scratch=(pltpu.VMEM((tokens, spread.shape[0]), LOW),),
+        flops=2 * tokens * model * out.shape[1],
+        moved=bytes_of(first, heads, back, branch, out),
+    )(first, heads, back, branch, spread)
+
+
 def feed_place_kernel(row_ref, piece, gate, up, down):
-    units = gate.shape[1]
-    gate[...] = piece[0, :, :units].astype(F32)
-    up[...] = piece[0, :, units : 2 * units].astype(F32)
-    down[...] = piece[0, :, 2 * units :].astype(F32).T
+    units, share = gate.shape[1], piece.shape[2]
+    for k in range(piece.shape[0]):
+        rows = slice(k * share, (k + 1) * share)
+        gate[rows, :] = piece[k, 0, :, :units].astype(F32)
+        up[rows, :] = piece[k, 0, :, units : 2 * units].astype(F32)
+    down[...] = jnp.concatenate(
+        [piece[k, 0, :, 2 * units :].astype(F32) for k in range(piece.shape[0])], axis=0
+    ).T
 
 
 def feed_place(row, pieces):
-    _, depth, triple = pieces.shape
-    units = triple // 3
+    count, _, share, triple = pieces.shape
+    units, depth = triple // 3, count * share
     outs = (shape((depth, 4 * units), F32), shape((depth, 4 * units), F32), shape((4 * units, depth), F32))
     return call(
         feed_place_kernel,
         outs,
-        [pl.BlockSpec((1, depth, triple), lambda j, s: (jnp.bitwise_xor(s[0], j), 0, 0))],
+        [pl.BlockSpec((count, 1, share, triple), lambda j, s: (0, jnp.bitwise_xor(s[0], j), 0, 0))],
         (
             pl.BlockSpec((depth, units), lambda j, s: (0, j)),
             pl.BlockSpec((depth, units), lambda j, s: (0, j)),
@@ -607,12 +880,6 @@
     inside = jnp.where((head < 3) & (entry >= SIDE), entry - SIDE + LANES // 2, entry)
     target = head * LANES + inside
     return (target[:, None] == jnp.arange(4 * LANES, dtype=jnp.int32)[None, :]).astype(LOW)
-
-
-def pad_heads(rows):
-    heads = rows.shape[0] // HEAD
-    split = rows.reshape(heads, HEAD, rows.shape[1])
-    return jnp.pad(split, ((0, 0), (0, LANES - HEAD), (0, 0))).reshape(heads * LANES, rows.shape[1])
 
 
 def on_device(
@@ -631,150 +898,206 @@
 ):
     row = lax.axis_index("row")
     core = lax.axis_index("col")
+    place = lax.axis_index("dp")
     blocks = lax.axis_size("dp")
     row_info = row.reshape(1).astype(jnp.int32)
     half, width = layer_input.shape
     tokens, model = 2 * half, 4 * width
     units = gate_weight.shape[1] // 4
+    rows = output_weight.shape[0]
+    chunk = rows // 4
     relative = [jnp.bitwise_xor(row, i) for i in range(4)]
-
+    live = Live(
+        x=layer_input,
+        cot=cotangent,
+        g=jnp.stack([first_gain, second_gain]),
+        gate=gate_weight,
+        up=up_weight,
+        down=down_weight,
+        out=output_weight,
+    )
+
+    gather_one(live, "x")
     packed = pack(row_info, query_weight, key_projection_weight, value_projection_weight)
-    xs = gather_row(layer_input)
-    gains = jnp.stack([first_gain, second_gain])
-    gains = jnp.concatenate(exchange_row([gains] * 4), axis=1)
-    mixer = jnp.concatenate(exchange_row([packed[i] for i in range(4)]), axis=0)
-    w_own = dot(mixer, spread_matrix()).astype(LOW)
-    w_oth = other(w_own)
-
+    fetch_one(live, "mix", [packed[i] for i in range(4)], place, blocks)
+    live["g"] = jnp.concatenate([live["g"], swap(live["g"], 1)], axis=1)
+    live.sync()
+
+    gather_two(live, "x")
+    fetch_two(live, "mix", blocks)
+    live["gains"] = jnp.concatenate([live["g"], swap(live.take("g"), 2)], axis=1)
     places, starts = sequence_starts(sequence_lengths[0], tokens)
-    cosine, sine = tables(places - starts)
-    start_row = starts[None, :]
-    first_blocks = starts[::TILE] // TILE
-    info = jnp.concatenate([core.reshape(1), first_blocks]).astype(jnp.int32)
-    cos_own = lax.dynamic_slice_in_dim(cosine, core * half, half, 0)
-    sin_own = lax.dynamic_slice_in_dim(sine, core * half, half, 0)
-
-    first, r1, qkv_own, qkv_oth = project(xs, gains[:1], w_own, w_oth, cos_own, sin_own)
-    qkv_got = other(qkv_oth)
-    keep, send, attended, lse = attend(info, qkv_own, qkv_got, start_row)
-    heads = gather_row(jnp.concatenate([keep, other(send)], axis=1))
-
-    out_w = jnp.concatenate(gather_row(output_weight), axis=1)
-    out_w_oth = other(out_w)
-    chunk = out_w.shape[0] // 4
-    ordered = []
+    live["cos"], live["sin"] = tables(places - starts)
+    live["start"] = starts[None, :]
+    live["info"] = jnp.concatenate([core.reshape(1), starts[::TILE] // TILE]).astype(jnp.int32)
+    gate, up, down, out = live.take("gate", "up", "down", "out")
     for i in range(4):
-        for matrix in (out_w, out_w_oth):
-            ordered.append(lax.dynamic_slice_in_dim(matrix, relative[i] * chunk, chunk, 0))
-    out_full = jnp.concatenate(ordered, axis=0)
-    out_mine = pad_heads(out_full[: 2 * chunk])
-
-    gate_up = [
-        jnp.concatenate(
-            [lax.dynamic_slice_in_dim(w, relative[i] * units, units, 1) for w in (gate_weight, up_weight)], axis=1
+        downs = lax.dynamic_slice_in_dim(down, relative[i] * units, units, 0)
+        live[f"odp{i}"] = jnp.concatenate([out, downs], axis=0)
+        live[f"gup{i}"] = jnp.concatenate(
+            [lax.dynamic_slice_in_dim(w, relative[i] * units, units, 1) for w in (gate, up)], axis=1
         )
-        for i in range(4)
-    ]
-    gu_own = jnp.concatenate(exchange_row(gate_up), axis=0)
-    gu_oth = other(gu_own)
-    down = [lax.dynamic_slice_in_dim(down_weight, relative[i] * units, units, 0) for i in range(4)]
-    d_own = jnp.concatenate(exchange_row(down), axis=1)
-    d_oth = other(d_own)
-    cot = jnp.concatenate(gather_row(cotangent), axis=1)
-
-    second, middle, r2 = middle_of(heads, xs, out_full, gains[1:])
-    hidden_own, hidden_oth, back_own, back_oth = feed(second, cot, gu_own, gu_oth, d_own, d_oth)
-
-    parts, sums = partial_sums(NT, back_own, back_oth, gu_own, gu_oth, second)
-    second_grad = scatter_row(parts)
-    inner = total_row(sums.reshape(8, half // 8)).reshape(half)
-    parts, _ = partial_sums(NN, hidden_own, hidden_oth, d_own, d_oth)
-    layer_output = (middle + scatter_row(parts)).astype(LOW)
-
-    def both(own, oth):
-        return own.astype(LOW), oth.astype(LOW)
-
-    g_own, g_oth = both(dot(second, back_own, TN), dot(second, back_oth, TN))
-    c_own, c_oth = both(dot(cot, hidden_own, TN), dot(cot, hidden_oth, TN))
-    feed_own = jnp.concatenate([g_own, c_own], axis=1)
-    feed_oth = jnp.concatenate([g_oth, c_oth], axis=1)
-    feed_sum = (feed_own.astype(F32) + other(feed_oth).astype(F32)).astype(LOW)
-    feed_sum = feed_sum.reshape(4, width, 3 * units)
-    share = width // blocks
-
-    def finish(take):
-        shard = chain_scatter(take, blocks)
-        return shard
-
-    feed_shard = finish(lambda s: lax.dynamic_slice_in_dim(feed_sum, s * share, share, 1))
-    feed_shard = jnp.stack(exchange_row([feed_shard[i] for i in range(4)]))
-    feed_all = chain_gather(feed_shard, blocks).reshape(4, width, 3 * units)
-    gate_total, up_total, down_total = feed_place(row_info, feed_all)
-
-    r2 = r2[:, :1]
-    middle_grad = (
+    spread = spread_matrix()
+    live.sync()
+
+    fetch_one(live, "od", live.take(*[f"odp{i}" for i in range(4)]), place, blocks)
+    mixer = fetched(live, "mix", place, blocks).reshape(model, 4 * HEAD)
+    live["w_own"] = dot(mixer, spread).astype(LOW)
+    live["w_oth"] = other(live["w_own"])
+    cos_own = lax.dynamic_slice_in_dim(live["cos"], core * half, half, 0)
+    sin_own = lax.dynamic_slice_in_dim(live["sin"], core * half, half, 0)
+    live["first"], live["r1"], live["qkv"], live["qkv_send"] = project(
+        gathered(live, "x"), live["gains"][:1], live["w_own"], live["w_oth"], cos_own, sin_own
+    )
+    live.sync()
+    fetch_one(live, "gu", live.take(*[f"gup{i}" for i in range(4)]), place, blocks)
+    fetch_two(live, "od", blocks)
+    live["qkv_got"] = other(live.take("qkv_send"))
+    live["keep"], live["send"], live["attended"], live["lse"] = attend(
+        live["info"], live["qkv"], live["qkv_got"], live["start"]
+    )
+    coming = ("odp",) if blocks % 2 == 0 else ()
+    live.sync(late=coming)
+    keep, send = live.take("keep", "send")
+    live["heads"] = jnp.concatenate([keep, other(send)], axis=1)
+    live.sync(late=coming)
+
+    gather_one(live, "heads")
+    gather_one(live, "cot")
+    fetch_two(live, "gu", blocks)
+    od_own = fetched(live, "od", place, blocks)
+    od_oth = other(od_own)
+    live["out_full"], live["out_mine"] = order(row_info, od_own[:, :rows], od_oth[:, :rows])
+    live["d_own"], live["d_oth"] = od_own[:, rows:], od_oth[:, rows:]
+    live.sync()
+
+    gather_two(live, "heads")
+    gather_two(live, "cot")
+    live["gu_own"] = fetched(live, "gu", place, blocks).reshape(model, 2 * units)
+    live["gu_oth"] = other(live["gu_own"])
+    live.sync()
+
+    live["second"], live["middle"], live["r2"], live["heads_all"] = middle_of(
+        gathered(live, "heads"), gathered(live, "x"), live["out_full"], live["gains"][1:]
+    )
+    live["cot_all"] = join(gathered(live, "cot"))
+
+    live["hid_own"], live["hid_oth"], live["back_own"], live["back_oth"] = feed(
+        live["second"], live["cot_all"], live["gu_own"], live["gu_oth"], live["d_own"], live["d_oth"]
+    )
+    parts, sums = partial_sums(
+        False, live["back_own"], live["back_oth"], live["gu_own"], live["gu_oth"], live["second"]
+    )
+    scatter_put(live, "sg", parts)
+    live["sums"] = sums.reshape(8, half // 8)
+    live.sync()
+
+    def added(own, got):
+        return (own.astype(F32) + got.astype(F32)).astype(LOW)
+
+    scatter_one(live, "sg")
+    live["sums"] = live["sums"] + swap(live["sums"], 1)
+    live["feed_send"] = feed_grads(live["second"], live["cot_all"], live["back_oth"], live["hid_oth"], blocks)
+    live["feed"] = feed_grads(live["second"], live["cot_all"], live["back_own"], live["hid_own"], blocks)
+    live.sync()
+
+    scatter_two(live, "sg")
+    live["inner"] = live["sums"] + swap(live.take("sums"), 2)
+    live["feed"] = added(live["feed"], other(live.take("feed_send")))
+    live.sync()
+
+    feed_sum = lax.psum_scatter(live.take("feed"), "dp", scatter_dimension=0)
+    second_grad = scattered(live, "sg")
+    inner = live.take("inner").reshape(half)
+    r2, middle = live["r2"][:, :1], live["middle"]
+    live["middle_grad"] = (
         cotangent.astype(F32)
         + r2 * second_gain[None, :] * second_grad
         - middle * (r2 * r2 * inner[:, None] / model)
     )
-    second_gain_part = jnp.sum(second_grad * middle * r2, axis=0)
-    branch = middle_grad.astype(LOW)
-    branch_all = jnp.concatenate(gather_row(branch), axis=1)
-    heads_grad = dot(branch_all, out_mine, NT).astype(LOW)
-    grad_own = heads_grad[:, : 2 * LANES]
-    grad_got = other(heads_grad[:, 2 * LANES :])
-    back_keep, back_send = attend_back(
-        info, qkv_own, qkv_got, grad_own, grad_got, attended, lse, start_row, cosine, sine
-    )
-    back_got = other(back_send)
-    parts, sums = partial_sums(NT, back_keep, back_got, w_own, w_oth, first)
-    first_grad = scatter_row(parts)
-    inner = total_row(sums.reshape(8, half // 8)).reshape(half)
-    r1 = r1[:, :1]
+    live["gain2"] = jnp.sum(second_grad * middle * r2, axis=0)
+    live["branch"] = live["middle_grad"].astype(LOW)
+    gather_one(live, "branch")
+    parts, _ = partial_sums(True, live["hid_own"], live["hid_oth"], live["d_own"], live["d_oth"])
+    scatter_put(live, "fo", parts)
+    live.sync()
+
+    gather_two(live, "branch")
+    live.sync()
+    live["grad"], live["grad_send"] = heads_grad_of(gathered(live, "branch"), live["out_mine"])
+    live["grad_got"] = other(live.take("grad_send"))
+    live.sync()
+
+    scatter_one(live, "fo")
+    live["bk"], live["bs"] = attend_back(
+        live["info"], live["qkv"], live["qkv_got"], live["grad"], live["grad_got"],
+        live["attended"], live["lse"], live["start"], live["cos"], live["sin"],
+    )
+    live["feed"] = feed_sum
+    live.sync()
+
+    live["feed"] = spread_row(live["feed"])
+    scatter_two(live, "fo")
+    live["bg"] = other(live.take("bs"))
+    live["mix_send"] = mix_grads(1, live["first"], live["heads_all"], live["bg"], live["branch"], spread)
+    live["mix"] = mix_grads(0, live["first"], live["heads_all"], live["bk"], live["branch"], spread)
+    live.sync()
+    feeds = lax.all_gather(live.take("feed"), "dp", axis=0)
+    live["mix"] = added(live["mix"], other(live.take("mix_send")))
+    parts, sums = partial_sums(False, live["bk"], live["bg"], live["w_own"], live["w_oth"], live["first"])
+    scatter_put(live, "fg", parts)
+    live["sums"] = sums.reshape(8, half // 8)
+    live.sync()
+
+    scatter_one(live, "fg")
+    live["sums"] = live["sums"] + swap(live["sums"], 1)
+    layer_output = (live["middle"] + scattered(live, "fo")).astype(LOW)
+    share = width // blocks
+    mixes = Scatter(live, "mix", blocks, (width, chunk))
+    mixes.step()
+    live.sync(mixes)
+
+    scatter_two(live, "fg")
+    live["inner"] = live["sums"] + swap(live.take("sums"), 2)
+    mixes.step()
+    live.sync(mixes)
+
+    mixes.step()
+    first_grad = scattered(live, "fg")
+    inner = live.take("inner").reshape(half)
+    r1 = live["r1"][:, :1]
     inputs = layer_input.astype(F32)
     input_gradient = (
-        middle_grad + r1 * first_gain[None, :] * first_grad - inputs * (r1 * r1 * inner[:, None] / model)
-    )
-    first_gain_part = jnp.sum(first_grad * inputs * r1, axis=0)
-
-    spread = spread_matrix()
-    flat_own = dot(back_keep, spread, NT).astype(LOW)
-    flat_got = dot(back_got, spread, NT).astype(LOW)
-    q_own, q_oth = both(dot(first, flat_own, TN), dot(first, flat_got, TN))
-    heads_all = jnp.concatenate(heads, axis=1)
-    o_all = dot(heads_all, branch, TN).astype(LOW).reshape(4, 2, chunk, width)
-    mix_own = jnp.concatenate([q_own.reshape(4, width, 2 * chunk), o_all[:, 0]], axis=1)
-    mix_oth = jnp.concatenate([q_oth.reshape(4, width, 2 * chunk), o_all[:, 1]], axis=1)
-    mix_sum = (mix_own.astype(F32) + other(mix_oth).astype(F32)).astype(LOW)
-    small = chunk // blocks
-
-    def take(s):
-        return jnp.concatenate(
-            [
-                lax.dynamic_slice_in_dim(mix_sum, s * share, share, 1),
-                lax.dynamic_slice_in_dim(mix_sum, width + s * small, small, 1),
-            ],
-            axis=1,
-        )
-
-    mix_shard = finish(take)
-    mix_shard = jnp.concatenate(
-        [jnp.stack(exchange_row([mix_shard[i, :share] for i in range(4)])), mix_shard[:, share:]], axis=1
-    )
-    mix_all = chain_gather(mix_shard, blocks)
-    query_total, key_total, value_total, output_total = mix_place(
-        row_info,
-        mix_all[:, :, :share].reshape(4, width, 2 * chunk),
-        mix_all[:, :, share:].reshape(4, chunk, width),
-    )
-
-    gain_parts = jnp.stack([first_gain_part, second_gain_part])
-    gain_parts = gain_parts + other(gain_parts)
-    gain_total = gain_parts
+        live["middle_grad"]
+        + r1 * first_gain[None, :] * first_grad
+        - inputs * (r1 * r1 * inner[:, None] / model)
+    )
+    gains = jnp.stack([jnp.sum(first_grad * inputs * r1, axis=0), live["gain2"]])
+    live["gains"] = gains + other(gains)
+    live.sync(mixes)
+
+    shard = mixes.finish()
+    turned = spread_row(shard[:, :share])
+    live["mix"] = jnp.concatenate([turned, shard[:, share:]], axis=1)
+    live.sync()
+    mixes = Gather(live, "mix", blocks)
+    mixes.step()
+    gain_total = live["gains"]
     for step in range(1, blocks):
         gain_total = gain_total + lax.ppermute(
-            gain_parts, "dp", [(i, (i + step) % blocks) for i in range(blocks)]
+            live["gains"], "dp", [(i, (i + step) % blocks) for i in range(blocks)]
         )
+    live["gains"] = gain_total
+    live.sync(mixes)
+    mixes.step()
+    live.sync(mixes)
+    mixes.step()
+    gate_total, up_total, down_total = feed_place(row_info, feeds)
+    mixes = mixes.finish().reshape(4, blocks, share + chunk // blocks, width)
+    query_total, key_total, value_total, output_total = mix_place(
+        row_info, mixes[:, :, :share].reshape(4, width, width), mixes[:, :, share:].reshape(4, chunk, width)
+    )
+    gain_total = live["gains"]
     return (
         layer_output,
         input_gradient,

time: 752 us -> 587 us (0.78)
  waiting for transfers between devices: 287 us -> 184 us
  Pallas kernels: 113 us -> 156 us
  matrix products: 35.1 us -> 1.1 us
  starting transfers between devices: 149 us -> 115 us
  other arithmetic: 79.5 us -> 47.7 us
  local copies, waits for them, and re-layouts: 72.9 us -> 53.9 us
  between operations: 4.71 us -> 17.8 us
    ppermute x27 -> x18, waiting for transfers between devices: 172 us -> 52 us  [the longest x6 33.8 us: step(): lax.ppermute(down, 'dp', [(count - 1 - i, count - 1 - j) for i, j in ups])]
    pallas_call x9 -> x16, Pallas kernels: 52.8 us -> 97.1 us  [the longest x6 34.7 us: partial_half(): call(functools.partial(partial_kernel, which, blocked), tuple(outs), spec...]
    dot_general x9 -> x1, matrix products: 35.1 us -> 1.1 us  [dot(): return lax.dot_general(left, right, dims, preferred_element_type=F32)]
    concatenate x13 -> x8, other arithmetic: 28.9 us -> 4.07 us  [the longest x1 2.17 us: on_device(): live[f'odp{i}'] = jnp.concatenate([out, downs], axis=0)]
    reduce_scatter x0 -> x1, waiting for transfers between devices: none -> 18.7 us  [on_device(): feed_sum = lax.psum_scatter(live.take('feed'), 'dp', scatter_dimension=0)]
    ppermute x56 -> x49, starting transfers between devices: 76.4 us -> 58.2 us  [swap(): return lax.ppermute(value, 'row', [(i, i ^ step) for i in range(4)])]
    ppermute x27 -> x18, starting transfers between devices: 70.9 us -> 56.3 us  [the longest x3 26 us: step(): self.up = lax.ppermute(up, 'dp', ups)]
    ppermute x56 -> x49, waiting for transfers between devices: 115 us -> 103 us  [swap(): return lax.ppermute(value, 'row', [(i, i ^ step) for i in range(4)])]
  transfers between devices with their start and end apart: 94 -> 79, of which waited for: 29 -> 38; matrix products, arithmetic and copies ran while one was open for 23% -> 13% of each run, Pallas kernels for 10% -> 19%
where the time goes in v2:
time: 587 us; the launch traced here: 576 us
  waiting for transfers between devices  184 us (31%)
  Pallas kernels  156 us (27%)
  starting transfers between devices  115 us (20%)
  local copies, waits for them, and re-layouts  53.9 us (9%)
  other arithmetic  47.7 us (8%)
  between operations  17.8 us (3%)
    ppermute x49, waiting for transfers between devices, swap(): return lax.ppermute(value, 'row', [(i, i ^ step) for i in range(4)])  103 us
    ppermute x49, starting transfers between devices, swap(): return lax.ppermute(value, 'row', [(i, i ^ step) for i in range(4)])  58.2 us
    pallas_call x6, Pallas kernels, partial_half(): call(functools.partial(partial_kernel, which, blocked), tuple(outs), spec...  34.7 us
    ppermute x6, waiting for transfers between devices, step(): lax.ppermute(down, 'dp', [(count - 1 - i, count - 1 - j) for i, j in ups])  33.8 us
    ppermute x3, starting transfers between devices, step(): self.up = lax.ppermute(up, 'dp', ups)  26 us
    pallas_call x1, Pallas kernels, attend_back(): call(attend_back_kernel, outs, [whole(own), whole(oth), whole(g_own), who...  22.2 us
    unnamed x200, local copies, waits for them, and re-layouts  22.2 us
    reduce_scatter x1, waiting for transfers between devices, on_device(): feed_sum = lax.psum_scatter(live.take('feed'), 'dp', scatter_dimension=0)  18.7 us
  transfers between devices with their start and end apart: 79, of which 38 were waited for; matrix products, arithmetic and copies ran while one was open for 13% of the time, Pallas kernels for 19%

profile of v2, /device:TPU:0, one launch (start us, length us, event | category | flops | bytes accessed | tf_op | source)
XLA Modules:
  0.0 576.0 jit_solution(15259784588756962777)
XLA Ops:
  7.2 3.0 collective-permute-start.4
  18.8 2.0 collective-permute-start
  24.9 5.6 fusion.6
  31.2 2.7 collective-permute-start.3
  34.0 3.2 collective-permute-done.3
  37.3 1.9 collective-permute-start.7
  47.0 2.2 pad_maximum_fusion.3
  53.7 2.3 constant_dynamic-slice_fusion.19
  56.6 1.9 constant_dynamic-slice_fusion.18
  65.3 8.0 %shard_map.204 = (bf16[1024,1536]{1,0:T(8,128)(2,1)}, f32[1024,128]{1,0:T(8,128)S(1)}, bf16[1024,512]{1,0:T(8,128)(2,1)S(1)}, bf16[1024,512]{1,0:T(8,128)(2,1)}) custom-call(bf16[1024,384]{1,0:T(8,128)(2,1)S(1)} %copy-done.11, bf16[1024,384]{1,0:T(8,128)(2,1)S(1)} %collective-permute-done.4.x1.refs_6_, bf16[1024,384]{1,0:T(8,128)(2,1)S(1)} %copy-done.19, ...), custom_call_target="tpu_custom_call" | custom-call | flops 50331648 | bytes 188416 | tf_op jit(solution)/shard_map/pallas_call | solution.py:389
  73.3 9.0 %collective-permute-done.12 = bf16[640,384]{1,0:T(8,128)(2,1)} collective-permute-done((bf16[640,384]{1,0:T(8,128)(2,1)}, bf16[640,384]{1,0:T(8,128)(2,1)}, u32[]{:S(2)}, u32[]{:S(2)}) %collective-permute-start.12) | collective-permute-done | bytes 491552 | tf_op jit(solution)/shard_map/ppermute | solution.py:32
  88.1 17.3 %shard_map.205 = (bf16[1024,192]{1,0:T(8,128)(2,1)S(1)}, bf16[1024,192]{1,0:T(8,128)(2,1)S(1)}, bf16[2048,256]{1,0:T(8,128)(2,1)S(1)}, f32[1,4096]{1,0:T(1,128)S(1)}) custom-call(s32[9]{0:T(128)S(1)} %pad_add_fusion.info, bf16[1024,512]{1,0:T(8,128)(2,1)S(1)} %get-tuple-element.858.own, bf16[1024,512]{1,0:T(8,128)(2,1)S(1)} %collective-permute-done.14.oth, ...), custom_call_target="tpu_custom_call" | custom-call | flops 67108864 | bytes 61696 | tf_op jit(solution)/shard_map/pallas_call | solution.py:472
  107.9 1.9 collective-permute-done.18
  110.8 8.0 %collective-permute-done.21 = bf16[3,640,384]{2,1,0:T(8,128)(2,1)} collective-permute-done((bf16[3,640,384]{2,1,0:T(8,128)(2,1)S(1)}, bf16[3,640,384]{2,1,0:T(8,128)(2,1)}, u32[]{:S(2)}, u32[]{:S(2)}) %collective-permute-start.21) | collective-permute-done | bytes 1474592 | tf_op jit(solution)/shard_map/ppermute | solution.py:40
  125.2 2.2 collective-permute-done.22
  130.9 4.2 shard_map.206
  135.2 2.2 slice.224.d_oth.w_oth
  137.4 4.7 collective-permute-done.19.x1
  143.6 14.1 %collective-permute-done.24.refs_1_ = bf16[1024,384]{1,0:T(8,128)(2,1)S(1)} collective-permute-done((bf16[1024,384]{1,0:T(8,128)(2,1)S(1)}, bf16[1024,384]{1,0:T(8,128)(2,1)S(1)}, u32[]{:S(2)}, u32[]{:S(2)}) %collective-permute-start.24) | collective-permute-done | bytes 786464 | tf_op jit(solution)/shard_map/ppermute | solution.py:32
  164.2 7.5 %collective-permute-done.26.bottom = bf16[512,384]{1,0:T(8,128)(2,1)S(1)} collective-permute-done((bf16[512,384]{1,0:T(8,128)(2,1)S(1)}, bf16[512,384]{1,0:T(8,128)(2,1)S(1)}, u32[]{:S(2)}, u32[]{:S(2)}) %collective-permute-start.26) | collective-permute-done | bytes 393248 | tf_op jit(solution)/shard_map/ppermute | solution.py:32
  172.4 7.4 %collective-permute-done.29.refs_4_ = bf16[512,384]{1,0:T(8,128)(2,1)S(1)} collective-permute-done((bf16[512,384]{1,0:T(8,128)(2,1)S(1)}, bf16[512,384]{1,0:T(8,128)(2,1)S(1)}, u32[]{:S(2)}, u32[]{:S(2)}) %collective-permute-start.29) | collective-permute-done | bytes 393248 | tf_op jit(solution)/shard_map/ppermute | solution.py:32
  181.9 2.0 shard_map.208.cot
  184.0 10.3 %shard_map.207 = (bf16[1024,1536]{1,0:T(8,128)(2,1)}, f32[1024,384]{1,0:T(8,128)}, f32[1024,128]{1,0:T(8,128)S(1)}, bf16[1024,1536]{1,0:T(8,128)(2,1)}) custom-call(bf16[1024,384]{1,0:T(8,128)(2,1)S(1)} %pad_maximum_fusion.13.refs_0_, bf16[1024,384]{1,0:T(8,128)(2,1)S(1)} %collective-permute-done.24.refs_1_, ...), custom_call_target="tpu_custom_call" | custom-call | flops 75497472 | bytes 303104 | tf_op jit(solution)/shard_map/pallas_call | solution.py:616
  194.3 17.1 %shard_map.209 = (bf16[1024,512]{1,0:T(8,128)(2,1)S(1)}, bf16[1024,512]{1,0:T(8,128)(2,1)S(1)}, bf16[1024,1024]{1,0:T(8,128)(2,1)}, bf16[1024,1024]{1,0:T(8,128)(2,1)}) custom-call(bf16[1024,1536]{1,0:T(8,128)(2,1)} %get-tuple-element.714.second.rest_0_, bf16[1024,1536]{1,0:T(8,128)(2,1)} %shard_map.208.cot, bf16[1536,1024]{1,0:T(8,128)(2,1)} %bitcast.88, ...), custom_call_target="tpu_custom_call" | custom-call | flops 150994944 | bytes 344064 | tf_op jit(solution)/shard_map/pallas_call | solution.py:666
  211.5 2.3 copy-done.1
  215.4 8.0 %shard_map.211 = (bf16[512,384]{1,0:T(8,128)(2,1)S(1)}, bf16[512,768]{1,0:T(8,128)(2,1)S(1)}, bf16[512,384]{1,0:T(8,128)(2,1)S(1)}, f32[512,128]{1,0:T(8,128)S(1)}) custom-call(bf16[1024,1024]{1,0:T(8,128)(2,1)S(1)} %copy-done.1, bf16[1024,1024]{1,0:T(8,128)(2,1)S(1)} %copy-done.3, bf16[1536,1024]{1,0:T(8,128)(2,1)} %bitcast.90, ...), custom_call_target="tpu_custom_call" | custom-call | flops 50331648 | bytes 159744 | tf_op jit(solution)/shard_map/pallas_call | solution.py:725
  223.4 8.1 %shard_map.210 = (bf16[512,384]{1,0:T(8,128)(2,1)S(1)}, bf16[512,768]{1,0:T(8,128)(2,1)S(1)}, bf16[512,384]{1,0:T(8,128)(2,1)S(1)}, f32[512,128]{1,0:T(8,128)S(1)}) custom-call(bf16[1024,1024]{1,0:T(8,128)(2,1)S(1)} %copy-done.1, bf16[1024,1024]{1,0:T(8,128)(2,1)S(1)} %copy-done.3, bf16[1536,1024]{1,0:T(8,128)(2,1)} %bitcast.91, ...), custom_call_target="tpu_custom_call" | custom-call | flops 50331648 | bytes 159744 | tf_op jit(solution)/shard_map/pallas_call | solution.py:725
  235.5 8.6 %shard_map.213 = bf16[4,4,96,1536]{3,2,1,0:T(8,128)(2,1)} custom-call(bf16[1024,1536]{1,0:T(8,128)(2,1)} %get-tuple-element.714.second.rest_0_, bf16[1024,1536]{1,0:T(8,128)(2,1)} %shard_map.208.cot, bf16[1024,1024]{1,0:T(8,128)(2,1)S(1)} %copy-done.4, bf16[1024,512]{1,0:T(8,128)(2,1)S(1)} %get-tuple-element.782.hidden.a_oth), custom_call_target="tpu_custom_call" | custom-call | flops 75497472 | bytes 221184 | tf_op jit(solution)/shard_map/pallas_call | solution.py:756
  244.1 8.6 %shard_map.212 = bf16[4,4,96,1536]{3,2,1,0:T(8,128)(2,1)} custom-call(bf16[1024,1536]{1,0:T(8,128)(2,1)} %get-tuple-element.714.second.rest_0_, bf16[1024,1536]{1,0:T(8,128)(2,1)} %shard_map.208.cot, bf16[1024,1024]{1,0:T(8,128)(2,1)S(1)} %copy-done.2, bf16[1024,512]{1,0:T(8,128)(2,1)S(1)} %get-tuple-element.781.hidden.a_own), custom_call_target="tpu_custom_call" | custom-call | flops 75497472 | bytes 221184 | tf_op jit(solution)/shard_map/pallas_call | solution.py:756
  258.1 2.8 collective-permute-done.34
  261.0 6.0 %add_convert_fusion = bf16[4,4,96,1536]{3,2,1,0:T(8,128)(2,1)} fusion(bf16[4,4,96,1536]{3,2,1,0:T(8,128)(2,1)S(1)} %collective-permute-done.34, bf16[4,4,96,1536]{3,2,1,0:T(8,128)(2,1)} %shard_map.212), kind=kLoop, calls=%fused_computation | loop fusion | flops 9437184 | bytes 14155776 | tf_op jit(solution)/shard_map/convert_element_type | solution.py:996
  270.9 2.3 fusion.18
  275.2 4.1 shard_map.215
  280.1 4.1 shard_map.214
  284.2 8.6 %collective-permute-done.38.x1 = bf16[1024,384]{1,0:T(8,128)(2,1)S(1)} collective-permute-done((bf16[1024,384]{1,0:T(8,128)(2,1)S(1)}, bf16[1024,384]{1,0:T(8,128)(2,1)S(1)}, u32[]{:S(2)}, u32[]{:S(2)}) %collective-permute-start.38) | collective-permute-done | bytes 786464 | tf_op jit(solution)/shard_map/ppermute | solution.py:32
  295.5 8.7 %collective-permute-done.40.bottom = bf16[512,384]{1,0:T(8,128)(2,1)S(1)} collective-permute-done((bf16[512,384]{1,0:T(8,128)(2,1)S(1)}, bf16[512,384]{1,0:T(8,128)(2,1)S(1)}, u32[]{:S(2)}, u32[]{:S(2)}) %collective-permute-start.40) | collective-permute-done | bytes 393248 | tf_op jit(solution)/shard_map/ppermute | solution.py:32
  304.7 2.4 shard_map.216
  307.2 1.9 collective-permute-done.42.g_oth
  311.1 22.2 %shard_map.217 = (bf16[1024,512]{1,0:T(8,128)(2,1)S(1)}, bf16[1024,512]{1,0:T(8,128)(2,1)}) custom-call(s32[9]{0:T(128)S(1)} %pad_add_fusion.info, bf16[1024,512]{1,0:T(8,128)(2,1)S(1)} %copy-done.22, bf16[1024,512]{1,0:T(8,128)(2,1)S(1)} %copy-done.24, bf16[1024,256]{1,0:T(8,128)(2,1)S(1)} %get-tuple-element.860.g_own, ...), custom_call_target="tpu_custom_call" | custom-call | flops 167772160 | bytes 98304 | tf_op jit(solution)/shard_map/pallas_call | solution.py:563
  334.2 18.7 %reduce-scatter.2.cloned.1.call-done = bf16[1,4,96,1536]{3,2,1,0:T(8,128)(2,1)} async-done(((bf16[4,4,96,1536]{3,2,1,0:T(8,128)(2,1)}), bf16[1,4,96,1536]{3,2,1,0:T(8,128)(2,1)}) %reduce-scatter.2.cloned.1.call-update) | async-done | bytes 1179664 | tf_op jit(solution)/shard_map/reduce_scatter | solution.py:1009
  361.1 3.2 collective-permute-done.46
  365.8 6.2 %shard_map.218 = bf16[4,576,384]{2,1,0:T(8,128)(2,1)S(1)} custom-call(bf16[1024,1536]{1,0:T(8,128)(2,1)} %get-tuple-element.906.first.rest_0_, bf16[1024,1536]{1,0:T(8,128)(2,1)} %get-tuple-element.896.heads, bf16[1024,512]{1,0:T(8,128)(2,1)S(1)} %get-tuple-element.903.back.a_own, bf16[1024,384]{1,0:T(8,128)(2,1)S(1)} %get-tuple-element.886.x0.branch, ...), custom_call_target="tpu_custom_call" | custom-call | flops 28311552 | bytes 154624 | tf_op jit(solution)/shard_map/pallas_call | solution.py:782
  373.3 6.2 %collective-permute-done.48 = bf16[96,1536]{1,0:T(8,128)(2,1)S(1)} collective-permute-done((bf16[96,1536]{1,0:T(8,128)(2,1)S(1)}, bf16[96,1536]{1,0:T(8,128)(2,1)S(1)}, u32[]{:S(2)}, u32[]{:S(2)}) %collective-permute-start.48) | collective-permute-done | bytes 294944 | tf_op jit(solution)/shard_map/ppermute | solution.py:32
  381.8 8.0 %shard_map.219 = bf16[4,576,384]{2,1,0:T(8,128)(2,1)} custom-call(bf16[1024,1536]{1,0:T(8,128)(2,1)} %get-tuple-element.906.first.rest_0_, bf16[1024,1536]{1,0:T(8,128)(2,1)} %get-tuple-element.896.heads, bf16[1024,512]{1,0:T(8,128)(2,1)} %collective-permute-done.45.back.a_oth, bf16[1024,384]{1,0:T(8,128)(2,1)S(1)} %get-tuple-element.886.x0.branch, ...), custom_call_target="tpu_custom_call" | custom-call | flops 28311552 | bytes 154624 | tf_op jit(solution)/shard_map/pallas_call | solution.py:782
  389.9 5.2 shard_map.221
  395.9 5.3 shard_map.220
  401.5 1.9 add_convert_fusion.1
  408.0 4.3 collective-permute-start.55
  413.0 10.7 %collective-permute-done.54 = f32[8,128]{1,0:T(8,128)S(1)} collective-permute-done((f32[8,128]{1,0:T(8,128)S(1)}, f32[8,128]{1,0:T(8,128)S(1)}, u32[]{:S(2)}, u32[]{:S(2)}) %collective-permute-start.54) | collective-permute-done | bytes 4128 | tf_op jit(solution)/shard_map/ppermute | solution.py:32
  427.3 1.9 add_convert_fusion.5
  429.8 1.9 add_convert_fusion.6
  431.7 4.8 collective-permute-start.60
  439.4 8.0 %collective-permute-done.59 = f32[8,128]{1,0:T(8,128)S(1)} collective-permute-done((f32[8,128]{1,0:T(8,128)S(1)}, f32[8,128]{1,0:T(8,128)S(1)}, u32[]{:S(2)}, u32[]{:S(2)}) %collective-permute-start.59) | collective-permute-done | bytes 4128 | tf_op jit(solution)/shard_map/ppermute | solution.py:32
  447.5 8.0 %collective-permute-done.60 = bf16[4,144,384]{2,1,0:T(8,128)(2,1)} collective-permute-done((bf16[4,144,384]{2,1,0:T(8,128)(2,1)}, bf16[4,144,384]{2,1,0:T(8,128)(2,1)}, u32[]{:S(2)}, u32[]{:S(2)}) %collective-permute-start.60) | collective-permute-done | bytes 442400 | tf_op jit(solution)/shard_map/ppermute | solution.py:169
  461.8 16.9 %collective-permute-start.63 = (bf16[4,144,384]{2,1,0:T(8,128)(2,1)}, bf16[4,144,384]{2,1,0:T(8,128)(2,1)}, u32[]{:S(2)}, u32[]{:S(2)}) collective-permute-start(bf16[4,144,384]{2,1,0:T(8,128)(2,1)} %add_convert_fusion.4), channel_id=1, source_target_pairs={{0,8},{8,16},{16,24},{1,9},{9,17},{17,25},{2,10},{10,18},{18,26},{... | collective-permute-start | bytes 1327112 | tf_op jit(solution)/shard_map/ppermute | solution.py:169
  484.5 18.3 %collective-permute-done.64 = bf16[4,144,384]{2,1,0:T(8,128)(2,1)} collective-permute-done((bf16[4,144,384]{2,1,0:T(8,128)(2,1)}, bf16[4,144,384]{2,1,0:T(8,128)(2,1)}, u32[]{:S(2)}, u32[]{:S(2)}) %collective-permute-start.64) | collective-permute-done | bytes 442400 | tf_op jit(solution)/shard_map/ppermute | solution.py:170
  513.4 11.2 %collective-permute-start.71 = (bf16[4,144,384]{2,1,0:T(8,128)(2,1)S(1)}, bf16[4,144,384]{2,1,0:T(8,128)(2,1)S(1)}, u32[]{:S(2)}, u32[]{:S(2)}) collective-permute-start(bf16[4,144,384]{2,1,0:T(8,128)(2,1)S(1)} %pad_maximum_fusion.17), channel_id=1, source_target_pairs={{0,8},{8,16},{16,24},{1,9},{9,17},{17,25},{2,10},{10,18},{18,26},{... | collective-permute-start | bytes 1327112 | tf_op jit(solution)/shard_map/ppermute | solution.py:203
  526.0 3.5 collective-permute-start.68
  531.0 2.8 collective-permute-start.70
  541.4 7.7 %collective-permute-done.74 = bf16[4,144,384]{2,1,0:T(8,128)(2,1)S(1)} collective-permute-done((bf16[4,144,384]{2,1,0:T(8,128)(2,1)S(1)}, bf16[4,144,384]{2,1,0:T(8,128)(2,1)S(1)}, u32[]{:S(2)}, u32[]{:S(2)}) %collective-permute-start.74) | collective-permute-done | bytes 442400 | tf_op jit(solution)/shard_map/ppermute | solution.py:204
  552.3 7.7 %collective-permute-done.76 = bf16[4,144,384]{2,1,0:T(8,128)(2,1)S(1)} collective-permute-done((bf16[4,144,384]{2,1,0:T(8,128)(2,1)S(1)}, bf16[4,144,384]{2,1,0:T(8,128)(2,1)S(1)}, u32[]{:S(2)}, u32[]{:S(2)}) %collective-permute-start.76) | collective-permute-done | bytes 442400 | tf_op jit(solution)/shard_map/ppermute | solution.py:204
  560.4 2.2 shard_map.222
  562.6 2.3 copy-done.20
  564.9 4.1 shard_map.223
  (447 shorter events, 147.7 us)
Async XLA Ops:
  7.2 345.7 %reduce-scatter.2.cloned.1.call-start = ((), (), s32[]{:S(2)}) async-start(), calls=%async_computation.1 | async-start | bytes 5898240 | tf_op jit(solution)/shard_map/reduce_scatter | solution.py:1009
  7.2 30.0 %collective-permute-start.4 = (bf16[1024,384]{1,0:T(8,128)(2,1)}, bf16[1024,384]{1,0:T(8,128)(2,1)S(1)}, u32[]{:S(2)}, u32[]{:S(2)}) collective-permute-start(bf16[1024,384]{1,0:T(8,128)(2,1)} %refs_5_), channel_id=1, source_target_pairs={{0,2},{2,0},{4,6},{6,4},{1,3},{3,1},{5,7},{7,5},{8,10},{10,8},{12,... | collective-permute-start | bytes 2359304 | tf_op jit(solution)/shard_map/ppermute | solution.py:32
  10.2 27.0 %collective-permute-start.5 = (bf16[1024,384]{1,0:T(8,128)(2,1)}, bf16[1024,384]{1,0:T(8,128)(2,1)S(1)}, u32[]{:S(2)}, u32[]{:S(2)}) collective-permute-start(bf16[1024,384]{1,0:T(8,128)(2,1)} %refs_5_), channel_id=1, source_target_pairs={{0,4},{2,6},{4,0},{6,2},{1,5},{3,7},{5,1},{7,3},{8,12},{10,14},{12... | collective-permute-start | bytes 2359304 | tf_op jit(solution)/shard_map/ppermute | solution.py:32
  17.1 16.9 %collective-permute-start.1 = (bf16[192,384]{1,0:T(8,128)(2,1)S(1)}, bf16[192,384]{1,0:T(8,128)(2,1)S(1)}, u32[]{:S(2)}, u32[]{:S(2)}) collective-permute-start(bf16[192,384]{1,0:T(8,128)(2,1)S(1)} %dynamic-slice_bitcast_fusion.2), channel_id=1, source_target_pairs={{0,2},{2,0},{4,6},{6,4},{1,3},{3,1},{5,7},{7,5},{8,10},{10,8},{12,... | collective-permute-start | bytes 442376 | tf_op jit(solution)/shard_map/ppermute | solution.py:32
  18.7 15.3 %collective-permute-start.2 = (bf16[192,384]{1,0:T(8,128)(2,1)S(1)}, bf16[192,384]{1,0:T(8,128)(2,1)S(1)}, u32[]{:S(2)}, u32[]{:S(2)}) collective-permute-start(bf16[192,384]{1,0:T(8,128)(2,1)S(1)} %dynamic-slice_bitcast_fusion.1), channel_id=1, source_target_pairs={{0,4},{2,6},{4,0},{6,2},{1,5},{3,7},{5,1},{7,3},{8,12},{10,14},{12... | collective-permute-start | bytes 442376 | tf_op jit(solution)/shard_map/ppermute | solution.py:32
  18.8 12.4 %collective-permute-start = (f32[2,384]{1,0:T(2,128)S(1)}, f32[2,384]{1,0:T(2,128)S(1)}, u32[]{:S(2)}, u32[]{:S(2)}) collective-permute-start(f32[2,384]{1,0:T(2,128)S(1)} %pad_maximum_fusion.22), channel_id=1, source_target_pairs={{0,2},{2,0},{4,6},{6,4},{1,3},{3,1},{5,7},{7,5},{8,10},{10,8},{12,... | collective-permute-start | bytes 9224 | tf_op jit(solution)/shard_map/ppermute | solution.py:32
  37.3 14.4 %collective-permute-start.7 = (bf16[3,192,384]{2,1,0:T(8,128)(2,1)S(1)}, bf16[3,192,384]{2,1,0:T(8,128)(2,1)S(1)}, u32[]{:S(2)}, u32[]{:S(2)}) collective-permute-start(bf16[3,192,384]{2,1,0:T(8,128)(2,1)S(1)} %pad_maximum_fusion.14), channel_id=1, source_target_pairs={{0,8},{8,0},{16,24},{24,16},{1,9},{9,1},{17,25},{25,17},{2,10},{10... | collective-permute-start | bytes 1327112 | tf_op jit(solution)/shard_map/ppermute | solution.py:40
  39.3 12.5 %collective-permute-start.8 = (bf16[512,384]{1,0:T(8,128)(2,1)S(1)}, bf16[512,384]{1,0:T(8,128)(2,1)S(1)}, u32[]{:S(2)}, u32[]{:S(2)}) collective-permute-start(bf16[512,384]{1,0:T(8,128)(2,1)S(1)} %slice.175), channel_id=1, source_target_pairs={{0,2},{2,0},{4,6},{6,4},{1,3},{3,1},{5,7},{7,5},{8,10},{10,8},{12,... | collective-permute-start | bytes 1179656 | tf_op jit(solution)/shard_map/ppermute | solution.py:32
  40.9 10.8 %collective-permute-start.9 = (bf16[512,384]{1,0:T(8,128)(2,1)S(1)}, bf16[512,384]{1,0:T(8,128)(2,1)S(1)}, u32[]{:S(2)}, u32[]{:S(2)}) collective-permute-start(bf16[512,384]{1,0:T(8,128)(2,1)S(1)} %slice.176), channel_id=1, source_target_pairs={{0,4},{2,6},{4,0},{6,2},{1,5},{3,7},{5,1},{7,3},{8,12},{10,14},{12... | collective-permute-start | bytes 1179656 | tf_op jit(solution)/shard_map/ppermute | solution.py:32
  42.5 8.6 %collective-permute-start.6 = (f32[2,768]{1,0:T(2,128)S(1)}, f32[2,768]{1,0:T(2,128)S(1)}, u32[]{:S(2)}, u32[]{:S(2)}) collective-permute-start(f32[2,768]{1,0:T(2,128)S(1)} %pad_maximum_fusion.19), channel_id=1, source_target_pairs={{0,4},{2,6},{4,0},{6,2},{1,5},{3,7},{5,1},{7,3},{8,12},{10,14},{12... | collective-permute-start | bytes 18440 | tf_op jit(solution)/shard_map/ppermute | solution.py:32
  53.6 11.6 %collective-permute-start.10 = (bf16[1536,512]{1,0:T(8,128)(2,1)S(1)}, bf16[1536,512]{1,0:T(8,128)(2,1)}, u32[]{:S(2)}, u32[]{:S(2)}) collective-permute-start(bf16[1536,512]{1,0:T(8,128)(2,1)S(1)} %convolution_convert_fusion.w_own), channel_id=1, source_target_pairs={{0,1},{1,0},{2,3},{3,2},{4,5},{5,4},{6,7},{7,6},{8,9},{9,8},{10,11... | collective-permute-start | bytes 4718600 | tf_op jit(solution)/shard_map/ppermute | solution.py:36
  56.1 17.2 %collective-permute-start.11 = (bf16[640,384]{1,0:T(8,128)(2,1)}, bf16[640,384]{1,0:T(8,128)(2,1)}, u32[]{:S(2)}, u32[]{:S(2)}) collective-permute-start(bf16[640,384]{1,0:T(8,128)(2,1)} %constant_dynamic-slice_fusion.19), channel_id=1, source_target_pairs={{0,2},{2,0},{4,6},{6,4},{1,3},{3,1},{5,7},{7,5},{8,10},{10,8},{12,... | collective-permute-start | bytes 1474568 | tf_op jit(solution)/shard_map/ppermute | solution.py:32
  58.5 23.8 %collective-permute-start.12 = (bf16[640,384]{1,0:T(8,128)(2,1)}, bf16[640,384]{1,0:T(8,128)(2,1)}, u32[]{:S(2)}, u32[]{:S(2)}) collective-permute-start(bf16[640,384]{1,0:T(8,128)(2,1)} %constant_dynamic-slice_fusion.18), channel_id=1, source_target_pairs={{0,4},{2,6},{4,0},{6,2},{1,5},{3,7},{5,1},{7,3},{8,12},{10,14},{12... | collective-permute-start | bytes 1474568 | tf_op jit(solution)/shard_map/ppermute | solution.py:32
  60.8 21.5 %collective-permute-start.13 = (bf16[640,384]{1,0:T(8,128)(2,1)}, bf16[640,384]{1,0:T(8,128)(2,1)}, u32[]{:S(2)}, u32[]{:S(2)}) collective-permute-start(bf16[640,384]{1,0:T(8,128)(2,1)} %constant_dynamic-slice_fusion.17), channel_id=1, source_target_pairs={{0,6},{2,4},{4,2},{6,0},{1,7},{3,5},{5,3},{7,1},{8,14},{10,12},{12... | collective-permute-start | bytes 1474568 | tf_op jit(solution)/shard_map/ppermute | solution.py:32
  84.0 34.9 %collective-permute-start.21 = (bf16[3,640,384]{2,1,0:T(8,128)(2,1)S(1)}, bf16[3,640,384]{2,1,0:T(8,128)(2,1)}, u32[]{:S(2)}, u32[]{:S(2)}) collective-permute-start(bf16[3,640,384]{2,1,0:T(8,128)(2,1)S(1)} %pad_maximum_fusion.2), channel_id=1, source_target_pairs={{0,8},{8,0},{16,24},{24,16},{1,9},{9,1},{17,25},{25,17},{2,10},{10... | collective-permute-start | bytes 4423688 | tf_op jit(solution)/shard_map/ppermute | solution.py:40
  84.3 22.6 %collective-permute-start.15 = (bf16[192,1024]{1,0:T(8,128)(2,1)S(1)}, bf16[192,1024]{1,0:T(8,128)(2,1)S(1)}, u32[]{:S(2)}, u32[]{:S(2)}) collective-permute-start(bf16[192,1024]{1,0:T(8,128)(2,1)S(1)} %constant_dynamic-slice_fusion.16), channel_id=1, source_target_pairs={{0,2},{2,0},{4,6},{6,4},{1,3},{3,1},{5,7},{7,5},{8,10},{10,8},{12,... | collective-permute-start | bytes 1179656 | tf_op jit(solution)/shard_map/ppermute | solution.py:32
  86.1 20.8 %collective-permute-start.16 = (bf16[192,1024]{1,0:T(8,128)(2,1)S(1)}, bf16[192,1024]{1,0:T(8,128)(2,1)S(1)}, u32[]{:S(2)}, u32[]{:S(2)}) collective-permute-start(bf16[192,1024]{1,0:T(8,128)(2,1)S(1)} %constant_dynamic-slice_fusion.15), channel_id=1, source_target_pairs={{0,4},{2,6},{4,0},{6,2},{1,5},{3,7},{5,1},{7,3},{8,12},{10,14},{12... | collective-permute-start | bytes 1179656 | tf_op jit(solution)/shard_map/ppermute | solution.py:32
  87.7 19.2 %collective-permute-start.17 = (bf16[192,1024]{1,0:T(8,128)(2,1)S(1)}, bf16[192,1024]{1,0:T(8,128)(2,1)S(1)}, u32[]{:S(2)}, u32[]{:S(2)}) collective-permute-start(bf16[192,1024]{1,0:T(8,128)(2,1)S(1)} %constant_dynamic-slice_fusion.14), channel_id=1, source_target_pairs={{0,6},{2,4},{4,2},{6,0},{1,7},{3,5},{5,3},{7,1},{8,14},{10,12},{12... | collective-permute-start | bytes 1179656 | tf_op jit(solution)/shard_map/ppermute | solution.py:32
  120.8 38.2 %collective-permute-start.23 = (bf16[3,192,1024]{2,1,0:T(8,128)(2,1)S(1)}, bf16[3,192,1024]{2,1,0:T(8,128)(2,1)S(1)}, u32[]{:S(2)}, u32[]{:S(2)}) collective-permute-start(bf16[3,192,1024]{2,1,0:T(8,128)(2,1)S(1)} %pad_maximum_fusion.7), channel_id=1, source_target_pairs={{0,8},{8,0},{16,24},{24,16},{1,9},{9,1},{17,25},{25,17},{2,10},{10... | collective-permute-start | bytes 3538952 | tf_op jit(solution)/shard_map/ppermute | solution.py:40
  121.6 20.4 %collective-permute-start.19 = (bf16[1024,384]{1,0:T(8,128)(2,1)S(1)}, bf16[1024,384]{1,0:T(8,128)(2,1)S(1)}, u32[]{:S(2)}, u32[]{:S(2)}) collective-permute-start(bf16[1024,384]{1,0:T(8,128)(2,1)S(1)} %copy-done.27), channel_id=1, source_target_pairs={{0,2},{2,0},{4,6},{6,4},{1,3},{3,1},{5,7},{7,5},{8,10},{10,8},{12,... | collective-permute-start | bytes 2359304 | tf_op jit(solution)/shard_map/ppermute | solution.py:32
  123.1 20.5 %collective-permute-start.20 = (bf16[1024,384]{1,0:T(8,128)(2,1)S(1)}, bf16[1024,384]{1,0:T(8,128)(2,1)S(1)}, u32[]{:S(2)}, u32[]{:S(2)}) collective-permute-start(bf16[1024,384]{1,0:T(8,128)(2,1)S(1)} %copy-done.27), channel_id=1, source_target_pairs={{0,4},{2,6},{4,0},{6,2},{1,5},{3,7},{5,1},{7,3},{8,12},{10,14},{12... | collective-permute-start | bytes 2359304 | tf_op jit(solution)/shard_map/ppermute | solution.py:32
  124.6 33.0 %collective-permute-start.24 = (bf16[1024,384]{1,0:T(8,128)(2,1)S(1)}, bf16[1024,384]{1,0:T(8,128)(2,1)S(1)}, u32[]{:S(2)}, u32[]{:S(2)}) collective-permute-start(bf16[1024,384]{1,0:T(8,128)(2,1)S(1)} %pad_maximum_fusion.13.refs_0_), channel_id=1, source_target_pairs={{0,2},{2,0},{4,6},{6,4},{1,3},{3,1},{5,7},{7,5},{8,10},{10,8},{12,... | collective-permute-start | bytes 2359304 | tf_op jit(solution)/shard_map/ppermute | solution.py:32
  127.4 31.6 %collective-permute-start.25 = (bf16[1024,384]{1,0:T(8,128)(2,1)S(1)}, bf16[1024,384]{1,0:T(8,128)(2,1)S(1)}, u32[]{:S(2)}, u32[]{:S(2)}) collective-permute-start(bf16[1024,384]{1,0:T(8,128)(2,1)S(1)} %pad_maximum_fusion.13.refs_0_), channel_id=1, source_target_pairs={{0,4},{2,6},{4,0},{6,2},{1,5},{3,7},{5,1},{7,3},{8,12},{10,14},{12... | collective-permute-start | bytes 2359304 | tf_op jit(solution)/shard_map/ppermute | solution.py:32
  159.7 20.4 %collective-permute-start.28 = (bf16[1536,1024]{1,0:T(8,128)(2,1)S(1)}, bf16[1536,1024]{1,0:T(8,128)(2,1)S(1)}, u32[]{:S(2)}, u32[]{:S(2)}) collective-permute-start(bf16[1536,1024]{1,0:T(8,128)(2,1)S(1)} %bitcast.87), channel_id=1, source_target_pairs={{0,1},{1,0},{2,3},{3,2},{4,5},{5,4},{6,7},{7,6},{8,9},{9,8},{10,11... | collective-permute-start | bytes 9437192 | tf_op jit(solution)/shard_map/ppermute | solution.py:36
  159.8 12.0 %collective-permute-start.26 = (bf16[512,384]{1,0:T(8,128)(2,1)S(1)}, bf16[512,384]{1,0:T(8,128)(2,1)S(1)}, u32[]{:S(2)}, u32[]{:S(2)}) collective-permute-start(bf16[512,384]{1,0:T(8,128)(2,1)S(1)} %slice.182), channel_id=1, source_target_pairs={{0,2},{2,0},{4,6},{6,4},{1,3},{3,1},{5,7},{7,5},{8,10},{10,8},{12,... | collective-permute-start | bytes 1179656 | tf_op jit(solution)/shard_map/ppermute | solution.py:32
  160.3 12.0 %collective-permute-start.27 = (bf16[512,384]{1,0:T(8,128)(2,1)S(1)}, bf16[512,384]{1,0:T(8,128)(2,1)S(1)}, u32[]{:S(2)}, u32[]{:S(2)}) collective-permute-start(bf16[512,384]{1,0:T(8,128)(2,1)S(1)} %slice.183), channel_id=1, source_target_pairs={{0,4},{2,6},{4,0},{6,2},{1,5},{3,7},{5,1},{7,3},{8,12},{10,14},{12... | collective-permute-start | bytes 1179656 | tf_op jit(solution)/shard_map/ppermute | solution.py:32
  162.1 17.7 %collective-permute-start.29 = (bf16[512,384]{1,0:T(8,128)(2,1)S(1)}, bf16[512,384]{1,0:T(8,128)(2,1)S(1)}, u32[]{:S(2)}, u32[]{:S(2)}) collective-permute-start(bf16[512,384]{1,0:T(8,128)(2,1)S(1)} %slice.184), channel_id=1, source_target_pairs={{0,2},{2,0},{4,6},{6,4},{1,3},{3,1},{5,7},{7,5},{8,10},{10,8},{12,... | collective-permute-start | bytes 1179656 | tf_op jit(solution)/shard_map/ppermute | solution.py:32
  163.7 16.4 %collective-permute-start.30 = (bf16[512,384]{1,0:T(8,128)(2,1)S(1)}, bf16[512,384]{1,0:T(8,128)(2,1)S(1)}, u32[]{:S(2)}, u32[]{:S(2)}) collective-permute-start(bf16[512,384]{1,0:T(8,128)(2,1)S(1)} %slice.185), channel_id=1, source_target_pairs={{0,4},{2,6},{4,0},{6,2},{1,5},{3,7},{5,1},{7,3},{8,12},{10,14},{12... | collective-permute-start | bytes 1179656 | tf_op jit(solution)/shard_map/ppermute | solution.py:32
  231.8 20.9 %collective-permute-start.31 = (bf16[512,768]{1,0:T(8,128)(2,1)S(1)}, bf16[512,768]{1,0:T(8,128)(2,1)S(1)}, u32[]{:S(2)}, u32[]{:S(2)}) collective-permute-start(bf16[512,768]{1,0:T(8,128)(2,1)S(1)} %get-tuple-element.727), channel_id=1, source_target_pairs={{0,2},{2,0},{4,6},{6,4},{1,3},{3,1},{5,7},{7,5},{8,10},{10,8},{12,... | collective-permute-start | bytes 2359304 | tf_op jit(solution)/shard_map/ppermute | solution.py:32
  233.5 19.3 %collective-permute-start.32 = (bf16[512,768]{1,0:T(8,128)(2,1)S(1)}, bf16[512,768]{1,0:T(8,128)(2,1)S(1)}, u32[]{:S(2)}, u32[]{:S(2)}) collective-permute-start(bf16[512,768]{1,0:T(8,128)(2,1)S(1)} %get-tuple-element.728), channel_id=1, source_target_pairs={{0,4},{2,6},{4,0},{6,2},{1,5},{3,7},{5,1},{7,3},{8,12},{10,14},{12... | collective-permute-start | bytes 2359304 | tf_op jit(solution)/shard_map/ppermute | solution.py:32
  235.0 17.8 %collective-permute-start.33 = (f32[8,128]{1,0:T(8,128)S(1)}, f32[8,128]{1,0:T(8,128)S(1)}, u32[]{:S(2)}, u32[]{:S(2)}) collective-permute-start(f32[8,128]{1,0:T(8,128)S(1)} %pad_maximum_fusion.20), channel_id=1, source_target_pairs={{0,2},{2,0},{4,6},{6,4},{1,3},{3,1},{5,7},{7,5},{8,10},{10,8},{12,... | collective-permute-start | bytes 12296 | tf_op jit(solution)/shard_map/ppermute | solution.py:32
  253.0 14.0 %collective-permute-start.37 = (bf16[512,384]{1,0:T(8,128)(2,1)S(1)}, bf16[512,384]{1,0:T(8,128)(2,1)}, u32[]{:S(2)}, u32[]{:S(2)}) collective-permute-start(bf16[512,384]{1,0:T(8,128)(2,1)S(1)} %add_convert_fusion.11), channel_id=1, source_target_pairs={{0,2},{2,0},{4,6},{6,4},{1,3},{3,1},{5,7},{7,5},{8,10},{10,8},{12,... | collective-permute-start | bytes 1179656 | tf_op jit(solution)/shard_map/ppermute | solution.py:32
  255.9 11.3 %collective-permute-start.36 = (bf16[512,384]{1,0:T(8,128)(2,1)}, bf16[512,384]{1,0:T(8,128)(2,1)}, u32[]{:S(2)}, u32[]{:S(2)}) collective-permute-start(bf16[512,384]{1,0:T(8,128)(2,1)} %add_convert_fusion.12), channel_id=1, source_target_pairs={{0,4},{2,6},{4,0},{6,2},{1,5},{3,7},{5,1},{7,3},{8,12},{10,14},{12... | collective-permute-start | bytes 1179656 | tf_op jit(solution)/shard_map/ppermute | solution.py:32
  267.2 295.4 %all-gather.3.cloned.1.call-start = ((), (), s32[]{:S(2)}) async-start(), calls=%async_computation.2 | async-start | bytes 5898240 | tf_op jit(solution)/shard_map/all_gather | solution.py:1045
  273.2 19.6 %collective-permute-start.38 = (bf16[1024,384]{1,0:T(8,128)(2,1)S(1)}, bf16[1024,384]{1,0:T(8,128)(2,1)S(1)}, u32[]{:S(2)}, u32[]{:S(2)}) collective-permute-start(bf16[1024,384]{1,0:T(8,128)(2,1)S(1)} %get-tuple-element.886.x0.branch), channel_id=1, source_target_pairs={{0,2},{2,0},{4,6},{6,4},{1,3},{3,1},{5,7},{7,5},{8,10},{10,8},{12,... | collective-permute-start | bytes 2359304 | tf_op jit(solution)/shard_map/ppermute | solution.py:32
  274.7 19.3 %collective-permute-start.39 = (bf16[1024,384]{1,0:T(8,128)(2,1)S(1)}, bf16[1024,384]{1,0:T(8,128)(2,1)S(1)}, u32[]{:S(2)}, u32[]{:S(2)}) collective-permute-start(bf16[1024,384]{1,0:T(8,128)(2,1)S(1)} %get-tuple-element.886.x0.branch), channel_id=1, source_target_pairs={{0,4},{2,6},{4,0},{6,2},{1,5},{3,7},{5,1},{7,3},{8,12},{10,14},{12... | collective-permute-start | bytes 2359304 | tf_op jit(solution)/shard_map/ppermute | solution.py:32
  294.0 10.2 %collective-permute-start.40 = (bf16[512,384]{1,0:T(8,128)(2,1)S(1)}, bf16[512,384]{1,0:T(8,128)(2,1)S(1)}, u32[]{:S(2)}, u32[]{:S(2)}) collective-permute-start(bf16[512,384]{1,0:T(8,128)(2,1)S(1)} %slice.194), channel_id=1, source_target_pairs={{0,2},{2,0},{4,6},{6,4},{1,3},{3,1},{5,7},{7,5},{8,10},{10,8},{12,... | collective-permute-start | bytes 1179656 | tf_op jit(solution)/shard_map/ppermute | solution.py:32
  294.7 9.9 %collective-permute-start.41 = (bf16[512,384]{1,0:T(8,128)(2,1)S(1)}, bf16[512,384]{1,0:T(8,128)(2,1)S(1)}, u32[]{:S(2)}, u32[]{:S(2)}) collective-permute-start(bf16[512,384]{1,0:T(8,128)(2,1)S(1)} %slice.195), channel_id=1, source_target_pairs={{0,4},{2,6},{4,0},{6,2},{1,5},{3,7},{5,1},{7,3},{8,12},{10,14},{12... | collective-permute-start | bytes 1179656 | tf_op jit(solution)/shard_map/ppermute | solution.py:32
  309.1 24.2 %collective-permute-start.43 = (bf16[512,768]{1,0:T(8,128)(2,1)S(1)}, bf16[512,768]{1,0:T(8,128)(2,1)S(1)}, u32[]{:S(2)}, u32[]{:S(2)}) collective-permute-start(bf16[512,768]{1,0:T(8,128)(2,1)S(1)} %get-tuple-element.871), channel_id=1, source_target_pairs={{0,2},{2,0},{4,6},{6,4},{1,3},{3,1},{5,7},{7,5},{8,10},{10,8},{12,... | collective-permute-start | bytes 2359304 | tf_op jit(solution)/shard_map/ppermute | solution.py:32
  310.5 23.6 %collective-permute-start.44 = (bf16[512,768]{1,0:T(8,128)(2,1)S(1)}, bf16[512,768]{1,0:T(8,128)(2,1)S(1)}, u32[]{:S(2)}, u32[]{:S(2)}) collective-permute-start(bf16[512,768]{1,0:T(8,128)(2,1)S(1)} %get-tuple-element.872), channel_id=1, source_target_pairs={{0,4},{2,6},{4,0},{6,2},{1,5},{3,7},{5,1},{7,3},{8,12},{10,14},{12... | collective-permute-start | bytes 2359304 | tf_op jit(solution)/shard_map/ppermute | solution.py:32
  352.9 27.8 %collective-permute-start.45 = (bf16[1024,512]{1,0:T(8,128)(2,1)}, bf16[1024,512]{1,0:T(8,128)(2,1)}, u32[]{:S(2)}, u32[]{:S(2)}) collective-permute-start(bf16[1024,512]{1,0:T(8,128)(2,1)} %get-tuple-element.884), channel_id=1, source_target_pairs={{0,1},{1,0},{2,3},{3,2},{4,5},{5,4},{6,7},{7,6},{8,9},{9,8},{10,11... | collective-permute-start | bytes 3145736 | tf_op jit(solution)/shard_map/ppermute | solution.py:36
  354.3 9.9 %collective-permute-start.46 = (bf16[96,1536]{1,0:T(8,128)(2,1)S(1)}, bf16[96,1536]{1,0:T(8,128)(2,1)S(1)}, u32[]{:S(2)}, u32[]{:S(2)}) collective-permute-start(bf16[96,1536]{1,0:T(8,128)(2,1)S(1)} %get-tuple-element.1033), channel_id=1, source_target_pairs={{0,2},{2,0},{4,6},{6,4},{1,3},{3,1},{5,7},{7,5},{8,10},{10,8},{12,... | collective-permute-start | bytes 884744 | tf_op jit(solution)/shard_map/ppermute | solution.py:32
  356.7 33.1 %collective-permute-start.50 = (bf16[512,384]{1,0:T(8,128)(2,1)}, bf16[512,384]{1,0:T(8,128)(2,1)}, u32[]{:S(2)}, u32[]{:S(2)}) collective-permute-start(bf16[512,384]{1,0:T(8,128)(2,1)} %add_convert_fusion.9), channel_id=1, source_target_pairs={{0,2},{2,0},{4,6},{6,4},{1,3},{3,1},{5,7},{7,5},{8,10},{10,8},{12,... | collective-permute-start | bytes 1179656 | tf_op jit(solution)/shard_map/ppermute | solution.py:32
  357.3 16.0 %collective-permute-start.47 = (bf16[96,1536]{1,0:T(8,128)(2,1)S(1)}, bf16[96,1536]{1,0:T(8,128)(2,1)S(1)}, u32[]{:S(2)}, u32[]{:S(2)}) collective-permute-start(bf16[96,1536]{1,0:T(8,128)(2,1)S(1)} %get-tuple-element.1032), channel_id=1, source_target_pairs={{0,4},{2,6},{4,0},{6,2},{1,5},{3,7},{5,1},{7,3},{8,12},{10,14},{12... | collective-permute-start | bytes 884744 | tf_op jit(solution)/shard_map/ppermute | solution.py:32
  358.7 20.8 %collective-permute-start.48 = (bf16[96,1536]{1,0:T(8,128)(2,1)S(1)}, bf16[96,1536]{1,0:T(8,128)(2,1)S(1)}, u32[]{:S(2)}, u32[]{:S(2)}) collective-permute-start(bf16[96,1536]{1,0:T(8,128)(2,1)S(1)} %get-tuple-element.1031), channel_id=1, source_target_pairs={{0,6},{2,4},{4,2},{6,0},{1,7},{3,5},{5,3},{7,1},{8,14},{10,12},{12... | collective-permute-start | bytes 884744 | tf_op jit(solution)/shard_map/ppermute | solution.py:32
  364.2 25.6 %collective-permute-start.49 = (bf16[512,384]{1,0:T(8,128)(2,1)}, bf16[512,384]{1,0:T(8,128)(2,1)}, u32[]{:S(2)}, u32[]{:S(2)}) collective-permute-start(bf16[512,384]{1,0:T(8,128)(2,1)} %add_convert_fusion.10), channel_id=1, source_target_pairs={{0,4},{2,6},{4,0},{6,2},{1,5},{3,7},{5,1},{7,3},{8,12},{10,14},{12... | collective-permute-start | bytes 1179656 | tf_op jit(solution)/shard_map/ppermute | solution.py:32
  389.8 11.7 %collective-permute-start.51 = (bf16[4,576,384]{2,1,0:T(8,128)(2,1)}, bf16[4,576,384]{2,1,0:T(8,128)(2,1)}, u32[]{:S(2)}, u32[]{:S(2)}) collective-permute-start(bf16[4,576,384]{2,1,0:T(8,128)(2,1)} %shard_map.219), channel_id=1, source_target_pairs={{0,1},{1,0},{2,3},{3,2},{4,5},{5,4},{6,7},{7,6},{8,9},{9,8},{10,11... | collective-permute-start | bytes 5308424 | tf_op jit(solution)/shard_map/ppermute | solution.py:36
  403.5 20.3 %collective-permute-start.52 = (bf16[512,768]{1,0:T(8,128)(2,1)}, bf16[512,768]{1,0:T(8,128)(2,1)S(1)}, u32[]{:S(2)}, u32[]{:S(2)}) collective-permute-start(bf16[512,768]{1,0:T(8,128)(2,1)} %get-tuple-element.934), channel_id=1, source_target_pairs={{0,2},{2,0},{4,6},{6,4},{1,3},{3,1},{5,7},{7,5},{8,10},{10,8},{12,... | collective-permute-start | bytes 2359304 | tf_op jit(solution)/shard_map/ppermute | solution.py:32
  405.0 19.8 %collective-permute-start.53 = (bf16[512,768]{1,0:T(8,128)(2,1)}, bf16[512,768]{1,0:T(8,128)(2,1)S(1)}, u32[]{:S(2)}, u32[]{:S(2)}) collective-permute-start(bf16[512,768]{1,0:T(8,128)(2,1)} %get-tuple-element.935), channel_id=1, source_target_pairs={{0,4},{2,6},{4,0},{6,2},{1,5},{3,7},{5,1},{7,3},{8,12},{10,14},{12... | collective-permute-start | bytes 2359304 | tf_op jit(solution)/shard_map/ppermute | solution.py:32
  405.8 18.0 %collective-permute-start.56 = (bf16[4,144,384]{2,1,0:T(8,128)(2,1)S(1)}, bf16[4,144,384]{2,1,0:T(8,128)(2,1)}, u32[]{:S(2)}, u32[]{:S(2)}) collective-permute-start(bf16[4,144,384]{2,1,0:T(8,128)(2,1)S(1)} %pad_maximum_fusion.16), channel_id=1, source_target_pairs={{24,16},{25,17},{26,18},{27,19},{28,20},{29,21},{30,22},{31,23}} | collective-permute-start | bytes 1327112 | tf_op jit(solution)/shard_map/ppermute | solution.py:170
  408.0 15.7 %collective-permute-start.55 = (bf16[4,144,384]{2,1,0:T(8,128)(2,1)}, bf16[4,144,384]{2,1,0:T(8,128)(2,1)}, u32[]{:S(2)}, u32[]{:S(2)}) collective-permute-start(bf16[4,144,384]{2,1,0:T(8,128)(2,1)} %pad_maximum_fusion.15), channel_id=1, source_target_pairs={{0,8},{1,9},{2,10},{3,11},{4,12},{5,13},{6,14},{7,15}} | collective-permute-start | bytes 1327112 | tf_op jit(solution)/shard_map/ppermute | solution.py:169
  412.4 11.4 %collective-permute-start.54 = (f32[8,128]{1,0:T(8,128)S(1)}, f32[8,128]{1,0:T(8,128)S(1)}, u32[]{:S(2)}, u32[]{:S(2)}) collective-permute-start(f32[8,128]{1,0:T(8,128)S(1)} %pad_maximum_fusion.21), channel_id=1, source_target_pairs={{0,2},{2,0},{4,6},{6,4},{1,3},{3,1},{5,7},{7,5},{8,10},{10,8},{12,... | collective-permute-start | bytes 12296 | tf_op jit(solution)/shard_map/ppermute | solution.py:32
  429.1 18.4 %collective-permute-start.61 = (bf16[4,144,384]{2,1,0:T(8,128)(2,1)}, bf16[4,144,384]{2,1,0:T(8,128)(2,1)S(1)}, u32[]{:S(2)}, u32[]{:S(2)}) collective-permute-start(bf16[4,144,384]{2,1,0:T(8,128)(2,1)} %add_convert_fusion.5), channel_id=1, source_target_pairs={{24,16},{16,8},{25,17},{17,9},{26,18},{18,10},{27,19},{19,11},{28,... | collective-permute-start | bytes 1327112 | tf_op jit(solution)/shard_map/ppermute | solution.py:170
  431.7 23.8 %collective-permute-start.60 = (bf16[4,144,384]{2,1,0:T(8,128)(2,1)}, bf16[4,144,384]{2,1,0:T(8,128)(2,1)}, u32[]{:S(2)}, u32[]{:S(2)}) collective-permute-start(bf16[4,144,384]{2,1,0:T(8,128)(2,1)} %add_convert_fusion.6), channel_id=1, source_target_pairs={{0,8},{8,16},{1,9},{9,17},{2,10},{10,18},{3,11},{11,19},{4,12},{12... | collective-permute-start | bytes 1327112 | tf_op jit(solution)/shard_map/ppermute | solution.py:169
  436.6 10.9 %collective-permute-start.58 = (bf16[512,384]{1,0:T(8,128)(2,1)S(1)}, bf16[512,384]{1,0:T(8,128)(2,1)S(1)}, u32[]{:S(2)}, u32[]{:S(2)}) collective-permute-start(bf16[512,384]{1,0:T(8,128)(2,1)S(1)} %add_convert_fusion.7), channel_id=1, source_target_pairs={{0,2},{2,0},{4,6},{6,4},{1,3},{3,1},{5,7},{7,5},{8,10},{10,8},{12,... | collective-permute-start | bytes 1179656 | tf_op jit(solution)/shard_map/ppermute | solution.py:32
  437.3 10.1 %collective-permute-start.57 = (bf16[512,384]{1,0:T(8,128)(2,1)S(1)}, bf16[512,384]{1,0:T(8,128)(2,1)S(1)}, u32[]{:S(2)}, u32[]{:S(2)}) collective-permute-start(bf16[512,384]{1,0:T(8,128)(2,1)S(1)} %add_convert_fusion.8), channel_id=1, source_target_pairs={{0,4},{2,6},{4,0},{6,2},{1,5},{3,7},{5,1},{7,3},{8,12},{10,14},{12... | collective-permute-start | bytes 1179656 | tf_op jit(solution)/shard_map/ppermute | solution.py:32
  438.0 9.5 %collective-permute-start.59 = (f32[8,128]{1,0:T(8,128)S(1)}, f32[8,128]{1,0:T(8,128)S(1)}, u32[]{:S(2)}, u32[]{:S(2)}) collective-permute-start(f32[8,128]{1,0:T(8,128)S(1)} %add.398), channel_id=1, source_target_pairs={{0,4},{2,6},{4,0},{6,2},{1,5},{3,7},{5,1},{7,3},{8,12},{10,14},{12... | collective-permute-start | bytes 12296 | tf_op jit(solution)/shard_map/ppermute | solution.py:32
  458.5 44.3 %collective-permute-start.64 = (bf16[4,144,384]{2,1,0:T(8,128)(2,1)}, bf16[4,144,384]{2,1,0:T(8,128)(2,1)}, u32[]{:S(2)}, u32[]{:S(2)}) collective-permute-start(bf16[4,144,384]{2,1,0:T(8,128)(2,1)} %add_convert_fusion.3), channel_id=1, source_target_pairs={{24,16},{16,8},{8,0},{25,17},{17,9},{9,1},{26,18},{18,10},{10,2},{... | collective-permute-start | bytes 1327112 | tf_op jit(solution)/shard_map/ppermute | solution.py:170
  461.8 41.0 %collective-permute-start.63 = (bf16[4,144,384]{2,1,0:T(8,128)(2,1)}, bf16[4,144,384]{2,1,0:T(8,128)(2,1)}, u32[]{:S(2)}, u32[]{:S(2)}) collective-permute-start(bf16[4,144,384]{2,1,0:T(8,128)(2,1)} %add_convert_fusion.4), channel_id=1, source_target_pairs={{0,8},{8,16},{16,24},{1,9},{9,17},{17,25},{2,10},{10,18},{18,26},{... | collective-permute-start | bytes 1327112 | tf_op jit(solution)/shard_map/ppermute | solution.py:169
  513.4 23.8 %collective-permute-start.71 = (bf16[4,144,384]{2,1,0:T(8,128)(2,1)S(1)}, bf16[4,144,384]{2,1,0:T(8,128)(2,1)S(1)}, u32[]{:S(2)}, u32[]{:S(2)}) collective-permute-start(bf16[4,144,384]{2,1,0:T(8,128)(2,1)S(1)} %pad_maximum_fusion.17), channel_id=1, source_target_pairs={{0,8},{8,16},{16,24},{1,9},{9,17},{17,25},{2,10},{10,18},{18,26},{... | collective-permute-start | bytes 1327112 | tf_op jit(solution)/shard_map/ppermute | solution.py:203
  524.7 12.5 %collective-permute-start.72 = (bf16[4,144,384]{2,1,0:T(8,128)(2,1)S(1)}, bf16[4,144,384]{2,1,0:T(8,128)(2,1)S(1)}, u32[]{:S(2)}, u32[]{:S(2)}) collective-permute-start(bf16[4,144,384]{2,1,0:T(8,128)(2,1)S(1)} %pad_maximum_fusion.17), channel_id=1, source_target_pairs={{24,16},{16,8},{8,0},{25,17},{17,9},{9,1},{26,18},{18,10},{10,2},{... | collective-permute-start | bytes 1327112 | tf_op jit(solution)/shard_map/ppermute | solution.py:204
  526.0 10.7 %collective-permute-start.68 = (f32[2,384]{1,0:T(2,128)S(1)}, f32[2,384]{1,0:T(2,128)S(1)}, u32[]{:S(2)}, u32[]{:S(2)}) collective-permute-start(f32[2,384]{1,0:T(2,128)S(1)} %fusion.17), channel_id=1, source_target_pairs={{0,8},{8,16},{16,24},{24,0},{1,9},{9,17},{17,25},{25,1},{2,10},{10... | collective-permute-start | bytes 9224 | tf_op jit(solution)/shard_map/ppermute | solution.py:1087
  537.9 11.2 %collective-permute-start.74 = (bf16[4,144,384]{2,1,0:T(8,128)(2,1)S(1)}, bf16[4,144,384]{2,1,0:T(8,128)(2,1)S(1)}, u32[]{:S(2)}, u32[]{:S(2)}) collective-permute-start(bf16[4,144,384]{2,1,0:T(8,128)(2,1)S(1)} %collective-permute-done.72), channel_id=1, source_target_pairs={{16,8},{8,0},{17,9},{9,1},{18,10},{10,2},{19,11},{11,3},{20,12},{1... | collective-permute-start | bytes 1327112 | tf_op jit(solution)/shard_map/ppermute | solution.py:204
  549.8 10.2 %collective-permute-start.76 = (bf16[4,144,384]{2,1,0:T(8,128)(2,1)S(1)}, bf16[4,144,384]{2,1,0:T(8,128)(2,1)S(1)}, u32[]{:S(2)}, u32[]{:S(2)}) collective-permute-start(bf16[4,144,384]{2,1,0:T(8,128)(2,1)S(1)} %collective-permute-done.74), channel_id=1, source_target_pairs={{8,0},{9,1},{10,2},{11,3},{12,4},{13,5},{14,6},{15,7}} | collective-permute-start | bytes 1327112 | tf_op jit(solution)/shard_map/ppermute | solution.py:204
  (115 other events, 994.4 us)
Sparse Core Ops, SparseCore 0:
  267.3 85.5 reduce-scatter.1
  413.2 108.4 all-gather.2

commit v3 on v2

--- a/solution.py
+++ b/solution.py
@@ -45,63 +45,45 @@
 
 
 class Live:
-    def __init__(self, **values):
-        self.values = values
-
-    def __getitem__(self, name):
-        return self.values[name]
-
-    def __setitem__(self, name, value):
-        self.values[name] = value
-
-    def take(self, *names):
-        found = [self.values.pop(name) for name in names]
-        return found if len(found) > 1 else found[0]
-
-    def sync(self, *chains, late=()):
-        left_out = {name: self.values.pop(name) for name in late}
-        moving = [chain.moving() for chain in chains]
-        self.values, moving = lax.optimization_barrier((self.values, moving))
-        self.values.update(left_out)
-        for chain, values in zip(chains, moving):
-            chain.landed(values)
-
-
-def gather_one(live, name):
-    live[name + "x"] = swap(live[name], 1)
-    live[name + "y"] = swap(live[name], 2)
-
-
-def gather_two(live, name):
-    half = live[name].shape[0] // 2
-    live[name + "t"] = swap(live[name + "x"][:half], 2)
-    live[name + "b"] = swap(live[name + "y"][half:], 1)
-
-
-def gathered(live, name):
-    return [live[name + end] for end in ("", "x", "y", "t", "b")]
-
-
-def fetch_one(live, name, pieces, place, count):
+    def sync(self):
+        self.__dict__.update(lax.optimization_barrier(dict(self.__dict__)))
+
+
+def ready(*values):
+    return lax.optimization_barrier(values)
+
+
+def gather_one(value):
+    return [value, swap(value, 1), swap(value, 2)]
+
+
+def gather_halves(found):
+    half = found[0].shape[0] // 2
+    return found[1][:half], found[2][half:]
+
+
+def gather_two(found, halves):
+    return found + [swap(halves[0], 2), swap(halves[1], 1)]
+
+
+def fetch_halves(pieces, place, count):
     parts = 2 if count % 2 == 0 else 1
     rows = pieces[0].shape[0] // parts
     at = (place % parts) * rows
-    live[name] = pieces[0]
-    for i in (1, 2, 3):
-        live[f"{name}{i}"] = swap(lax.dynamic_slice_in_dim(pieces[i], at, rows, 0), i)
-
-
-def fetch_two(live, name, count):
-    live[name + "m"] = jnp.stack(live.take(*[f"{name}{i}" for i in (1, 2, 3)]))
-    if count % 2 == 0:
-        live[name + "p"] = pair(live[name + "m"], count)
-
-
-def fetched(live, name, place, count):
-    own, mine = live.take(name, name + "m")
-    if count % 2:
+    return [lax.dynamic_slice_in_dim(pieces[i], at, rows, 0) for i in (1, 2, 3)]
+
+
+def fetch_one(halves):
+    return [swap(half, i) for i, half in enumerate(halves, 1)]
+
+
+def fetch_two(mine, count):
+    return pair(mine, count) if count % 2 == 0 else ()
+
+
+def fetched(own, mine, theirs, place):
+    if isinstance(theirs, tuple):
         return jnp.concatenate([own[None], mine])
-    theirs = live.take(name + "p")
     rows = mine.shape[1]
     bit = place % 2
     zero = jnp.zeros((), jnp.int32)
@@ -111,121 +93,108 @@
     return lax.dynamic_update_slice(result, theirs, (zero + 1, (1 - bit) * rows, zero))
 
 
-SUMS = ("own_a", "far_a", "near_a", "own_b", "far_b", "near_b")
-
-
-def scatter_put(live, name, parts):
-    for end, part in zip(SUMS, parts):
-        live[name + end] = part
-
-
-def scatter_one(live, name):
-    live[name + "got_a"] = swap(live.take(name + "far_a"), 1)
-    live[name + "got_b"] = swap(live.take(name + "far_b"), 2)
-
-
-def scatter_two(live, name):
-    got_a, got_b = live[name + "got_a"], live[name + "got_b"]
-    width = got_a.shape[1] // 2
-    send_a = (live.take(name + "near_a").astype(F32) + got_a[:, width:].astype(F32)).astype(LOW)
-    send_b = (live.take(name + "near_b").astype(F32) + got_b[:, width:].astype(F32)).astype(LOW)
-    live[name + "last_a"] = swap(send_a, 2)
-    live[name + "last_b"] = swap(send_b, 1)
-
-
-def scattered(live, name):
-    halves = []
-    for end in ("a", "b"):
-        own, got, last = live.take(name + "own_" + end, name + "got_" + end, name + "last_" + end)
-        halves.append(own.astype(F32) + got[:, : own.shape[1]].astype(F32) + last.astype(F32))
-    return jnp.concatenate(halves, axis=0)
-
-
-class Scatter:
-    def __init__(self, live, name, count, rows=()):
-        self.live, self.name, self.count, self.at, self.rows = live, name, count, 1, rows
-        self.place = lax.axis_index("dp")
-
-    def part(self, number):
-        total = self.live[self.name]
-        rows = self.rows if self.rows else (total.shape[1],)
-        found, at = [], 0
-        for count in rows:
-            size = count // self.count
-            found.append(lax.dynamic_slice_in_dim(total, at + number * size, size, 1))
-            at = at + count
-        return found[0] if len(found) == 1 else jnp.concatenate(found, axis=1)
-
-    def step(self):
-        count, at, place = self.count, self.at, self.place
-        if at >= count:
-            return
-        up = self.part(jnp.clip(count - at + place, 0, count - 1))
-        down = self.part(jnp.clip(place - (count - at), 0, count - 1))
-        if at > 1:
-            up = (up.astype(F32) + self.up.astype(F32)).astype(LOW)
-            down = (down.astype(F32) + self.down.astype(F32)).astype(LOW)
-        ups = [(i, i + 1) for i in range(min(at, count - 1))]
-        self.up = lax.ppermute(up, "dp", ups)
-        self.down = lax.ppermute(down, "dp", [(count - 1 - i, count - 1 - j) for i, j in ups])
-        self.at = at + 1
-
-    def moving(self):
-        return (self.up, self.down) if self.at > 1 else ()
-
-    def landed(self, values):
-        if values:
-            self.up, self.down = values
-
-    def finish(self):
-        while self.at < self.count:
-            self.step()
-        own = self.part(self.place)
-        if self.count > 1:
-            own = (own.astype(F32) + self.up.astype(F32) + self.down.astype(F32)).astype(LOW)
-        self.live.take(self.name)
-        return own
-
-
-class Gather:
-    def __init__(self, live, name, count):
-        self.live, self.name, self.count = live, name, count
-        self.place = lax.axis_index("dp")
-        self.ups, self.downs = [], []
-
-    def step(self):
-        count, at = self.count, len(self.ups) + 1
-        if at >= count:
-            return
-        own = self.live[self.name]
-        up, down = self.ups[-1] if self.ups else own, self.downs[-1] if self.downs else own
-        ups = [(i, i + 1) for i in range(at - 1, count - 1)]
-        self.ups.append(lax.ppermute(up, "dp", ups))
-        self.downs.append(lax.ppermute(down, "dp", [(count - 1 - i, count - 1 - j) for i, j in ups]))
-
-    def moving(self):
-        return (self.ups, self.downs)
-
-    def landed(self, values):
-        self.ups, self.downs = values
-
-    def finish(self):
-        while len(self.ups) + 1 < self.count:
-            self.step()
-        count, place = self.count, self.place
-        shard = self.live.take(self.name)
-        dims = (shard.shape[0], count) + shard.shape[1:]
-        zero = jnp.zeros((), jnp.int32)
-        result = jnp.zeros(dims, shard.dtype)
-
-        def put(result, piece, at):
-            return lax.dynamic_update_slice(result, piece[:, None], (zero, at) + (zero,) * (len(dims) - 2))
-
-        for at, (up, down) in enumerate(zip(self.ups, self.downs), 1):
-            result = put(result, up, jnp.where(place - at >= 0, place - at, place))
-            result = put(result, down, jnp.where(place + at < count, place + at, place))
-        result = put(result, shard, place)
-        return result.reshape(dims[0], count * dims[2], dims[3])
+def scatter_one(parts):
+    own, far_a, near_a, far_b, near_b = parts
+    return own, swap(far_a, 1), near_a, swap(far_b, 2), near_b
+
+
+def scatter_halves(parts):
+    own, got_a, near_a, got_b, near_b = parts
+    width = own.shape[1]
+    send_a = (near_a.astype(F32) + got_a[:, width:].astype(F32)).astype(LOW)
+    send_b = (near_b.astype(F32) + got_b[:, width:].astype(F32)).astype(LOW)
+    return send_a, send_b
+
+
+def scatter_two(parts, halves):
+    own, got_a, _, got_b, _ = parts
+    return own, got_a, swap(halves[0], 2), got_b, swap(halves[1], 1)
+
+
+def scattered(parts):
+    own, got_a, last_a, got_b, last_b = parts
+    width, half = own.shape[1], got_a.shape[0]
+    upper = own[:half].astype(F32) + got_a[:, :width].astype(F32) + last_a.astype(F32)
+    lower = own[half:].astype(F32) + got_b[:, :width].astype(F32) + last_b.astype(F32)
+    return jnp.concatenate([upper, lower], axis=0)
+
+
+def shard_of(total, rows, number, count):
+    found, at = [], 0
+    for part in rows:
+        size = part // count
+        found.append(lax.dynamic_slice_in_dim(total, at + number * size, size, 1))
+        at = at + part
+    return found[0] if len(found) == 1 else jnp.concatenate(found, axis=1)
+
+
+def turn(value, step, count):
+    return lax.ppermute(value, "dp", [(i, (i + step) % count) for i in range(count)])
+
+
+def chain_up(count, first, last):
+    return [(i, i + 1) for i in range(first, last)]
+
+
+def chain_down(count, first, last):
+    return [(count - 1 - i, count - 2 - i) for i in range(first, last)]
+
+
+def chain_parts(step, total, rows, count, before):
+    if step >= count:
+        return ()
+    place = lax.axis_index("dp")
+    up = shard_of(total, rows, jnp.clip(count - step + place, 0, count - 1), count)
+    down = shard_of(total, rows, jnp.clip(place - (count - step), 0, count - 1), count)
+    if before:
+        up = (up.astype(F32) + before[0].astype(F32)).astype(LOW)
+        down = (down.astype(F32) + before[1].astype(F32)).astype(LOW)
+    return up, down
+
+
+def chain_sum(step, parts, count, before):
+    if step >= count:
+        return before
+    last = min(step, count - 1)
+    up, down = parts
+    return [lax.ppermute(up, "dp", chain_up(count, 0, last)), lax.ppermute(down, "dp", chain_down(count, 0, last))]
+
+
+def chain_sums(first, total, rows, count, before):
+    for step in range(first, count):
+        before = chain_sum(step, chain_parts(step, total, rows, count, before), count, before)
+    return before
+
+
+def chain_summed(total, rows, count, before):
+    own = shard_of(total, rows, lax.axis_index("dp"), count)
+    if before:
+        own = (own.astype(F32) + before[0].astype(F32) + before[1].astype(F32)).astype(LOW)
+    return own
+
+
+def chain_spread(first, last, shard, count, found):
+    for step in range(first, min(last, count)):
+        up, down = found[-1] if found else (shard, shard)
+        up = lax.ppermute(up, "dp", chain_up(count, step - 1, count - 1))
+        down = lax.ppermute(down, "dp", chain_down(count, step - 1, count - 1))
+        found = found + [(up, down)]
+    return found
+
+
+def chain_joined(shard, count, found):
+    place = lax.axis_index("dp")
+    dims = (shard.shape[0], count) + shard.shape[1:]
+    zero = jnp.zeros((), jnp.int32)
+    result = jnp.zeros(dims, shard.dtype)
+
+    def put(result, piece, at):
+        return lax.dynamic_update_slice(result, piece[:, None], (zero, at) + (zero,) * (len(dims) - 2))
+
+    for step, (up, down) in enumerate(found, 1):
+        result = put(result, up, jnp.where(place - step >= 0, place - step, place))
+        result = put(result, down, jnp.where(place + step < count, place + step, place))
+    return put(result, shard, place)
 
 
 def call(kernel, out_shape, in_specs, out_specs, grid=(), scratch=(), prefetch=0, flops=0, moved=0):
@@ -340,21 +309,23 @@
     )(*pieces, weight)
 
 
-def pack_kernel(row_ref, q_ref, k_ref, v_ref, out_ref):
+def pack_kernel(row_ref, gain_ref, q_ref, k_ref, v_ref, out_ref):
     row = row_ref[0]
+    gain = gain_ref[...]
     query, key = q_ref.shape[1] // 4, k_ref.shape[1] // 4
+    scaled = lambda ref, size, j: (ref[:, j * size : (j + 1) * size].astype(F32) * gain).astype(LOW)
     for j in range(4):
         at = jnp.bitwise_xor(row, j)
-        out_ref[at, :, :query] = q_ref[:, j * query : (j + 1) * query]
-        out_ref[at, :, query : query + key] = k_ref[:, j * key : (j + 1) * key]
-        out_ref[at, :, query + key :] = v_ref[:, j * key : (j + 1) * key]
-
-
-def pack(row, query_weight, key_weight, value_weight):
+        out_ref[at, :, :query] = scaled(q_ref, query, j)
+        out_ref[at, :, query : query + key] = scaled(k_ref, key, j)
+        out_ref[at, :, query + key :] = scaled(v_ref, key, j)
+
+
+def pack(row, gain, query_weight, key_weight, value_weight):
     depth = query_weight.shape[0]
     width = (query_weight.shape[1] + 2 * key_weight.shape[1]) // 4
     out = shape((4, depth, width))
-    arrays = (query_weight, key_weight, value_weight)
+    arrays = (gain, query_weight, key_weight, value_weight)
     return call(
         pack_kernel,
         out,
@@ -366,11 +337,11 @@
     )(row, *arrays)
 
 
-def project_kernel(x0, x1, x2, top, bottom, gain, w_own, w_oth, cos, sin, first, r1, own, oth):
+def project_kernel(x0, x1, x2, top, bottom, w_own, w_oth, cos, sin, first, r1, own, oth):
     upper = pl.program_id(0) < pl.num_programs(0) // 2
     x = read_pieces((x0, x1, x2, top, bottom), upper).astype(F32)
     inverse = lax.rsqrt(jnp.mean(x * x, axis=1, keepdims=True) + EPSILON)
-    normed = (x * inverse * gain[...]).astype(LOW)
+    normed = (x * inverse).astype(LOW)
     first[...] = normed
     r1[...] = jnp.broadcast_to(inverse, r1.shape)
     for weight, out in ((w_own, own), (w_oth, oth)):
@@ -382,7 +353,7 @@
         out[:, 3 * LANES :] = heads[:, 3 * LANES :].astype(LOW)
 
 
-def project(xs, gain, w_own, w_oth, cos, sin):
+def project(xs, w_own, w_oth, cos, sin):
     tokens, width = xs[0].shape
     rows = lambda n: pl.BlockSpec((TILE, n), lambda b: (b, 0))
     outs = (shape((tokens, 4 * width)), shape((tokens, LANES), F32), shape((tokens, 512)), shape((tokens, 512)))
@@ -390,12 +361,12 @@
         project_kernel,
         outs,
         piece_specs(width, TILE, tokens // TILE)
-        + [whole(gain), whole(w_own), whole(w_oth), rows(LANES), rows(LANES)],
+        + [whole(w_own), whole(w_oth), rows(LANES), rows(LANES)],
         tuple(rows(o.shape[1]) for o in outs),
         grid=(tokens // TILE,),
         flops=2 * tokens * 4 * width * 1024,
         moved=bytes_of(*xs, w_own, w_oth, *outs),
-    )(*xs, gain, w_own, w_oth, cos, sin)
+    )(*xs, w_own, w_oth, cos, sin)
 
 
 def stack_heads(ref, rows):
@@ -592,19 +563,19 @@
 
 
 def middle_kernel(*refs):
-    weight, gain, second, middle, r2, joined = refs[10:]
+    weight, second, middle, r2, joined = refs[10:]
     upper = pl.program_id(0) < pl.num_programs(0) // 2
     heads = read_pieces(refs[:5], upper)
     joined[...] = heads
     x = read_pieces(refs[5:10], upper).astype(F32)
     value = x + dot(heads, weight[...])
     inverse = lax.rsqrt(jnp.mean(value * value, axis=1, keepdims=True) + EPSILON)
-    second[...] = (value * inverse * gain[...]).astype(LOW)
+    second[...] = (value * inverse).astype(LOW)
     middle[...] = value[:, : middle.shape[1]]
     r2[...] = jnp.broadcast_to(inverse, r2.shape)
 
 
-def middle_of(heads, xs, weight, gain):
+def middle_of(heads, xs, weight):
     tokens, width = xs[0].shape
     rows = lambda n: pl.BlockSpec((TILE, n), lambda b: (b, 0))
     outs = (
@@ -616,12 +587,12 @@
     return call(
         middle_kernel,
         outs,
-        piece_specs(width, TILE, tokens // TILE) * 2 + [whole(weight), whole(gain)],
+        piece_specs(width, TILE, tokens // TILE) * 2 + [whole(weight)],
         tuple(rows(o.shape[1]) for o in outs),
         grid=(tokens // TILE,),
         flops=2 * tokens * 16 * width * width,
         moved=bytes_of(*heads, *xs, weight, *outs),
-    )(*heads, *xs, weight, gain)
+    )(*heads, *xs, weight)
 
 
 def feed_kernel(second, cot, g_own, u_own, g_oth, u_oth, d_own, d_oth, hidden_own, hidden_oth, back_own, back_oth):
@@ -683,61 +654,69 @@
     )(second, cot, gu_own, gu_own, gu_oth, gu_oth, d_own, d_oth)
 
 
-def partial_kernel(which, blocked, a_own, a_oth, w_own, w_oth, *rest):
-    if len(rest) == 5:
-        against, own, far, near, sums = rest
+def partial_kernel(blocked, a_own, a_oth, w_own, w_oth, *rest):
+    upper = pl.program_id(0) < pl.num_programs(0) // 2
+    if len(rest) == 7:
+        against, own, far_a, near_a, far_b, near_b, sums = rest
     else:
-        own, far, near = rest
+        own, far_a, near_a, far_b, near_b = rest
     width = own.shape[1]
     total = 0.0
     left, right = a_own[...], a_oth[...]
-    for k, target in enumerate((own, far if not which else near, near if not which else far, far)):
+    found = []
+    for k in range(4):
         columns = slice(k * width, (k + 1) * width)
         if blocked:
             value = dot(left, w_own[k]) + dot(right, w_oth[k])
         else:
             value = dot(left, w_own[columns, :], NT) + dot(right, w_oth[columns, :], NT)
-        if len(rest) == 5:
+        if len(rest) == 7:
             total = total + jnp.sum(value * against[:, columns].astype(F32), axis=1, keepdims=True)
-        if target is far:
-            place = width if k == 3 else 0
-            far[:, place : place + width] = value.astype(LOW)
-        else:
-            target[...] = value.astype(LOW)
-    if len(rest) == 5:
+        found.append(value.astype(LOW))
+    own[...] = found[0]
+    if len(rest) == 7:
         sums[...] = jnp.broadcast_to(total, sums.shape)
 
-
-def partial_half(which, blocked, a_own, a_oth, w_own, w_oth, against):
+    @pl.when(upper)
+    def _():
+        far_a[:, :width] = found[1]
+        far_a[:, width:] = found[3]
+        near_a[...] = found[2]
+
+    @pl.when(jnp.logical_not(upper))
+    def _():
+        far_b[:, :width] = found[2]
+        far_b[:, width:] = found[3]
+        near_b[...] = found[1]
+
+
+def partial_sums(blocked, a_own, a_oth, w_own, w_oth, against=None):
     tokens, depth = a_own.shape
     model = 4 * w_own.shape[2] if blocked else w_own.shape[0]
     half, width = tokens // 2, model // 4
-    blocks = half // TILE
-    read = lambda n: pl.BlockSpec((TILE, n), lambda b: (which * blocks + b, 0))
-    write = lambda n: pl.BlockSpec((TILE, n), lambda b: (b, 0))
-    outs = [shape((half, width)), shape((half, 2 * width)), shape((half, width))]
+    blocks = tokens // TILE
+    plain = lambda n: pl.BlockSpec((TILE, n), lambda b: (b, 0))
+    early = lambda n: pl.BlockSpec((TILE, n), lambda b: (jnp.minimum(b, blocks // 2 - 1), 0))
+    late = lambda n: pl.BlockSpec((TILE, n), lambda b: (jnp.maximum(b - blocks // 2, 0), 0))
+    outs = [shape((tokens, width))] + [shape((half, 2 * width)), shape((half, width))] * 2
+    writes = [plain(width), early(2 * width), early(width), late(2 * width), late(width)]
     args = [a_own, a_oth, w_own, w_oth]
-    specs = [read(depth), read(depth), whole(w_own), whole(w_oth)]
+    specs = [plain(depth), plain(depth), whole(w_own), whole(w_oth)]
     if against is not None:
-        outs.append(shape((half, LANES), F32))
+        outs.append(shape((tokens, LANES), F32))
+        writes.append(plain(LANES))
         args.append(against)
-        specs.append(read(model))
-    return call(
-        functools.partial(partial_kernel, which, blocked),
+        specs.append(plain(model))
+    found = call(
+        functools.partial(partial_kernel, blocked),
         tuple(outs),
         specs,
-        tuple(write(o.shape[1]) for o in outs),
+        tuple(writes),
         grid=(blocks,),
-        flops=4 * half * depth * model,
-        moved=bytes_of(w_own, w_oth, *outs) + half * 4 * depth,
+        flops=4 * tokens * depth * model,
+        moved=bytes_of(*args, *outs),
     )(*args)
-
-
-def partial_sums(blocked, a_own, a_oth, w_own, w_oth, against=None):
-    first = partial_half(0, blocked, a_own, a_oth, w_own, w_oth, against)
-    second = partial_half(1, blocked, a_own, a_oth, w_own, w_oth, against)
-    sums = None if against is None else jnp.concatenate([first[3][:, 0], second[3][:, 0]])
-    return (first[0], first[1], first[2], second[0], second[1], second[2]), sums
+    return found[:5], None if against is None else found[5][:, 0].reshape(8, tokens // 8)
 
 
 def feed_grads_kernel(second, cot, back, hidden, out):
@@ -791,25 +770,28 @@
     )(first, heads, back, branch, spread)
 
 
-def feed_place_kernel(row_ref, piece, gate, up, down):
+def feed_place_kernel(row_ref, piece, gain, gate, up, down):
     units, share = gate.shape[1], piece.shape[2]
     for k in range(piece.shape[0]):
         rows = slice(k * share, (k + 1) * share)
-        gate[rows, :] = piece[k, 0, :, :units].astype(F32)
-        up[rows, :] = piece[k, 0, :, units : 2 * units].astype(F32)
+        gate[rows, :] = piece[k, 0, :, :units].astype(F32) * gain[rows, :]
+        up[rows, :] = piece[k, 0, :, units : 2 * units].astype(F32) * gain[rows, :]
     down[...] = jnp.concatenate(
         [piece[k, 0, :, 2 * units :].astype(F32) for k in range(piece.shape[0])], axis=0
     ).T
 
 
-def feed_place(row, pieces):
+def feed_place(row, pieces, gain):
     count, _, share, triple = pieces.shape
     units, depth = triple // 3, count * share
     outs = (shape((depth, 4 * units), F32), shape((depth, 4 * units), F32), shape((4 * units, depth), F32))
     return call(
         feed_place_kernel,
         outs,
-        [pl.BlockSpec((count, 1, share, triple), lambda j, s: (0, jnp.bitwise_xor(s[0], j), 0, 0))],
+        [
+            pl.BlockSpec((count, 1, share, triple), lambda j, s: (0, jnp.bitwise_xor(s[0], j), 0, 0)),
+            whole(gain),
+        ],
         (
             pl.BlockSpec((depth, units), lambda j, s: (0, j)),
             pl.BlockSpec((depth, units), lambda j, s: (0, j)),
@@ -818,21 +800,21 @@
         grid=(4,),
         prefetch=1,
         moved=bytes_of(pieces, *outs),
-    )(row, pieces)
-
-
-def mix_place_kernel(row_ref, pieces, heads, query, key, value, output):
+    )(row, pieces, gain)
+
+
+def mix_place_kernel(row_ref, pieces, heads, gain, query, key, value, output):
     row = row_ref[0]
     wide, narrow = query.shape[1] // 4, key.shape[1] // 4
     for j in range(4):
-        piece = pieces[jnp.bitwise_xor(row, j)].astype(F32)
+        piece = pieces[jnp.bitwise_xor(row, j)].astype(F32) * gain[...]
         query[:, j * wide : (j + 1) * wide] = piece[:, :wide]
         key[:, j * narrow : (j + 1) * narrow] = piece[:, wide : wide + narrow]
         value[:, j * narrow : (j + 1) * narrow] = piece[:, wide + narrow :]
         output[j * wide : (j + 1) * wide, :] = heads[jnp.bitwise_xor(row, j)].astype(F32)
 
 
-def mix_place(row, pieces, heads):
+def mix_place(row, pieces, heads, gain):
     _, depth, width = pieces.shape
     wide, narrow = width // 2, width // 4
     outs = (
@@ -844,12 +826,12 @@
     return call(
         mix_place_kernel,
         outs,
-        [whole(pieces), whole(heads)],
+        [whole(pieces), whole(heads), whole(gain)],
         tuple(whole(o) for o in outs),
         grid=(1,),
         prefetch=1,
         moved=bytes_of(pieces, heads, *outs),
-    )(row, pieces, heads)
+    )(row, pieces, heads, gain)
 
 
 def sequence_starts(lengths, tokens):
@@ -907,197 +889,213 @@
     rows = output_weight.shape[0]
     chunk = rows // 4
     relative = [jnp.bitwise_xor(row, i) for i in range(4)]
-    live = Live(
-        x=layer_input,
-        cot=cotangent,
-        g=jnp.stack([first_gain, second_gain]),
-        gate=gate_weight,
-        up=up_weight,
-        down=down_weight,
-        out=output_weight,
-    )
-
-    gather_one(live, "x")
-    packed = pack(row_info, query_weight, key_projection_weight, value_projection_weight)
-    fetch_one(live, "mix", [packed[i] for i in range(4)], place, blocks)
-    live["g"] = jnp.concatenate([live["g"], swap(live["g"], 1)], axis=1)
-    live.sync()
-
-    gather_two(live, "x")
-    fetch_two(live, "mix", blocks)
-    live["gains"] = jnp.concatenate([live["g"], swap(live.take("g"), 2)], axis=1)
-    places, starts = sequence_starts(sequence_lengths[0], tokens)
-    live["cos"], live["sin"] = tables(places - starts)
-    live["start"] = starts[None, :]
-    live["info"] = jnp.concatenate([core.reshape(1), starts[::TILE] // TILE]).astype(jnp.int32)
-    gate, up, down, out = live.take("gate", "up", "down", "out")
-    for i in range(4):
-        downs = lax.dynamic_slice_in_dim(down, relative[i] * units, units, 0)
-        live[f"odp{i}"] = jnp.concatenate([out, downs], axis=0)
-        live[f"gup{i}"] = jnp.concatenate(
-            [lax.dynamic_slice_in_dim(w, relative[i] * units, units, 1) for w in (gate, up)], axis=1
-        )
+    live = Live()
+    live.x, live.cot = layer_input, cotangent
+
+    live.xs = gather_one(live.x)
+    gains = [gain[:, None] for gain in (first_gain, second_gain)]
+    packed = pack(row_info, gains[0], query_weight, key_projection_weight, value_projection_weight)
+    mixer = [packed[i] for i in range(4)]
+    halves, weights = ready(
+        fetch_halves(mixer, place, blocks), (gate_weight, up_weight, down_weight, output_weight, gains[1])
+    )
+    live.mixer_one = fetch_one(halves)
+    live.mixer_own, live.lengths = mixer[0], sequence_lengths[0]
+    gate, up, down, out, gain = weights
+    downs = [lax.dynamic_slice_in_dim(down, relative[i] * units, units, 0) for i in range(4)]
+    out_down = [jnp.concatenate([out, downs[i]], axis=0) for i in range(4)]
+    scaled = lambda weight, i: (
+        lax.dynamic_slice_in_dim(weight, relative[i] * units, units, 1).astype(F32) * gain
+    ).astype(LOW)
+    gate_up = [jnp.concatenate([scaled(gate, i), scaled(up, i)], axis=1) for i in range(4)]
+    live.od_own, live.od_halves = out_down[0], fetch_halves(out_down, place, blocks)
+    live.gu_own, live.gu_halves = gate_up[0], fetch_halves(gate_up, place, blocks)
+    live.sync()
+
+    halves, mine = ready(gather_halves(live.xs), jnp.stack(live.mixer_one))
+    live.xs = gather_two(live.xs, halves)
+    live.mixer = (live.mixer_own, mine, fetch_two(mine, blocks))
+    places, starts = sequence_starts(live.lengths, tokens)
+    live.cos, live.sin = tables(places - starts)
+    live.start = starts[None, :]
+    live.info = jnp.concatenate([core.reshape(1), starts[::TILE] // TILE]).astype(jnp.int32)
     spread = spread_matrix()
-    live.sync()
-
-    fetch_one(live, "od", live.take(*[f"odp{i}" for i in range(4)]), place, blocks)
-    mixer = fetched(live, "mix", place, blocks).reshape(model, 4 * HEAD)
-    live["w_own"] = dot(mixer, spread).astype(LOW)
-    live["w_oth"] = other(live["w_own"])
-    cos_own = lax.dynamic_slice_in_dim(live["cos"], core * half, half, 0)
-    sin_own = lax.dynamic_slice_in_dim(live["sin"], core * half, half, 0)
-    live["first"], live["r1"], live["qkv"], live["qkv_send"] = project(
-        gathered(live, "x"), live["gains"][:1], live["w_own"], live["w_oth"], cos_own, sin_own
-    )
-    live.sync()
-    fetch_one(live, "gu", live.take(*[f"gup{i}" for i in range(4)]), place, blocks)
-    fetch_two(live, "od", blocks)
-    live["qkv_got"] = other(live.take("qkv_send"))
-    live["keep"], live["send"], live["attended"], live["lse"] = attend(
-        live["info"], live["qkv"], live["qkv_got"], live["start"]
-    )
-    coming = ("odp",) if blocks % 2 == 0 else ()
-    live.sync(late=coming)
-    keep, send = live.take("keep", "send")
-    live["heads"] = jnp.concatenate([keep, other(send)], axis=1)
-    live.sync(late=coming)
-
-    gather_one(live, "heads")
-    gather_one(live, "cot")
-    fetch_two(live, "gu", blocks)
-    od_own = fetched(live, "od", place, blocks)
-    od_oth = other(od_own)
-    live["out_full"], live["out_mine"] = order(row_info, od_own[:, :rows], od_oth[:, :rows])
-    live["d_own"], live["d_oth"] = od_own[:, rows:], od_oth[:, rows:]
-    live.sync()
-
-    gather_two(live, "heads")
-    gather_two(live, "cot")
-    live["gu_own"] = fetched(live, "gu", place, blocks).reshape(model, 2 * units)
-    live["gu_oth"] = other(live["gu_own"])
-    live.sync()
-
-    live["second"], live["middle"], live["r2"], live["heads_all"] = middle_of(
-        gathered(live, "heads"), gathered(live, "x"), live["out_full"], live["gains"][1:]
-    )
-    live["cot_all"] = join(gathered(live, "cot"))
-
-    live["hid_own"], live["hid_oth"], live["back_own"], live["back_oth"] = feed(
-        live["second"], live["cot_all"], live["gu_own"], live["gu_oth"], live["d_own"], live["d_oth"]
-    )
-    parts, sums = partial_sums(
-        False, live["back_own"], live["back_oth"], live["gu_own"], live["gu_oth"], live["second"]
-    )
-    scatter_put(live, "sg", parts)
-    live["sums"] = sums.reshape(8, half // 8)
+    del live.mixer_one, live.mixer_own, live.lengths
+    live.sync()
+
+    live.od_one = fetch_one(live.od_halves)
+    live.w_own = dot(fetched(*live.mixer, place).reshape(model, 4 * HEAD), spread).astype(LOW)
+    live.w_oth = other(live.w_own)
+    cos_own = lax.dynamic_slice_in_dim(live.cos, core * half, half, 0)
+    sin_own = lax.dynamic_slice_in_dim(live.sin, core * half, half, 0)
+    live.first, live.r1, live.qkv, live.send = project(
+        live.xs, live.w_own, live.w_oth, cos_own, sin_own
+    )
+    del live.mixer, live.od_halves
+    live.sync()
+    halves, send, live.od_mine = ready(live.gu_halves, live.send, jnp.stack(live.od_one))
+    live.od_theirs = fetch_two(live.od_mine, blocks)
+    live.gu_one = fetch_one(halves)
+    live.qkv_got = other(send)
+    live.keep, live.send, live.attended, live.lse = attend(live.info, live.qkv, live.qkv_got, live.start)
+    del live.od_one, live.gu_halves
+    live.sync()
+    live.heads = jnp.concatenate([live.keep, other(live.send)], axis=1)
+    live.gu_mine = jnp.stack(live.gu_one)
+    del live.keep, live.send, live.gu_one
+    live.sync()
+
+    live.gu_theirs = fetch_two(live.gu_mine, blocks)
+    live.heads = gather_one(live.heads)
+    live.cots = gather_one(live.cot)
+    live.od_own = fetched(live.od_own, live.od_mine, live.od_theirs, place)
+    del live.od_mine, live.od_theirs
+    live.sync()
+
+    halves, more = ready(gather_halves(live.heads), gather_halves(live.cots))
+    live.heads = gather_two(live.heads, halves)
+    live.cots = gather_two(live.cots, more)
+    od_oth = other(live.od_own)
+    live.out_full, live.out_mine = order(row_info, live.od_own[:, :rows], od_oth[:, :rows])
+    live.d_own, live.d_oth = live.od_own[:, rows:], od_oth[:, rows:]
+    live.gu_own = fetched(live.gu_own, live.gu_mine, live.gu_theirs, place).reshape(model, 2 * units)
+    del live.od_own, live.gu_mine, live.gu_theirs
+    live.sync()
+    live.gu_oth = other(live.gu_own)
+    live.cot_all = join(live.cots)
+    del live.cots
+
+    live.second, live.middle, live.r2, live.heads_all = middle_of(live.heads, live.xs, live.out_full)
+    del live.heads, live.xs, live.out_full
+    live.hid_own, live.hid_oth, live.back_own, live.back_oth = feed(
+        live.second, live.cot_all, live.gu_own, live.gu_oth, live.d_own, live.d_oth
+    )
+    live.sg, live.sums = partial_sums(False, live.back_own, live.back_oth, live.gu_own, live.gu_oth, live.second)
+    del live.gu_own, live.gu_oth
     live.sync()
 
     def added(own, got):
         return (own.astype(F32) + got.astype(F32)).astype(LOW)
 
-    scatter_one(live, "sg")
-    live["sums"] = live["sums"] + swap(live["sums"], 1)
-    live["feed_send"] = feed_grads(live["second"], live["cot_all"], live["back_oth"], live["hid_oth"], blocks)
-    live["feed"] = feed_grads(live["second"], live["cot_all"], live["back_own"], live["hid_own"], blocks)
-    live.sync()
-
-    scatter_two(live, "sg")
-    live["inner"] = live["sums"] + swap(live.take("sums"), 2)
-    live["feed"] = added(live["feed"], other(live.take("feed_send")))
-    live.sync()
-
-    feed_sum = lax.psum_scatter(live.take("feed"), "dp", scatter_dimension=0)
-    second_grad = scattered(live, "sg")
-    inner = live.take("inner").reshape(half)
-    r2, middle = live["r2"][:, :1], live["middle"]
-    live["middle_grad"] = (
-        cotangent.astype(F32)
-        + r2 * second_gain[None, :] * second_grad
-        - middle * (r2 * r2 * inner[:, None] / model)
-    )
-    live["gain2"] = jnp.sum(second_grad * middle * r2, axis=0)
-    live["branch"] = live["middle_grad"].astype(LOW)
-    gather_one(live, "branch")
-    parts, _ = partial_sums(True, live["hid_own"], live["hid_oth"], live["d_own"], live["d_oth"])
-    scatter_put(live, "fo", parts)
-    live.sync()
-
-    gather_two(live, "branch")
-    live.sync()
-    live["grad"], live["grad_send"] = heads_grad_of(gathered(live, "branch"), live["out_mine"])
-    live["grad_got"] = other(live.take("grad_send"))
-    live.sync()
-
-    scatter_one(live, "fo")
-    live["bk"], live["bs"] = attend_back(
-        live["info"], live["qkv"], live["qkv_got"], live["grad"], live["grad_got"],
-        live["attended"], live["lse"], live["start"], live["cos"], live["sin"],
-    )
-    live["feed"] = feed_sum
-    live.sync()
-
-    live["feed"] = spread_row(live["feed"])
-    scatter_two(live, "fo")
-    live["bg"] = other(live.take("bs"))
-    live["mix_send"] = mix_grads(1, live["first"], live["heads_all"], live["bg"], live["branch"], spread)
-    live["mix"] = mix_grads(0, live["first"], live["heads_all"], live["bk"], live["branch"], spread)
-    live.sync()
-    feeds = lax.all_gather(live.take("feed"), "dp", axis=0)
-    live["mix"] = added(live["mix"], other(live.take("mix_send")))
-    parts, sums = partial_sums(False, live["bk"], live["bg"], live["w_own"], live["w_oth"], live["first"])
-    scatter_put(live, "fg", parts)
-    live["sums"] = sums.reshape(8, half // 8)
-    live.sync()
-
-    scatter_one(live, "fg")
-    live["sums"] = live["sums"] + swap(live["sums"], 1)
-    layer_output = (live["middle"] + scattered(live, "fo")).astype(LOW)
-    share = width // blocks
-    mixes = Scatter(live, "mix", blocks, (width, chunk))
-    mixes.step()
-    live.sync(mixes)
-
-    scatter_two(live, "fg")
-    live["inner"] = live["sums"] + swap(live.take("sums"), 2)
-    mixes.step()
-    live.sync(mixes)
-
-    mixes.step()
-    first_grad = scattered(live, "fg")
-    inner = live.take("inner").reshape(half)
-    r1 = live["r1"][:, :1]
-    inputs = layer_input.astype(F32)
+    live.sg = scatter_one(live.sg)
+    live.sums = (live.sums, swap(live.sums, 1))
+    live.feed_oth = feed_grads(live.second, live.cot_all, live.back_oth, live.hid_oth, blocks)
+    live.feed_own = feed_grads(live.second, live.cot_all, live.back_own, live.hid_own, blocks)
+    del live.back_own, live.back_oth, live.second, live.cot_all
+    live.sync()
+
+    halves, sums, feed_oth = ready(scatter_halves(live.sg), live.sums[0] + live.sums[1], live.feed_oth)
+    live.sg = scatter_two(live.sg, halves)
+    live.sums = (sums, swap(sums, 2))
+    live.feed_got = other(feed_oth)
+    del live.feed_oth
+    live.sync()
+
+    second_grad = scattered(live.sg)
+    inner = (live.sums[0] + live.sums[1]).reshape(half)
+    r2 = live.r2[:, :1]
+    live.middle_grad = (
+        live.cot.astype(F32)
+        + r2 * second_grad
+        - live.middle * (r2 * r2 * inner[:, None] / model)
+    )
+    live.branch = live.middle_grad.astype(LOW)
+    live.branches = gather_one(*ready(live.branch))
+    feed_sum = lax.psum_scatter(added(live.feed_own, live.feed_got), "dp", scatter_dimension=0)
+    live.fo, _ = partial_sums(True, live.hid_own, live.hid_oth, live.d_own, live.d_oth)
+    del live.feed_own, live.feed_got, live.hid_own, live.hid_oth, live.d_own, live.d_oth
+    live.gain_part = jnp.sum(second_grad * live.middle * r2, axis=0) / second_gain
+    del live.sg, live.sums, live.cot, live.r2
+    live.sync()
+
+    live.branches = gather_two(live.branches, ready(*gather_halves(live.branches)))
+    live.sync()
+    live.grad, live.send = heads_grad_of(live.branches, live.out_mine)
+    live.grad_got = other(live.send)
+    del live.branches, live.out_mine, live.send
+    live.sync()
+
+    live.fo = scatter_one(live.fo)
+    live.bk, live.send = attend_back(
+        live.info, live.qkv, live.qkv_got, live.grad, live.grad_got,
+        live.attended, live.lse, live.start, live.cos, live.sin,
+    )
+    del live.qkv, live.qkv_got, live.grad, live.grad_got, live.attended, live.lse, live.start, live.info
+    live.sync()
+
+    halves, send = ready(scatter_halves(live.fo), live.send)
+    live.fo = scatter_two(live.fo, halves)
+    live.bg = other(send)
+    live.mix_oth = mix_grads(1, live.first, live.heads_all, live.bg, live.branch, spread)
+    live.mix_own = mix_grads(0, live.first, live.heads_all, live.bk, live.branch, spread)
+    del live.send
+    live.sync()
+    live.mix = added(live.mix_own, other(live.mix_oth))
+    live.feed_sum = feed_sum
+    del live.mix_own, live.mix_oth
+    live.sync()
+    mix_rows, share = (width, chunk), width // blocks
+    parts, (bk, bg), shard = ready(
+        chain_parts(1, live.mix, mix_rows, blocks, []), (live.bk, live.bg), live.feed_sum
+    )
+    live.feed_sum = spread_row(shard)
+    live.moving = chain_sum(1, parts, blocks, [])
+    live.fg, live.sums = partial_sums(False, bk, bg, live.w_own, live.w_oth, live.first)
+    del live.bk, live.bg, live.w_own, live.w_oth, live.first
+    live.sync()
+
+    feeds = lax.all_gather(live.feed_sum, "dp", axis=0)
+    parts = ready(*chain_parts(2, live.mix, mix_rows, blocks, live.moving))
+    live.moving = chain_sum(2, parts, blocks, live.moving)
+    live.fg = scatter_one(live.fg)
+    live.sums = (live.sums, swap(live.sums, 1))
+    layer_output = (live.middle + scattered(live.fo)).astype(LOW)
+    del live.fo, live.middle, live.feed_sum
+    live.sync()
+
+    halves, sums, parts = ready(
+        scatter_halves(live.fg),
+        live.sums[0] + live.sums[1],
+        chain_parts(3, live.mix, mix_rows, blocks, live.moving),
+    )
+    live.moving = chain_sum(3, parts, blocks, live.moving)
+    live.fg = scatter_two(live.fg, halves)
+    live.sums = (sums, swap(sums, 2))
+    live.sync()
+
+    live.moving = chain_sums(4, live.mix, mix_rows, blocks, live.moving)
+    (shard,) = ready(chain_summed(live.mix, mix_rows, blocks, live.moving))
+    turned = spread_row(shard[:, :share])
+    live.mix = jnp.concatenate([turned, shard[:, share:]], axis=1)
+    live.sync()
+    mix, _ = ready(live.mix, live.fg)
+    live.moving = chain_spread(1, 2, mix, blocks, [])
+    first_grad = scattered(live.fg)
+    inner = (live.sums[0] + live.sums[1]).reshape(half)
+    r1 = live.r1[:, :1]
+    inputs = live.x.astype(F32)
     input_gradient = (
-        live["middle_grad"]
-        + r1 * first_gain[None, :] * first_grad
+        live.middle_grad
+        + r1 * first_grad
         - inputs * (r1 * r1 * inner[:, None] / model)
     )
-    gains = jnp.stack([jnp.sum(first_grad * inputs * r1, axis=0), live["gain2"]])
-    live["gains"] = gains + other(gains)
-    live.sync(mixes)
-
-    shard = mixes.finish()
-    turned = spread_row(shard[:, :share])
-    live["mix"] = jnp.concatenate([turned, shard[:, share:]], axis=1)
-    live.sync()
-    mixes = Gather(live, "mix", blocks)
-    mixes.step()
-    gain_total = live["gains"]
-    for step in range(1, blocks):
-        gain_total = gain_total + lax.ppermute(
-            live["gains"], "dp", [(i, (i + step) % blocks) for i in range(blocks)]
-        )
-    live["gains"] = gain_total
-    live.sync(mixes)
-    mixes.step()
-    live.sync(mixes)
-    mixes.step()
-    gate_total, up_total, down_total = feed_place(row_info, feeds)
-    mixes = mixes.finish().reshape(4, blocks, share + chunk // blocks, width)
+    gains = jnp.stack([jnp.sum(first_grad * inputs * r1, axis=0) / first_gain, live.gain_part])
+    live.gains = gains + other(gains)
+    del live.fg, live.sums, live.r1, live.x, live.middle_grad, live.gain_part
+    live.sync()
+    live.moving = chain_spread(2, 3, live.mix, blocks, live.moving)
+    live.got = [turn(live.gains, step, blocks) for step in range(1, blocks)]
+    live.sync()
+    gain_total = live.gains + sum(live.got)
+    moving = chain_spread(3, blocks, live.mix, blocks, live.moving)
+    mixes = chain_joined(live.mix, blocks, moving)
+    gate_total, up_total, down_total = feed_place(row_info, feeds, second_gain[:, None])
     query_total, key_total, value_total, output_total = mix_place(
-        row_info, mixes[:, :, :share].reshape(4, width, width), mixes[:, :, share:].reshape(4, chunk, width)
-    )
-    gain_total = live["gains"]
+        row_info,
+        mixes[:, :, :share].reshape(4, width, width),
+        mixes[:, :, share:].reshape(4, chunk, width),
+        first_gain[:, None],
+    )
     return (
         layer_output,
         input_gradient,

time: 587 us -> 550 us (0.937)
  waiting for transfers between devices: 184 us -> 153 us
  Pallas kernels: 156 us -> 144 us
  other arithmetic: 47.7 us -> 56.9 us
    reduce_scatter x1, waiting for transfers between devices: 18.7 us -> 0.49 us  [on_device(): lax.psum_scatter(added(live.feed_own, live.feed_got), 'dp', scatter_dimen...]
    ppermute x49 -> x47, waiting for transfers between devices: 103 us -> 90.3 us  [swap(): return lax.ppermute(value, 'row', [(i, i ^ step) for i in range(4)])]
    dynamic_slice x21 -> x14, local copies, waits for them, and re-layouts: 17.7 us -> 9.62 us  [the longest x3 4.75 us: fetch_halves(): return [lax.dynamic_slice_in_dim(pieces[i], at, rows, 0) for i in (1, 2, 3)]]
    ppermute x49 -> x47, starting transfers between devices: 58.2 us -> 51.9 us  [swap(): return lax.ppermute(value, 'row', [(i, i ^ step) for i in range(4)])]
    pallas_call x7 -> x4, Pallas kernels: 36.9 us -> 31.2 us  [the longest x3 28.4 us: partial_sums(): call(functools.partial(partial_kernel, blocked), tuple(outs), specs, tupl...]
    convert_element_type x13 -> x14, other arithmetic: 14.1 us -> 17.3 us  [the longest x2 3.82 us: chain_parts(): up = (up.astype(F32) + before[0].astype(F32)).astype(LOW)]
    unnamed x200 -> x178, local copies, waits for them, and re-layouts: 22.2 us -> 22.1 us
  transfers between devices with their start and end apart: 79 -> 77, of which waited for: 38 -> 37; matrix products, arithmetic and copies ran while one was open for 13% -> 13% of each run, Pallas kernels for 19% -> 20%
where the time goes in v3:
time: 550 us; the launch traced here: 544 us
  waiting for transfers between devices  153 us (28%)
  Pallas kernels  144 us (26%)
  starting transfers between devices  115 us (21%)
  other arithmetic  56.9 us (10%)
  local copies, waits for them, and re-layouts  54.4 us (10%)
  between operations  17.7 us (3%)
    ppermute x47, waiting for transfers between devices, swap(): return lax.ppermute(value, 'row', [(i, i ^ step) for i in range(4)])  90.3 us
    ppermute x47, starting transfers between devices, swap(): return lax.ppermute(value, 'row', [(i, i ^ step) for i in range(4)])  51.9 us
    pallas_call x3, Pallas kernels, partial_sums(): call(functools.partial(partial_kernel, blocked), tuple(outs), specs, tupl...  28.4 us
    ppermute x3, starting transfers between devices, chain_sum(): lax.ppermute(up, 'dp', chain_up(count, 0, last))  24.9 us
    unnamed x178, local copies, waits for them, and re-layouts  22.1 us
    ppermute x3, starting transfers between devices, turn(): lax.ppermute(value, 'dp', [(i, (i + step) % count) for i in range(count)])  20.1 us
    pallas_call x1, Pallas kernels, attend_back(): call(attend_back_kernel, outs, [whole(own), whole(oth), whole(g_own), who...  18.3 us
    pallas_call x1, Pallas kernels, feed(): call(feed_kernel, outs, [whole(second), whole(cot), column(early), column...  17.3 us
  transfers between devices with their start and end apart: 77, of which 37 were waited for; matrix products, arithmetic and copies ran while one was open for 13% of the time, Pallas kernels for 20%

profile of v3, /device:TPU:0, one launch (start us, length us, event | category | flops | bytes accessed | tf_op | source)
XLA Modules:
  0.0 543.9 jit_solution(1003045697305714372)
XLA Ops:
  7.2 3.0 collective-permute-start.3
  22.6 2.9 collective-permute-start.2
  25.5 3.5 multiply_convert_fusion.1
  31.4 2.1 pad_maximum_fusion.6
  35.7 2.3 fusion.8
  47.6 5.8 %fusion.6 = (f32[2048,128]{1,0:T(8,128)}, f32[2048,128]{1,0:T(8,128)}) fusion(f32[128]{0:T(128)S(1)} %get-tuple-element.1214, f32[128]{0:T(128)S(1)} %get-tuple-element.1215, f32[2048]{0:T(1024)S(1)} %get-tuple-element.1212, pred[128]{0:T(512)(128)(4,1)S(1)} %broadcast_compare_fusion), kind=kLoop, calls=%fused_computation.23 | loop fusion | flops 1048576 | bytes 2106496 | tf_op jit(solution)/shard_map/jit(_where)/select_n | solution.py:855
  53.4 2.4 collective-permute-done.6.top.refs_8_
  57.3 2.2 convolution_convert_fusion.w_own
  65.3 8.0 %shard_map.204 = (bf16[1024,1536]{1,0:T(8,128)(2,1)}, f32[1024,128]{1,0:T(8,128)S(1)}, bf16[1024,512]{1,0:T(8,128)(2,1)S(1)}, bf16[1024,512]{1,0:T(8,128)(2,1)}) custom-call(bf16[1024,384]{1,0:T(8,128)(2,1)S(1)} %copy-done.5, bf16[1024,384]{1,0:T(8,128)(2,1)S(1)} %collective-permute-done.3.x1.refs_6_, ...), custom_call_target="tpu_custom_call" | custom-call | flops 50331648 | bytes 188416 | tf_op jit(solution)/shard_map/pallas_call | solution.py:360
  73.4 10.7 %collective-permute-done.10 = bf16[640,384]{1,0:T(8,128)(2,1)} collective-permute-done((bf16[640,384]{1,0:T(8,128)(2,1)}, bf16[640,384]{1,0:T(8,128)(2,1)}, u32[]{:S(2)}, u32[]{:S(2)}) %collective-permute-start.10) | collective-permute-done | bytes 491552 | tf_op jit(solution)/shard_map/ppermute | solution.py:32
  89.5 2.0 collective-permute-start.15
  91.5 14.4 %shard_map.205 = (bf16[1024,192]{1,0:T(8,128)(2,1)S(1)}, bf16[1024,192]{1,0:T(8,128)(2,1)S(1)}, bf16[2048,256]{1,0:T(8,128)(2,1)S(1)}, f32[1,4096]{1,0:T(1,128)S(1)}) custom-call(s32[9]{0:T(128)S(1)} %pad_add_fusion.info, bf16[1024,512]{1,0:T(8,128)(2,1)S(1)} %get-tuple-element.966.own, bf16[1024,512]{1,0:T(8,128)(2,1)S(1)} %collective-permute-done.12.oth, ...), custom_call_target="tpu_custom_call" | custom-call | flops 67108864 | bytes 61696 | tf_op jit(solution)/shard_map/pallas_call | solution.py:443
  105.9 2.3 collective-permute-done.15
  108.3 12.2 %collective-permute-done.16 = bf16[3,640,384]{2,1,0:T(8,128)(2,1)S(1)} collective-permute-done((bf16[3,640,384]{2,1,0:T(8,128)(2,1)S(1)}, bf16[3,640,384]{2,1,0:T(8,128)(2,1)S(1)}, u32[]{:S(2)}, u32[]{:S(2)}) %collective-permute-start.16) | collective-permute-done | bytes 1474592 | tf_op jit(solution)/shard_map/ppermute | solution.py:40
  131.2 13.0 %collective-permute-done.18.x1 = bf16[1024,384]{1,0:T(8,128)(2,1)S(1)} collective-permute-done((bf16[1024,384]{1,0:T(8,128)(2,1)S(1)}, bf16[1024,384]{1,0:T(8,128)(2,1)S(1)}, u32[]{:S(2)}, u32[]{:S(2)}) %collective-permute-start.18) | collective-permute-done | bytes 786464 | tf_op jit(solution)/shard_map/ppermute | solution.py:32
  144.8 15.3 %collective-permute-done.21.refs_1_ = bf16[1024,384]{1,0:T(8,128)(2,1)} collective-permute-done((bf16[1024,384]{1,0:T(8,128)(2,1)S(1)}, bf16[1024,384]{1,0:T(8,128)(2,1)}, u32[]{:S(2)}, u32[]{:S(2)}) %collective-permute-start.21) | collective-permute-done | bytes 786464 | tf_op jit(solution)/shard_map/ppermute | solution.py:32
  171.3 2.0 copy-done.64
  173.3 1.7 slice.230.oth
  175.0 4.3 shard_map.206
  183.4 1.9 shard_map.208.cot
  186.2 10.3 %shard_map.207 = (bf16[1024,1536]{1,0:T(8,128)(2,1)}, f32[1024,384]{1,0:T(8,128)}, f32[1024,128]{1,0:T(8,128)S(1)}, bf16[1024,1536]{1,0:T(8,128)(2,1)}) custom-call(bf16[1024,384]{1,0:T(8,128)(2,1)S(1)} %copy-done.26, bf16[1024,384]{1,0:T(8,128)(2,1)} %collective-permute-done.21.refs_1_, bf16[1024,384]{1,0:T(8,128)(2,1)} %collective-permute-done.22.refs_2_, ...), custom_call_target="tpu_custom_call" | custom-call | flops 75497472 | bytes 303104 | tf_op jit(solution)/shard_map/pallas_call | solution.py:587
  196.5 17.3 %shard_map.209 = (bf16[1024,512]{1,0:T(8,128)(2,1)S(1)}, bf16[1024,512]{1,0:T(8,128)(2,1)S(1)}, bf16[1024,1024]{1,0:T(8,128)(2,1)}, bf16[1024,1024]{1,0:T(8,128)(2,1)}) custom-call(bf16[1024,1536]{1,0:T(8,128)(2,1)} %get-tuple-element.809.second.rest_0_, bf16[1024,1536]{1,0:T(8,128)(2,1)} %shard_map.208.cot, bf16[1536,1024]{1,0:T(8,128)(2,1)} %bitcast.87, ...), custom_call_target="tpu_custom_call" | custom-call | flops 150994944 | bytes 344064 | tf_op jit(solution)/shard_map/pallas_call | solution.py:637
  213.8 2.3 copy-done.3
  216.1 13.4 %shard_map.210 = (bf16[1024,384]{1,0:T(8,128)(2,1)S(1)}, bf16[512,768]{1,0:T(8,128)(2,1)S(1)}, bf16[512,384]{1,0:T(8,128)(2,1)S(1)}, bf16[512,768]{1,0:T(8,128)(...) custom-call(bf16[1024,1024]{1,0:T(8,128)(2,1)S(1)} %copy-done.3, ...), custom_call_target="tpu_custom_call" | custom-call | flops 100663296 | bytes 270336 | tf_op jit(solution)/shard_map/pallas_call | solution.py:710
  232.9 8.5 %shard_map.212 = bf16[4,4,96,1536]{3,2,1,0:T(8,128)(2,1)} custom-call(bf16[1024,1536]{1,0:T(8,128)(2,1)} %get-tuple-element.809.second.rest_0_, bf16[1024,1536]{1,0:T(8,128)(2,1)} %shard_map.208.cot, bf16[1024,1024]{1,0:T(8,128)(2,1)S(1)} %copy-done.4, bf16[1024,512]{1,0:T(8,128)(2,1)S(1)} %get-tuple-element.884.hidden.a_own), custom_call_target="tpu_custom_call" | custom-call | flops 75497472 | bytes 221184 | tf_op jit(solution)/shard_map/pallas_call | solution.py:735
  241.4 8.6 %shard_map.211 = bf16[4,4,96,1536]{3,2,1,0:T(8,128)(2,1)} custom-call(bf16[1024,1536]{1,0:T(8,128)(2,1)} %get-tuple-element.809.second.rest_0_, bf16[1024,1536]{1,0:T(8,128)(2,1)} %shard_map.208.cot, bf16[1024,1024]{1,0:T(8,128)(2,1)S(1)} %copy-done.2, bf16[1024,512]{1,0:T(8,128)(2,1)S(1)} %get-tuple-element.885.hidden.a_oth), custom_call_target="tpu_custom_call" | custom-call | flops 75497472 | bytes 221184 | tf_op jit(solution)/shard_map/pallas_call | solution.py:735
  253.9 8.1 %collective-permute-done.35 = f32[8,128]{1,0:T(8,128)S(1)} collective-permute-done((f32[8,128]{1,0:T(8,128)S(1)}, f32[8,128]{1,0:T(8,128)S(1)}, u32[]{:S(2)}, u32[]{:S(2)}) %collective-permute-start.35) | collective-permute-done | bytes 4128 | tf_op jit(solution)/shard_map/ppermute | solution.py:32
  263.4 6.0 %add_convert_fusion = bf16[4,4,96,1536]{3,2,1,0:T(8,128)(2,1)} fusion(bf16[4,4,96,1536]{3,2,1,0:T(8,128)(2,1)S(1)} %collective-permute-done.32, bf16[4,4,96,1536]{3,2,1,0:T(8,128)(2,1)} %shard_map.212), kind=kLoop, calls=%fused_computation | loop fusion | flops 9437184 | bytes 14155776 | tf_op jit(solution)/shard_map/convert_element_type | solution.py:978
  276.8 7.2 %shard_map.213 = (bf16[1024,384]{1,0:T(8,128)(2,1)S(1)}, bf16[512,768]{1,0:T(8,128)(2,1)S(1)}, bf16[512,384]{1,0:T(8,128)(2,1)S(1)}, bf16[512,768]{1,0:T(8,128)(2,1)S(1)}, bf16[512,384]{1,0:T(8,128)(2,1)S(1)}) custom-call(bf16[1024,512]{1,0:T(8,128)(2,1)S(1)} %copy-done.13, bf16[1024,512]{1,0:T(8,128)(2,1)S(1)} %copy-done.15, bf16[4,512,384]{2,1,0:T(8,128)(2,1)} %copy-done, ...), custom_call_target="tpu_custom_call" | custom-call | flops 50331648 | bytes 131072 | tf_op jit(solution)/shard_map/pallas_call | solution.py:710
  284.0 9.2 %collective-permute-done.36.x1 = bf16[1024,384]{1,0:T(8,128)(2,1)S(1)} collective-permute-done((bf16[1024,384]{1,0:T(8,128)(2,1)S(1)}, bf16[1024,384]{1,0:T(8,128)(2,1)S(1)}, u32[]{:S(2)}, u32[]{:S(2)}) %collective-permute-start.36) | collective-permute-done | bytes 786464 | tf_op jit(solution)/shard_map/ppermute | solution.py:32
  296.1 7.6 %collective-permute-done.38.top = bf16[512,384]{1,0:T(8,128)(2,1)S(1)} collective-permute-done((bf16[512,384]{1,0:T(8,128)(2,1)S(1)}, bf16[512,384]{1,0:T(8,128)(2,1)S(1)}, u32[]{:S(2)}, u32[]{:S(2)}) %collective-permute-start.38) | collective-permute-done | bytes 393248 | tf_op jit(solution)/shard_map/ppermute | solution.py:32
  304.5 2.4 shard_map.214
  307.0 1.9 collective-permute-done.40.g_oth
  310.6 18.3 %shard_map.215 = (bf16[1024,512]{1,0:T(8,128)(2,1)S(1)}, bf16[1024,512]{1,0:T(8,128)(2,1)S(1)}) custom-call(s32[9]{0:T(128)S(1)} %pad_add_fusion.info, bf16[1024,512]{1,0:T(8,128)(2,1)S(1)} %copy-done.17, bf16[1024,512]{1,0:T(8,128)(2,1)S(1)} %copy-done.19, bf16[1024,256]{1,0:T(8,128)(2,1)S(1)} %get-tuple-element.968.g_own, ...), custom_call_target="tpu_custom_call" | custom-call | flops 167772160 | bytes 98304 | tf_op jit(solution)/shard_map/pallas_call | solution.py:534
  331.9 6.1 %shard_map.217 = bf16[4,576,384]{2,1,0:T(8,128)(2,1)S(1)} custom-call(bf16[1024,1536]{1,0:T(8,128)(2,1)} %get-tuple-element.1040.first.rest_0_, bf16[1024,1536]{1,0:T(8,128)(2,1)} %get-tuple-element.1005.heads, bf16[1024,512]{1,0:T(8,128)(2,1)S(1)} %get-tuple-element.1036.back.a_own, bf16[1024,384]{1,0:T(8,128)(2,1)S(1)} %get-tuple-element.999.x0.branch, ...), custom_call_target="tpu_custom_call" | custom-call | flops 28311552 | bytes 154624 | tf_op jit(solution)/shard_map/pallas_call | solution.py:761
  338.1 7.8 %shard_map.216 = bf16[4,576,384]{2,1,0:T(8,128)(2,1)} custom-call(bf16[1024,1536]{1,0:T(8,128)(2,1)} %get-tuple-element.1040.first.rest_0_, bf16[1024,1536]{1,0:T(8,128)(2,1)} %get-tuple-element.1005.heads, bf16[1024,512]{1,0:T(8,128)(2,1)S(1)} %collective-permute-done.43.back.a_oth, bf16[1024,384]{1,0:T(8,128)(2,1)S(1)} %get-tuple-element.999.x0.branch, ...), custom_call_target="tpu_custom_call" | custom-call | flops 28311552 | bytes 154624 | tf_op jit(solution)/shard_map/pallas_call | solution.py:761
  347.4 4.0 collective-permute-done.46
  351.4 3.1 add_convert_fusion.1
  363.5 4.2 collective-permute-start.50
  369.1 7.9 %shard_map.218 = (bf16[1024,384]{1,0:T(8,128)(2,1)S(1)}, bf16[512,768]{1,0:T(8,128)(2,1)S(1)}, bf16[512,384]{1,0:T(8,128)(2,1)S(1)}, bf16[512,768]{1,0:T(8,128)(...) custom-call(bf16[1024,512]{1,0:T(8,128)(2,1)S(1)} %get-tuple-element.1036.back.a_own, ...), custom_call_target="tpu_custom_call" | custom-call | flops 50331648 | bytes 188416 | tf_op jit(solution)/shard_map/pallas_call | solution.py:710
  381.3 2.4 pad_maximum_fusion.4
  386.9 1.9 add_convert_fusion.5
  388.8 1.9 add_convert_fusion.6
  390.7 2.1 collective-permute-start.54
  395.0 7.2 %collective-permute-done.56 = f32[8,128]{1,0:T(8,128)S(1)} collective-permute-done((f32[8,128]{1,0:T(8,128)S(1)}, f32[8,128]{1,0:T(8,128)S(1)}, u32[]{:S(2)}, u32[]{:S(2)}) %collective-permute-start.56) | collective-permute-done | bytes 4128 | tf_op jit(solution)/shard_map/ppermute | solution.py:32
  402.2 5.4 collective-permute-done.54
  408.9 1.9 add_convert_fusion.4
  410.8 1.8 add_convert_fusion.7
  412.7 1.8 add_convert_fusion.8
  414.5 18.6 %collective-permute-start.59 = (bf16[4,144,384]{2,1,0:T(8,128)(2,1)}, bf16[4,144,384]{2,1,0:T(8,128)(2,1)S(1)}, u32[]{:S(2)}, u32[]{:S(2)}) collective-permute-start(bf16[4,144,384]{2,1,0:T(8,128)(2,1)} %add_convert_fusion.4), channel_id=1, source_target_pairs={{0,8},{8,16},{16,24},{1,9},{9,17},{17,25},{2,10},{10,18},{18,26},{... | collective-permute-start | bytes 1327112 | tf_op jit(solution)/shard_map/ppermute | solution.py:160
  434.6 1.9 collective-permute-start.61
  436.6 6.1 %collective-permute-done.61 = f32[8,128]{1,0:T(8,128)S(1)} collective-permute-done((f32[8,128]{1,0:T(8,128)S(1)}, f32[8,128]{1,0:T(8,128)S(1)}, u32[]{:S(2)}, u32[]{:S(2)}) %collective-permute-start.61) | collective-permute-done | bytes 4128 | tf_op jit(solution)/shard_map/ppermute | solution.py:32
  442.7 6.0 %collective-permute-done.59 = bf16[4,144,384]{2,1,0:T(8,128)(2,1)S(1)} collective-permute-done((bf16[4,144,384]{2,1,0:T(8,128)(2,1)}, bf16[4,144,384]{2,1,0:T(8,128)(2,1)S(1)}, u32[]{:S(2)}, u32[]{:S(2)}) %collective-permute-start.59) | collective-permute-done | bytes 442400 | tf_op jit(solution)/shard_map/ppermute | solution.py:160
  448.7 15.2 %collective-permute-done.60 = bf16[4,144,384]{2,1,0:T(8,128)(2,1)S(1)} collective-permute-done((bf16[4,144,384]{2,1,0:T(8,128)(2,1)S(1)}, bf16[4,144,384]{2,1,0:T(8,128)(2,1)S(1)}, u32[]{:S(2)}, u32[]{:S(2)}) %collective-permute-start.60) | collective-permute-done | bytes 442400 | tf_op jit(solution)/shard_map/ppermute | solution.py:160
  464.3 3.4 collective-permute-start.64
  470.1 4.4 collective-permute-start.66
  476.4 1.8 convert_add_fusion.1
  481.5 7.5 %collective-permute-done.66 = bf16[4,144,384]{2,1,0:T(8,128)(2,1)} collective-permute-done((bf16[4,144,384]{2,1,0:T(8,128)(2,1)S(1)}, bf16[4,144,384]{2,1,0:T(8,128)(2,1)}, u32[]{:S(2)}, u32[]{:S(2)}) %collective-permute-start.66) | collective-permute-done | bytes 442400 | tf_op jit(solution)/shard_map/ppermute | solution.py:179
  492.4 15.7 %collective-permute-start.68 = (f32[2,384]{1,0:T(2,128)S(1)}, f32[2,384]{1,0:T(2,128)S(1)}, u32[]{:S(2)}, u32[]{:S(2)}) collective-permute-start(f32[2,384]{1,0:T(2,128)S(1)} %fusion.23), channel_id=1, source_target_pairs={{0,8},{8,16},{16,24},{24,0},{1,9},{9,17},{17,25},{25,1},{2,10},{10... | collective-permute-start | bytes 9224 | tf_op jit(solution)/shard_map/ppermute | solution.py:132
  509.6 2.8 collective-permute-start.70
  521.5 5.7 %collective-permute-done.74 = bf16[4,144,384]{2,1,0:T(8,128)(2,1)S(1)} collective-permute-done((bf16[4,144,384]{2,1,0:T(8,128)(2,1)S(1)}, bf16[4,144,384]{2,1,0:T(8,128)(2,1)S(1)}, u32[]{:S(2)}, u32[]{:S(2)}) %collective-permute-start.74) | collective-permute-done | bytes 442400 | tf_op jit(solution)/shard_map/ppermute | solution.py:180
  527.6 2.7 shard_map.219
  530.3 2.3 copy-done.11
  532.6 4.2 shard_map.220
  (405 shorter events, 135.1 us)
Async XLA Ops:
  7.2 347.9 %reduce-scatter.2.cloned.1.call-start = ((), (), s32[]{:S(2)}) async-start(), calls=%async_computation.1 | async-start | bytes 5898240 | tf_op jit(solution)/shard_map/reduce_scatter | solution.py:1004
  7.2 30.8 %collective-permute-start.3 = (bf16[1024,384]{1,0:T(8,128)(2,1)}, bf16[1024,384]{1,0:T(8,128)(2,1)S(1)}, u32[]{:S(2)}, u32[]{:S(2)}) collective-permute-start(bf16[1024,384]{1,0:T(8,128)(2,1)} %refs_5_), channel_id=1, source_target_pairs={{0,2},{2,0},{4,6},{6,4},{1,3},{3,1},{5,7},{7,5},{8,10},{10,8},{12,... | collective-permute-start | bytes 2359304 | tf_op jit(solution)/shard_map/ppermute | solution.py:32
  10.2 27.8 %collective-permute-start.4 = (bf16[1024,384]{1,0:T(8,128)(2,1)}, bf16[1024,384]{1,0:T(8,128)(2,1)S(1)}, u32[]{:S(2)}, u32[]{:S(2)}) collective-permute-start(bf16[1024,384]{1,0:T(8,128)(2,1)} %refs_5_), channel_id=1, source_target_pairs={{0,4},{2,6},{4,0},{6,2},{1,5},{3,7},{5,1},{7,3},{8,12},{10,14},{12... | collective-permute-start | bytes 2359304 | tf_op jit(solution)/shard_map/ppermute | solution.py:32
  22.0 16.1 %collective-permute-start = (bf16[192,384]{1,0:T(8,128)(2,1)}, bf16[192,384]{1,0:T(8,128)(2,1)S(1)}, u32[]{:S(2)}, u32[]{:S(2)}) collective-permute-start(bf16[192,384]{1,0:T(8,128)(2,1)} %dynamic-slice_bitcast_fusion.2), channel_id=1, source_target_pairs={{0,2},{2,0},{4,6},{6,4},{1,3},{3,1},{5,7},{7,5},{8,10},{10,8},{12,... | collective-permute-start | bytes 442376 | tf_op jit(solution)/shard_map/ppermute | solution.py:32
  22.5 15.5 %collective-permute-start.1 = (bf16[192,384]{1,0:T(8,128)(2,1)}, bf16[192,384]{1,0:T(8,128)(2,1)}, u32[]{:S(2)}, u32[]{:S(2)}) collective-permute-start(bf16[192,384]{1,0:T(8,128)(2,1)} %dynamic-slice_bitcast_fusion.1), channel_id=1, source_target_pairs={{0,4},{2,6},{4,0},{6,2},{1,5},{3,7},{5,1},{7,3},{8,12},{10,14},{12... | collective-permute-start | bytes 442376 | tf_op jit(solution)/shard_map/ppermute | solution.py:32
  22.6 15.5 %collective-permute-start.2 = (bf16[192,384]{1,0:T(8,128)(2,1)}, bf16[192,384]{1,0:T(8,128)(2,1)}, u32[]{:S(2)}, u32[]{:S(2)}) collective-permute-start(bf16[192,384]{1,0:T(8,128)(2,1)} %dynamic-slice_bitcast_fusion), channel_id=1, source_target_pairs={{0,6},{2,4},{4,2},{6,0},{1,7},{3,5},{5,3},{7,1},{8,14},{10,12},{12... | collective-permute-start | bytes 442376 | tf_op jit(solution)/shard_map/ppermute | solution.py:32
  44.8 11.3 %collective-permute-start.5 = (bf16[3,192,384]{2,1,0:T(8,128)(2,1)S(1)}, bf16[3,192,384]{2,1,0:T(8,128)(2,1)}, u32[]{:S(2)}, u32[]{:S(2)}) collective-permute-start(bf16[3,192,384]{2,1,0:T(8,128)(2,1)S(1)} %pad_maximum_fusion.8), channel_id=1, source_target_pairs={{0,8},{8,0},{16,24},{24,16},{1,9},{9,1},{17,25},{25,17},{2,10},{10... | collective-permute-start | bytes 1327112 | tf_op jit(solution)/shard_map/ppermute | solution.py:40
  46.4 9.4 %collective-permute-start.6 = (bf16[512,384]{1,0:T(8,128)(2,1)}, bf16[512,384]{1,0:T(8,128)(2,1)S(1)}, u32[]{:S(2)}, u32[]{:S(2)}) collective-permute-start(bf16[512,384]{1,0:T(8,128)(2,1)} %slice.178), channel_id=1, source_target_pairs={{0,4},{2,6},{4,0},{6,2},{1,5},{3,7},{5,1},{7,3},{8,12},{10,14},{12... | collective-permute-start | bytes 1179656 | tf_op jit(solution)/shard_map/ppermute | solution.py:32
  46.9 9.1 %collective-permute-start.7 = (bf16[512,384]{1,0:T(8,128)(2,1)}, bf16[512,384]{1,0:T(8,128)(2,1)S(1)}, u32[]{:S(2)}, u32[]{:S(2)}) collective-permute-start(bf16[512,384]{1,0:T(8,128)(2,1)} %slice.179), channel_id=1, source_target_pairs={{0,2},{2,0},{4,6},{6,4},{1,3},{3,1},{5,7},{7,5},{8,10},{10,8},{12,... | collective-permute-start | bytes 1179656 | tf_op jit(solution)/shard_map/ppermute | solution.py:32
  59.6 24.5 %collective-permute-start.10 = (bf16[640,384]{1,0:T(8,128)(2,1)}, bf16[640,384]{1,0:T(8,128)(2,1)}, u32[]{:S(2)}, u32[]{:S(2)}) collective-permute-start(bf16[640,384]{1,0:T(8,128)(2,1)} %get-tuple-element.626), channel_id=1, source_target_pairs={{0,4},{2,6},{4,0},{6,2},{1,5},{3,7},{5,1},{7,3},{8,12},{10,14},{12... | collective-permute-start | bytes 1474568 | tf_op jit(solution)/shard_map/ppermute | solution.py:32
  61.1 23.0 %collective-permute-start.11 = (bf16[640,384]{1,0:T(8,128)(2,1)}, bf16[640,384]{1,0:T(8,128)(2,1)}, u32[]{:S(2)}, u32[]{:S(2)}) collective-permute-start(bf16[640,384]{1,0:T(8,128)(2,1)} %get-tuple-element.627), channel_id=1, source_target_pairs={{0,6},{2,4},{4,2},{6,0},{1,7},{3,5},{5,3},{7,1},{8,14},{10,12},{12... | collective-permute-start | bytes 1474568 | tf_op jit(solution)/shard_map/ppermute | solution.py:32
  61.6 23.7 %collective-permute-start.9 = (bf16[640,384]{1,0:T(8,128)(2,1)}, bf16[640,384]{1,0:T(8,128)(2,1)}, u32[]{:S(2)}, u32[]{:S(2)}) collective-permute-start(bf16[640,384]{1,0:T(8,128)(2,1)} %get-tuple-element.625), channel_id=1, source_target_pairs={{0,2},{2,0},{4,6},{6,4},{1,3},{3,1},{5,7},{7,5},{8,10},{10,8},{12,... | collective-permute-start | bytes 1474568 | tf_op jit(solution)/shard_map/ppermute | solution.py:32
  86.8 33.7 %collective-permute-start.16 = (bf16[3,640,384]{2,1,0:T(8,128)(2,1)S(1)}, bf16[3,640,384]{2,1,0:T(8,128)(2,1)S(1)}, u32[]{:S(2)}, u32[]{:S(2)}) collective-permute-start(bf16[3,640,384]{2,1,0:T(8,128)(2,1)S(1)} %pad_maximum_fusion.2), channel_id=1, source_target_pairs={{0,8},{8,0},{16,24},{24,16},{1,9},{9,1},{17,25},{25,17},{2,10},{10... | collective-permute-start | bytes 4423688 | tf_op jit(solution)/shard_map/ppermute | solution.py:40
  87.9 18.0 %collective-permute-start.13 = (bf16[192,1024]{1,0:T(8,128)(2,1)S(1)}, bf16[192,1024]{1,0:T(8,128)(2,1)S(1)}, u32[]{:S(2)}, u32[]{:S(2)}) collective-permute-start(bf16[192,1024]{1,0:T(8,128)(2,1)S(1)} %copy-done.81), channel_id=1, source_target_pairs={{0,2},{2,0},{4,6},{6,4},{1,3},{3,1},{5,7},{7,5},{8,10},{10,8},{12,... | collective-permute-start | bytes 1179656 | tf_op jit(solution)/shard_map/ppermute | solution.py:32
  88.5 17.4 %collective-permute-start.14 = (bf16[192,1024]{1,0:T(8,128)(2,1)S(1)}, bf16[192,1024]{1,0:T(8,128)(2,1)S(1)}, u32[]{:S(2)}, u32[]{:S(2)}) collective-permute-start(bf16[192,1024]{1,0:T(8,128)(2,1)S(1)} %copy-done.80), channel_id=1, source_target_pairs={{0,4},{2,6},{4,0},{6,2},{1,5},{3,7},{5,1},{7,3},{8,12},{10,14},{12... | collective-permute-start | bytes 1179656 | tf_op jit(solution)/shard_map/ppermute | solution.py:32
  89.5 18.8 %collective-permute-start.15 = (bf16[192,1024]{1,0:T(8,128)(2,1)S(1)}, bf16[192,1024]{1,0:T(8,128)(2,1)S(1)}, u32[]{:S(2)}, u32[]{:S(2)}) collective-permute-start(bf16[192,1024]{1,0:T(8,128)(2,1)S(1)} %copy-done.79), channel_id=1, source_target_pairs={{0,6},{2,4},{4,2},{6,0},{1,7},{3,5},{5,3},{7,1},{8,14},{10,12},{12... | collective-permute-start | bytes 1179656 | tf_op jit(solution)/shard_map/ppermute | solution.py:32
  122.7 37.6 %collective-permute-start.20 = (bf16[3,192,1024]{2,1,0:T(8,128)(2,1)}, bf16[3,192,1024]{2,1,0:T(8,128)(2,1)}, u32[]{:S(2)}, u32[]{:S(2)}) collective-permute-start(bf16[3,192,1024]{2,1,0:T(8,128)(2,1)} %pad_maximum_fusion.3), channel_id=1, source_target_pairs={{0,8},{8,0},{16,24},{24,16},{1,9},{9,1},{17,25},{25,17},{2,10},{10... | collective-permute-start | bytes 3538952 | tf_op jit(solution)/shard_map/ppermute | solution.py:40
  123.8 20.4 %collective-permute-start.18 = (bf16[1024,384]{1,0:T(8,128)(2,1)S(1)}, bf16[1024,384]{1,0:T(8,128)(2,1)S(1)}, u32[]{:S(2)}, u32[]{:S(2)}) collective-permute-start(bf16[1024,384]{1,0:T(8,128)(2,1)S(1)} %copy-done.22), channel_id=1, source_target_pairs={{0,2},{2,0},{4,6},{6,4},{1,3},{3,1},{5,7},{7,5},{8,10},{10,8},{12,... | collective-permute-start | bytes 2359304 | tf_op jit(solution)/shard_map/ppermute | solution.py:32
  124.3 20.5 %collective-permute-start.19 = (bf16[1024,384]{1,0:T(8,128)(2,1)S(1)}, bf16[1024,384]{1,0:T(8,128)(2,1)S(1)}, u32[]{:S(2)}, u32[]{:S(2)}) collective-permute-start(bf16[1024,384]{1,0:T(8,128)(2,1)S(1)} %copy-done.22), channel_id=1, source_target_pairs={{0,4},{2,6},{4,0},{6,2},{1,5},{3,7},{5,1},{7,3},{8,12},{10,14},{12... | collective-permute-start | bytes 2359304 | tf_op jit(solution)/shard_map/ppermute | solution.py:32
  125.3 34.8 %collective-permute-start.21 = (bf16[1024,384]{1,0:T(8,128)(2,1)S(1)}, bf16[1024,384]{1,0:T(8,128)(2,1)}, u32[]{:S(2)}, u32[]{:S(2)}) collective-permute-start(bf16[1024,384]{1,0:T(8,128)(2,1)S(1)} %pad_maximum_fusion.7.refs_0_), channel_id=1, source_target_pairs={{0,2},{2,0},{4,6},{6,4},{1,3},{3,1},{5,7},{7,5},{8,10},{10,8},{12,... | collective-permute-start | bytes 2359304 | tf_op jit(solution)/shard_map/ppermute | solution.py:32
  126.8 33.5 %collective-permute-start.22 = (bf16[1024,384]{1,0:T(8,128)(2,1)S(1)}, bf16[1024,384]{1,0:T(8,128)(2,1)}, u32[]{:S(2)}, u32[]{:S(2)}) collective-permute-start(bf16[1024,384]{1,0:T(8,128)(2,1)S(1)} %pad_maximum_fusion.7.refs_0_), channel_id=1, source_target_pairs={{0,4},{2,6},{4,0},{6,2},{1,5},{3,7},{5,1},{7,3},{8,12},{10,14},{12... | collective-permute-start | bytes 2359304 | tf_op jit(solution)/shard_map/ppermute | solution.py:32
  160.3 11.0 %collective-permute-start.25 = (bf16[4,1280,384]{2,1,0:T(8,128)(2,1)S(1)}, bf16[4,1280,384]{2,1,0:T(8,128)(2,1)S(1)}, u32[]{:S(2)}, u32[]{:S(2)}) collective-permute-start(bf16[4,1280,384]{2,1,0:T(8,128)(2,1)S(1)} %constant_dynamic-update-slice_fusion.2), channel_id=1, source_target_pairs={{0,1},{1,0},{2,3},{3,2},{4,5},{5,4},{6,7},{7,6},{8,9},{9,8},{10,11... | collective-permute-start | bytes 11796488 | tf_op jit(solution)/shard_map/ppermute | solution.py:36
  162.5 19.6 %collective-permute-start.23 = (bf16[512,384]{1,0:T(8,128)(2,1)S(1)}, bf16[512,384]{1,0:T(8,128)(2,1)S(1)}, u32[]{:S(2)}, u32[]{:S(2)}) collective-permute-start(bf16[512,384]{1,0:T(8,128)(2,1)S(1)} %slice.182), channel_id=1, source_target_pairs={{0,4},{2,6},{4,0},{6,2},{1,5},{3,7},{5,1},{7,3},{8,12},{10,14},{12... | collective-permute-start | bytes 1179656 | tf_op jit(solution)/shard_map/ppermute | solution.py:32
  163.6 18.6 %collective-permute-start.24 = (bf16[512,384]{1,0:T(8,128)(2,1)S(1)}, bf16[512,384]{1,0:T(8,128)(2,1)S(1)}, u32[]{:S(2)}, u32[]{:S(2)}) collective-permute-start(bf16[512,384]{1,0:T(8,128)(2,1)S(1)} %slice.183), channel_id=1, source_target_pairs={{0,2},{2,0},{4,6},{6,4},{1,3},{3,1},{5,7},{7,5},{8,10},{10,8},{12,... | collective-permute-start | bytes 1179656 | tf_op jit(solution)/shard_map/ppermute | solution.py:32
  165.1 17.5 %collective-permute-start.26 = (bf16[512,384]{1,0:T(8,128)(2,1)S(1)}, bf16[512,384]{1,0:T(8,128)(2,1)S(1)}, u32[]{:S(2)}, u32[]{:S(2)}) collective-permute-start(bf16[512,384]{1,0:T(8,128)(2,1)S(1)} %slice.180), channel_id=1, source_target_pairs={{0,4},{2,6},{4,0},{6,2},{1,5},{3,7},{5,1},{7,3},{8,12},{10,14},{12... | collective-permute-start | bytes 1179656 | tf_op jit(solution)/shard_map/ppermute | solution.py:32
  166.1 17.1 %collective-permute-start.27 = (bf16[512,384]{1,0:T(8,128)(2,1)S(1)}, bf16[512,384]{1,0:T(8,128)(2,1)S(1)}, u32[]{:S(2)}, u32[]{:S(2)}) collective-permute-start(bf16[512,384]{1,0:T(8,128)(2,1)S(1)} %slice.181), channel_id=1, source_target_pairs={{0,2},{2,0},{4,6},{6,4},{1,3},{3,1},{5,7},{7,5},{8,10},{10,8},{12,... | collective-permute-start | bytes 1179656 | tf_op jit(solution)/shard_map/ppermute | solution.py:32
  183.3 13.2 %collective-permute-start.28 = (bf16[1536,1024]{1,0:T(8,128)(2,1)S(1)}, bf16[1536,1024]{1,0:T(8,128)(2,1)}, u32[]{:S(2)}, u32[]{:S(2)}) collective-permute-start(bf16[1536,1024]{1,0:T(8,128)(2,1)S(1)} %bitcast.86), channel_id=1, source_target_pairs={{0,1},{1,0},{2,3},{3,2},{4,5},{5,4},{6,7},{7,6},{8,9},{9,8},{10,11... | collective-permute-start | bytes 9437192 | tf_op jit(solution)/shard_map/ppermute | solution.py:36
  229.7 20.3 %collective-permute-start.29 = (bf16[512,768]{1,0:T(8,128)(2,1)S(1)}, bf16[512,768]{1,0:T(8,128)(2,1)S(1)}, u32[]{:S(2)}, u32[]{:S(2)}) collective-permute-start(bf16[512,768]{1,0:T(8,128)(2,1)S(1)} %get-tuple-element.826), channel_id=1, source_target_pairs={{0,2},{2,0},{4,6},{6,4},{1,3},{3,1},{5,7},{7,5},{8,10},{10,8},{12,... | collective-permute-start | bytes 2359304 | tf_op jit(solution)/shard_map/ppermute | solution.py:32
  231.3 18.8 %collective-permute-start.30 = (bf16[512,768]{1,0:T(8,128)(2,1)S(1)}, bf16[512,768]{1,0:T(8,128)(2,1)S(1)}, u32[]{:S(2)}, u32[]{:S(2)}) collective-permute-start(bf16[512,768]{1,0:T(8,128)(2,1)S(1)} %get-tuple-element.828), channel_id=1, source_target_pairs={{0,4},{2,6},{4,0},{6,2},{1,5},{3,7},{5,1},{7,3},{8,12},{10,14},{12... | collective-permute-start | bytes 2359304 | tf_op jit(solution)/shard_map/ppermute | solution.py:32
  232.3 17.7 %collective-permute-start.31 = (f32[8,128]{1,0:T(8,128)S(1)}, f32[8,128]{1,0:T(8,128)S(1)}, u32[]{:S(2)}, u32[]{:S(2)}) collective-permute-start(f32[8,128]{1,0:T(8,128)S(1)} %bitcast.104), channel_id=1, source_target_pairs={{0,2},{2,0},{4,6},{6,4},{1,3},{3,1},{5,7},{7,5},{8,10},{10,8},{12,... | collective-permute-start | bytes 12296 | tf_op jit(solution)/shard_map/ppermute | solution.py:32
  250.3 12.4 %collective-permute-start.32 = (bf16[4,4,96,1536]{3,2,1,0:T(8,128)(2,1)}, bf16[4,4,96,1536]{3,2,1,0:T(8,128)(2,1)S(1)}, u32[]{:S(2)}, u32[]{:S(2)}) collective-permute-start(bf16[4,4,96,1536]{3,2,1,0:T(8,128)(2,1)} %shard_map.211), channel_id=1, source_target_pairs={{0,1},{1,0},{2,3},{3,2},{4,5},{5,4},{6,7},{7,6},{8,9},{9,8},{10,11... | collective-permute-start | bytes 14155784 | tf_op jit(solution)/shard_map/ppermute | solution.py:36
  250.4 11.6 %collective-permute-start.33 = (bf16[512,384]{1,0:T(8,128)(2,1)S(1)}, bf16[512,384]{1,0:T(8,128)(2,1)S(1)}, u32[]{:S(2)}, u32[]{:S(2)}) collective-permute-start(bf16[512,384]{1,0:T(8,128)(2,1)S(1)} %add_convert_fusion.12), channel_id=1, source_target_pairs={{0,4},{2,6},{4,0},{6,2},{1,5},{3,7},{5,1},{7,3},{8,12},{10,14},{12... | collective-permute-start | bytes 1179656 | tf_op jit(solution)/shard_map/ppermute | solution.py:32
  251.5 11.2 %collective-permute-start.34 = (bf16[512,384]{1,0:T(8,128)(2,1)S(1)}, bf16[512,384]{1,0:T(8,128)(2,1)S(1)}, u32[]{:S(2)}, u32[]{:S(2)}) collective-permute-start(bf16[512,384]{1,0:T(8,128)(2,1)S(1)} %add_convert_fusion.11), channel_id=1, source_target_pairs={{0,2},{2,0},{4,6},{6,4},{1,3},{3,1},{5,7},{7,5},{8,10},{10,8},{12,... | collective-permute-start | bytes 1179656 | tf_op jit(solution)/shard_map/ppermute | solution.py:32
  252.9 9.1 %collective-permute-start.35 = (f32[8,128]{1,0:T(8,128)S(1)}, f32[8,128]{1,0:T(8,128)S(1)}, u32[]{:S(2)}, u32[]{:S(2)}) collective-permute-start(f32[8,128]{1,0:T(8,128)S(1)} %add.382), channel_id=1, source_target_pairs={{0,4},{2,6},{4,0},{6,2},{1,5},{3,7},{5,1},{7,3},{8,12},{10,14},{12... | collective-permute-start | bytes 12296 | tf_op jit(solution)/shard_map/ppermute | solution.py:32
  269.5 260.8 %all-gather.3.cloned.1.call-start = ((), (), s32[]{:S(2)}) async-start(), calls=%async_computation.2 | async-start | bytes 5898240 | tf_op jit(solution)/shard_map/all_gather | solution.py:1047
  274.4 18.8 %collective-permute-start.36 = (bf16[1024,384]{1,0:T(8,128)(2,1)S(1)}, bf16[1024,384]{1,0:T(8,128)(2,1)S(1)}, u32[]{:S(2)}, u32[]{:S(2)}) collective-permute-start(bf16[1024,384]{1,0:T(8,128)(2,1)S(1)} %get-tuple-element.999.x0.branch), channel_id=1, source_target_pairs={{0,2},{2,0},{4,6},{6,4},{1,3},{3,1},{5,7},{7,5},{8,10},{10,8},{12,... | collective-permute-start | bytes 2359304 | tf_op jit(solution)/shard_map/ppermute | solution.py:32
  275.8 18.5 %collective-permute-start.37 = (bf16[1024,384]{1,0:T(8,128)(2,1)S(1)}, bf16[1024,384]{1,0:T(8,128)(2,1)S(1)}, u32[]{:S(2)}, u32[]{:S(2)}) collective-permute-start(bf16[1024,384]{1,0:T(8,128)(2,1)S(1)} %get-tuple-element.999.x0.branch), channel_id=1, source_target_pairs={{0,4},{2,6},{4,0},{6,2},{1,5},{3,7},{5,1},{7,3},{8,12},{10,14},{12... | collective-permute-start | bytes 2359304 | tf_op jit(solution)/shard_map/ppermute | solution.py:32
  294.4 9.3 %collective-permute-start.38 = (bf16[512,384]{1,0:T(8,128)(2,1)S(1)}, bf16[512,384]{1,0:T(8,128)(2,1)S(1)}, u32[]{:S(2)}, u32[]{:S(2)}) collective-permute-start(bf16[512,384]{1,0:T(8,128)(2,1)S(1)} %slice.196), channel_id=1, source_target_pairs={{0,4},{2,6},{4,0},{6,2},{1,5},{3,7},{5,1},{7,3},{8,12},{10,14},{12... | collective-permute-start | bytes 1179656 | tf_op jit(solution)/shard_map/ppermute | solution.py:32
  295.5 9.0 %collective-permute-start.39 = (bf16[512,384]{1,0:T(8,128)(2,1)S(1)}, bf16[512,384]{1,0:T(8,128)(2,1)S(1)}, u32[]{:S(2)}, u32[]{:S(2)}) collective-permute-start(bf16[512,384]{1,0:T(8,128)(2,1)S(1)} %slice.197), channel_id=1, source_target_pairs={{0,2},{2,0},{4,6},{6,4},{1,3},{3,1},{5,7},{7,5},{8,10},{10,8},{12,... | collective-permute-start | bytes 1179656 | tf_op jit(solution)/shard_map/ppermute | solution.py:32
  308.9 20.0 %collective-permute-start.41 = (bf16[512,768]{1,0:T(8,128)(2,1)S(1)}, bf16[512,768]{1,0:T(8,128)(2,1)S(1)}, u32[]{:S(2)}, u32[]{:S(2)}) collective-permute-start(bf16[512,768]{1,0:T(8,128)(2,1)S(1)} %get-tuple-element.979), channel_id=1, source_target_pairs={{0,2},{2,0},{4,6},{6,4},{1,3},{3,1},{5,7},{7,5},{8,10},{10,8},{12,... | collective-permute-start | bytes 2359304 | tf_op jit(solution)/shard_map/ppermute | solution.py:32
  309.5 19.4 %collective-permute-start.42 = (bf16[512,768]{1,0:T(8,128)(2,1)S(1)}, bf16[512,768]{1,0:T(8,128)(2,1)S(1)}, u32[]{:S(2)}, u32[]{:S(2)}) collective-permute-start(bf16[512,768]{1,0:T(8,128)(2,1)S(1)} %get-tuple-element.981), channel_id=1, source_target_pairs={{0,4},{2,6},{4,0},{6,2},{1,5},{3,7},{5,1},{7,3},{8,12},{10,14},{12... | collective-permute-start | bytes 2359304 | tf_op jit(solution)/shard_map/ppermute | solution.py:32
  329.2 8.9 %collective-permute-start.43 = (bf16[1024,512]{1,0:T(8,128)(2,1)S(1)}, bf16[1024,512]{1,0:T(8,128)(2,1)S(1)}, u32[]{:S(2)}, u32[]{:S(2)}) collective-permute-start(bf16[1024,512]{1,0:T(8,128)(2,1)S(1)} %get-tuple-element.997), channel_id=1, source_target_pairs={{0,1},{1,0},{2,3},{3,2},{4,5},{5,4},{6,7},{7,6},{8,9},{9,8},{10,11... | collective-permute-start | bytes 3145736 | tf_op jit(solution)/shard_map/ppermute | solution.py:36
  329.2 16.6 %collective-permute-start.44 = (bf16[512,384]{1,0:T(8,128)(2,1)S(1)}, bf16[512,384]{1,0:T(8,128)(2,1)S(1)}, u32[]{:S(2)}, u32[]{:S(2)}) collective-permute-start(bf16[512,384]{1,0:T(8,128)(2,1)S(1)} %add_convert_fusion.10), channel_id=1, source_target_pairs={{0,4},{2,6},{4,0},{6,2},{1,5},{3,7},{5,1},{7,3},{8,12},{10,14},{12... | collective-permute-start | bytes 1179656 | tf_op jit(solution)/shard_map/ppermute | solution.py:32
  330.3 15.6 %collective-permute-start.45 = (bf16[512,384]{1,0:T(8,128)(2,1)S(1)}, bf16[512,384]{1,0:T(8,128)(2,1)S(1)}, u32[]{:S(2)}, u32[]{:S(2)}) collective-permute-start(bf16[512,384]{1,0:T(8,128)(2,1)S(1)} %add_convert_fusion.9), channel_id=1, source_target_pairs={{0,2},{2,0},{4,6},{6,4},{1,3},{3,1},{5,7},{7,5},{8,10},{10,8},{12,... | collective-permute-start | bytes 1179656 | tf_op jit(solution)/shard_map/ppermute | solution.py:32
  360.0 21.2 %collective-permute-start.47 = (bf16[96,1536]{1,0:T(8,128)(2,1)}, bf16[96,1536]{1,0:T(8,128)(2,1)}, u32[]{:S(2)}, u32[]{:S(2)}) collective-permute-start(bf16[96,1536]{1,0:T(8,128)(2,1)} %get-tuple-element.1185), channel_id=1, source_target_pairs={{0,2},{2,0},{4,6},{6,4},{1,3},{3,1},{5,7},{7,5},{8,10},{10,8},{12,... | collective-permute-start | bytes 884744 | tf_op jit(solution)/shard_map/ppermute | solution.py:32
  361.5 19.7 %collective-permute-start.48 = (bf16[96,1536]{1,0:T(8,128)(2,1)}, bf16[96,1536]{1,0:T(8,128)(2,1)}, u32[]{:S(2)}, u32[]{:S(2)}) collective-permute-start(bf16[96,1536]{1,0:T(8,128)(2,1)} %get-tuple-element.1184), channel_id=1, source_target_pairs={{0,4},{2,6},{4,0},{6,2},{1,5},{3,7},{5,1},{7,3},{8,12},{10,14},{12... | collective-permute-start | bytes 884744 | tf_op jit(solution)/shard_map/ppermute | solution.py:32
  363.0 18.3 %collective-permute-start.49 = (bf16[96,1536]{1,0:T(8,128)(2,1)}, bf16[96,1536]{1,0:T(8,128)(2,1)}, u32[]{:S(2)}, u32[]{:S(2)}) collective-permute-start(bf16[96,1536]{1,0:T(8,128)(2,1)} %get-tuple-element.1183), channel_id=1, source_target_pairs={{0,6},{2,4},{4,2},{6,0},{1,7},{3,5},{5,3},{7,1},{8,14},{10,12},{12... | collective-permute-start | bytes 884744 | tf_op jit(solution)/shard_map/ppermute | solution.py:32
  363.5 20.2 %collective-permute-start.50 = (bf16[4,144,384]{2,1,0:T(8,128)(2,1)}, bf16[4,144,384]{2,1,0:T(8,128)(2,1)}, u32[]{:S(2)}, u32[]{:S(2)}) collective-permute-start(bf16[4,144,384]{2,1,0:T(8,128)(2,1)} %pad_maximum_fusion.9), channel_id=1, source_target_pairs={{0,8},{1,9},{2,10},{3,11},{4,12},{5,13},{6,14},{7,15}} | collective-permute-start | bytes 1327112 | tf_op jit(solution)/shard_map/ppermute | solution.py:160
  367.7 16.0 %collective-permute-start.51 = (bf16[4,144,384]{2,1,0:T(8,128)(2,1)}, bf16[4,144,384]{2,1,0:T(8,128)(2,1)}, u32[]{:S(2)}, u32[]{:S(2)}) collective-permute-start(bf16[4,144,384]{2,1,0:T(8,128)(2,1)} %pad_maximum_fusion.10), channel_id=1, source_target_pairs={{24,16},{25,17},{26,18},{27,19},{28,20},{29,21},{30,22},{31,23}} | collective-permute-start | bytes 1327112 | tf_op jit(solution)/shard_map/ppermute | solution.py:160
  383.7 23.8 %collective-permute-start.52 = (bf16[512,768]{1,0:T(8,128)(2,1)S(1)}, bf16[512,768]{1,0:T(8,128)(2,1)}, u32[]{:S(2)}, u32[]{:S(2)}) collective-permute-start(bf16[512,768]{1,0:T(8,128)(2,1)S(1)} %copy-done.56), channel_id=1, source_target_pairs={{0,2},{2,0},{4,6},{6,4},{1,3},{3,1},{5,7},{7,5},{8,10},{10,8},{12,... | collective-permute-start | bytes 2359304 | tf_op jit(solution)/shard_map/ppermute | solution.py:32
  385.3 22.3 %collective-permute-start.53 = (bf16[512,768]{1,0:T(8,128)(2,1)S(1)}, bf16[512,768]{1,0:T(8,128)(2,1)}, u32[]{:S(2)}, u32[]{:S(2)}) collective-permute-start(bf16[512,768]{1,0:T(8,128)(2,1)S(1)} %copy-done.54), channel_id=1, source_target_pairs={{0,4},{2,6},{4,0},{6,2},{1,5},{3,7},{5,1},{7,3},{8,12},{10,14},{12... | collective-permute-start | bytes 2359304 | tf_op jit(solution)/shard_map/ppermute | solution.py:32
  390.7 16.9 %collective-permute-start.54 = (bf16[4,144,384]{2,1,0:T(8,128)(2,1)}, bf16[4,144,384]{2,1,0:T(8,128)(2,1)}, u32[]{:S(2)}, u32[]{:S(2)}) collective-permute-start(bf16[4,144,384]{2,1,0:T(8,128)(2,1)} %add_convert_fusion.6), channel_id=1, source_target_pairs={{0,8},{8,16},{1,9},{9,17},{2,10},{10,18},{3,11},{11,19},{4,12},{12... | collective-permute-start | bytes 1327112 | tf_op jit(solution)/shard_map/ppermute | solution.py:160
  392.7 14.8 %collective-permute-start.55 = (bf16[4,144,384]{2,1,0:T(8,128)(2,1)}, bf16[4,144,384]{2,1,0:T(8,128)(2,1)}, u32[]{:S(2)}, u32[]{:S(2)}) collective-permute-start(bf16[4,144,384]{2,1,0:T(8,128)(2,1)} %add_convert_fusion.5), channel_id=1, source_target_pairs={{24,16},{16,8},{25,17},{17,9},{26,18},{18,10},{27,19},{19,11},{28,... | collective-permute-start | bytes 1327112 | tf_op jit(solution)/shard_map/ppermute | solution.py:160
  414.5 34.2 %collective-permute-start.59 = (bf16[4,144,384]{2,1,0:T(8,128)(2,1)}, bf16[4,144,384]{2,1,0:T(8,128)(2,1)S(1)}, u32[]{:S(2)}, u32[]{:S(2)}) collective-permute-start(bf16[4,144,384]{2,1,0:T(8,128)(2,1)} %add_convert_fusion.4), channel_id=1, source_target_pairs={{0,8},{8,16},{16,24},{1,9},{9,17},{17,25},{2,10},{10,18},{18,26},{... | collective-permute-start | bytes 1327112 | tf_op jit(solution)/shard_map/ppermute | solution.py:160
  433.2 30.7 %collective-permute-start.60 = (bf16[4,144,384]{2,1,0:T(8,128)(2,1)S(1)}, bf16[4,144,384]{2,1,0:T(8,128)(2,1)S(1)}, u32[]{:S(2)}, u32[]{:S(2)}) collective-permute-start(bf16[4,144,384]{2,1,0:T(8,128)(2,1)S(1)} %add_convert_fusion.3), channel_id=1, source_target_pairs={{24,16},{16,8},{8,0},{25,17},{17,9},{9,1},{26,18},{18,10},{10,2},{... | collective-permute-start | bytes 1327112 | tf_op jit(solution)/shard_map/ppermute | solution.py:160
  434.5 8.2 %collective-permute-start.57 = (bf16[512,384]{1,0:T(8,128)(2,1)}, bf16[512,384]{1,0:T(8,128)(2,1)}, u32[]{:S(2)}, u32[]{:S(2)}) collective-permute-start(bf16[512,384]{1,0:T(8,128)(2,1)} %add_convert_fusion.8), channel_id=1, source_target_pairs={{0,4},{2,6},{4,0},{6,2},{1,5},{3,7},{5,1},{7,3},{8,12},{10,14},{12... | collective-permute-start | bytes 1179656 | tf_op jit(solution)/shard_map/ppermute | solution.py:32
  434.6 8.2 %collective-permute-start.58 = (bf16[512,384]{1,0:T(8,128)(2,1)}, bf16[512,384]{1,0:T(8,128)(2,1)}, u32[]{:S(2)}, u32[]{:S(2)}) collective-permute-start(bf16[512,384]{1,0:T(8,128)(2,1)} %add_convert_fusion.7), channel_id=1, source_target_pairs={{0,2},{2,0},{4,6},{6,4},{1,3},{3,1},{5,7},{7,5},{8,10},{10,8},{12,... | collective-permute-start | bytes 1179656 | tf_op jit(solution)/shard_map/ppermute | solution.py:32
  434.6 8.0 %collective-permute-start.61 = (f32[8,128]{1,0:T(8,128)S(1)}, f32[8,128]{1,0:T(8,128)S(1)}, u32[]{:S(2)}, u32[]{:S(2)}) collective-permute-start(f32[8,128]{1,0:T(8,128)S(1)} %add.416), channel_id=1, source_target_pairs={{0,4},{2,6},{4,0},{6,2},{1,5},{3,7},{5,1},{7,3},{8,12},{10,14},{12... | collective-permute-start | bytes 12296 | tf_op jit(solution)/shard_map/ppermute | solution.py:32
  470.1 18.8 %collective-permute-start.66 = (bf16[4,144,384]{2,1,0:T(8,128)(2,1)S(1)}, bf16[4,144,384]{2,1,0:T(8,128)(2,1)}, u32[]{:S(2)}, u32[]{:S(2)}) collective-permute-start(bf16[4,144,384]{2,1,0:T(8,128)(2,1)S(1)} %pad_maximum_fusion.11), channel_id=1, source_target_pairs={{0,8},{8,16},{16,24},{1,9},{9,17},{17,25},{2,10},{10,18},{18,26},{... | collective-permute-start | bytes 1327112 | tf_op jit(solution)/shard_map/ppermute | solution.py:179
  474.5 14.5 %collective-permute-start.67 = (bf16[4,144,384]{2,1,0:T(8,128)(2,1)S(1)}, bf16[4,144,384]{2,1,0:T(8,128)(2,1)}, u32[]{:S(2)}, u32[]{:S(2)}) collective-permute-start(bf16[4,144,384]{2,1,0:T(8,128)(2,1)S(1)} %pad_maximum_fusion.11), channel_id=1, source_target_pairs={{24,16},{16,8},{8,0},{25,17},{17,9},{9,1},{26,18},{18,10},{10,2},{... | collective-permute-start | bytes 1327112 | tf_op jit(solution)/shard_map/ppermute | solution.py:180
  489.0 27.3 %collective-permute-start.71 = (bf16[4,144,384]{2,1,0:T(8,128)(2,1)}, bf16[4,144,384]{2,1,0:T(8,128)(2,1)S(1)}, u32[]{:S(2)}, u32[]{:S(2)}) collective-permute-start(bf16[4,144,384]{2,1,0:T(8,128)(2,1)} %collective-permute-done.66), channel_id=1, source_target_pairs={{8,16},{16,24},{9,17},{17,25},{10,18},{18,26},{11,19},{19,27},{12,... | collective-permute-start | bytes 1327112 | tf_op jit(solution)/shard_map/ppermute | solution.py:179
  489.7 26.7 %collective-permute-start.72 = (bf16[4,144,384]{2,1,0:T(8,128)(2,1)}, bf16[4,144,384]{2,1,0:T(8,128)(2,1)S(1)}, u32[]{:S(2)}, u32[]{:S(2)}) collective-permute-start(bf16[4,144,384]{2,1,0:T(8,128)(2,1)} %collective-permute-done.67), channel_id=1, source_target_pairs={{16,8},{8,0},{17,9},{9,1},{18,10},{10,2},{19,11},{11,3},{20,12},{1... | collective-permute-start | bytes 1327112 | tf_op jit(solution)/shard_map/ppermute | solution.py:180
  492.4 21.1 %collective-permute-start.68 = (f32[2,384]{1,0:T(2,128)S(1)}, f32[2,384]{1,0:T(2,128)S(1)}, u32[]{:S(2)}, u32[]{:S(2)}) collective-permute-start(f32[2,384]{1,0:T(2,128)S(1)} %fusion.23), channel_id=1, source_target_pairs={{0,8},{8,16},{16,24},{24,0},{1,9},{9,17},{17,25},{25,1},{2,10},{10... | collective-permute-start | bytes 9224 | tf_op jit(solution)/shard_map/ppermute | solution.py:132
  517.0 10.2 %collective-permute-start.74 = (bf16[4,144,384]{2,1,0:T(8,128)(2,1)S(1)}, bf16[4,144,384]{2,1,0:T(8,128)(2,1)S(1)}, u32[]{:S(2)}, u32[]{:S(2)}) collective-permute-start(bf16[4,144,384]{2,1,0:T(8,128)(2,1)S(1)} %collective-permute-done.72), channel_id=1, source_target_pairs={{8,0},{9,1},{10,2},{11,3},{12,4},{13,5},{14,6},{15,7}} | collective-permute-start | bytes 1327112 | tf_op jit(solution)/shard_map/ppermute | solution.py:180
  (102 other events, 883.4 us)
Sparse Core Ops, SparseCore 0:
  269.6 85.4 reduce-scatter.1
  386.9 114.1 all-gather.2

commit v4 on v3

--- a/solution.py
+++ b/solution.py
@@ -257,6 +257,20 @@
     )(*pieces)
 
 
+def split_low(value):
+    high = lax.reduce_precision(value, 8, 7)
+    rest = value - high
+    middle = lax.reduce_precision(rest, 8, 7)
+    terms = [high, middle, rest - middle]
+    spare = jnp.zeros((16 - 3 * value.shape[0], value.shape[1]), F32)
+    return jnp.concatenate(terms + [spare], axis=0).astype(LOW)
+
+
+def unsplit(rows, count):
+    terms = [rows[i * count : (i + 1) * count].astype(F32) for i in range(3)]
+    return terms[0] + terms[1] + terms[2]
+
+
 def order_kernel(row_ref, own, oth, full, mine):
     row = row_ref[0]
     features, chunk = own.shape[2], own.shape[1] // 4
@@ -385,6 +399,23 @@
     return (key >= start) & (key <= query)
 
 
+def over_keys(info, block, step):
+    count = (info.shape[0] - 1) // 2
+    first, whole_from = info[1 + block], jnp.minimum(info[1 + count + block], block)
+
+    def masked(number, carry):
+        step(number, True)
+        return carry
+
+    def plain(number, carry):
+        step(number, False)
+        return carry
+
+    lax.fori_loop(first, whole_from, masked, 0)
+    lax.fori_loop(whole_from, block, plain, 0)
+    step(block, True)
+
+
 def attend_kernel(info, own, oth, start_ref, keep, send, out, lse, full, values, top, total, acc):
     block = pl.program_id(0)
     core = info[0]
@@ -403,10 +434,11 @@
     total[...] = jnp.zeros(total.shape, F32)
     acc[...] = jnp.zeros(acc.shape, F32)
 
-    def step(number, _):
+    def step(number, masked):
         keys = pl.ds(pl.multiple_of(number * TILE, TILE), TILE)
         scores = dot(full[keys, 2 * LANES : 3 * LANES], query, NT) * (FACTOR * LOG2E)
-        scores = jnp.where(allowed_keys(number, start, place), scores, -1e30)
+        if masked:
+            scores = jnp.where(allowed_keys(number, start, place), scores, -1e30)
         before = top[...]
         now = jnp.maximum(before, jnp.max(scores, axis=0, keepdims=True))
         weight = jnp.exp2(scores - now)
@@ -414,9 +446,8 @@
         top[...] = now
         total[...] = total[...] * scale + jnp.sum(weight, axis=0, keepdims=True)
         acc[...] = acc[...] * scale + dot(values[:, keys], weight.astype(LOW))
-        return 0
-
-    lax.fori_loop(info[1 + block], block + 1, step, 0)
+
+    over_keys(info, block, step)
     lse[...] = top[...] + jnp.log2(total[...])
     result = (acc[...] / total[...]).T.astype(LOW)
     out[:, :LANES] = result[:TILE]
@@ -497,19 +528,19 @@
     delta = jnp.sum((grad.astype(F32) * reply.astype(F32)).T, axis=0, keepdims=True)
     d_query[...] = jnp.zeros(d_query.shape, F32)
 
-    def step(number, _):
+    def step(number, masked):
         keys = pl.ds(pl.multiple_of(number * TILE, TILE), TILE)
         scores = dot(full[keys, 2 * LANES : 3 * LANES], query, NT) * (FACTOR * LOG2E)
-        scores = jnp.where(allowed_keys(number, start, place), scores, -1e30)
+        if masked:
+            scores = jnp.where(allowed_keys(number, start, place), scores, -1e30)
         weight = jnp.exp2(scores - level)
         pressure = dot(full[keys, 3 * LANES :], grad, NT)
         slope = (weight * (pressure - delta) * FACTOR).astype(LOW)
         d_values[keys, :] += dot(weight.astype(LOW), grad)
         d_keys[keys, :] += dot(slope, query)
         d_query[...] += dot(keys_t[:, keys], slope)
-        return 0
-
-    lax.fori_loop(info[1 + block], block + 1, step, 0)
+
+    over_keys(info, block, step)
     turned = d_query[...].T
     for h in range(2):
         part = turned[h * TILE : (h + 1) * TILE]
@@ -664,15 +695,14 @@
     total = 0.0
     left, right = a_own[...], a_oth[...]
     found = []
-    for k in range(4):
-        columns = slice(k * width, (k + 1) * width)
-        if blocked:
-            value = dot(left, w_own[k]) + dot(right, w_oth[k])
-        else:
-            value = dot(left, w_own[columns, :], NT) + dot(right, w_oth[columns, :], NT)
-        if len(rest) == 7:
-            total = total + jnp.sum(value * against[:, columns].astype(F32), axis=1, keepdims=True)
-        found.append(value.astype(LOW))
+    if blocked:
+        for k in range(4):
+            found.append((dot(left, w_own[k]) + dot(right, w_oth[k])).astype(LOW))
+    else:
+        value = dot(left, w_own[...], NT) + dot(right, w_oth[...], NT)
+        total = jnp.sum(value * against[...].astype(F32), axis=1, keepdims=True)
+        low = value.astype(LOW)
+        found = [low[:, k * width : (k + 1) * width] for k in range(4)]
     own[...] = found[0]
     if len(rest) == 7:
         sums[...] = jnp.broadcast_to(total, sums.shape)
@@ -743,31 +773,28 @@
     )(second, cot, back, hidden)
 
 
-def mix_grads_kernel(which, first, heads, back, branch, spread, out, flat):
+def mix_grads_kernel(first, back, spread, out, flat):
     @pl.when(pl.program_id(0) == 0)
     def _():
         flat[...] = dot(back[...], spread[...], NT).astype(LOW)
 
-    width, chunk = first.shape[1], heads.shape[1] // 2
-    out[0, :width, :] = dot(first[...], flat[...], TN).astype(LOW)
-    out[0, width:, :] = dot(heads[:, which * chunk : (which + 1) * chunk], branch[...], TN).astype(LOW)
-
-
-def mix_grads(which, first, heads, back, branch, spread):
+    out[0] = dot(first[...], flat[...], TN).astype(LOW)
+
+
+def mix_grads(first, back, spread):
     tokens, model = first.shape
     width = model // 4
-    out = shape((4, width + width // 2, width))
-    block = pl.BlockSpec((tokens, width), lambda i: (0, i))
-    return call(
-        functools.partial(mix_grads_kernel, which),
+    out = shape((4, width, spread.shape[0]))
+    return call(
+        mix_grads_kernel,
         out,
-        [block, block, whole(back), whole(branch), whole(spread)],
+        [pl.BlockSpec((tokens, width), lambda i: (0, i)), whole(back), whole(spread)],
         pl.BlockSpec((1,) + out.shape[1:], lambda i: (i, 0, 0)),
         grid=(4,),
         scratch=(pltpu.VMEM((tokens, spread.shape[0]), LOW),),
-        flops=2 * tokens * model * out.shape[1],
-        moved=bytes_of(first, heads, back, branch, out),
-    )(first, heads, back, branch, spread)
+        flops=2 * tokens * model * out.shape[2],
+        moved=bytes_of(first, back, out),
+    )(first, back, spread)
 
 
 def feed_place_kernel(row_ref, piece, gain, gate, up, down):
@@ -918,7 +945,8 @@
     places, starts = sequence_starts(live.lengths, tokens)
     live.cos, live.sin = tables(places - starts)
     live.start = starts[None, :]
-    live.info = jnp.concatenate([core.reshape(1), starts[::TILE] // TILE]).astype(jnp.int32)
+    last_starts = (starts[TILE - 1 :: TILE] + TILE - 1) // TILE
+    live.info = jnp.concatenate([core.reshape(1), starts[::TILE] // TILE, last_starts]).astype(jnp.int32)
     spread = spread_matrix()
     del live.mixer_one, live.mixer_own, live.lengths
     live.sync()
@@ -1009,12 +1037,18 @@
     live.sync()
 
     live.branches = gather_two(live.branches, ready(*gather_halves(live.branches)))
+    live.o_all = dot(live.heads_all, live.branch, TN).astype(LOW).reshape(4, 2, chunk, width)
+    del live.heads_all, live.branch
     live.sync()
     live.grad, live.send = heads_grad_of(live.branches, live.out_mine)
     live.grad_got = other(live.send)
-    del live.branches, live.out_mine, live.send
-    live.sync()
-
+    live.o = added(live.o_all[:, 0], other(live.o_all[:, 1]))
+    del live.branches, live.out_mine, live.send, live.o_all
+    live.sync()
+
+    o_rows, mix_rows, share = (chunk,), (width,), width // blocks
+    parts = ready(*chain_parts(1, live.o, o_rows, blocks, []))
+    live.o_moving = chain_sum(1, parts, blocks, [])
     live.fo = scatter_one(live.fo)
     live.bk, live.send = attend_back(
         live.info, live.qkv, live.qkv_got, live.grad, live.grad_got,
@@ -1023,53 +1057,56 @@
     del live.qkv, live.qkv_got, live.grad, live.grad_got, live.attended, live.lse, live.start, live.info
     live.sync()
 
-    halves, send = ready(scatter_halves(live.fo), live.send)
+    halves, send, parts = ready(
+        scatter_halves(live.fo), live.send, chain_parts(2, live.o, o_rows, blocks, live.o_moving)
+    )
+    live.o_moving = chain_sum(2, parts, blocks, live.o_moving)
     live.fo = scatter_two(live.fo, halves)
     live.bg = other(send)
-    live.mix_oth = mix_grads(1, live.first, live.heads_all, live.bg, live.branch, spread)
-    live.mix_own = mix_grads(0, live.first, live.heads_all, live.bk, live.branch, spread)
+    live.mix_oth = mix_grads(live.first, live.bg, spread)
+    live.mix_own = mix_grads(live.first, live.bk, spread)
     del live.send
     live.sync()
+    live.feed_sum = spread_row(feed_sum)
     live.mix = added(live.mix_own, other(live.mix_oth))
-    live.feed_sum = feed_sum
+    live.moving = chain_sum(1, chain_parts(1, live.mix, mix_rows, blocks, []), blocks, [])
     del live.mix_own, live.mix_oth
     live.sync()
-    mix_rows, share = (width, chunk), width // blocks
-    parts, (bk, bg), shard = ready(
-        chain_parts(1, live.mix, mix_rows, blocks, []), (live.bk, live.bg), live.feed_sum
-    )
-    live.feed_sum = spread_row(shard)
-    live.moving = chain_sum(1, parts, blocks, [])
+    parts, more, (bk, bg) = ready(
+        chain_parts(2, live.mix, mix_rows, blocks, live.moving),
+        chain_parts(3, live.o, o_rows, blocks, live.o_moving),
+        (live.bk, live.bg),
+    )
+    live.moving = chain_sum(2, parts, blocks, live.moving)
+    live.o_moving = chain_sum(3, more, blocks, live.o_moving)
+    feeds = lax.all_gather(live.feed_sum, "dp", axis=0)
     live.fg, live.sums = partial_sums(False, bk, bg, live.w_own, live.w_oth, live.first)
     del live.bk, live.bg, live.w_own, live.w_oth, live.first
     live.sync()
 
-    feeds = lax.all_gather(live.feed_sum, "dp", axis=0)
-    parts = ready(*chain_parts(2, live.mix, mix_rows, blocks, live.moving))
-    live.moving = chain_sum(2, parts, blocks, live.moving)
+    live.o_moving = chain_sums(4, live.o, o_rows, blocks, live.o_moving)
+    live.o = chain_summed(live.o, o_rows, blocks, live.o_moving)
+    del live.o_moving
+    parts = ready(*chain_parts(3, live.mix, mix_rows, blocks, live.moving))
+    live.moving = chain_sum(3, parts, blocks, live.moving)
     live.fg = scatter_one(live.fg)
     live.sums = (live.sums, swap(live.sums, 1))
     layer_output = (live.middle + scattered(live.fo)).astype(LOW)
     del live.fo, live.middle, live.feed_sum
     live.sync()
 
-    halves, sums, parts = ready(
+    live.moving = chain_sums(4, live.mix, mix_rows, blocks, live.moving)
+    halves, sums, shard = ready(
         scatter_halves(live.fg),
         live.sums[0] + live.sums[1],
-        chain_parts(3, live.mix, mix_rows, blocks, live.moving),
-    )
-    live.moving = chain_sum(3, parts, blocks, live.moving)
+        chain_summed(live.mix, mix_rows, blocks, live.moving),
+    )
     live.fg = scatter_two(live.fg, halves)
     live.sums = (sums, swap(sums, 2))
-    live.sync()
-
-    live.moving = chain_sums(4, live.mix, mix_rows, blocks, live.moving)
-    (shard,) = ready(chain_summed(live.mix, mix_rows, blocks, live.moving))
-    turned = spread_row(shard[:, :share])
-    live.mix = jnp.concatenate([turned, shard[:, share:]], axis=1)
-    live.sync()
-    mix, _ = ready(live.mix, live.fg)
-    live.moving = chain_spread(1, 2, mix, blocks, [])
+    live.mix = spread_row(shard)
+    del live.moving
+    live.sync()
+
     first_grad = scattered(live.fg)
     inner = (live.sums[0] + live.sums[1]).reshape(half)
     r1 = live.r1[:, :1]
@@ -1080,22 +1117,28 @@
         - inputs * (r1 * r1 * inner[:, None] / model)
     )
     gains = jnp.stack([jnp.sum(first_grad * inputs * r1, axis=0) / first_gain, live.gain_part])
-    live.gains = gains + other(gains)
-    del live.fg, live.sums, live.r1, live.x, live.middle_grad, live.gain_part
+    carried = split_low(gains + other(gains))[None]
+    carried = jnp.concatenate([carried, jnp.zeros((3,) + carried.shape[1:], LOW)], axis=0)
+    live.mix = jnp.concatenate([live.mix, live.o, carried], axis=1)
+    del live.fg, live.sums, live.r1, live.x, live.middle_grad, live.gain_part, live.o
+    live.sync()
+    live.moving = chain_spread(1, 2, live.mix, blocks, [])
     live.sync()
     live.moving = chain_spread(2, 3, live.mix, blocks, live.moving)
-    live.got = [turn(live.gains, step, blocks) for step in range(1, blocks)]
-    live.sync()
-    gain_total = live.gains + sum(live.got)
+    placed = feed_place(row_info, feeds, second_gain[:, None])
+    live.placed = placed
+    live.sync()
     moving = chain_spread(3, blocks, live.mix, blocks, live.moving)
     mixes = chain_joined(live.mix, blocks, moving)
-    gate_total, up_total, down_total = feed_place(row_info, feeds, second_gain[:, None])
+    gate_total, up_total, down_total = live.placed
+    last = share + chunk // blocks
     query_total, key_total, value_total, output_total = mix_place(
         row_info,
         mixes[:, :, :share].reshape(4, width, width),
-        mixes[:, :, share:].reshape(4, chunk, width),
+        mixes[:, :, share:last].reshape(4, chunk, width),
         first_gain[:, None],
     )
+    gain_total = sum(unsplit(mixes[0, k, last:], 2) for k in range(blocks))
     return (
         layer_output,
         input_gradient,

time: 550 us -> 537 us (0.976)
  starting transfers between devices: 115 us -> 103 us
  waiting for transfers between devices: 153 us -> 162 us
  Pallas kernels: 144 us -> 137 us
    ppermute x3 -> x0, starting transfers between devices: 20.1 us -> none  [turn(): lax.ppermute(value, 'dp', [(i, (i + step) % count) for i in range(count)])]
    ppermute x3, waiting for transfers between devices: 5.68 us -> 22.7 us  [chain_spread(): down = lax.ppermute(down, 'dp', chain_down(count, step - 1, count - 1))]
    reduce_scatter x1, waiting for transfers between devices: 0.49 us -> 7.15 us  [on_device(): lax.psum_scatter(added(live.feed_own, live.feed_got), 'dp', scatter_dimen...]
    pallas_call x2, Pallas kernels: 14 us -> 7.79 us  [mix_grads(): call(mix_grads_kernel, out, [pl.BlockSpec((tokens, width), lambda i: (0,...]
    ppermute x3 -> x6, waiting for transfers between devices: 11.4 us -> 5.84 us  [chain_sum(): lax.ppermute(up, 'dp', chain_up(count, 0, last))]
    ppermute x3 -> x6, starting transfers between devices: 24.9 us -> 29.8 us  [chain_sum(): lax.ppermute(up, 'dp', chain_up(count, 0, last))]
    unnamed x178 -> x198, local copies, waits for them, and re-layouts: 22.1 us -> 23.7 us
    ppermute x3 -> x6, waiting for transfers between devices: 15.2 us -> 14.9 us  [chain_sum(): lax.ppermute(down, 'dp', chain_down(count, 0, last))]
  transfers between devices with their start and end apart: 77 -> 81, of which waited for: 37 -> 35; matrix products, arithmetic and copies ran while one was open for 13% -> 14% of each run, Pallas kernels for 20% -> 20%
where the time goes in v4:
time: 537 us; the launch traced here: 531 us
  waiting for transfers between devices  162 us (30%)
  Pallas kernels  137 us (26%)
  starting transfers between devices  103 us (19%)
  other arithmetic  54.4 us (10%)
  local copies, waits for them, and re-layouts  52.3 us (10%)
  between operations  18.2 us (3%)
    ppermute x47, waiting for transfers between devices, swap(): return lax.ppermute(value, 'row', [(i, i ^ step) for i in range(4)])  86.7 us
    ppermute x47, starting transfers between devices, swap(): return lax.ppermute(value, 'row', [(i, i ^ step) for i in range(4)])  54.8 us
    ppermute x6, starting transfers between devices, chain_sum(): lax.ppermute(up, 'dp', chain_up(count, 0, last))  29.8 us
    pallas_call x3, Pallas kernels, partial_sums(): call(functools.partial(partial_kernel, blocked), tuple(outs), specs, tupl...  28 us
    unnamed x198, local copies, waits for them, and re-layouts  23.7 us
    ppermute x3, waiting for transfers between devices, chain_spread(): down = lax.ppermute(down, 'dp', chain_down(count, step - 1, count - 1))  22.7 us
    pallas_call x1, Pallas kernels, attend_back(): call(attend_back_kernel, outs, [whole(own), whole(oth), whole(g_own), who...  17.8 us
    pallas_call x2, Pallas kernels, feed_grads(): call(feed_grads_kernel, out, [block, block, whole(back), whole(hidden)],...  17.3 us
  transfers between devices with their start and end apart: 81, of which 35 were waited for; matrix products, arithmetic and copies ran while one was open for 14% of the time, Pallas kernels for 20%

profile of v4, /device:TPU:0, one launch (start us, length us, event | category | flops | bytes accessed | tf_op | source)
XLA Modules:
  0.0 530.9 jit_solution(8443881142488315906)
XLA Ops:
  7.2 3.0 collective-permute-start.3
  22.6 2.9 collective-permute-start.2
  25.6 3.5 multiply_convert_fusion.1
  31.5 2.1 pad_maximum_fusion.6
  35.7 2.3 fusion.11
  46.2 6.0 %fusion.7 = (f32[2048,128]{1,0:T(8,128)}, f32[2048,128]{1,0:T(8,128)}) fusion(f32[128]{0:T(128)S(1)} %get-tuple-element.1213, f32[128]{0:T(128)S(1)} %get-tuple-element.1214, f32[2048]{0:T(1024)S(1)} %get-tuple-element.1211, pred[128]{0:T(512)(128)(4,1)S(1)} %broadcast_compare_fusion), kind=kLoop, calls=%fused_computation.26 | loop fusion | flops 1048576 | bytes 2106496 | tf_op jit(solution)/shard_map/jit(_where)/select_n | solution.py:882
  52.3 2.0 collective-permute-done.6.top.refs_8_
  54.8 2.2 convolution_convert_fusion.w_own
  62.8 8.1 %shard_map.204 = (bf16[1024,1536]{1,0:T(8,128)(2,1)}, f32[1024,128]{1,0:T(8,128)S(1)}, bf16[1024,512]{1,0:T(8,128)(2,1)S(1)}, bf16[1024,512]{1,0:T(8,128)(2,1)}) custom-call(bf16[1024,384]{1,0:T(8,128)(2,1)S(1)} %copy-done.6, bf16[1024,384]{1,0:T(8,128)(2,1)S(1)} %collective-permute-done.3.x1.refs_6_, ...), custom_call_target="tpu_custom_call" | custom-call | flops 50331648 | bytes 188416 | tf_op jit(solution)/shard_map/pallas_call | solution.py:374
  70.9 10.6 %collective-permute-done.10 = bf16[640,384]{1,0:T(8,128)(2,1)} collective-permute-done((bf16[640,384]{1,0:T(8,128)(2,1)}, bf16[640,384]{1,0:T(8,128)(2,1)}, u32[]{:S(2)}, u32[]{:S(2)}) %collective-permute-start.10) | collective-permute-done | bytes 491552 | tf_op jit(solution)/shard_map/ppermute | solution.py:32
  87.0 2.1 collective-permute-start.15
  89.0 14.3 %shard_map.205 = (bf16[1024,192]{1,0:T(8,128)(2,1)S(1)}, bf16[1024,192]{1,0:T(8,128)(2,1)S(1)}, bf16[2048,256]{1,0:T(8,128)(2,1)S(1)}, f32[1,4096]{1,0:T(1,128)S(1)}) custom-call(s32[17]{0:T(128)S(1)} %pad_add_fusion.info, bf16[1024,512]{1,0:T(8,128)(2,1)S(1)} %get-tuple-element.963.own, bf16[1024,512]{1,0:T(8,128)(2,1)S(1)} %collective-permute-done.12.oth, ...), custom_call_target="tpu_custom_call" | custom-call | flops 67108864 | bytes 61696 | tf_op jit(solution)/shard_map/pallas_call | solution.py:474
  103.4 2.3 collective-permute-done.15
  105.7 12.2 %collective-permute-done.16 = bf16[3,640,384]{2,1,0:T(8,128)(2,1)S(1)} collective-permute-done((bf16[3,640,384]{2,1,0:T(8,128)(2,1)S(1)}, bf16[3,640,384]{2,1,0:T(8,128)(2,1)S(1)}, u32[]{:S(2)}, u32[]{:S(2)}) %collective-permute-start.16) | collective-permute-done | bytes 1474592 | tf_op jit(solution)/shard_map/ppermute | solution.py:40
  128.8 13.0 %collective-permute-done.18.x1 = bf16[1024,384]{1,0:T(8,128)(2,1)S(1)} collective-permute-done((bf16[1024,384]{1,0:T(8,128)(2,1)S(1)}, bf16[1024,384]{1,0:T(8,128)(2,1)S(1)}, u32[]{:S(2)}, u32[]{:S(2)}) %collective-permute-start.18) | collective-permute-done | bytes 786464 | tf_op jit(solution)/shard_map/ppermute | solution.py:32
  142.4 15.2 %collective-permute-done.21.refs_1_ = bf16[1024,384]{1,0:T(8,128)(2,1)} collective-permute-done((bf16[1024,384]{1,0:T(8,128)(2,1)S(1)}, bf16[1024,384]{1,0:T(8,128)(2,1)}, u32[]{:S(2)}, u32[]{:S(2)}) %collective-permute-start.21) | collective-permute-done | bytes 786464 | tf_op jit(solution)/shard_map/ppermute | solution.py:32
  168.9 1.9 copy-done.69
  170.8 1.8 slice.318.oth
  172.6 4.3 shard_map.206
  178.1 1.7 slice.317.d_oth.w_oth
  180.9 2.0 shard_map.208.cot
  183.7 10.3 %shard_map.207 = (bf16[1024,1536]{1,0:T(8,128)(2,1)}, f32[1024,384]{1,0:T(8,128)}, f32[1024,128]{1,0:T(8,128)S(1)}, bf16[1024,1536]{1,0:T(8,128)(2,1)}) custom-call(bf16[1024,384]{1,0:T(8,128)(2,1)S(1)} %copy-done.31, bf16[1024,384]{1,0:T(8,128)(2,1)} %collective-permute-done.21.refs_1_, bf16[1024,384]{1,0:T(8,128)(2,1)} %collective-permute-done.22.refs_2_, ...), custom_call_target="tpu_custom_call" | custom-call | flops 75497472 | bytes 303104 | tf_op jit(solution)/shard_map/pallas_call | solution.py:618
  194.0 17.2 %shard_map.209 = (bf16[1024,512]{1,0:T(8,128)(2,1)S(1)}, bf16[1024,512]{1,0:T(8,128)(2,1)S(1)}, bf16[1024,1024]{1,0:T(8,128)(2,1)}, bf16[1024,1024]{1,0:T(8,128)(2,1)}) custom-call(bf16[1024,1536]{1,0:T(8,128)(2,1)} %get-tuple-element.807.second.rest_0_, bf16[1024,1536]{1,0:T(8,128)(2,1)} %shard_map.208.cot, bf16[1536,1024]{1,0:T(8,128)(2,1)} %bitcast.104, ...), custom_call_target="tpu_custom_call" | custom-call | flops 150994944 | bytes 344064 | tf_op jit(solution)/shard_map/pallas_call | solution.py:668
  211.3 2.3 copy-done.4
  213.7 11.3 %shard_map.210 = (bf16[1024,384]{1,0:T(8,128)(2,1)S(1)}, bf16[512,768]{1,0:T(8,128)(2,1)S(1)}, bf16[512,384]{1,0:T(8,128)(2,1)S(1)}, bf16[512,768]{1,0:T(8,128)(...) custom-call(bf16[1024,1024]{1,0:T(8,128)(2,1)S(1)} %copy-done.4, ...), custom_call_target="tpu_custom_call" | custom-call | flops 100663296 | bytes 270336 | tf_op jit(solution)/shard_map/pallas_call | solution.py:740
  228.4 8.6 %shard_map.212 = bf16[4,4,96,1536]{3,2,1,0:T(8,128)(2,1)} custom-call(bf16[1024,1536]{1,0:T(8,128)(2,1)} %get-tuple-element.807.second.rest_0_, bf16[1024,1536]{1,0:T(8,128)(2,1)} %shard_map.208.cot, bf16[1024,1024]{1,0:T(8,128)(2,1)S(1)} %copy-done.5, bf16[1024,512]{1,0:T(8,128)(2,1)S(1)} %get-tuple-element.882.hidden.a_own), custom_call_target="tpu_custom_call" | custom-call | flops 75497472 | bytes 221184 | tf_op jit(solution)/shard_map/pallas_call | solution.py:765
  237.1 8.6 %shard_map.211 = bf16[4,4,96,1536]{3,2,1,0:T(8,128)(2,1)} custom-call(bf16[1024,1536]{1,0:T(8,128)(2,1)} %get-tuple-element.807.second.rest_0_, bf16[1024,1536]{1,0:T(8,128)(2,1)} %shard_map.208.cot, bf16[1024,1024]{1,0:T(8,128)(2,1)S(1)} %copy-done.3, bf16[1024,512]{1,0:T(8,128)(2,1)S(1)} %get-tuple-element.883.hidden.a_oth), custom_call_target="tpu_custom_call" | custom-call | flops 75497472 | bytes 221184 | tf_op jit(solution)/shard_map/pallas_call | solution.py:765
  249.6 8.0 %collective-permute-done.35 = f32[8,128]{1,0:T(8,128)S(1)} collective-permute-done((f32[8,128]{1,0:T(8,128)S(1)}, f32[8,128]{1,0:T(8,128)S(1)}, u32[]{:S(2)}, u32[]{:S(2)}) %collective-permute-start.35) | collective-permute-done | bytes 4128 | tf_op jit(solution)/shard_map/ppermute | solution.py:32
  259.0 6.1 %add_convert_fusion = bf16[4,4,96,1536]{3,2,1,0:T(8,128)(2,1)} fusion(bf16[4,4,96,1536]{3,2,1,0:T(8,128)(2,1)S(1)} %collective-permute-done.32, bf16[4,4,96,1536]{3,2,1,0:T(8,128)(2,1)} %shard_map.212), kind=kLoop, calls=%fused_computation | loop fusion | flops 9437184 | bytes 14155776 | tf_op jit(solution)/shard_map/convert_element_type | solution.py:1006
  268.4 1.7 fusion.30
  273.2 8.6 %shard_map.213 = (bf16[1024,384]{1,0:T(8,128)(2,1)S(1)}, bf16[512,768]{1,0:T(8,128)(2,1)}, bf16[512,384]{1,0:T(8,128)(2,1)S(1)}, bf16[512,768]{1,0:T(8,128)(2,1)}, bf16[512,384]{1,0:T(8,128)(2,1)S(1)}) custom-call(bf16[1024,512]{1,0:T(8,128)(2,1)S(1)} %copy-done.16, bf16[1024,512]{1,0:T(8,128)(2,1)S(1)} %copy-done.18, bf16[4,512,384]{2,1,0:T(8,128)(2,1)} %copy-done.1, ...), custom_call_target="tpu_custom_call" | custom-call | flops 50331648 | bytes 131072 | tf_op jit(solution)/shard_map/pallas_call | solution.py:740
  281.7 7.1 %collective-permute-done.36.x1 = bf16[1024,384]{1,0:T(8,128)(2,1)S(1)} collective-permute-done((bf16[1024,384]{1,0:T(8,128)(2,1)S(1)}, bf16[1024,384]{1,0:T(8,128)(2,1)S(1)}, u32[]{:S(2)}, u32[]{:S(2)}) %collective-permute-start.36) | collective-permute-done | bytes 786464 | tf_op jit(solution)/shard_map/ppermute | solution.py:32
  291.8 1.8 convolution_convert_fusion.1
  293.7 5.7 %collective-permute-done.38.top = bf16[512,384]{1,0:T(8,128)(2,1)S(1)} collective-permute-done((bf16[512,384]{1,0:T(8,128)(2,1)S(1)}, bf16[512,384]{1,0:T(8,128)(2,1)S(1)}, u32[]{:S(2)}, u32[]{:S(2)}) %collective-permute-start.38) | collective-permute-done | bytes 393248 | tf_op jit(solution)/shard_map/ppermute | solution.py:32
  300.4 2.5 shard_map.214
  306.5 1.8 constant_dynamic-slice_fusion.2
  308.2 3.4 collective-permute-start.44
  313.0 17.8 %shard_map.215 = (bf16[1024,512]{1,0:T(8,128)(2,1)S(1)}, bf16[1024,512]{1,0:T(8,128)(2,1)S(1)}) custom-call(s32[17]{0:T(128)S(1)} %pad_add_fusion.info, bf16[1024,512]{1,0:T(8,128)(2,1)S(1)} %copy-done.20, bf16[1024,512]{1,0:T(8,128)(2,1)S(1)} %copy-done.22, bf16[1024,256]{1,0:T(8,128)(2,1)S(1)} %get-tuple-element.965.g_own, ...), custom_call_target="tpu_custom_call" | custom-call | flops 167772160 | bytes 98304 | tf_op jit(solution)/shard_map/pallas_call | solution.py:565
  339.2 3.5 shard_map.217
  342.8 4.3 shard_map.216
  349.3 7.2 %reduce-scatter.2.cloned.1.call-done = bf16[1,4,96,1536]{3,2,1,0:T(8,128)(2,1)} async-done(((bf16[4,4,96,1536]{3,2,1,0:T(8,128)(2,1)}), bf16[1,4,96,1536]{3,2,1,0:T(8,128)(2,1)}) %reduce-scatter.2.cloned.1.call-update) | async-done | bytes 1179664 | tf_op jit(solution)/shard_map/reduce_scatter | solution.py:1032
  364.7 3.0 collective-permute-done.51
  367.7 6.2 %collective-permute-done.52 = bf16[96,1536]{1,0:T(8,128)(2,1)S(1)} collective-permute-done((bf16[96,1536]{1,0:T(8,128)(2,1)S(1)}, bf16[96,1536]{1,0:T(8,128)(2,1)S(1)}, u32[]{:S(2)}, u32[]{:S(2)}) %collective-permute-start.52) | collective-permute-done | bytes 294944 | tf_op jit(solution)/shard_map/ppermute | solution.py:32
  380.3 7.4 %collective-permute-start.59 = (bf16[4,48,384]{2,1,0:T(8,128)(2,1)S(1)}, bf16[4,48,384]{2,1,0:T(8,128)(2,1)S(1)}, u32[]{:S(2)}, u32[]{:S(2)}) collective-permute-start(bf16[4,48,384]{2,1,0:T(8,128)(2,1)S(1)} %get-tuple-element.1064), channel_id=1, source_target_pairs={{0,8},{8,16},{16,24},{1,9},{9,17},{17,25},{2,10},{10,18},{18,26},{... | collective-permute-start | bytes 442376 | tf_op jit(solution)/shard_map/ppermute | solution.py:160
  389.0 8.1 %shard_map.218 = (bf16[1024,384]{1,0:T(8,128)(2,1)S(1)}, bf16[512,768]{1,0:T(8,128)(2,1)}, bf16[512,384]{1,0:T(8,128)(2,1)S(1)}, bf16[512,768]{1,0:T(8,128)(2,1)...) custom-call(bf16[1024,512]{1,0:T(8,128)(2,1)S(1)} %copy-done.24, bf16[1024,512]{1,0:T(8,128)(2,1)S(1)} %copy-done.26, ...), custom_call_target="tpu_custom_call" | custom-call | flops 50331648 | bytes 188416 | tf_op jit(solution)/shard_map/pallas_call | solution.py:740
  398.7 4.2 collective-permute-done.60
  405.8 2.2 add_convert_fusion.9
  408.0 15.1 %collective-permute-start.63 = (bf16[4,96,384]{2,1,0:T(8,128)(2,1)}, bf16[4,96,384]{2,1,0:T(8,128)(2,1)S(1)}, u32[]{:S(2)}, u32[]{:S(2)}) collective-permute-start(bf16[4,96,384]{2,1,0:T(8,128)(2,1)} %get-tuple-element.1085), channel_id=1, source_target_pairs={{0,8},{8,16},{16,24},{1,9},{9,17},{17,25},{2,10},{10,18},{18,26},{... | collective-permute-start | bytes 884744 | tf_op jit(solution)/shard_map/ppermute | solution.py:160
  424.3 2.0 collective-permute-start.65
  428.0 5.8 %collective-permute-done.63 = bf16[4,96,384]{2,1,0:T(8,128)(2,1)S(1)} collective-permute-done((bf16[4,96,384]{2,1,0:T(8,128)(2,1)}, bf16[4,96,384]{2,1,0:T(8,128)(2,1)S(1)}, u32[]{:S(2)}, u32[]{:S(2)}) %collective-permute-start.63) | collective-permute-done | bytes 294944 | tf_op jit(solution)/shard_map/ppermute | solution.py:160
  433.8 10.7 %collective-permute-done.64 = bf16[4,96,384]{2,1,0:T(8,128)(2,1)} collective-permute-done((bf16[4,96,384]{2,1,0:T(8,128)(2,1)}, bf16[4,96,384]{2,1,0:T(8,128)(2,1)}, u32[]{:S(2)}, u32[]{:S(2)}) %collective-permute-start.64) | collective-permute-done | bytes 294944 | tf_op jit(solution)/shard_map/ppermute | solution.py:160
  447.0 2.8 collective-permute-start.66
  452.1 2.7 collective-permute-start.70
  454.7 3.7 collective-permute-done.68
  458.8 3.3 collective-permute-done.71
  463.5 1.7 convert_add_fusion.2
  471.5 10.1 %collective-permute-done.73 = bf16[4,160,384]{2,1,0:T(8,128)(2,1)S(1)} collective-permute-done((bf16[4,160,384]{2,1,0:T(8,128)(2,1)S(1)}, bf16[4,160,384]{2,1,0:T(8,128)(2,1)S(1)}, u32[]{:S(2)}, u32[]{:S(2)}) %collective-permute-start.73) | collective-permute-done | bytes 491552 | tf_op jit(solution)/shard_map/ppermute | solution.py:179
  481.6 6.8 %collective-permute-done.74 = bf16[4,160,384]{2,1,0:T(8,128)(2,1)S(1)} collective-permute-done((bf16[4,160,384]{2,1,0:T(8,128)(2,1)S(1)}, bf16[4,160,384]{2,1,0:T(8,128)(2,1)S(1)}, u32[]{:S(2)}, u32[]{:S(2)}) %collective-permute-start.74) | collective-permute-done | bytes 491552 | tf_op jit(solution)/shard_map/ppermute | solution.py:180
  491.1 1.7 convert_add_fusion.4
  493.9 2.3 copy-done.12
  496.2 4.2 shard_map.219
  500.4 4.8 collective-permute-done.76
  508.9 11.0 %collective-permute-done.78 = bf16[4,160,384]{2,1,0:T(8,128)(2,1)S(1)} collective-permute-done((bf16[4,160,384]{2,1,0:T(8,128)(2,1)S(1)}, bf16[4,160,384]{2,1,0:T(8,128)(2,1)S(1)}, u32[]{:S(2)}, u32[]{:S(2)}) %collective-permute-start.78) | collective-permute-done | bytes 491552 | tf_op jit(solution)/shard_map/ppermute | solution.py:180
  520.9 2.7 shard_map.220
  (434 shorter events, 138.7 us)
Async XLA Ops:
  7.2 349.2 %reduce-scatter.2.cloned.1.call-start = ((), (), s32[]{:S(2)}) async-start(), calls=%async_computation.1 | async-start | bytes 5898240 | tf_op jit(solution)/shard_map/reduce_scatter | solution.py:1032
  7.2 30.8 %collective-permute-start.3 = (bf16[1024,384]{1,0:T(8,128)(2,1)}, bf16[1024,384]{1,0:T(8,128)(2,1)S(1)}, u32[]{:S(2)}, u32[]{:S(2)}) collective-permute-start(bf16[1024,384]{1,0:T(8,128)(2,1)} %refs_5_), channel_id=1, source_target_pairs={{0,2},{2,0},{4,6},{6,4},{1,3},{3,1},{5,7},{7,5},{8,10},{10,8},{12,... | collective-permute-start | bytes 2359304 | tf_op jit(solution)/shard_map/ppermute | solution.py:32
  10.2 27.8 %collective-permute-start.4 = (bf16[1024,384]{1,0:T(8,128)(2,1)}, bf16[1024,384]{1,0:T(8,128)(2,1)S(1)}, u32[]{:S(2)}, u32[]{:S(2)}) collective-permute-start(bf16[1024,384]{1,0:T(8,128)(2,1)} %refs_5_), channel_id=1, source_target_pairs={{0,4},{2,6},{4,0},{6,2},{1,5},{3,7},{5,1},{7,3},{8,12},{10,14},{12... | collective-permute-start | bytes 2359304 | tf_op jit(solution)/shard_map/ppermute | solution.py:32
  22.0 16.0 %collective-permute-start = (bf16[192,384]{1,0:T(8,128)(2,1)}, bf16[192,384]{1,0:T(8,128)(2,1)S(1)}, u32[]{:S(2)}, u32[]{:S(2)}) collective-permute-start(bf16[192,384]{1,0:T(8,128)(2,1)} %dynamic-slice_bitcast_fusion.2), channel_id=1, source_target_pairs={{0,2},{2,0},{4,6},{6,4},{1,3},{3,1},{5,7},{7,5},{8,10},{10,8},{12,... | collective-permute-start | bytes 442376 | tf_op jit(solution)/shard_map/ppermute | solution.py:32
  22.5 15.5 %collective-permute-start.1 = (bf16[192,384]{1,0:T(8,128)(2,1)}, bf16[192,384]{1,0:T(8,128)(2,1)}, u32[]{:S(2)}, u32[]{:S(2)}) collective-permute-start(bf16[192,384]{1,0:T(8,128)(2,1)} %dynamic-slice_bitcast_fusion.1), channel_id=1, source_target_pairs={{0,4},{2,6},{4,0},{6,2},{1,5},{3,7},{5,1},{7,3},{8,12},{10,14},{12... | collective-permute-start | bytes 442376 | tf_op jit(solution)/shard_map/ppermute | solution.py:32
  22.6 15.4 %collective-permute-start.2 = (bf16[192,384]{1,0:T(8,128)(2,1)}, bf16[192,384]{1,0:T(8,128)(2,1)}, u32[]{:S(2)}, u32[]{:S(2)}) collective-permute-start(bf16[192,384]{1,0:T(8,128)(2,1)} %dynamic-slice_bitcast_fusion), channel_id=1, source_target_pairs={{0,6},{2,4},{4,2},{6,0},{1,7},{3,5},{5,3},{7,1},{8,14},{10,12},{12... | collective-permute-start | bytes 442376 | tf_op jit(solution)/shard_map/ppermute | solution.py:32
  43.5 11.0 %collective-permute-start.5 = (bf16[3,192,384]{2,1,0:T(8,128)(2,1)S(1)}, bf16[3,192,384]{2,1,0:T(8,128)(2,1)S(1)}, u32[]{:S(2)}, u32[]{:S(2)}) collective-permute-start(bf16[3,192,384]{2,1,0:T(8,128)(2,1)S(1)} %pad_maximum_fusion.8), channel_id=1, source_target_pairs={{0,8},{8,0},{16,24},{24,16},{1,9},{9,1},{17,25},{25,17},{2,10},{10... | collective-permute-start | bytes 1327112 | tf_op jit(solution)/shard_map/ppermute | solution.py:40
  57.0 24.5 %collective-permute-start.10 = (bf16[640,384]{1,0:T(8,128)(2,1)}, bf16[640,384]{1,0:T(8,128)(2,1)}, u32[]{:S(2)}, u32[]{:S(2)}) collective-permute-start(bf16[640,384]{1,0:T(8,128)(2,1)} %get-tuple-element.624), channel_id=1, source_target_pairs={{0,4},{2,6},{4,0},{6,2},{1,5},{3,7},{5,1},{7,3},{8,12},{10,14},{12... | collective-permute-start | bytes 1474568 | tf_op jit(solution)/shard_map/ppermute | solution.py:32
  58.6 23.0 %collective-permute-start.11 = (bf16[640,384]{1,0:T(8,128)(2,1)}, bf16[640,384]{1,0:T(8,128)(2,1)}, u32[]{:S(2)}, u32[]{:S(2)}) collective-permute-start(bf16[640,384]{1,0:T(8,128)(2,1)} %get-tuple-element.625), channel_id=1, source_target_pairs={{0,6},{2,4},{4,2},{6,0},{1,7},{3,5},{5,3},{7,1},{8,14},{10,12},{12... | collective-permute-start | bytes 1474568 | tf_op jit(solution)/shard_map/ppermute | solution.py:32
  59.1 23.7 %collective-permute-start.9 = (bf16[640,384]{1,0:T(8,128)(2,1)}, bf16[640,384]{1,0:T(8,128)(2,1)}, u32[]{:S(2)}, u32[]{:S(2)}) collective-permute-start(bf16[640,384]{1,0:T(8,128)(2,1)} %get-tuple-element.623), channel_id=1, source_target_pairs={{0,2},{2,0},{4,6},{6,4},{1,3},{3,1},{5,7},{7,5},{8,10},{10,8},{12,... | collective-permute-start | bytes 1474568 | tf_op jit(solution)/shard_map/ppermute | solution.py:32
  84.3 33.7 %collective-permute-start.16 = (bf16[3,640,384]{2,1,0:T(8,128)(2,1)S(1)}, bf16[3,640,384]{2,1,0:T(8,128)(2,1)S(1)}, u32[]{:S(2)}, u32[]{:S(2)}) collective-permute-start(bf16[3,640,384]{2,1,0:T(8,128)(2,1)S(1)} %pad_maximum_fusion.2), channel_id=1, source_target_pairs={{0,8},{8,0},{16,24},{24,16},{1,9},{9,1},{17,25},{25,17},{2,10},{10... | collective-permute-start | bytes 4423688 | tf_op jit(solution)/shard_map/ppermute | solution.py:40
  85.5 17.9 %collective-permute-start.13 = (bf16[192,1024]{1,0:T(8,128)(2,1)S(1)}, bf16[192,1024]{1,0:T(8,128)(2,1)S(1)}, u32[]{:S(2)}, u32[]{:S(2)}) collective-permute-start(bf16[192,1024]{1,0:T(8,128)(2,1)S(1)} %copy-done.80), channel_id=1, source_target_pairs={{0,2},{2,0},{4,6},{6,4},{1,3},{3,1},{5,7},{7,5},{8,10},{10,8},{12,... | collective-permute-start | bytes 1179656 | tf_op jit(solution)/shard_map/ppermute | solution.py:32
  86.1 17.3 %collective-permute-start.14 = (bf16[192,1024]{1,0:T(8,128)(2,1)S(1)}, bf16[192,1024]{1,0:T(8,128)(2,1)S(1)}, u32[]{:S(2)}, u32[]{:S(2)}) collective-permute-start(bf16[192,1024]{1,0:T(8,128)(2,1)S(1)} %copy-done.79), channel_id=1, source_target_pairs={{0,4},{2,6},{4,0},{6,2},{1,5},{3,7},{5,1},{7,3},{8,12},{10,14},{12... | collective-permute-start | bytes 1179656 | tf_op jit(solution)/shard_map/ppermute | solution.py:32
  87.0 18.8 %collective-permute-start.15 = (bf16[192,1024]{1,0:T(8,128)(2,1)S(1)}, bf16[192,1024]{1,0:T(8,128)(2,1)S(1)}, u32[]{:S(2)}, u32[]{:S(2)}) collective-permute-start(bf16[192,1024]{1,0:T(8,128)(2,1)S(1)} %copy-done.78), channel_id=1, source_target_pairs={{0,6},{2,4},{4,2},{6,0},{1,7},{3,5},{5,3},{7,1},{8,14},{10,12},{12... | collective-permute-start | bytes 1179656 | tf_op jit(solution)/shard_map/ppermute | solution.py:32
  120.2 37.7 %collective-permute-start.20 = (bf16[3,192,1024]{2,1,0:T(8,128)(2,1)}, bf16[3,192,1024]{2,1,0:T(8,128)(2,1)}, u32[]{:S(2)}, u32[]{:S(2)}) collective-permute-start(bf16[3,192,1024]{2,1,0:T(8,128)(2,1)} %pad_maximum_fusion.3), channel_id=1, source_target_pairs={{0,8},{8,0},{16,24},{24,16},{1,9},{9,1},{17,25},{25,17},{2,10},{10... | collective-permute-start | bytes 3538952 | tf_op jit(solution)/shard_map/ppermute | solution.py:40
  121.4 20.4 %collective-permute-start.18 = (bf16[1024,384]{1,0:T(8,128)(2,1)S(1)}, bf16[1024,384]{1,0:T(8,128)(2,1)S(1)}, u32[]{:S(2)}, u32[]{:S(2)}) collective-permute-start(bf16[1024,384]{1,0:T(8,128)(2,1)S(1)} %copy-done.27), channel_id=1, source_target_pairs={{0,2},{2,0},{4,6},{6,4},{1,3},{3,1},{5,7},{7,5},{8,10},{10,8},{12,... | collective-permute-start | bytes 2359304 | tf_op jit(solution)/shard_map/ppermute | solution.py:32
  121.9 20.5 %collective-permute-start.19 = (bf16[1024,384]{1,0:T(8,128)(2,1)S(1)}, bf16[1024,384]{1,0:T(8,128)(2,1)S(1)}, u32[]{:S(2)}, u32[]{:S(2)}) collective-permute-start(bf16[1024,384]{1,0:T(8,128)(2,1)S(1)} %copy-done.27), channel_id=1, source_target_pairs={{0,4},{2,6},{4,0},{6,2},{1,5},{3,7},{5,1},{7,3},{8,12},{10,14},{12... | collective-permute-start | bytes 2359304 | tf_op jit(solution)/shard_map/ppermute | solution.py:32
  122.8 34.8 %collective-permute-start.21 = (bf16[1024,384]{1,0:T(8,128)(2,1)S(1)}, bf16[1024,384]{1,0:T(8,128)(2,1)}, u32[]{:S(2)}, u32[]{:S(2)}) collective-permute-start(bf16[1024,384]{1,0:T(8,128)(2,1)S(1)} %pad_maximum_fusion.7.refs_0_), channel_id=1, source_target_pairs={{0,2},{2,0},{4,6},{6,4},{1,3},{3,1},{5,7},{7,5},{8,10},{10,8},{12,... | collective-permute-start | bytes 2359304 | tf_op jit(solution)/shard_map/ppermute | solution.py:32
  124.3 33.6 %collective-permute-start.22 = (bf16[1024,384]{1,0:T(8,128)(2,1)S(1)}, bf16[1024,384]{1,0:T(8,128)(2,1)}, u32[]{:S(2)}, u32[]{:S(2)}) collective-permute-start(bf16[1024,384]{1,0:T(8,128)(2,1)S(1)} %pad_maximum_fusion.7.refs_0_), channel_id=1, source_target_pairs={{0,4},{2,6},{4,0},{6,2},{1,5},{3,7},{5,1},{7,3},{8,12},{10,14},{12... | collective-permute-start | bytes 2359304 | tf_op jit(solution)/shard_map/ppermute | solution.py:32
  157.9 11.0 %collective-permute-start.25 = (bf16[4,1280,384]{2,1,0:T(8,128)(2,1)S(1)}, bf16[4,1280,384]{2,1,0:T(8,128)(2,1)S(1)}, u32[]{:S(2)}, u32[]{:S(2)}) collective-permute-start(bf16[4,1280,384]{2,1,0:T(8,128)(2,1)S(1)} %constant_dynamic-update-slice_fusion.2), channel_id=1, source_target_pairs={{0,1},{1,0},{2,3},{3,2},{4,5},{5,4},{6,7},{7,6},{8,9},{9,8},{10,11... | collective-permute-start | bytes 11796488 | tf_op jit(solution)/shard_map/ppermute | solution.py:36
  160.1 19.7 %collective-permute-start.23 = (bf16[512,384]{1,0:T(8,128)(2,1)S(1)}, bf16[512,384]{1,0:T(8,128)(2,1)S(1)}, u32[]{:S(2)}, u32[]{:S(2)}) collective-permute-start(bf16[512,384]{1,0:T(8,128)(2,1)S(1)} %slice.254), channel_id=1, source_target_pairs={{0,4},{2,6},{4,0},{6,2},{1,5},{3,7},{5,1},{7,3},{8,12},{10,14},{12... | collective-permute-start | bytes 1179656 | tf_op jit(solution)/shard_map/ppermute | solution.py:32
  161.0 18.8 %collective-permute-start.24 = (bf16[512,384]{1,0:T(8,128)(2,1)S(1)}, bf16[512,384]{1,0:T(8,128)(2,1)S(1)}, u32[]{:S(2)}, u32[]{:S(2)}) collective-permute-start(bf16[512,384]{1,0:T(8,128)(2,1)S(1)} %slice.255), channel_id=1, source_target_pairs={{0,2},{2,0},{4,6},{6,4},{1,3},{3,1},{5,7},{7,5},{8,10},{10,8},{12,... | collective-permute-start | bytes 1179656 | tf_op jit(solution)/shard_map/ppermute | solution.py:32
  162.5 17.6 %collective-permute-start.26 = (bf16[512,384]{1,0:T(8,128)(2,1)S(1)}, bf16[512,384]{1,0:T(8,128)(2,1)S(1)}, u32[]{:S(2)}, u32[]{:S(2)}) collective-permute-start(bf16[512,384]{1,0:T(8,128)(2,1)S(1)} %slice.252), channel_id=1, source_target_pairs={{0,4},{2,6},{4,0},{6,2},{1,5},{3,7},{5,1},{7,3},{8,12},{10,14},{12... | collective-permute-start | bytes 1179656 | tf_op jit(solution)/shard_map/ppermute | solution.py:32
  163.7 17.0 %collective-permute-start.27 = (bf16[512,384]{1,0:T(8,128)(2,1)S(1)}, bf16[512,384]{1,0:T(8,128)(2,1)S(1)}, u32[]{:S(2)}, u32[]{:S(2)}) collective-permute-start(bf16[512,384]{1,0:T(8,128)(2,1)S(1)} %slice.253), channel_id=1, source_target_pairs={{0,2},{2,0},{4,6},{6,4},{1,3},{3,1},{5,7},{7,5},{8,10},{10,8},{12,... | collective-permute-start | bytes 1179656 | tf_op jit(solution)/shard_map/ppermute | solution.py:32
  180.8 13.3 %collective-permute-start.28 = (bf16[1536,1024]{1,0:T(8,128)(2,1)S(1)}, bf16[1536,1024]{1,0:T(8,128)(2,1)}, u32[]{:S(2)}, u32[]{:S(2)}) collective-permute-start(bf16[1536,1024]{1,0:T(8,128)(2,1)S(1)} %bitcast.103), channel_id=1, source_target_pairs={{0,1},{1,0},{2,3},{3,2},{4,5},{5,4},{6,7},{7,6},{8,9},{9,8},{10,11... | collective-permute-start | bytes 9437192 | tf_op jit(solution)/shard_map/ppermute | solution.py:36
  225.2 20.5 %collective-permute-start.29 = (bf16[512,768]{1,0:T(8,128)(2,1)S(1)}, bf16[512,768]{1,0:T(8,128)(2,1)S(1)}, u32[]{:S(2)}, u32[]{:S(2)}) collective-permute-start(bf16[512,768]{1,0:T(8,128)(2,1)S(1)} %get-tuple-element.824), channel_id=1, source_target_pairs={{0,2},{2,0},{4,6},{6,4},{1,3},{3,1},{5,7},{7,5},{8,10},{10,8},{12,... | collective-permute-start | bytes 2359304 | tf_op jit(solution)/shard_map/ppermute | solution.py:32
  226.7 19.0 %collective-permute-start.30 = (bf16[512,768]{1,0:T(8,128)(2,1)S(1)}, bf16[512,768]{1,0:T(8,128)(2,1)S(1)}, u32[]{:S(2)}, u32[]{:S(2)}) collective-permute-start(bf16[512,768]{1,0:T(8,128)(2,1)S(1)} %get-tuple-element.826), channel_id=1, source_target_pairs={{0,4},{2,6},{4,0},{6,2},{1,5},{3,7},{5,1},{7,3},{8,12},{10,14},{12... | collective-permute-start | bytes 2359304 | tf_op jit(solution)/shard_map/ppermute | solution.py:32
  227.9 17.8 %collective-permute-start.31 = (f32[8,128]{1,0:T(8,128)S(1)}, f32[8,128]{1,0:T(8,128)S(1)}, u32[]{:S(2)}, u32[]{:S(2)}) collective-permute-start(f32[8,128]{1,0:T(8,128)S(1)} %bitcast.125), channel_id=1, source_target_pairs={{0,2},{2,0},{4,6},{6,4},{1,3},{3,1},{5,7},{7,5},{8,10},{10,8},{12,... | collective-permute-start | bytes 12296 | tf_op jit(solution)/shard_map/ppermute | solution.py:32
  246.0 12.3 %collective-permute-start.32 = (bf16[4,4,96,1536]{3,2,1,0:T(8,128)(2,1)}, bf16[4,4,96,1536]{3,2,1,0:T(8,128)(2,1)S(1)}, u32[]{:S(2)}, u32[]{:S(2)}) collective-permute-start(bf16[4,4,96,1536]{3,2,1,0:T(8,128)(2,1)} %shard_map.211), channel_id=1, source_target_pairs={{0,1},{1,0},{2,3},{3,2},{4,5},{5,4},{6,7},{7,6},{8,9},{9,8},{10,11... | collective-permute-start | bytes 14155784 | tf_op jit(solution)/shard_map/ppermute | solution.py:36
  246.0 11.6 %collective-permute-start.33 = (bf16[512,384]{1,0:T(8,128)(2,1)S(1)}, bf16[512,384]{1,0:T(8,128)(2,1)S(1)}, u32[]{:S(2)}, u32[]{:S(2)}) collective-permute-start(bf16[512,384]{1,0:T(8,128)(2,1)S(1)} %add_convert_fusion.7), channel_id=1, source_target_pairs={{0,4},{2,6},{4,0},{6,2},{1,5},{3,7},{5,1},{7,3},{8,12},{10,14},{12... | collective-permute-start | bytes 1179656 | tf_op jit(solution)/shard_map/ppermute | solution.py:32
  247.1 11.2 %collective-permute-start.34 = (bf16[512,384]{1,0:T(8,128)(2,1)S(1)}, bf16[512,384]{1,0:T(8,128)(2,1)S(1)}, u32[]{:S(2)}, u32[]{:S(2)}) collective-permute-start(bf16[512,384]{1,0:T(8,128)(2,1)S(1)} %add_convert_fusion.6), channel_id=1, source_target_pairs={{0,2},{2,0},{4,6},{6,4},{1,3},{3,1},{5,7},{7,5},{8,10},{10,8},{12,... | collective-permute-start | bytes 1179656 | tf_op jit(solution)/shard_map/ppermute | solution.py:32
  248.5 9.2 %collective-permute-start.35 = (f32[8,128]{1,0:T(8,128)S(1)}, f32[8,128]{1,0:T(8,128)S(1)}, u32[]{:S(2)}, u32[]{:S(2)}) collective-permute-start(f32[8,128]{1,0:T(8,128)S(1)} %add.417), channel_id=1, source_target_pairs={{0,4},{2,6},{4,0},{6,2},{1,5},{3,7},{5,1},{7,3},{8,12},{10,14},{12... | collective-permute-start | bytes 12296 | tf_op jit(solution)/shard_map/ppermute | solution.py:32
  265.1 228.7 %all-gather.3.cloned.1.call-start = ((), (), s32[]{:S(2)}) async-start(), calls=%async_computation.2 | async-start | bytes 5898240 | tf_op jit(solution)/shard_map/all_gather | solution.py:1082
  270.0 18.8 %collective-permute-start.36 = (bf16[1024,384]{1,0:T(8,128)(2,1)S(1)}, bf16[1024,384]{1,0:T(8,128)(2,1)S(1)}, u32[]{:S(2)}, u32[]{:S(2)}) collective-permute-start(bf16[1024,384]{1,0:T(8,128)(2,1)S(1)} %get-tuple-element.941.x0), channel_id=1, source_target_pairs={{0,2},{2,0},{4,6},{6,4},{1,3},{3,1},{5,7},{7,5},{8,10},{10,8},{12,... | collective-permute-start | bytes 2359304 | tf_op jit(solution)/shard_map/ppermute | solution.py:32
  271.4 18.5 %collective-permute-start.37 = (bf16[1024,384]{1,0:T(8,128)(2,1)S(1)}, bf16[1024,384]{1,0:T(8,128)(2,1)S(1)}, u32[]{:S(2)}, u32[]{:S(2)}) collective-permute-start(bf16[1024,384]{1,0:T(8,128)(2,1)S(1)} %get-tuple-element.941.x0), channel_id=1, source_target_pairs={{0,4},{2,6},{4,0},{6,2},{1,5},{3,7},{5,1},{7,3},{8,12},{10,14},{12... | collective-permute-start | bytes 2359304 | tf_op jit(solution)/shard_map/ppermute | solution.py:32
  290.1 9.3 %collective-permute-start.38 = (bf16[512,384]{1,0:T(8,128)(2,1)S(1)}, bf16[512,384]{1,0:T(8,128)(2,1)S(1)}, u32[]{:S(2)}, u32[]{:S(2)}) collective-permute-start(bf16[512,384]{1,0:T(8,128)(2,1)S(1)} %slice.268), channel_id=1, source_target_pairs={{0,4},{2,6},{4,0},{6,2},{1,5},{3,7},{5,1},{7,3},{8,12},{10,14},{12... | collective-permute-start | bytes 1179656 | tf_op jit(solution)/shard_map/ppermute | solution.py:32
  304.9 25.9 %collective-permute-start.42 = (bf16[512,768]{1,0:T(8,128)(2,1)}, bf16[512,768]{1,0:T(8,128)(2,1)}, u32[]{:S(2)}, u32[]{:S(2)}) collective-permute-start(bf16[512,768]{1,0:T(8,128)(2,1)} %get-tuple-element.975), channel_id=1, source_target_pairs={{0,2},{2,0},{4,6},{6,4},{1,3},{3,1},{5,7},{7,5},{8,10},{10,8},{12,... | collective-permute-start | bytes 2359304 | tf_op jit(solution)/shard_map/ppermute | solution.py:32
  305.5 25.3 %collective-permute-start.43 = (bf16[512,768]{1,0:T(8,128)(2,1)}, bf16[512,768]{1,0:T(8,128)(2,1)}, u32[]{:S(2)}, u32[]{:S(2)}) collective-permute-start(bf16[512,768]{1,0:T(8,128)(2,1)} %get-tuple-element.977), channel_id=1, source_target_pairs={{0,4},{2,6},{4,0},{6,2},{1,5},{3,7},{5,1},{7,3},{8,12},{10,14},{12... | collective-permute-start | bytes 2359304 | tf_op jit(solution)/shard_map/ppermute | solution.py:32
  308.2 22.6 %collective-permute-start.44 = (bf16[4,48,384]{2,1,0:T(8,128)(2,1)}, bf16[4,48,384]{2,1,0:T(8,128)(2,1)S(1)}, u32[]{:S(2)}, u32[]{:S(2)}) collective-permute-start(bf16[4,48,384]{2,1,0:T(8,128)(2,1)} %get-tuple-element.983), channel_id=1, source_target_pairs={{0,8},{1,9},{2,10},{3,11},{4,12},{5,13},{6,14},{7,15}} | collective-permute-start | bytes 442376 | tf_op jit(solution)/shard_map/ppermute | solution.py:160
  311.6 19.1 %collective-permute-start.45 = (bf16[4,48,384]{2,1,0:T(8,128)(2,1)}, bf16[4,48,384]{2,1,0:T(8,128)(2,1)}, u32[]{:S(2)}, u32[]{:S(2)}) collective-permute-start(bf16[4,48,384]{2,1,0:T(8,128)(2,1)} %get-tuple-element.984), channel_id=1, source_target_pairs={{24,16},{25,17},{26,18},{27,19},{28,20},{29,21},{30,22},{31,23}} | collective-permute-start | bytes 442376 | tf_op jit(solution)/shard_map/ppermute | solution.py:160
  334.6 12.4 %collective-permute-start.47 = (bf16[512,384]{1,0:T(8,128)(2,1)S(1)}, bf16[512,384]{1,0:T(8,128)(2,1)S(1)}, u32[]{:S(2)}, u32[]{:S(2)}) collective-permute-start(bf16[512,384]{1,0:T(8,128)(2,1)S(1)} %add_convert_fusion.5), channel_id=1, source_target_pairs={{0,4},{2,6},{4,0},{6,2},{1,5},{3,7},{5,1},{7,3},{8,12},{10,14},{12... | collective-permute-start | bytes 1179656 | tf_op jit(solution)/shard_map/ppermute | solution.py:32
  335.6 12.1 %collective-permute-start.48 = (bf16[512,384]{1,0:T(8,128)(2,1)S(1)}, bf16[512,384]{1,0:T(8,128)(2,1)S(1)}, u32[]{:S(2)}, u32[]{:S(2)}) collective-permute-start(bf16[512,384]{1,0:T(8,128)(2,1)S(1)} %add_convert_fusion.4), channel_id=1, source_target_pairs={{0,2},{2,0},{4,6},{6,4},{1,3},{3,1},{5,7},{7,5},{8,10},{10,8},{12,... | collective-permute-start | bytes 1179656 | tf_op jit(solution)/shard_map/ppermute | solution.py:32
  337.0 10.0 %collective-permute-start.49 = (bf16[4,48,384]{2,1,0:T(8,128)(2,1)S(1)}, bf16[4,48,384]{2,1,0:T(8,128)(2,1)S(1)}, u32[]{:S(2)}, u32[]{:S(2)}) collective-permute-start(bf16[4,48,384]{2,1,0:T(8,128)(2,1)S(1)} %get-tuple-element.1007), channel_id=1, source_target_pairs={{0,8},{8,16},{1,9},{9,17},{2,10},{10,18},{3,11},{11,19},{4,12},{12... | collective-permute-start | bytes 442376 | tf_op jit(solution)/shard_map/ppermute | solution.py:160
  349.3 12.0 %collective-permute-start.54 = (bf16[4,384,384]{2,1,0:T(8,128)(2,1)}, bf16[4,384,384]{2,1,0:T(8,128)(2,1)S(1)}, u32[]{:S(2)}, u32[]{:S(2)}) collective-permute-start(bf16[4,384,384]{2,1,0:T(8,128)(2,1)} %shard_map.216), channel_id=1, source_target_pairs={{0,1},{1,0},{2,3},{3,2},{4,5},{5,4},{6,7},{7,6},{8,9},{9,8},{10,11... | collective-permute-start | bytes 3538952 | tf_op jit(solution)/shard_map/ppermute | solution.py:36
  357.7 10.0 %collective-permute-start.51 = (bf16[96,1536]{1,0:T(8,128)(2,1)S(1)}, bf16[96,1536]{1,0:T(8,128)(2,1)S(1)}, u32[]{:S(2)}, u32[]{:S(2)}) collective-permute-start(bf16[96,1536]{1,0:T(8,128)(2,1)S(1)} %get-tuple-element.1175), channel_id=1, source_target_pairs={{0,2},{2,0},{4,6},{6,4},{1,3},{3,1},{5,7},{7,5},{8,10},{10,8},{12,... | collective-permute-start | bytes 884744 | tf_op jit(solution)/shard_map/ppermute | solution.py:32
  359.2 14.6 %collective-permute-start.52 = (bf16[96,1536]{1,0:T(8,128)(2,1)S(1)}, bf16[96,1536]{1,0:T(8,128)(2,1)S(1)}, u32[]{:S(2)}, u32[]{:S(2)}) collective-permute-start(bf16[96,1536]{1,0:T(8,128)(2,1)S(1)} %get-tuple-element.1174), channel_id=1, source_target_pairs={{0,4},{2,6},{4,0},{6,2},{1,5},{3,7},{5,1},{7,3},{8,12},{10,14},{12... | collective-permute-start | bytes 884744 | tf_op jit(solution)/shard_map/ppermute | solution.py:32
  360.7 13.2 %collective-permute-start.53 = (bf16[96,1536]{1,0:T(8,128)(2,1)S(1)}, bf16[96,1536]{1,0:T(8,128)(2,1)S(1)}, u32[]{:S(2)}, u32[]{:S(2)}) collective-permute-start(bf16[96,1536]{1,0:T(8,128)(2,1)S(1)} %get-tuple-element.1173), channel_id=1, source_target_pairs={{0,6},{2,4},{4,2},{6,0},{1,7},{3,5},{5,3},{7,1},{8,14},{10,12},{12... | collective-permute-start | bytes 884744 | tf_op jit(solution)/shard_map/ppermute | solution.py:32
  362.7 12.3 %collective-permute-start.55 = (bf16[4,96,384]{2,1,0:T(8,128)(2,1)S(1)}, bf16[4,96,384]{2,1,0:T(8,128)(2,1)S(1)}, u32[]{:S(2)}, u32[]{:S(2)}) collective-permute-start(bf16[4,96,384]{2,1,0:T(8,128)(2,1)S(1)} %get-tuple-element.1171), channel_id=1, source_target_pairs={{0,8},{1,9},{2,10},{3,11},{4,12},{5,13},{6,14},{7,15}} | collective-permute-start | bytes 884744 | tf_op jit(solution)/shard_map/ppermute | solution.py:160
  364.0 11.0 %collective-permute-start.56 = (bf16[4,96,384]{2,1,0:T(8,128)(2,1)S(1)}, bf16[4,96,384]{2,1,0:T(8,128)(2,1)S(1)}, u32[]{:S(2)}, u32[]{:S(2)}) collective-permute-start(bf16[4,96,384]{2,1,0:T(8,128)(2,1)S(1)} %get-tuple-element.1170), channel_id=1, source_target_pairs={{24,16},{25,17},{26,18},{27,19},{28,20},{29,21},{30,22},{31,23}} | collective-permute-start | bytes 884744 | tf_op jit(solution)/shard_map/ppermute | solution.py:160
  378.3 24.6 %collective-permute-start.57 = (bf16[4,96,384]{2,1,0:T(8,128)(2,1)S(1)}, bf16[4,96,384]{2,1,0:T(8,128)(2,1)S(1)}, u32[]{:S(2)}, u32[]{:S(2)}) collective-permute-start(bf16[4,96,384]{2,1,0:T(8,128)(2,1)S(1)} %get-tuple-element.1062), channel_id=1, source_target_pairs={{0,8},{8,16},{1,9},{9,17},{2,10},{10,18},{3,11},{11,19},{4,12},{12... | collective-permute-start | bytes 884744 | tf_op jit(solution)/shard_map/ppermute | solution.py:160
  379.6 23.2 %collective-permute-start.58 = (bf16[4,96,384]{2,1,0:T(8,128)(2,1)S(1)}, bf16[4,96,384]{2,1,0:T(8,128)(2,1)S(1)}, u32[]{:S(2)}, u32[]{:S(2)}) collective-permute-start(bf16[4,96,384]{2,1,0:T(8,128)(2,1)S(1)} %get-tuple-element.1063), channel_id=1, source_target_pairs={{24,16},{16,8},{25,17},{17,9},{26,18},{18,10},{27,19},{19,11},{28,... | collective-permute-start | bytes 884744 | tf_op jit(solution)/shard_map/ppermute | solution.py:160
  380.3 18.4 %collective-permute-start.59 = (bf16[4,48,384]{2,1,0:T(8,128)(2,1)S(1)}, bf16[4,48,384]{2,1,0:T(8,128)(2,1)S(1)}, u32[]{:S(2)}, u32[]{:S(2)}) collective-permute-start(bf16[4,48,384]{2,1,0:T(8,128)(2,1)S(1)} %get-tuple-element.1064), channel_id=1, source_target_pairs={{0,8},{8,16},{16,24},{1,9},{9,17},{17,25},{2,10},{10,18},{18,26},{... | collective-permute-start | bytes 442376 | tf_op jit(solution)/shard_map/ppermute | solution.py:160
  387.7 15.1 %collective-permute-start.60 = (bf16[4,48,384]{2,1,0:T(8,128)(2,1)S(1)}, bf16[4,48,384]{2,1,0:T(8,128)(2,1)S(1)}, u32[]{:S(2)}, u32[]{:S(2)}) collective-permute-start(bf16[4,48,384]{2,1,0:T(8,128)(2,1)S(1)} %get-tuple-element.1065), channel_id=1, source_target_pairs={{24,16},{16,8},{8,0},{25,17},{17,9},{9,1},{26,18},{18,10},{10,2},{... | collective-permute-start | bytes 442376 | tf_op jit(solution)/shard_map/ppermute | solution.py:160
  403.6 41.0 %collective-permute-start.61 = (bf16[512,768]{1,0:T(8,128)(2,1)}, bf16[512,768]{1,0:T(8,128)(2,1)S(1)}, u32[]{:S(2)}, u32[]{:S(2)}) collective-permute-start(bf16[512,768]{1,0:T(8,128)(2,1)} %get-tuple-element.1076), channel_id=1, source_target_pairs={{0,2},{2,0},{4,6},{6,4},{1,3},{3,1},{5,7},{7,5},{8,10},{10,8},{12,... | collective-permute-start | bytes 2359304 | tf_op jit(solution)/shard_map/ppermute | solution.py:32
  404.9 39.7 %collective-permute-start.62 = (bf16[512,768]{1,0:T(8,128)(2,1)}, bf16[512,768]{1,0:T(8,128)(2,1)}, u32[]{:S(2)}, u32[]{:S(2)}) collective-permute-start(bf16[512,768]{1,0:T(8,128)(2,1)} %get-tuple-element.1078), channel_id=1, source_target_pairs={{0,4},{2,6},{4,0},{6,2},{1,5},{3,7},{5,1},{7,3},{8,12},{10,14},{12... | collective-permute-start | bytes 2359304 | tf_op jit(solution)/shard_map/ppermute | solution.py:32
  408.0 25.9 %collective-permute-start.63 = (bf16[4,96,384]{2,1,0:T(8,128)(2,1)}, bf16[4,96,384]{2,1,0:T(8,128)(2,1)S(1)}, u32[]{:S(2)}, u32[]{:S(2)}) collective-permute-start(bf16[4,96,384]{2,1,0:T(8,128)(2,1)} %get-tuple-element.1085), channel_id=1, source_target_pairs={{0,8},{8,16},{16,24},{1,9},{9,17},{17,25},{2,10},{10,18},{18,26},{... | collective-permute-start | bytes 884744 | tf_op jit(solution)/shard_map/ppermute | solution.py:160
  423.0 21.5 %collective-permute-start.64 = (bf16[4,96,384]{2,1,0:T(8,128)(2,1)}, bf16[4,96,384]{2,1,0:T(8,128)(2,1)}, u32[]{:S(2)}, u32[]{:S(2)}) collective-permute-start(bf16[4,96,384]{2,1,0:T(8,128)(2,1)} %get-tuple-element.1086), channel_id=1, source_target_pairs={{24,16},{16,8},{8,0},{25,17},{17,9},{9,1},{26,18},{18,10},{10,2},{... | collective-permute-start | bytes 884744 | tf_op jit(solution)/shard_map/ppermute | solution.py:160
  447.0 15.0 %collective-permute-start.66 = (bf16[512,384]{1,0:T(8,128)(2,1)S(1)}, bf16[512,384]{1,0:T(8,128)(2,1)S(1)}, u32[]{:S(2)}, u32[]{:S(2)}) collective-permute-start(bf16[512,384]{1,0:T(8,128)(2,1)S(1)} %add_convert_fusion.3), channel_id=1, source_target_pairs={{0,4},{2,6},{4,0},{6,2},{1,5},{3,7},{5,1},{7,3},{8,12},{10,14},{12... | collective-permute-start | bytes 1179656 | tf_op jit(solution)/shard_map/ppermute | solution.py:32
  449.9 12.2 %collective-permute-start.67 = (bf16[512,384]{1,0:T(8,128)(2,1)S(1)}, bf16[512,384]{1,0:T(8,128)(2,1)S(1)}, u32[]{:S(2)}, u32[]{:S(2)}) collective-permute-start(bf16[512,384]{1,0:T(8,128)(2,1)S(1)} %add_convert_fusion.2), channel_id=1, source_target_pairs={{0,2},{2,0},{4,6},{6,4},{1,3},{3,1},{5,7},{7,5},{8,10},{10,8},{12,... | collective-permute-start | bytes 1179656 | tf_op jit(solution)/shard_map/ppermute | solution.py:32
  468.6 13.0 %collective-permute-start.73 = (bf16[4,160,384]{2,1,0:T(8,128)(2,1)S(1)}, bf16[4,160,384]{2,1,0:T(8,128)(2,1)S(1)}, u32[]{:S(2)}, u32[]{:S(2)}) collective-permute-start(bf16[4,160,384]{2,1,0:T(8,128)(2,1)S(1)} %fusion.10), channel_id=1, source_target_pairs={{0,8},{8,16},{16,24},{1,9},{9,17},{17,25},{2,10},{10,18},{18,26},{... | collective-permute-start | bytes 1474568 | tf_op jit(solution)/shard_map/ppermute | solution.py:179
  470.0 18.4 %collective-permute-start.74 = (bf16[4,160,384]{2,1,0:T(8,128)(2,1)S(1)}, bf16[4,160,384]{2,1,0:T(8,128)(2,1)S(1)}, u32[]{:S(2)}, u32[]{:S(2)}) collective-permute-start(bf16[4,160,384]{2,1,0:T(8,128)(2,1)S(1)} %fusion.10), channel_id=1, source_target_pairs={{24,16},{16,8},{8,0},{25,17},{17,9},{9,1},{26,18},{18,10},{10,2},{... | collective-permute-start | bytes 1474568 | tf_op jit(solution)/shard_map/ppermute | solution.py:180
  488.4 12.0 %collective-permute-start.75 = (bf16[4,160,384]{2,1,0:T(8,128)(2,1)S(1)}, bf16[4,160,384]{2,1,0:T(8,128)(2,1)}, u32[]{:S(2)}, u32[]{:S(2)}) collective-permute-start(bf16[4,160,384]{2,1,0:T(8,128)(2,1)S(1)} %collective-permute-done.73), channel_id=1, source_target_pairs={{8,16},{16,24},{9,17},{17,25},{10,18},{18,26},{11,19},{19,27},{12,... | collective-permute-start | bytes 1474568 | tf_op jit(solution)/shard_map/ppermute | solution.py:179
  489.8 15.4 %collective-permute-start.76 = (bf16[4,160,384]{2,1,0:T(8,128)(2,1)S(1)}, bf16[4,160,384]{2,1,0:T(8,128)(2,1)S(1)}, u32[]{:S(2)}, u32[]{:S(2)}) collective-permute-start(bf16[4,160,384]{2,1,0:T(8,128)(2,1)S(1)} %collective-permute-done.74), channel_id=1, source_target_pairs={{16,8},{8,0},{17,9},{9,1},{18,10},{10,2},{19,11},{11,3},{20,12},{1... | collective-permute-start | bytes 1474568 | tf_op jit(solution)/shard_map/ppermute | solution.py:180
  505.9 14.0 %collective-permute-start.78 = (bf16[4,160,384]{2,1,0:T(8,128)(2,1)S(1)}, bf16[4,160,384]{2,1,0:T(8,128)(2,1)S(1)}, u32[]{:S(2)}, u32[]{:S(2)}) collective-permute-start(bf16[4,160,384]{2,1,0:T(8,128)(2,1)S(1)} %collective-permute-done.76), channel_id=1, source_target_pairs={{8,0},{9,1},{10,2},{11,3},{12,4},{13,5},{14,6},{15,7}} | collective-permute-start | bytes 1474568 | tf_op jit(solution)/shard_map/ppermute | solution.py:180
  (116 other events, 1039.0 us)
Sparse Core Ops, SparseCore 0:
  265.2 91.1 reduce-scatter.1
  375.9 106.4 all-gather.2

commit v5 on v4

--- a/solution.py
+++ b/solution.py
@@ -412,7 +412,14 @@
         return carry
 
     lax.fori_loop(first, whole_from, masked, 0)
-    lax.fori_loop(whole_from, block, plain, 0)
+    def both(pair, carry):
+        step(whole_from + 2 * pair, False)
+        step(whole_from + 2 * pair + 1, False)
+        return carry
+
+    pairs = (block - whole_from) // 2
+    lax.fori_loop(0, pairs, both, 0)
+    lax.fori_loop(whole_from + 2 * pairs, block, plain, 0)
     step(block, True)
 
 
@@ -951,7 +958,7 @@
     del live.mixer_one, live.mixer_own, live.lengths
     live.sync()
 
-    live.od_one = fetch_one(live.od_halves)
+    live.gu_one = fetch_one(live.gu_halves)
     live.w_own = dot(fetched(*live.mixer, place).reshape(model, 4 * HEAD), spread).astype(LOW)
     live.w_oth = other(live.w_own)
     cos_own = lax.dynamic_slice_in_dim(live.cos, core * half, half, 0)
@@ -959,35 +966,35 @@
     live.first, live.r1, live.qkv, live.send = project(
         live.xs, live.w_own, live.w_oth, cos_own, sin_own
     )
-    del live.mixer, live.od_halves
-    live.sync()
-    halves, send, live.od_mine = ready(live.gu_halves, live.send, jnp.stack(live.od_one))
-    live.od_theirs = fetch_two(live.od_mine, blocks)
-    live.gu_one = fetch_one(halves)
+    del live.mixer, live.gu_halves
+    live.sync()
+    halves, send, live.gu_mine = ready(live.od_halves, live.send, jnp.stack(live.gu_one))
+    live.gu_theirs = fetch_two(live.gu_mine, blocks)
+    live.od_one = fetch_one(halves)
     live.qkv_got = other(send)
     live.keep, live.send, live.attended, live.lse = attend(live.info, live.qkv, live.qkv_got, live.start)
-    del live.od_one, live.gu_halves
+    del live.gu_one, live.od_halves
     live.sync()
     live.heads = jnp.concatenate([live.keep, other(live.send)], axis=1)
-    live.gu_mine = jnp.stack(live.gu_one)
-    del live.keep, live.send, live.gu_one
-    live.sync()
-
-    live.gu_theirs = fetch_two(live.gu_mine, blocks)
+    live.od_mine = jnp.stack(live.od_one)
+    del live.keep, live.send, live.od_one
+    live.sync()
+
+    live.od_theirs = fetch_two(live.od_mine, blocks)
     live.heads = gather_one(live.heads)
     live.cots = gather_one(live.cot)
-    live.od_own = fetched(live.od_own, live.od_mine, live.od_theirs, place)
-    del live.od_mine, live.od_theirs
+    live.gu_own = fetched(live.gu_own, live.gu_mine, live.gu_theirs, place).reshape(model, 2 * units)
+    del live.gu_mine, live.gu_theirs
     live.sync()
 
     halves, more = ready(gather_halves(live.heads), gather_halves(live.cots))
     live.heads = gather_two(live.heads, halves)
     live.cots = gather_two(live.cots, more)
+    live.od_own = fetched(live.od_own, live.od_mine, live.od_theirs, place)
     od_oth = other(live.od_own)
     live.out_full, live.out_mine = order(row_info, live.od_own[:, :rows], od_oth[:, :rows])
     live.d_own, live.d_oth = live.od_own[:, rows:], od_oth[:, rows:]
-    live.gu_own = fetched(live.gu_own, live.gu_mine, live.gu_theirs, place).reshape(model, 2 * units)
-    del live.od_own, live.gu_mine, live.gu_theirs
+    del live.od_own, live.od_mine, live.od_theirs
     live.sync()
     live.gu_oth = other(live.gu_own)
     live.cot_all = join(live.cots)

time: 537 us -> 530 us (0.987)
  waiting for transfers between devices: 162 us -> 148 us
    ppermute x3, waiting for transfers between devices: 12.2 us -> 1.71 us  [pair(): return lax.ppermute(value, 'dp', [(i, i ^ 1) for i in range(count)])]
    unnamed x198 -> x196, local copies, waits for them, and re-layouts: 23.7 us -> 22.9 us
  transfers between devices with their start and end apart: 81 -> 81, of which waited for: 35 -> 36; matrix products, arithmetic and copies ran while one was open for 14% -> 13% of each run, Pallas kernels for 20% -> 21%
where the time goes in v5:
time: 530 us; the launch traced here: 524 us
  waiting for transfers between devices  148 us (28%)
  Pallas kernels  141 us (27%)
  starting transfers between devices  105 us (20%)
  other arithmetic  54.5 us (10%)
  local copies, waits for them, and re-layouts  51.5 us (10%)
  between operations  18.1 us (3%)
    ppermute x47, waiting for transfers between devices, swap(): return lax.ppermute(value, 'row', [(i, i ^ step) for i in range(4)])  90.8 us
    ppermute x47, starting transfers between devices, swap(): return lax.ppermute(value, 'row', [(i, i ^ step) for i in range(4)])  52 us
    ppermute x6, starting transfers between devices, chain_sum(): lax.ppermute(up, 'dp', chain_up(count, 0, last))  32.4 us
    pallas_call x3, Pallas kernels, partial_sums(): call(functools.partial(partial_kernel, blocked), tuple(outs), specs, tupl...  27.8 us
    unnamed x196, local copies, waits for them, and re-layouts  22.9 us
    pallas_call x1, Pallas kernels, attend_back(): call(attend_back_kernel, outs, [whole(own), whole(oth), whole(g_own), who...  20.2 us
    ppermute x3, waiting for transfers between devices, chain_spread(): down = lax.ppermute(down, 'dp', chain_down(count, step - 1, count - 1))  18.8 us
    pallas_call x2, Pallas kernels, feed_grads(): call(feed_grads_kernel, out, [block, block, whole(back), whole(hidden)],...  17.2 us
  transfers between devices with their start and end apart: 81, of which 36 were waited for; matrix products, arithmetic and copies ran while one was open for 13% of the time, Pallas kernels for 21%

profile of v5, /device:TPU:0, one launch (start us, length us, event | category | flops | bytes accessed | tf_op | source)
XLA Modules:
  0.0 523.6 jit_solution(6487518672525698104)
XLA Ops:
  7.2 3.0 collective-permute-start.3
  22.6 2.9 collective-permute-start.2
  25.6 3.5 multiply_convert_fusion.1
  31.4 2.1 pad_maximum_fusion.6
  35.6 2.3 fusion.11
  46.2 6.1 %fusion.7 = (f32[2048,128]{1,0:T(8,128)}, f32[2048,128]{1,0:T(8,128)}) fusion(f32[128]{0:T(128)S(1)} %get-tuple-element.1213, f32[128]{0:T(128)S(1)} %get-tuple-element.1214, f32[2048]{0:T(1024)S(1)} %get-tuple-element.1211, pred[128]{0:T(512)(128)(4,1)S(1)} %broadcast_compare_fusion), kind=kLoop, calls=%fused_computation.26 | loop fusion | flops 1048576 | bytes 2106496 | tf_op jit(solution)/shard_map/jit(_where)/select_n | solution.py:889
  52.3 1.9 collective-permute-done.6.top.refs_8_
  54.7 2.2 convolution_convert_fusion.w_own
  62.7 8.1 %shard_map.204 = (bf16[1024,1536]{1,0:T(8,128)(2,1)}, f32[1024,128]{1,0:T(8,128)S(1)}, bf16[1024,512]{1,0:T(8,128)(2,1)S(1)}, bf16[1024,512]{1,0:T(8,128)(2,1)}) custom-call(bf16[1024,384]{1,0:T(8,128)(2,1)S(1)} %copy-done.6, bf16[1024,384]{1,0:T(8,128)(2,1)S(1)} %collective-permute-done.3.x1.refs_6_, ...), custom_call_target="tpu_custom_call" | custom-call | flops 50331648 | bytes 188416 | tf_op jit(solution)/shard_map/pallas_call | solution.py:374
  70.8 6.4 %collective-permute-done.10 = bf16[192,1024]{1,0:T(8,128)(2,1)} collective-permute-done((bf16[192,1024]{1,0:T(8,128)(2,1)}, bf16[192,1024]{1,0:T(8,128)(2,1)}, u32[]{:S(2)}, u32[]{:S(2)}) %collective-permute-start.10) | collective-permute-done | bytes 393248 | tf_op jit(solution)/shard_map/ppermute | solution.py:32
  82.4 2.1 collective-permute-start.16
  84.5 16.7 %shard_map.205 = (bf16[1024,192]{1,0:T(8,128)(2,1)S(1)}, bf16[1024,192]{1,0:T(8,128)(2,1)S(1)}, bf16[2048,256]{1,0:T(8,128)(2,1)S(1)}, f32[1,4096]{1,0:T(1,128)S(1)}) custom-call(s32[17]{0:T(128)S(1)} %pad_add_fusion.info, bf16[1024,512]{1,0:T(8,128)(2,1)S(1)} %get-tuple-element.963.own, bf16[1024,512]{1,0:T(8,128)(2,1)S(1)} %collective-permute-done.12.oth, ...), custom_call_target="tpu_custom_call" | custom-call | flops 67108864 | bytes 61696 | tf_op jit(solution)/shard_map/pallas_call | solution.py:481
  101.2 4.3 collective-permute-done.16
  105.5 1.7 collective-permute-done.13
  117.7 13.3 %collective-permute-done.18.x1 = bf16[1024,384]{1,0:T(8,128)(2,1)S(1)} collective-permute-done((bf16[1024,384]{1,0:T(8,128)(2,1)S(1)}, bf16[1024,384]{1,0:T(8,128)(2,1)S(1)}, u32[]{:S(2)}, u32[]{:S(2)}) %collective-permute-start.18) | collective-permute-done | bytes 786464 | tf_op jit(solution)/shard_map/ppermute | solution.py:32
  131.6 15.2 %collective-permute-done.20.refs_1_ = bf16[1024,384]{1,0:T(8,128)(2,1)} collective-permute-done((bf16[1024,384]{1,0:T(8,128)(2,1)S(1)}, bf16[1024,384]{1,0:T(8,128)(2,1)}, u32[]{:S(2)}, u32[]{:S(2)}) %collective-permute-start.20) | collective-permute-done | bytes 786464 | tf_op jit(solution)/shard_map/ppermute | solution.py:32
  147.5 1.7 constant_dynamic-update-slice_fusion.1
  149.2 1.7 constant_dynamic-update-slice_fusion
  157.7 2.0 copy-done.70
  161.3 4.2 shard_map.206
  166.8 1.7 slice.317.d_oth.w_oth
  168.5 4.6 collective-permute-done.26.refs_3_
  174.2 1.9 shard_map.208.cot
  177.0 10.3 %shard_map.207 = (bf16[1024,1536]{1,0:T(8,128)(2,1)}, f32[1024,384]{1,0:T(8,128)}, f32[1024,128]{1,0:T(8,128)S(1)}, bf16[1024,1536]{1,0:T(8,128)(2,1)}) custom-call(bf16[1024,384]{1,0:T(8,128)(2,1)S(1)} %copy-done.31, bf16[1024,384]{1,0:T(8,128)(2,1)} %collective-permute-done.20.refs_1_, bf16[1024,384]{1,0:T(8,128)(2,1)} %collective-permute-done.21.refs_2_, ...), custom_call_target="tpu_custom_call" | custom-call | flops 75497472 | bytes 303104 | tf_op jit(solution)/shard_map/pallas_call | solution.py:625
  187.4 17.2 %shard_map.209 = (bf16[1024,512]{1,0:T(8,128)(2,1)S(1)}, bf16[1024,512]{1,0:T(8,128)(2,1)S(1)}, bf16[1024,1024]{1,0:T(8,128)(2,1)}, bf16[1024,1024]{1,0:T(8,128)(2,1)}) custom-call(bf16[1024,1536]{1,0:T(8,128)(2,1)} %get-tuple-element.807.second.rest_0_, bf16[1024,1536]{1,0:T(8,128)(2,1)} %shard_map.208.cot, bf16[1536,1024]{1,0:T(8,128)(2,1)} %bitcast.104, ...), custom_call_target="tpu_custom_call" | custom-call | flops 150994944 | bytes 344064 | tf_op jit(solution)/shard_map/pallas_call | solution.py:675
  204.6 2.3 copy-done.4
  207.0 11.3 %shard_map.210 = (bf16[1024,384]{1,0:T(8,128)(2,1)S(1)}, bf16[512,768]{1,0:T(8,128)(2,1)S(1)}, bf16[512,384]{1,0:T(8,128)(2,1)S(1)}, bf16[512,768]{1,0:T(8,128)(...) custom-call(bf16[1024,1024]{1,0:T(8,128)(2,1)S(1)} %copy-done.4, ...), custom_call_target="tpu_custom_call" | custom-call | flops 100663296 | bytes 270336 | tf_op jit(solution)/shard_map/pallas_call | solution.py:747
  221.4 8.6 %shard_map.212 = bf16[4,4,96,1536]{3,2,1,0:T(8,128)(2,1)} custom-call(bf16[1024,1536]{1,0:T(8,128)(2,1)} %get-tuple-element.807.second.rest_0_, bf16[1024,1536]{1,0:T(8,128)(2,1)} %shard_map.208.cot, bf16[1024,1024]{1,0:T(8,128)(2,1)S(1)} %copy-done.5, bf16[1024,512]{1,0:T(8,128)(2,1)S(1)} %get-tuple-element.882.hidden.a_own), custom_call_target="tpu_custom_call" | custom-call | flops 75497472 | bytes 221184 | tf_op jit(solution)/shard_map/pallas_call | solution.py:772
  230.0 8.6 %shard_map.211 = bf16[4,4,96,1536]{3,2,1,0:T(8,128)(2,1)} custom-call(bf16[1024,1536]{1,0:T(8,128)(2,1)} %get-tuple-element.807.second.rest_0_, bf16[1024,1536]{1,0:T(8,128)(2,1)} %shard_map.208.cot, bf16[1024,1024]{1,0:T(8,128)(2,1)S(1)} %copy-done.3, bf16[1024,512]{1,0:T(8,128)(2,1)S(1)} %get-tuple-element.883.hidden.a_oth), custom_call_target="tpu_custom_call" | custom-call | flops 75497472 | bytes 221184 | tf_op jit(solution)/shard_map/pallas_call | solution.py:772
  242.6 8.2 %collective-permute-done.35 = f32[8,128]{1,0:T(8,128)S(1)} collective-permute-done((f32[8,128]{1,0:T(8,128)S(1)}, f32[8,128]{1,0:T(8,128)S(1)}, u32[]{:S(2)}, u32[]{:S(2)}) %collective-permute-start.35) | collective-permute-done | bytes 4128 | tf_op jit(solution)/shard_map/ppermute | solution.py:32
  252.2 6.1 %add_convert_fusion = bf16[4,4,96,1536]{3,2,1,0:T(8,128)(2,1)} fusion(bf16[4,4,96,1536]{3,2,1,0:T(8,128)(2,1)S(1)} %collective-permute-done.32, bf16[4,4,96,1536]{3,2,1,0:T(8,128)(2,1)} %shard_map.212), kind=kLoop, calls=%fused_computation | loop fusion | flops 9437184 | bytes 14155776 | tf_op jit(solution)/shard_map/convert_element_type | solution.py:1013
  266.1 8.6 %shard_map.213 = (bf16[1024,384]{1,0:T(8,128)(2,1)S(1)}, bf16[512,768]{1,0:T(8,128)(2,1)}, bf16[512,384]{1,0:T(8,128)(2,1)S(1)}, bf16[512,768]{1,0:T(8,128)(2,1)}, bf16[512,384]{1,0:T(8,128)(2,1)S(1)}) custom-call(bf16[1024,512]{1,0:T(8,128)(2,1)S(1)} %copy-done.16, bf16[1024,512]{1,0:T(8,128)(2,1)S(1)} %copy-done.18, bf16[4,512,384]{2,1,0:T(8,128)(2,1)} %copy-done.1, ...), custom_call_target="tpu_custom_call" | custom-call | flops 50331648 | bytes 131072 | tf_op jit(solution)/shard_map/pallas_call | solution.py:747
  274.7 7.3 %collective-permute-done.36.x1 = bf16[1024,384]{1,0:T(8,128)(2,1)S(1)} collective-permute-done((bf16[1024,384]{1,0:T(8,128)(2,1)S(1)}, bf16[1024,384]{1,0:T(8,128)(2,1)S(1)}, u32[]{:S(2)}, u32[]{:S(2)}) %collective-permute-start.36) | collective-permute-done | bytes 786464 | tf_op jit(solution)/shard_map/ppermute | solution.py:32
  284.9 1.8 convolution_convert_fusion.1
  286.8 5.9 %collective-permute-done.38.top = bf16[512,384]{1,0:T(8,128)(2,1)S(1)} collective-permute-done((bf16[512,384]{1,0:T(8,128)(2,1)S(1)}, bf16[512,384]{1,0:T(8,128)(2,1)S(1)}, u32[]{:S(2)}, u32[]{:S(2)}) %collective-permute-start.38) | collective-permute-done | bytes 393248 | tf_op jit(solution)/shard_map/ppermute | solution.py:32
  293.3 2.5 shard_map.214
  299.7 1.8 constant_dynamic-slice_fusion.2
  301.4 3.1 collective-permute-start.44
  305.9 20.2 %shard_map.215 = (bf16[1024,512]{1,0:T(8,128)(2,1)S(1)}, bf16[1024,512]{1,0:T(8,128)(2,1)S(1)}) custom-call(s32[17]{0:T(128)S(1)} %pad_add_fusion.info, bf16[1024,512]{1,0:T(8,128)(2,1)S(1)} %copy-done.20, bf16[1024,512]{1,0:T(8,128)(2,1)S(1)} %copy-done.22, bf16[1024,256]{1,0:T(8,128)(2,1)S(1)} %get-tuple-element.965.g_own, ...), custom_call_target="tpu_custom_call" | custom-call | flops 167772160 | bytes 98304 | tf_op jit(solution)/shard_map/pallas_call | solution.py:572
  334.7 3.5 shard_map.217
  338.3 4.3 shard_map.216
  344.7 4.6 reduce-scatter.2.cloned.1.call-done
  357.6 3.0 collective-permute-done.51
  360.6 6.2 %collective-permute-done.52 = bf16[96,1536]{1,0:T(8,128)(2,1)S(1)} collective-permute-done((bf16[96,1536]{1,0:T(8,128)(2,1)S(1)}, bf16[96,1536]{1,0:T(8,128)(2,1)S(1)}, u32[]{:S(2)}, u32[]{:S(2)}) %collective-permute-start.52) | collective-permute-done | bytes 294944 | tf_op jit(solution)/shard_map/ppermute | solution.py:32
  373.5 7.4 %collective-permute-start.59 = (bf16[4,48,384]{2,1,0:T(8,128)(2,1)S(1)}, bf16[4,48,384]{2,1,0:T(8,128)(2,1)S(1)}, u32[]{:S(2)}, u32[]{:S(2)}) collective-permute-start(bf16[4,48,384]{2,1,0:T(8,128)(2,1)S(1)} %get-tuple-element.1064), channel_id=1, source_target_pairs={{0,8},{8,16},{16,24},{1,9},{9,17},{17,25},{2,10},{10,18},{18,26},{... | collective-permute-start | bytes 442376 | tf_op jit(solution)/shard_map/ppermute | solution.py:160
  382.2 7.9 %shard_map.218 = (bf16[1024,384]{1,0:T(8,128)(2,1)S(1)}, bf16[512,768]{1,0:T(8,128)(2,1)}, bf16[512,384]{1,0:T(8,128)(2,1)S(1)}, bf16[512,768]{1,0:T(8,128)(2,1)...) custom-call(bf16[1024,512]{1,0:T(8,128)(2,1)S(1)} %copy-done.24, bf16[1024,512]{1,0:T(8,128)(2,1)S(1)} %copy-done.26, ...), custom_call_target="tpu_custom_call" | custom-call | flops 50331648 | bytes 188416 | tf_op jit(solution)/shard_map/pallas_call | solution.py:747
  391.6 4.4 collective-permute-done.60
  398.9 2.2 add_convert_fusion.9
  401.1 18.0 %collective-permute-start.63 = (bf16[4,96,384]{2,1,0:T(8,128)(2,1)}, bf16[4,96,384]{2,1,0:T(8,128)(2,1)S(1)}, u32[]{:S(2)}, u32[]{:S(2)}) collective-permute-start(bf16[4,96,384]{2,1,0:T(8,128)(2,1)} %get-tuple-element.1085), channel_id=1, source_target_pairs={{0,8},{8,16},{16,24},{1,9},{9,17},{17,25},{2,10},{10,18},{18,26},{... | collective-permute-start | bytes 884744 | tf_op jit(solution)/shard_map/ppermute | solution.py:160
  422.4 1.7 collective-permute-done.65
  424.1 5.8 %collective-permute-done.63 = bf16[4,96,384]{2,1,0:T(8,128)(2,1)S(1)} collective-permute-done((bf16[4,96,384]{2,1,0:T(8,128)(2,1)}, bf16[4,96,384]{2,1,0:T(8,128)(2,1)S(1)}, u32[]{:S(2)}, u32[]{:S(2)}) %collective-permute-start.63) | collective-permute-done | bytes 294944 | tf_op jit(solution)/shard_map/ppermute | solution.py:160
  429.9 10.9 %collective-permute-done.64 = bf16[4,96,384]{2,1,0:T(8,128)(2,1)} collective-permute-done((bf16[4,96,384]{2,1,0:T(8,128)(2,1)}, bf16[4,96,384]{2,1,0:T(8,128)(2,1)}, u32[]{:S(2)}, u32[]{:S(2)}) %collective-permute-start.64) | collective-permute-done | bytes 294944 | tf_op jit(solution)/shard_map/ppermute | solution.py:160
  447.5 2.1 collective-permute-start.70
  449.5 3.9 collective-permute-done.68
  454.2 2.8 collective-permute-done.71
  458.5 1.7 convert_add_fusion.2
  463.6 3.9 collective-permute-start.73
  469.0 9.3 %collective-permute-done.73 = bf16[4,160,384]{2,1,0:T(8,128)(2,1)S(1)} collective-permute-done((bf16[4,160,384]{2,1,0:T(8,128)(2,1)S(1)}, bf16[4,160,384]{2,1,0:T(8,128)(2,1)S(1)}, u32[]{:S(2)}, u32[]{:S(2)}) %collective-permute-start.73) | collective-permute-done | bytes 491552 | tf_op jit(solution)/shard_map/ppermute | solution.py:179
  478.2 4.3 collective-permute-done.74
  487.9 2.3 copy-done.12
  490.3 4.2 shard_map.219
  494.5 3.9 collective-permute-done.76
  502.1 10.6 %collective-permute-done.78 = bf16[4,160,384]{2,1,0:T(8,128)(2,1)S(1)} collective-permute-done((bf16[4,160,384]{2,1,0:T(8,128)(2,1)S(1)}, bf16[4,160,384]{2,1,0:T(8,128)(2,1)S(1)}, u32[]{:S(2)}, u32[]{:S(2)}) %collective-permute-start.78) | collective-permute-done | bytes 491552 | tf_op jit(solution)/shard_map/ppermute | solution.py:180
  513.6 2.7 shard_map.220
  (432 shorter events, 140.6 us)
Async XLA Ops:
  7.2 342.2 %reduce-scatter.2.cloned.1.call-start = ((), (), s32[]{:S(2)}) async-start(), calls=%async_computation.1 | async-start | bytes 5898240 | tf_op jit(solution)/shard_map/reduce_scatter | solution.py:1039
  7.2 30.7 %collective-permute-start.3 = (bf16[1024,384]{1,0:T(8,128)(2,1)}, bf16[1024,384]{1,0:T(8,128)(2,1)S(1)}, u32[]{:S(2)}, u32[]{:S(2)}) collective-permute-start(bf16[1024,384]{1,0:T(8,128)(2,1)} %refs_5_), channel_id=1, source_target_pairs={{0,2},{2,0},{4,6},{6,4},{1,3},{3,1},{5,7},{7,5},{8,10},{10,8},{12,... | collective-permute-start | bytes 2359304 | tf_op jit(solution)/shard_map/ppermute | solution.py:32
  10.2 27.8 %collective-permute-start.4 = (bf16[1024,384]{1,0:T(8,128)(2,1)}, bf16[1024,384]{1,0:T(8,128)(2,1)S(1)}, u32[]{:S(2)}, u32[]{:S(2)}) collective-permute-start(bf16[1024,384]{1,0:T(8,128)(2,1)} %refs_5_), channel_id=1, source_target_pairs={{0,4},{2,6},{4,0},{6,2},{1,5},{3,7},{5,1},{7,3},{8,12},{10,14},{12... | collective-permute-start | bytes 2359304 | tf_op jit(solution)/shard_map/ppermute | solution.py:32
  22.0 16.0 %collective-permute-start = (bf16[192,384]{1,0:T(8,128)(2,1)}, bf16[192,384]{1,0:T(8,128)(2,1)S(1)}, u32[]{:S(2)}, u32[]{:S(2)}) collective-permute-start(bf16[192,384]{1,0:T(8,128)(2,1)} %dynamic-slice_bitcast_fusion.2), channel_id=1, source_target_pairs={{0,2},{2,0},{4,6},{6,4},{1,3},{3,1},{5,7},{7,5},{8,10},{10,8},{12,... | collective-permute-start | bytes 442376 | tf_op jit(solution)/shard_map/ppermute | solution.py:32
  22.5 15.4 %collective-permute-start.1 = (bf16[192,384]{1,0:T(8,128)(2,1)}, bf16[192,384]{1,0:T(8,128)(2,1)}, u32[]{:S(2)}, u32[]{:S(2)}) collective-permute-start(bf16[192,384]{1,0:T(8,128)(2,1)} %dynamic-slice_bitcast_fusion.1), channel_id=1, source_target_pairs={{0,4},{2,6},{4,0},{6,2},{1,5},{3,7},{5,1},{7,3},{8,12},{10,14},{12... | collective-permute-start | bytes 442376 | tf_op jit(solution)/shard_map/ppermute | solution.py:32
  22.6 15.4 %collective-permute-start.2 = (bf16[192,384]{1,0:T(8,128)(2,1)}, bf16[192,384]{1,0:T(8,128)(2,1)}, u32[]{:S(2)}, u32[]{:S(2)}) collective-permute-start(bf16[192,384]{1,0:T(8,128)(2,1)} %dynamic-slice_bitcast_fusion), channel_id=1, source_target_pairs={{0,6},{2,4},{4,2},{6,0},{1,7},{3,5},{5,3},{7,1},{8,14},{10,12},{12... | collective-permute-start | bytes 442376 | tf_op jit(solution)/shard_map/ppermute | solution.py:32
  43.4 11.0 %collective-permute-start.5 = (bf16[3,192,384]{2,1,0:T(8,128)(2,1)S(1)}, bf16[3,192,384]{2,1,0:T(8,128)(2,1)S(1)}, u32[]{:S(2)}, u32[]{:S(2)}) collective-permute-start(bf16[3,192,384]{2,1,0:T(8,128)(2,1)S(1)} %pad_maximum_fusion.8), channel_id=1, source_target_pairs={{0,8},{8,0},{16,24},{24,16},{1,9},{9,1},{17,25},{25,17},{2,10},{10... | collective-permute-start | bytes 1327112 | tf_op jit(solution)/shard_map/ppermute | solution.py:40
  45.0 9.2 %collective-permute-start.6 = (bf16[512,384]{1,0:T(8,128)(2,1)S(1)}, bf16[512,384]{1,0:T(8,128)(2,1)S(1)}, u32[]{:S(2)}, u32[]{:S(2)}) collective-permute-start(bf16[512,384]{1,0:T(8,128)(2,1)S(1)} %slice.250), channel_id=1, source_target_pairs={{0,4},{2,6},{4,0},{6,2},{1,5},{3,7},{5,1},{7,3},{8,12},{10,14},{12... | collective-permute-start | bytes 1179656 | tf_op jit(solution)/shard_map/ppermute | solution.py:32
  57.0 20.3 %collective-permute-start.10 = (bf16[192,1024]{1,0:T(8,128)(2,1)}, bf16[192,1024]{1,0:T(8,128)(2,1)}, u32[]{:S(2)}, u32[]{:S(2)}) collective-permute-start(bf16[192,1024]{1,0:T(8,128)(2,1)} %fusion.15), channel_id=1, source_target_pairs={{0,4},{2,6},{4,0},{6,2},{1,5},{3,7},{5,1},{7,3},{8,12},{10,14},{12... | collective-permute-start | bytes 1179656 | tf_op jit(solution)/shard_map/ppermute | solution.py:32
  58.5 18.8 %collective-permute-start.11 = (bf16[192,1024]{1,0:T(8,128)(2,1)}, bf16[192,1024]{1,0:T(8,128)(2,1)}, u32[]{:S(2)}, u32[]{:S(2)}) collective-permute-start(bf16[192,1024]{1,0:T(8,128)(2,1)} %fusion.14), channel_id=1, source_target_pairs={{0,6},{2,4},{4,2},{6,0},{1,7},{3,5},{5,3},{7,1},{8,14},{10,12},{12... | collective-permute-start | bytes 1179656 | tf_op jit(solution)/shard_map/ppermute | solution.py:32
  59.0 19.5 %collective-permute-start.9 = (bf16[192,1024]{1,0:T(8,128)(2,1)}, bf16[192,1024]{1,0:T(8,128)(2,1)}, u32[]{:S(2)}, u32[]{:S(2)}) collective-permute-start(bf16[192,1024]{1,0:T(8,128)(2,1)} %fusion.16), channel_id=1, source_target_pairs={{0,2},{2,0},{4,6},{6,4},{1,3},{3,1},{5,7},{7,5},{8,10},{10,8},{12,... | collective-permute-start | bytes 1179656 | tf_op jit(solution)/shard_map/ppermute | solution.py:32
  79.9 27.3 %collective-permute-start.13 = (bf16[3,192,1024]{2,1,0:T(8,128)(2,1)S(1)}, bf16[3,192,1024]{2,1,0:T(8,128)(2,1)S(1)}, u32[]{:S(2)}, u32[]{:S(2)}) collective-permute-start(bf16[3,192,1024]{2,1,0:T(8,128)(2,1)S(1)} %pad_maximum_fusion.3), channel_id=1, source_target_pairs={{0,8},{8,0},{16,24},{24,16},{1,9},{9,1},{17,25},{25,17},{2,10},{10... | collective-permute-start | bytes 3538952 | tf_op jit(solution)/shard_map/ppermute | solution.py:40
  81.0 20.2 %collective-permute-start.14 = (bf16[640,384]{1,0:T(8,128)(2,1)S(1)}, bf16[640,384]{1,0:T(8,128)(2,1)S(1)}, u32[]{:S(2)}, u32[]{:S(2)}) collective-permute-start(bf16[640,384]{1,0:T(8,128)(2,1)S(1)} %copy-done.80), channel_id=1, source_target_pairs={{0,2},{2,0},{4,6},{6,4},{1,3},{3,1},{5,7},{7,5},{8,10},{10,8},{12,... | collective-permute-start | bytes 1474568 | tf_op jit(solution)/shard_map/ppermute | solution.py:32
  81.6 19.7 %collective-permute-start.15 = (bf16[640,384]{1,0:T(8,128)(2,1)S(1)}, bf16[640,384]{1,0:T(8,128)(2,1)S(1)}, u32[]{:S(2)}, u32[]{:S(2)}) collective-permute-start(bf16[640,384]{1,0:T(8,128)(2,1)S(1)} %copy-done.79), channel_id=1, source_target_pairs={{0,4},{2,6},{4,0},{6,2},{1,5},{3,7},{5,1},{7,3},{8,12},{10,14},{12... | collective-permute-start | bytes 1474568 | tf_op jit(solution)/shard_map/ppermute | solution.py:32
  82.4 23.1 %collective-permute-start.16 = (bf16[640,384]{1,0:T(8,128)(2,1)S(1)}, bf16[640,384]{1,0:T(8,128)(2,1)S(1)}, u32[]{:S(2)}, u32[]{:S(2)}) collective-permute-start(bf16[640,384]{1,0:T(8,128)(2,1)S(1)} %copy-done.78), channel_id=1, source_target_pairs={{0,6},{2,4},{4,2},{6,0},{1,7},{3,5},{5,3},{7,1},{8,14},{10,12},{12... | collective-permute-start | bytes 1474568 | tf_op jit(solution)/shard_map/ppermute | solution.py:32
  109.5 37.7 %collective-permute-start.22 = (bf16[3,640,384]{2,1,0:T(8,128)(2,1)}, bf16[3,640,384]{2,1,0:T(8,128)(2,1)}, u32[]{:S(2)}, u32[]{:S(2)}) collective-permute-start(bf16[3,640,384]{2,1,0:T(8,128)(2,1)} %pad_maximum_fusion.2), channel_id=1, source_target_pairs={{0,8},{8,0},{16,24},{24,16},{1,9},{9,1},{17,25},{25,17},{2,10},{10... | collective-permute-start | bytes 4423688 | tf_op jit(solution)/shard_map/ppermute | solution.py:40
  110.6 20.4 %collective-permute-start.18 = (bf16[1024,384]{1,0:T(8,128)(2,1)S(1)}, bf16[1024,384]{1,0:T(8,128)(2,1)S(1)}, u32[]{:S(2)}, u32[]{:S(2)}) collective-permute-start(bf16[1024,384]{1,0:T(8,128)(2,1)S(1)} %copy-done.27), channel_id=1, source_target_pairs={{0,2},{2,0},{4,6},{6,4},{1,3},{3,1},{5,7},{7,5},{8,10},{10,8},{12,... | collective-permute-start | bytes 2359304 | tf_op jit(solution)/shard_map/ppermute | solution.py:32
  111.2 20.5 %collective-permute-start.19 = (bf16[1024,384]{1,0:T(8,128)(2,1)S(1)}, bf16[1024,384]{1,0:T(8,128)(2,1)S(1)}, u32[]{:S(2)}, u32[]{:S(2)}) collective-permute-start(bf16[1024,384]{1,0:T(8,128)(2,1)S(1)} %copy-done.27), channel_id=1, source_target_pairs={{0,4},{2,6},{4,0},{6,2},{1,5},{3,7},{5,1},{7,3},{8,12},{10,14},{12... | collective-permute-start | bytes 2359304 | tf_op jit(solution)/shard_map/ppermute | solution.py:32
  112.0 34.8 %collective-permute-start.20 = (bf16[1024,384]{1,0:T(8,128)(2,1)S(1)}, bf16[1024,384]{1,0:T(8,128)(2,1)}, u32[]{:S(2)}, u32[]{:S(2)}) collective-permute-start(bf16[1024,384]{1,0:T(8,128)(2,1)S(1)} %pad_maximum_fusion.7.refs_0_), channel_id=1, source_target_pairs={{0,2},{2,0},{4,6},{6,4},{1,3},{3,1},{5,7},{7,5},{8,10},{10,8},{12,... | collective-permute-start | bytes 2359304 | tf_op jit(solution)/shard_map/ppermute | solution.py:32
  113.5 33.6 %collective-permute-start.21 = (bf16[1024,384]{1,0:T(8,128)(2,1)S(1)}, bf16[1024,384]{1,0:T(8,128)(2,1)}, u32[]{:S(2)}, u32[]{:S(2)}) collective-permute-start(bf16[1024,384]{1,0:T(8,128)(2,1)S(1)} %pad_maximum_fusion.7.refs_0_), channel_id=1, source_target_pairs={{0,4},{2,6},{4,0},{6,2},{1,5},{3,7},{5,1},{7,3},{8,12},{10,14},{12... | collective-permute-start | bytes 2359304 | tf_op jit(solution)/shard_map/ppermute | solution.py:32
  153.1 15.4 %collective-permute-start.23 = (bf16[512,384]{1,0:T(8,128)(2,1)S(1)}, bf16[512,384]{1,0:T(8,128)(2,1)S(1)}, u32[]{:S(2)}, u32[]{:S(2)}) collective-permute-start(bf16[512,384]{1,0:T(8,128)(2,1)S(1)} %slice.254), channel_id=1, source_target_pairs={{0,4},{2,6},{4,0},{6,2},{1,5},{3,7},{5,1},{7,3},{8,12},{10,14},{12... | collective-permute-start | bytes 1179656 | tf_op jit(solution)/shard_map/ppermute | solution.py:32
  154.4 14.1 %collective-permute-start.24 = (bf16[512,384]{1,0:T(8,128)(2,1)S(1)}, bf16[512,384]{1,0:T(8,128)(2,1)S(1)}, u32[]{:S(2)}, u32[]{:S(2)}) collective-permute-start(bf16[512,384]{1,0:T(8,128)(2,1)S(1)} %slice.255), channel_id=1, source_target_pairs={{0,2},{2,0},{4,6},{6,4},{1,3},{3,1},{5,7},{7,5},{8,10},{10,8},{12,... | collective-permute-start | bytes 1179656 | tf_op jit(solution)/shard_map/ppermute | solution.py:32
  155.9 17.2 %collective-permute-start.26 = (bf16[512,384]{1,0:T(8,128)(2,1)S(1)}, bf16[512,384]{1,0:T(8,128)(2,1)S(1)}, u32[]{:S(2)}, u32[]{:S(2)}) collective-permute-start(bf16[512,384]{1,0:T(8,128)(2,1)S(1)} %slice.252), channel_id=1, source_target_pairs={{0,4},{2,6},{4,0},{6,2},{1,5},{3,7},{5,1},{7,3},{8,12},{10,14},{12... | collective-permute-start | bytes 1179656 | tf_op jit(solution)/shard_map/ppermute | solution.py:32
  156.7 17.4 %collective-permute-start.27 = (bf16[512,384]{1,0:T(8,128)(2,1)S(1)}, bf16[512,384]{1,0:T(8,128)(2,1)S(1)}, u32[]{:S(2)}, u32[]{:S(2)}) collective-permute-start(bf16[512,384]{1,0:T(8,128)(2,1)S(1)} %slice.253), channel_id=1, source_target_pairs={{0,2},{2,0},{4,6},{6,4},{1,3},{3,1},{5,7},{7,5},{8,10},{10,8},{12,... | collective-permute-start | bytes 1179656 | tf_op jit(solution)/shard_map/ppermute | solution.py:32
  174.1 13.3 %collective-permute-start.28 = (bf16[1536,1024]{1,0:T(8,128)(2,1)S(1)}, bf16[1536,1024]{1,0:T(8,128)(2,1)}, u32[]{:S(2)}, u32[]{:S(2)}) collective-permute-start(bf16[1536,1024]{1,0:T(8,128)(2,1)S(1)} %bitcast.103), channel_id=1, source_target_pairs={{0,1},{1,0},{2,3},{3,2},{4,5},{5,4},{6,7},{7,6},{8,9},{9,8},{10,11... | collective-permute-start | bytes 9437192 | tf_op jit(solution)/shard_map/ppermute | solution.py:36
  218.5 20.2 %collective-permute-start.29 = (bf16[512,768]{1,0:T(8,128)(2,1)S(1)}, bf16[512,768]{1,0:T(8,128)(2,1)S(1)}, u32[]{:S(2)}, u32[]{:S(2)}) collective-permute-start(bf16[512,768]{1,0:T(8,128)(2,1)S(1)} %get-tuple-element.824), channel_id=1, source_target_pairs={{0,2},{2,0},{4,6},{6,4},{1,3},{3,1},{5,7},{7,5},{8,10},{10,8},{12,... | collective-permute-start | bytes 2359304 | tf_op jit(solution)/shard_map/ppermute | solution.py:32
  220.1 18.8 %collective-permute-start.30 = (bf16[512,768]{1,0:T(8,128)(2,1)S(1)}, bf16[512,768]{1,0:T(8,128)(2,1)S(1)}, u32[]{:S(2)}, u32[]{:S(2)}) collective-permute-start(bf16[512,768]{1,0:T(8,128)(2,1)S(1)} %get-tuple-element.826), channel_id=1, source_target_pairs={{0,4},{2,6},{4,0},{6,2},{1,5},{3,7},{5,1},{7,3},{8,12},{10,14},{12... | collective-permute-start | bytes 2359304 | tf_op jit(solution)/shard_map/ppermute | solution.py:32
  220.9 17.8 %collective-permute-start.31 = (f32[8,128]{1,0:T(8,128)S(1)}, f32[8,128]{1,0:T(8,128)S(1)}, u32[]{:S(2)}, u32[]{:S(2)}) collective-permute-start(f32[8,128]{1,0:T(8,128)S(1)} %bitcast.125), channel_id=1, source_target_pairs={{0,2},{2,0},{4,6},{6,4},{1,3},{3,1},{5,7},{7,5},{8,10},{10,8},{12,... | collective-permute-start | bytes 12296 | tf_op jit(solution)/shard_map/ppermute | solution.py:32
  239.1 12.4 %collective-permute-start.32 = (bf16[4,4,96,1536]{3,2,1,0:T(8,128)(2,1)}, bf16[4,4,96,1536]{3,2,1,0:T(8,128)(2,1)S(1)}, u32[]{:S(2)}, u32[]{:S(2)}) collective-permute-start(bf16[4,4,96,1536]{3,2,1,0:T(8,128)(2,1)} %shard_map.211), channel_id=1, source_target_pairs={{0,1},{1,0},{2,3},{3,2},{4,5},{5,4},{6,7},{7,6},{8,9},{9,8},{10,11... | collective-permute-start | bytes 14155784 | tf_op jit(solution)/shard_map/ppermute | solution.py:36
  239.1 11.6 %collective-permute-start.33 = (bf16[512,384]{1,0:T(8,128)(2,1)S(1)}, bf16[512,384]{1,0:T(8,128)(2,1)S(1)}, u32[]{:S(2)}, u32[]{:S(2)}) collective-permute-start(bf16[512,384]{1,0:T(8,128)(2,1)S(1)} %add_convert_fusion.7), channel_id=1, source_target_pairs={{0,4},{2,6},{4,0},{6,2},{1,5},{3,7},{5,1},{7,3},{8,12},{10,14},{12... | collective-permute-start | bytes 1179656 | tf_op jit(solution)/shard_map/ppermute | solution.py:32
  240.3 11.2 %collective-permute-start.34 = (bf16[512,384]{1,0:T(8,128)(2,1)S(1)}, bf16[512,384]{1,0:T(8,128)(2,1)S(1)}, u32[]{:S(2)}, u32[]{:S(2)}) collective-permute-start(bf16[512,384]{1,0:T(8,128)(2,1)S(1)} %add_convert_fusion.6), channel_id=1, source_target_pairs={{0,2},{2,0},{4,6},{6,4},{1,3},{3,1},{5,7},{7,5},{8,10},{10,8},{12,... | collective-permute-start | bytes 1179656 | tf_op jit(solution)/shard_map/ppermute | solution.py:32
  241.8 9.0 %collective-permute-start.35 = (f32[8,128]{1,0:T(8,128)S(1)}, f32[8,128]{1,0:T(8,128)S(1)}, u32[]{:S(2)}, u32[]{:S(2)}) collective-permute-start(f32[8,128]{1,0:T(8,128)S(1)} %add.417), channel_id=1, source_target_pairs={{0,4},{2,6},{4,0},{6,2},{1,5},{3,7},{5,1},{7,3},{8,12},{10,14},{12... | collective-permute-start | bytes 12296 | tf_op jit(solution)/shard_map/ppermute | solution.py:32
  258.3 229.6 %all-gather.3.cloned.1.call-start = ((), (), s32[]{:S(2)}) async-start(), calls=%async_computation.2 | async-start | bytes 5898240 | tf_op jit(solution)/shard_map/all_gather | solution.py:1089
  263.2 18.8 %collective-permute-start.36 = (bf16[1024,384]{1,0:T(8,128)(2,1)S(1)}, bf16[1024,384]{1,0:T(8,128)(2,1)S(1)}, u32[]{:S(2)}, u32[]{:S(2)}) collective-permute-start(bf16[1024,384]{1,0:T(8,128)(2,1)S(1)} %get-tuple-element.941.x0), channel_id=1, source_target_pairs={{0,2},{2,0},{4,6},{6,4},{1,3},{3,1},{5,7},{7,5},{8,10},{10,8},{12,... | collective-permute-start | bytes 2359304 | tf_op jit(solution)/shard_map/ppermute | solution.py:32
  264.7 18.5 %collective-permute-start.37 = (bf16[1024,384]{1,0:T(8,128)(2,1)S(1)}, bf16[1024,384]{1,0:T(8,128)(2,1)S(1)}, u32[]{:S(2)}, u32[]{:S(2)}) collective-permute-start(bf16[1024,384]{1,0:T(8,128)(2,1)S(1)} %get-tuple-element.941.x0), channel_id=1, source_target_pairs={{0,4},{2,6},{4,0},{6,2},{1,5},{3,7},{5,1},{7,3},{8,12},{10,14},{12... | collective-permute-start | bytes 2359304 | tf_op jit(solution)/shard_map/ppermute | solution.py:32
  283.3 9.3 %collective-permute-start.38 = (bf16[512,384]{1,0:T(8,128)(2,1)S(1)}, bf16[512,384]{1,0:T(8,128)(2,1)S(1)}, u32[]{:S(2)}, u32[]{:S(2)}) collective-permute-start(bf16[512,384]{1,0:T(8,128)(2,1)S(1)} %slice.268), channel_id=1, source_target_pairs={{0,4},{2,6},{4,0},{6,2},{1,5},{3,7},{5,1},{7,3},{8,12},{10,14},{12... | collective-permute-start | bytes 1179656 | tf_op jit(solution)/shard_map/ppermute | solution.py:32
  297.9 28.3 %collective-permute-start.42 = (bf16[512,768]{1,0:T(8,128)(2,1)}, bf16[512,768]{1,0:T(8,128)(2,1)}, u32[]{:S(2)}, u32[]{:S(2)}) collective-permute-start(bf16[512,768]{1,0:T(8,128)(2,1)} %get-tuple-element.975), channel_id=1, source_target_pairs={{0,2},{2,0},{4,6},{6,4},{1,3},{3,1},{5,7},{7,5},{8,10},{10,8},{12,... | collective-permute-start | bytes 2359304 | tf_op jit(solution)/shard_map/ppermute | solution.py:32
  298.6 27.6 %collective-permute-start.43 = (bf16[512,768]{1,0:T(8,128)(2,1)}, bf16[512,768]{1,0:T(8,128)(2,1)}, u32[]{:S(2)}, u32[]{:S(2)}) collective-permute-start(bf16[512,768]{1,0:T(8,128)(2,1)} %get-tuple-element.977), channel_id=1, source_target_pairs={{0,4},{2,6},{4,0},{6,2},{1,5},{3,7},{5,1},{7,3},{8,12},{10,14},{12... | collective-permute-start | bytes 2359304 | tf_op jit(solution)/shard_map/ppermute | solution.py:32
  301.4 24.8 %collective-permute-start.44 = (bf16[4,48,384]{2,1,0:T(8,128)(2,1)}, bf16[4,48,384]{2,1,0:T(8,128)(2,1)S(1)}, u32[]{:S(2)}, u32[]{:S(2)}) collective-permute-start(bf16[4,48,384]{2,1,0:T(8,128)(2,1)} %get-tuple-element.983), channel_id=1, source_target_pairs={{0,8},{1,9},{2,10},{3,11},{4,12},{5,13},{6,14},{7,15}} | collective-permute-start | bytes 442376 | tf_op jit(solution)/shard_map/ppermute | solution.py:160
  304.6 21.6 %collective-permute-start.45 = (bf16[4,48,384]{2,1,0:T(8,128)(2,1)}, bf16[4,48,384]{2,1,0:T(8,128)(2,1)}, u32[]{:S(2)}, u32[]{:S(2)}) collective-permute-start(bf16[4,48,384]{2,1,0:T(8,128)(2,1)} %get-tuple-element.984), channel_id=1, source_target_pairs={{24,16},{25,17},{26,18},{27,19},{28,20},{29,21},{30,22},{31,23}} | collective-permute-start | bytes 442376 | tf_op jit(solution)/shard_map/ppermute | solution.py:160
  330.1 12.5 %collective-permute-start.47 = (bf16[512,384]{1,0:T(8,128)(2,1)S(1)}, bf16[512,384]{1,0:T(8,128)(2,1)S(1)}, u32[]{:S(2)}, u32[]{:S(2)}) collective-permute-start(bf16[512,384]{1,0:T(8,128)(2,1)S(1)} %add_convert_fusion.5), channel_id=1, source_target_pairs={{0,4},{2,6},{4,0},{6,2},{1,5},{3,7},{5,1},{7,3},{8,12},{10,14},{12... | collective-permute-start | bytes 1179656 | tf_op jit(solution)/shard_map/ppermute | solution.py:32
  331.1 12.1 %collective-permute-start.48 = (bf16[512,384]{1,0:T(8,128)(2,1)S(1)}, bf16[512,384]{1,0:T(8,128)(2,1)S(1)}, u32[]{:S(2)}, u32[]{:S(2)}) collective-permute-start(bf16[512,384]{1,0:T(8,128)(2,1)S(1)} %add_convert_fusion.4), channel_id=1, source_target_pairs={{0,2},{2,0},{4,6},{6,4},{1,3},{3,1},{5,7},{7,5},{8,10},{10,8},{12,... | collective-permute-start | bytes 1179656 | tf_op jit(solution)/shard_map/ppermute | solution.py:32
  332.5 10.0 %collective-permute-start.49 = (bf16[4,48,384]{2,1,0:T(8,128)(2,1)S(1)}, bf16[4,48,384]{2,1,0:T(8,128)(2,1)S(1)}, u32[]{:S(2)}, u32[]{:S(2)}) collective-permute-start(bf16[4,48,384]{2,1,0:T(8,128)(2,1)S(1)} %get-tuple-element.1007), channel_id=1, source_target_pairs={{0,8},{8,16},{1,9},{9,17},{2,10},{10,18},{3,11},{11,19},{4,12},{12... | collective-permute-start | bytes 442376 | tf_op jit(solution)/shard_map/ppermute | solution.py:160
  344.7 9.5 %collective-permute-start.54 = (bf16[4,384,384]{2,1,0:T(8,128)(2,1)}, bf16[4,384,384]{2,1,0:T(8,128)(2,1)S(1)}, u32[]{:S(2)}, u32[]{:S(2)}) collective-permute-start(bf16[4,384,384]{2,1,0:T(8,128)(2,1)} %shard_map.216), channel_id=1, source_target_pairs={{0,1},{1,0},{2,3},{3,2},{4,5},{5,4},{6,7},{7,6},{8,9},{9,8},{10,11... | collective-permute-start | bytes 3538952 | tf_op jit(solution)/shard_map/ppermute | solution.py:36
  350.7 10.0 %collective-permute-start.51 = (bf16[96,1536]{1,0:T(8,128)(2,1)S(1)}, bf16[96,1536]{1,0:T(8,128)(2,1)S(1)}, u32[]{:S(2)}, u32[]{:S(2)}) collective-permute-start(bf16[96,1536]{1,0:T(8,128)(2,1)S(1)} %get-tuple-element.1175), channel_id=1, source_target_pairs={{0,2},{2,0},{4,6},{6,4},{1,3},{3,1},{5,7},{7,5},{8,10},{10,8},{12,... | collective-permute-start | bytes 884744 | tf_op jit(solution)/shard_map/ppermute | solution.py:32
  352.2 14.6 %collective-permute-start.52 = (bf16[96,1536]{1,0:T(8,128)(2,1)S(1)}, bf16[96,1536]{1,0:T(8,128)(2,1)S(1)}, u32[]{:S(2)}, u32[]{:S(2)}) collective-permute-start(bf16[96,1536]{1,0:T(8,128)(2,1)S(1)} %get-tuple-element.1174), channel_id=1, source_target_pairs={{0,4},{2,6},{4,0},{6,2},{1,5},{3,7},{5,1},{7,3},{8,12},{10,14},{12... | collective-permute-start | bytes 884744 | tf_op jit(solution)/shard_map/ppermute | solution.py:32
  353.6 13.2 %collective-permute-start.53 = (bf16[96,1536]{1,0:T(8,128)(2,1)S(1)}, bf16[96,1536]{1,0:T(8,128)(2,1)S(1)}, u32[]{:S(2)}, u32[]{:S(2)}) collective-permute-start(bf16[96,1536]{1,0:T(8,128)(2,1)S(1)} %get-tuple-element.1173), channel_id=1, source_target_pairs={{0,6},{2,4},{4,2},{6,0},{1,7},{3,5},{5,3},{7,1},{8,14},{10,12},{12... | collective-permute-start | bytes 884744 | tf_op jit(solution)/shard_map/ppermute | solution.py:32
  355.6 12.3 %collective-permute-start.55 = (bf16[4,96,384]{2,1,0:T(8,128)(2,1)S(1)}, bf16[4,96,384]{2,1,0:T(8,128)(2,1)S(1)}, u32[]{:S(2)}, u32[]{:S(2)}) collective-permute-start(bf16[4,96,384]{2,1,0:T(8,128)(2,1)S(1)} %get-tuple-element.1171), channel_id=1, source_target_pairs={{0,8},{1,9},{2,10},{3,11},{4,12},{5,13},{6,14},{7,15}} | collective-permute-start | bytes 884744 | tf_op jit(solution)/shard_map/ppermute | solution.py:160
  357.0 11.0 %collective-permute-start.56 = (bf16[4,96,384]{2,1,0:T(8,128)(2,1)S(1)}, bf16[4,96,384]{2,1,0:T(8,128)(2,1)S(1)}, u32[]{:S(2)}, u32[]{:S(2)}) collective-permute-start(bf16[4,96,384]{2,1,0:T(8,128)(2,1)S(1)} %get-tuple-element.1170), channel_id=1, source_target_pairs={{24,16},{25,17},{26,18},{27,19},{28,20},{29,21},{30,22},{31,23}} | collective-permute-start | bytes 884744 | tf_op jit(solution)/shard_map/ppermute | solution.py:160
  371.2 24.8 %collective-permute-start.57 = (bf16[4,96,384]{2,1,0:T(8,128)(2,1)S(1)}, bf16[4,96,384]{2,1,0:T(8,128)(2,1)S(1)}, u32[]{:S(2)}, u32[]{:S(2)}) collective-permute-start(bf16[4,96,384]{2,1,0:T(8,128)(2,1)S(1)} %get-tuple-element.1062), channel_id=1, source_target_pairs={{0,8},{8,16},{1,9},{9,17},{2,10},{10,18},{3,11},{11,19},{4,12},{12... | collective-permute-start | bytes 884744 | tf_op jit(solution)/shard_map/ppermute | solution.py:160
  372.5 23.5 %collective-permute-start.58 = (bf16[4,96,384]{2,1,0:T(8,128)(2,1)S(1)}, bf16[4,96,384]{2,1,0:T(8,128)(2,1)S(1)}, u32[]{:S(2)}, u32[]{:S(2)}) collective-permute-start(bf16[4,96,384]{2,1,0:T(8,128)(2,1)S(1)} %get-tuple-element.1063), channel_id=1, source_target_pairs={{24,16},{16,8},{25,17},{17,9},{26,18},{18,10},{27,19},{19,11},{28,... | collective-permute-start | bytes 884744 | tf_op jit(solution)/shard_map/ppermute | solution.py:160
  373.5 18.1 %collective-permute-start.59 = (bf16[4,48,384]{2,1,0:T(8,128)(2,1)S(1)}, bf16[4,48,384]{2,1,0:T(8,128)(2,1)S(1)}, u32[]{:S(2)}, u32[]{:S(2)}) collective-permute-start(bf16[4,48,384]{2,1,0:T(8,128)(2,1)S(1)} %get-tuple-element.1064), channel_id=1, source_target_pairs={{0,8},{8,16},{16,24},{1,9},{9,17},{17,25},{2,10},{10,18},{18,26},{... | collective-permute-start | bytes 442376 | tf_op jit(solution)/shard_map/ppermute | solution.py:160
  380.9 15.1 %collective-permute-start.60 = (bf16[4,48,384]{2,1,0:T(8,128)(2,1)S(1)}, bf16[4,48,384]{2,1,0:T(8,128)(2,1)S(1)}, u32[]{:S(2)}, u32[]{:S(2)}) collective-permute-start(bf16[4,48,384]{2,1,0:T(8,128)(2,1)S(1)} %get-tuple-element.1065), channel_id=1, source_target_pairs={{24,16},{16,8},{8,0},{25,17},{17,9},{9,1},{26,18},{18,10},{10,2},{... | collective-permute-start | bytes 442376 | tf_op jit(solution)/shard_map/ppermute | solution.py:160
  396.8 44.0 %collective-permute-start.61 = (bf16[512,768]{1,0:T(8,128)(2,1)}, bf16[512,768]{1,0:T(8,128)(2,1)S(1)}, u32[]{:S(2)}, u32[]{:S(2)}) collective-permute-start(bf16[512,768]{1,0:T(8,128)(2,1)} %get-tuple-element.1076), channel_id=1, source_target_pairs={{0,2},{2,0},{4,6},{6,4},{1,3},{3,1},{5,7},{7,5},{8,10},{10,8},{12,... | collective-permute-start | bytes 2359304 | tf_op jit(solution)/shard_map/ppermute | solution.py:32
  398.1 42.7 %collective-permute-start.62 = (bf16[512,768]{1,0:T(8,128)(2,1)}, bf16[512,768]{1,0:T(8,128)(2,1)}, u32[]{:S(2)}, u32[]{:S(2)}) collective-permute-start(bf16[512,768]{1,0:T(8,128)(2,1)} %get-tuple-element.1078), channel_id=1, source_target_pairs={{0,4},{2,6},{4,0},{6,2},{1,5},{3,7},{5,1},{7,3},{8,12},{10,14},{12... | collective-permute-start | bytes 2359304 | tf_op jit(solution)/shard_map/ppermute | solution.py:32
  401.1 28.8 %collective-permute-start.63 = (bf16[4,96,384]{2,1,0:T(8,128)(2,1)}, bf16[4,96,384]{2,1,0:T(8,128)(2,1)S(1)}, u32[]{:S(2)}, u32[]{:S(2)}) collective-permute-start(bf16[4,96,384]{2,1,0:T(8,128)(2,1)} %get-tuple-element.1085), channel_id=1, source_target_pairs={{0,8},{8,16},{16,24},{1,9},{9,17},{17,25},{2,10},{10,18},{18,26},{... | collective-permute-start | bytes 884744 | tf_op jit(solution)/shard_map/ppermute | solution.py:160
  419.1 21.7 %collective-permute-start.64 = (bf16[4,96,384]{2,1,0:T(8,128)(2,1)}, bf16[4,96,384]{2,1,0:T(8,128)(2,1)}, u32[]{:S(2)}, u32[]{:S(2)}) collective-permute-start(bf16[4,96,384]{2,1,0:T(8,128)(2,1)} %get-tuple-element.1086), channel_id=1, source_target_pairs={{24,16},{16,8},{8,0},{25,17},{17,9},{9,1},{26,18},{18,10},{10,2},{... | collective-permute-start | bytes 884744 | tf_op jit(solution)/shard_map/ppermute | solution.py:160
  443.2 13.8 %collective-permute-start.66 = (bf16[512,384]{1,0:T(8,128)(2,1)S(1)}, bf16[512,384]{1,0:T(8,128)(2,1)S(1)}, u32[]{:S(2)}, u32[]{:S(2)}) collective-permute-start(bf16[512,384]{1,0:T(8,128)(2,1)S(1)} %add_convert_fusion.3), channel_id=1, source_target_pairs={{0,4},{2,6},{4,0},{6,2},{1,5},{3,7},{5,1},{7,3},{8,12},{10,14},{12... | collective-permute-start | bytes 1179656 | tf_op jit(solution)/shard_map/ppermute | solution.py:32
  444.8 12.2 %collective-permute-start.67 = (bf16[512,384]{1,0:T(8,128)(2,1)S(1)}, bf16[512,384]{1,0:T(8,128)(2,1)S(1)}, u32[]{:S(2)}, u32[]{:S(2)}) collective-permute-start(bf16[512,384]{1,0:T(8,128)(2,1)S(1)} %add_convert_fusion.2), channel_id=1, source_target_pairs={{0,2},{2,0},{4,6},{6,4},{1,3},{3,1},{5,7},{7,5},{8,10},{10,8},{12,... | collective-permute-start | bytes 1179656 | tf_op jit(solution)/shard_map/ppermute | solution.py:32
  463.6 14.7 %collective-permute-start.73 = (bf16[4,160,384]{2,1,0:T(8,128)(2,1)S(1)}, bf16[4,160,384]{2,1,0:T(8,128)(2,1)S(1)}, u32[]{:S(2)}, u32[]{:S(2)}) collective-permute-start(bf16[4,160,384]{2,1,0:T(8,128)(2,1)S(1)} %fusion.10), channel_id=1, source_target_pairs={{0,8},{8,16},{16,24},{1,9},{9,17},{17,25},{2,10},{10,18},{18,26},{... | collective-permute-start | bytes 1474568 | tf_op jit(solution)/shard_map/ppermute | solution.py:179
  467.4 15.1 %collective-permute-start.74 = (bf16[4,160,384]{2,1,0:T(8,128)(2,1)S(1)}, bf16[4,160,384]{2,1,0:T(8,128)(2,1)S(1)}, u32[]{:S(2)}, u32[]{:S(2)}) collective-permute-start(bf16[4,160,384]{2,1,0:T(8,128)(2,1)S(1)} %fusion.10), channel_id=1, source_target_pairs={{24,16},{16,8},{8,0},{25,17},{17,9},{9,1},{26,18},{18,10},{10,2},{... | collective-permute-start | bytes 1474568 | tf_op jit(solution)/shard_map/ppermute | solution.py:180
  482.5 12.0 %collective-permute-start.75 = (bf16[4,160,384]{2,1,0:T(8,128)(2,1)S(1)}, bf16[4,160,384]{2,1,0:T(8,128)(2,1)}, u32[]{:S(2)}, u32[]{:S(2)}) collective-permute-start(bf16[4,160,384]{2,1,0:T(8,128)(2,1)S(1)} %collective-permute-done.73), channel_id=1, source_target_pairs={{8,16},{16,24},{9,17},{17,25},{10,18},{18,26},{11,19},{19,27},{12,... | collective-permute-start | bytes 1474568 | tf_op jit(solution)/shard_map/ppermute | solution.py:179
  483.9 14.5 %collective-permute-start.76 = (bf16[4,160,384]{2,1,0:T(8,128)(2,1)S(1)}, bf16[4,160,384]{2,1,0:T(8,128)(2,1)S(1)}, u32[]{:S(2)}, u32[]{:S(2)}) collective-permute-start(bf16[4,160,384]{2,1,0:T(8,128)(2,1)S(1)} %collective-permute-done.74), channel_id=1, source_target_pairs={{16,8},{8,0},{17,9},{9,1},{18,10},{10,2},{19,11},{11,3},{20,12},{1... | collective-permute-start | bytes 1474568 | tf_op jit(solution)/shard_map/ppermute | solution.py:180
  499.1 13.6 %collective-permute-start.78 = (bf16[4,160,384]{2,1,0:T(8,128)(2,1)S(1)}, bf16[4,160,384]{2,1,0:T(8,128)(2,1)S(1)}, u32[]{:S(2)}, u32[]{:S(2)}) collective-permute-start(bf16[4,160,384]{2,1,0:T(8,128)(2,1)S(1)} %collective-permute-done.76), channel_id=1, source_target_pairs={{8,0},{9,1},{10,2},{11,3},{12,4},{13,5},{14,6},{15,7}} | collective-permute-start | bytes 1474568 | tf_op jit(solution)/shard_map/ppermute | solution.py:180
  (115 other events, 1082.6 us)
Sparse Core Ops, SparseCore 0:
  258.4 90.8 reduce-scatter.1
  368.8 103.5 all-gather.2

commit v6 on v5

--- a/solution.py
+++ b/solution.py
@@ -157,6 +157,11 @@
         return before
     last = min(step, count - 1)
     up, down = parts
+    if step == 1 and count > 3:
+        place = lax.axis_index("dp")
+        sent = jnp.where(place == 0, up, down)
+        got = lax.ppermute(sent, "dp", chain_up(count, 0, 1) + chain_down(count, 0, 1))
+        return [jnp.where(place == 1, got, 0), jnp.where(place == count - 2, got, 0)]
     return [lax.ppermute(up, "dp", chain_up(count, 0, last)), lax.ppermute(down, "dp", chain_down(count, 0, last))]
 
 
@@ -176,6 +181,14 @@
 def chain_spread(first, last, shard, count, found):
     for step in range(first, min(last, count)):
         up, down = found[-1] if found else (shard, shard)
+        if step == count - 1 and count > 3:
+            place = lax.axis_index("dp")
+            sent = jnp.where(place == count - 2, up, down)
+            got = lax.ppermute(
+                sent, "dp", chain_up(count, count - 2, count - 1) + chain_down(count, count - 2, count - 1)
+            )
+            found = found + [(got, got)]
+            continue
         up = lax.ppermute(up, "dp", chain_up(count, step - 1, count - 1))
         down = lax.ppermute(down, "dp", chain_down(count, step - 1, count - 1))
         found = found + [(up, down)]

time: 530 us -> 529 us (level)
  waiting for transfers between devices: 148 us -> 158 us
  Pallas kernels: 141 us -> 134 us
    ppermute x0 -> x3, waiting for transfers between devices: none -> 12.7 us  [the longest x1 11.1 us: chain_spread(): lax.ppermute(sent, 'dp', chain_up(count, count - 2, count - 1) + chain_do...]
    ppermute x0 -> x3, starting transfers between devices: none -> 12.1 us  [the longest x2 10.8 us: chain_sum(): lax.ppermute(sent, 'dp', chain_up(count, 0, 1) + chain_down(count, 0, 1))]
    ppermute x6 -> x4, starting transfers between devices: 32.4 us -> 21.1 us  [chain_sum(): lax.ppermute(up, 'dp', chain_up(count, 0, last))]
    ppermute x3 -> x2, waiting for transfers between devices: 18.8 us -> 8.23 us  [chain_spread(): down = lax.ppermute(down, 'dp', chain_down(count, step - 1, count - 1))]
    ppermute x3 -> x2, waiting for transfers between devices: 9.26 us -> 14.4 us  [chain_spread(): up = lax.ppermute(up, 'dp', chain_up(count, step - 1, count - 1))]
    ppermute x6 -> x4, waiting for transfers between devices: 15.3 us -> 12.1 us  [chain_sum(): lax.ppermute(down, 'dp', chain_down(count, 0, last))]
    unnamed x196 -> x192, local copies, waits for them, and re-layouts: 22.9 us -> 22.5 us
  transfers between devices with their start and end apart: 81 -> 78, of which waited for: 36 -> 38; matrix products, arithmetic and copies ran while one was open for 13% -> 13% of each run, Pallas kernels for 21% -> 20%
where the time goes in v6:
time: 529 us; the launch traced here: 522 us
  waiting for transfers between devices  158 us (30%)
  Pallas kernels  134 us (25%)
  starting transfers between devices  102 us (19%)
  other arithmetic  55.9 us (11%)
  local copies, waits for them, and re-layouts  50.2 us (9%)
  between operations  18.2 us (3%)
    ppermute x47, waiting for transfers between devices, swap(): return lax.ppermute(value, 'row', [(i, i ^ step) for i in range(4)])  95.1 us
    ppermute x47, starting transfers between devices, swap(): return lax.ppermute(value, 'row', [(i, i ^ step) for i in range(4)])  54.1 us
    pallas_call x3, Pallas kernels, partial_sums(): call(functools.partial(partial_kernel, blocked), tuple(outs), specs, tupl...  27.4 us
    unnamed x192, local copies, waits for them, and re-layouts  22.5 us
    ppermute x4, starting transfers between devices, chain_sum(): lax.ppermute(up, 'dp', chain_up(count, 0, last))  21.1 us
    pallas_call x1, Pallas kernels, feed(): call(feed_kernel, outs, [whole(second), whole(cot), column(early), column...  17.2 us
    pallas_call x2, Pallas kernels, feed_grads(): call(feed_grads_kernel, out, [block, block, whole(back), whole(hidden)],...  17.1 us
    pallas_call x1, Pallas kernels, attend_back(): call(attend_back_kernel, outs, [whole(own), whole(oth), whole(g_own), who...  16.8 us
  transfers between devices with their start and end apart: 78, of which 38 were waited for; matrix products, arithmetic and copies ran while one was open for 13% of the time, Pallas kernels for 20%

profile of v6, /device:TPU:0, one launch (start us, length us, event | category | flops | bytes accessed | tf_op | source)
XLA Modules:
  0.0 521.9 jit_solution(2656434867192239008)
XLA Ops:
  7.2 3.0 collective-permute-start.3
  22.6 2.9 collective-permute-start.2
  25.6 3.5 multiply_convert_fusion.1
  31.5 2.1 pad_maximum_fusion.6
  35.7 2.3 fusion.11
  46.2 6.1 %fusion.7 = (f32[2048,128]{1,0:T(8,128)}, f32[2048,128]{1,0:T(8,128)}) fusion(f32[128]{0:T(128)S(1)} %get-tuple-element.1215, f32[128]{0:T(128)S(1)} %get-tuple-element.1216, f32[2048]{0:T(1024)S(1)} %get-tuple-element.1213, pred[128]{0:T(512)(128)(4,1)S(1)} %broadcast_compare_fusion), kind=kLoop, calls=%fused_computation.26 | loop fusion | flops 1048576 | bytes 2106496 | tf_op jit(solution)/shard_map/jit(_where)/select_n | solution.py:902
  52.3 2.0 collective-permute-done.6.top.refs_8_
  54.8 2.2 convolution_convert_fusion.w_own
  62.7 8.0 %shard_map.204 = (bf16[1024,1536]{1,0:T(8,128)(2,1)}, f32[1024,128]{1,0:T(8,128)S(1)}, bf16[1024,512]{1,0:T(8,128)(2,1)S(1)}, bf16[1024,512]{1,0:T(8,128)(2,1)}) custom-call(bf16[1024,384]{1,0:T(8,128)(2,1)S(1)} %copy-done.6, bf16[1024,384]{1,0:T(8,128)(2,1)S(1)} %collective-permute-done.3.x1.refs_6_, ...), custom_call_target="tpu_custom_call" | custom-call | flops 50331648 | bytes 188416 | tf_op jit(solution)/shard_map/pallas_call | solution.py:387
  70.8 6.5 %collective-permute-done.10 = bf16[192,1024]{1,0:T(8,128)(2,1)} collective-permute-done((bf16[192,1024]{1,0:T(8,128)(2,1)}, bf16[192,1024]{1,0:T(8,128)(2,1)}, u32[]{:S(2)}, u32[]{:S(2)}) %collective-permute-start.10) | collective-permute-done | bytes 393248 | tf_op jit(solution)/shard_map/ppermute | solution.py:32
  82.5 2.1 collective-permute-start.16
  84.6 13.5 %shard_map.205 = (bf16[1024,192]{1,0:T(8,128)(2,1)S(1)}, bf16[1024,192]{1,0:T(8,128)(2,1)S(1)}, bf16[2048,256]{1,0:T(8,128)(2,1)S(1)}, f32[1,4096]{1,0:T(1,128)S(1)}) custom-call(s32[17]{0:T(128)S(1)} %pad_add_fusion.info, bf16[1024,512]{1,0:T(8,128)(2,1)S(1)} %get-tuple-element.963.own, bf16[1024,512]{1,0:T(8,128)(2,1)S(1)} %collective-permute-done.12.oth, ...), custom_call_target="tpu_custom_call" | custom-call | flops 67108864 | bytes 61696 | tf_op jit(solution)/shard_map/pallas_call | solution.py:494
  98.1 7.5 %collective-permute-done.16 = bf16[640,384]{1,0:T(8,128)(2,1)S(1)} collective-permute-done((bf16[640,384]{1,0:T(8,128)(2,1)S(1)}, bf16[640,384]{1,0:T(8,128)(2,1)S(1)}, u32[]{:S(2)}, u32[]{:S(2)}) %collective-permute-start.16) | collective-permute-done | bytes 491552 | tf_op jit(solution)/shard_map/ppermute | solution.py:32
  105.5 1.7 collective-permute-done.13
  117.8 13.3 %collective-permute-done.18.x1 = bf16[1024,384]{1,0:T(8,128)(2,1)S(1)} collective-permute-done((bf16[1024,384]{1,0:T(8,128)(2,1)S(1)}, bf16[1024,384]{1,0:T(8,128)(2,1)S(1)}, u32[]{:S(2)}, u32[]{:S(2)}) %collective-permute-start.18) | collective-permute-done | bytes 786464 | tf_op jit(solution)/shard_map/ppermute | solution.py:32
  131.7 15.3 %collective-permute-done.20.refs_1_ = bf16[1024,384]{1,0:T(8,128)(2,1)} collective-permute-done((bf16[1024,384]{1,0:T(8,128)(2,1)S(1)}, bf16[1024,384]{1,0:T(8,128)(2,1)}, u32[]{:S(2)}, u32[]{:S(2)}) %collective-permute-start.20) | collective-permute-done | bytes 786464 | tf_op jit(solution)/shard_map/ppermute | solution.py:32
  149.2 1.7 constant_dynamic-update-slice_fusion
  157.7 2.0 copy-done.69
  161.4 4.2 shard_map.206
  166.8 1.7 slice.317.d_oth.w_oth
  168.6 4.6 collective-permute-done.26.refs_3_
  174.2 1.9 shard_map.208.cot
  177.1 10.3 %shard_map.207 = (bf16[1024,1536]{1,0:T(8,128)(2,1)}, f32[1024,384]{1,0:T(8,128)}, f32[1024,128]{1,0:T(8,128)S(1)}, bf16[1024,1536]{1,0:T(8,128)(2,1)}) custom-call(bf16[1024,384]{1,0:T(8,128)(2,1)S(1)} %copy-done.30, bf16[1024,384]{1,0:T(8,128)(2,1)} %collective-permute-done.20.refs_1_, bf16[1024,384]{1,0:T(8,128)(2,1)} %collective-permute-done.21.refs_2_, ...), custom_call_target="tpu_custom_call" | custom-call | flops 75497472 | bytes 303104 | tf_op jit(solution)/shard_map/pallas_call | solution.py:638
  187.3 17.2 %shard_map.209 = (bf16[1024,512]{1,0:T(8,128)(2,1)S(1)}, bf16[1024,512]{1,0:T(8,128)(2,1)S(1)}, bf16[1024,1024]{1,0:T(8,128)(2,1)}, bf16[1024,1024]{1,0:T(8,128)(2,1)}) custom-call(bf16[1024,1536]{1,0:T(8,128)(2,1)} %get-tuple-element.807.second.rest_0_, bf16[1024,1536]{1,0:T(8,128)(2,1)} %shard_map.208.cot, bf16[1536,1024]{1,0:T(8,128)(2,1)} %bitcast.102, ...), custom_call_target="tpu_custom_call" | custom-call | flops 150994944 | bytes 344064 | tf_op jit(solution)/shard_map/pallas_call | solution.py:688
  204.6 2.3 copy-done.4
  207.0 11.3 %shard_map.210 = (bf16[1024,384]{1,0:T(8,128)(2,1)S(1)}, bf16[512,768]{1,0:T(8,128)(2,1)S(1)}, bf16[512,384]{1,0:T(8,128)(2,1)S(1)}, bf16[512,768]{1,0:T(8,128)(...) custom-call(bf16[1024,1024]{1,0:T(8,128)(2,1)S(1)} %copy-done.4, ...), custom_call_target="tpu_custom_call" | custom-call | flops 100663296 | bytes 270336 | tf_op jit(solution)/shard_map/pallas_call | solution.py:760
  221.4 8.6 %shard_map.212 = bf16[4,4,96,1536]{3,2,1,0:T(8,128)(2,1)} custom-call(bf16[1024,1536]{1,0:T(8,128)(2,1)} %get-tuple-element.807.second.rest_0_, bf16[1024,1536]{1,0:T(8,128)(2,1)} %shard_map.208.cot, bf16[1024,1024]{1,0:T(8,128)(2,1)S(1)} %copy-done.5, bf16[1024,512]{1,0:T(8,128)(2,1)S(1)} %get-tuple-element.882.hidden.a_own), custom_call_target="tpu_custom_call" | custom-call | flops 75497472 | bytes 221184 | tf_op jit(solution)/shard_map/pallas_call | solution.py:785
  230.0 8.5 %shard_map.211 = bf16[4,4,96,1536]{3,2,1,0:T(8,128)(2,1)} custom-call(bf16[1024,1536]{1,0:T(8,128)(2,1)} %get-tuple-element.807.second.rest_0_, bf16[1024,1536]{1,0:T(8,128)(2,1)} %shard_map.208.cot, bf16[1024,1024]{1,0:T(8,128)(2,1)S(1)} %copy-done.3, bf16[1024,512]{1,0:T(8,128)(2,1)S(1)} %get-tuple-element.883.hidden.a_oth), custom_call_target="tpu_custom_call" | custom-call | flops 75497472 | bytes 221184 | tf_op jit(solution)/shard_map/pallas_call | solution.py:785
  242.5 8.3 %collective-permute-done.35 = f32[8,128]{1,0:T(8,128)S(1)} collective-permute-done((f32[8,128]{1,0:T(8,128)S(1)}, f32[8,128]{1,0:T(8,128)S(1)}, u32[]{:S(2)}, u32[]{:S(2)}) %collective-permute-start.35) | collective-permute-done | bytes 4128 | tf_op jit(solution)/shard_map/ppermute | solution.py:32
  252.1 6.0 %add_convert_fusion = bf16[4,4,96,1536]{3,2,1,0:T(8,128)(2,1)} fusion(bf16[4,4,96,1536]{3,2,1,0:T(8,128)(2,1)S(1)} %collective-permute-done.32, bf16[4,4,96,1536]{3,2,1,0:T(8,128)(2,1)} %shard_map.212), kind=kLoop, calls=%fused_computation | loop fusion | flops 9437184 | bytes 14155776 | tf_op jit(solution)/shard_map/convert_element_type | solution.py:1026
  265.9 8.2 %shard_map.213 = (bf16[1024,384]{1,0:T(8,128)(2,1)S(1)}, bf16[512,768]{1,0:T(8,128)(2,1)}, bf16[512,384]{1,0:T(8,128)(2,1)S(1)}, bf16[512,768]{1,0:T(8,128)(2,1)}, bf16[512,384]{1,0:T(8,128)(2,1)S(1)}) custom-call(bf16[1024,512]{1,0:T(8,128)(2,1)S(1)} %copy-done.15, bf16[1024,512]{1,0:T(8,128)(2,1)S(1)} %copy-done.17, bf16[4,512,384]{2,1,0:T(8,128)(2,1)} %copy-done.1, ...), custom_call_target="tpu_custom_call" | custom-call | flops 50331648 | bytes 131072 | tf_op jit(solution)/shard_map/pallas_call | solution.py:760
  274.2 7.6 %collective-permute-done.36.x1 = bf16[1024,384]{1,0:T(8,128)(2,1)S(1)} collective-permute-done((bf16[1024,384]{1,0:T(8,128)(2,1)S(1)}, bf16[1024,384]{1,0:T(8,128)(2,1)S(1)}, u32[]{:S(2)}, u32[]{:S(2)}) %collective-permute-start.36) | collective-permute-done | bytes 786464 | tf_op jit(solution)/shard_map/ppermute | solution.py:32
  284.8 1.9 convolution_convert_fusion.1
  286.7 5.7 %collective-permute-done.38.top = bf16[512,384]{1,0:T(8,128)(2,1)S(1)} collective-permute-done((bf16[512,384]{1,0:T(8,128)(2,1)S(1)}, bf16[512,384]{1,0:T(8,128)(2,1)S(1)}, u32[]{:S(2)}, u32[]{:S(2)}) %collective-permute-start.38) | collective-permute-done | bytes 393248 | tf_op jit(solution)/shard_map/ppermute | solution.py:32
  293.2 2.5 shard_map.214
  301.2 3.1 collective-permute-start.44
  304.4 16.8 %shard_map.215 = (bf16[1024,512]{1,0:T(8,128)(2,1)S(1)}, bf16[1024,512]{1,0:T(8,128)(2,1)S(1)}) custom-call(s32[17]{0:T(128)S(1)} %pad_add_fusion.info, bf16[1024,512]{1,0:T(8,128)(2,1)S(1)} %copy-done.19, bf16[1024,512]{1,0:T(8,128)(2,1)S(1)} %copy-done.21, bf16[1024,256]{1,0:T(8,128)(2,1)S(1)} %get-tuple-element.965.g_own, ...), custom_call_target="tpu_custom_call" | custom-call | flops 167772160 | bytes 98304 | tf_op jit(solution)/shard_map/pallas_call | solution.py:585
  329.9 3.5 shard_map.217
  333.5 4.3 shard_map.216
  339.3 3.1 collective-permute-done.53
  345.1 7.6 %collective-permute-start.54 = (bf16[4,96,384]{2,1,0:T(8,128)(2,1)S(1)}, bf16[4,96,384]{2,1,0:T(8,128)(2,1)S(1)}, u32[]{:S(2)}, u32[]{:S(2)}) collective-permute-start(bf16[4,96,384]{2,1,0:T(8,128)(2,1)S(1)} %dynamic-slice_select_fusion), channel_id=1, source_target_pairs={{0,8},{24,16},{1,9},{25,17},{2,10},{26,18},{3,11},{27,19},{4,12},{... | collective-permute-start | bytes 884744 | tf_op jit(solution)/shard_map/ppermute | solution.py:163
  360.0 4.0 collective-permute-done.50
  364.0 6.4 %collective-permute-done.51 = bf16[96,1536]{1,0:T(8,128)(2,1)S(1)} collective-permute-done((bf16[96,1536]{1,0:T(8,128)(2,1)S(1)}, bf16[96,1536]{1,0:T(8,128)(2,1)S(1)}, u32[]{:S(2)}, u32[]{:S(2)}) %collective-permute-start.51) | collective-permute-done | bytes 294944 | tf_op jit(solution)/shard_map/ppermute | solution.py:32
  376.4 3.4 collective-permute-start.57
  381.1 7.8 %shard_map.218 = (bf16[1024,384]{1,0:T(8,128)(2,1)S(1)}, bf16[512,768]{1,0:T(8,128)(2,1)}, bf16[512,384]{1,0:T(8,128)(2,1)S(1)}, bf16[512,768]{1,0:T(8,128)(2,1)...) custom-call(bf16[1024,512]{1,0:T(8,128)(2,1)S(1)} %copy-done.23, bf16[1024,512]{1,0:T(8,128)(2,1)S(1)} %copy-done.25, ...), custom_call_target="tpu_custom_call" | custom-call | flops 50331648 | bytes 188416 | tf_op jit(solution)/shard_map/pallas_call | solution.py:760
  390.4 2.2 collective-permute-done.57
  392.5 2.4 collective-permute-done.58
  397.7 2.2 add_convert_fusion.9
  399.8 14.8 %collective-permute-start.61 = (bf16[4,96,384]{2,1,0:T(8,128)(2,1)}, bf16[4,96,384]{2,1,0:T(8,128)(2,1)S(1)}, u32[]{:S(2)}, u32[]{:S(2)}) collective-permute-start(bf16[4,96,384]{2,1,0:T(8,128)(2,1)} %get-tuple-element.1085), channel_id=1, source_target_pairs={{0,8},{8,16},{16,24},{1,9},{9,17},{17,25},{2,10},{10,18},{18,26},{... | collective-permute-start | bytes 884744 | tf_op jit(solution)/shard_map/ppermute | solution.py:165
  419.6 5.8 %collective-permute-done.61 = bf16[4,96,384]{2,1,0:T(8,128)(2,1)S(1)} collective-permute-done((bf16[4,96,384]{2,1,0:T(8,128)(2,1)}, bf16[4,96,384]{2,1,0:T(8,128)(2,1)S(1)}, u32[]{:S(2)}, u32[]{:S(2)}) %collective-permute-start.61) | collective-permute-done | bytes 294944 | tf_op jit(solution)/shard_map/ppermute | solution.py:165
  425.5 9.7 %collective-permute-done.62 = bf16[4,96,384]{2,1,0:T(8,128)(2,1)S(1)} collective-permute-done((bf16[4,96,384]{2,1,0:T(8,128)(2,1)}, bf16[4,96,384]{2,1,0:T(8,128)(2,1)S(1)}, u32[]{:S(2)}, u32[]{:S(2)}) %collective-permute-start.62) | collective-permute-done | bytes 294944 | tf_op jit(solution)/shard_map/ppermute | solution.py:165
  437.5 2.7 collective-permute-start.64
  440.2 2.7 collective-permute-start.65
  443.2 3.3 collective-permute-start.68
  446.5 3.0 collective-permute-done.66
  449.8 3.2 collective-permute-done.69
  459.6 1.8 collective-permute-start.71
  463.0 14.4 %collective-permute-done.71 = bf16[4,160,384]{2,1,0:T(8,128)(2,1)S(1)} collective-permute-done((bf16[4,160,384]{2,1,0:T(8,128)(2,1)S(1)}, bf16[4,160,384]{2,1,0:T(8,128)(2,1)S(1)}, u32[]{:S(2)}, u32[]{:S(2)}) %collective-permute-start.71) | collective-permute-done | bytes 491552 | tf_op jit(solution)/shard_map/ppermute | solution.py:192
  477.4 2.6 collective-permute-done.72
  484.6 2.3 copy-done.12
  486.9 4.2 shard_map.219
  491.1 5.7 %collective-permute-done.74 = bf16[4,160,384]{2,1,0:T(8,128)(2,1)S(1)} collective-permute-done((bf16[4,160,384]{2,1,0:T(8,128)(2,1)}, bf16[4,160,384]{2,1,0:T(8,128)(2,1)S(1)}, u32[]{:S(2)}, u32[]{:S(2)}) %collective-permute-start.74) | collective-permute-done | bytes 491552 | tf_op jit(solution)/shard_map/ppermute | solution.py:193
  499.8 11.1 %collective-permute-done.75 = bf16[4,160,384]{2,1,0:T(8,128)(2,1)S(1)} collective-permute-done((bf16[4,160,384]{2,1,0:T(8,128)(2,1)S(1)}, bf16[4,160,384]{2,1,0:T(8,128)(2,1)S(1)}, u32[]{:S(2)}, u32[]{:S(2)}) %collective-permute-start.75) | collective-permute-done | bytes 491552 | tf_op jit(solution)/shard_map/ppermute | solution.py:187
  511.9 2.7 shard_map.220
  (426 shorter events, 140.5 us)
Async XLA Ops:
  7.2 345.6 %reduce-scatter.2.cloned.1.call-start = ((), (), s32[]{:S(2)}) async-start(), calls=%async_computation.1 | async-start | bytes 5898240 | tf_op jit(solution)/shard_map/reduce_scatter | solution.py:1052
  7.2 30.8 %collective-permute-start.3 = (bf16[1024,384]{1,0:T(8,128)(2,1)}, bf16[1024,384]{1,0:T(8,128)(2,1)S(1)}, u32[]{:S(2)}, u32[]{:S(2)}) collective-permute-start(bf16[1024,384]{1,0:T(8,128)(2,1)} %refs_5_), channel_id=1, source_target_pairs={{0,2},{2,0},{4,6},{6,4},{1,3},{3,1},{5,7},{7,5},{8,10},{10,8},{12,... | collective-permute-start | bytes 2359304 | tf_op jit(solution)/shard_map/ppermute | solution.py:32
  10.2 27.8 %collective-permute-start.4 = (bf16[1024,384]{1,0:T(8,128)(2,1)}, bf16[1024,384]{1,0:T(8,128)(2,1)S(1)}, u32[]{:S(2)}, u32[]{:S(2)}) collective-permute-start(bf16[1024,384]{1,0:T(8,128)(2,1)} %refs_5_), channel_id=1, source_target_pairs={{0,4},{2,6},{4,0},{6,2},{1,5},{3,7},{5,1},{7,3},{8,12},{10,14},{12... | collective-permute-start | bytes 2359304 | tf_op jit(solution)/shard_map/ppermute | solution.py:32
  22.0 16.0 %collective-permute-start = (bf16[192,384]{1,0:T(8,128)(2,1)}, bf16[192,384]{1,0:T(8,128)(2,1)S(1)}, u32[]{:S(2)}, u32[]{:S(2)}) collective-permute-start(bf16[192,384]{1,0:T(8,128)(2,1)} %dynamic-slice_bitcast_fusion.2), channel_id=1, source_target_pairs={{0,2},{2,0},{4,6},{6,4},{1,3},{3,1},{5,7},{7,5},{8,10},{10,8},{12,... | collective-permute-start | bytes 442376 | tf_op jit(solution)/shard_map/ppermute | solution.py:32
  22.5 15.4 %collective-permute-start.1 = (bf16[192,384]{1,0:T(8,128)(2,1)}, bf16[192,384]{1,0:T(8,128)(2,1)}, u32[]{:S(2)}, u32[]{:S(2)}) collective-permute-start(bf16[192,384]{1,0:T(8,128)(2,1)} %dynamic-slice_bitcast_fusion.1), channel_id=1, source_target_pairs={{0,4},{2,6},{4,0},{6,2},{1,5},{3,7},{5,1},{7,3},{8,12},{10,14},{12... | collective-permute-start | bytes 442376 | tf_op jit(solution)/shard_map/ppermute | solution.py:32
  22.6 15.4 %collective-permute-start.2 = (bf16[192,384]{1,0:T(8,128)(2,1)}, bf16[192,384]{1,0:T(8,128)(2,1)}, u32[]{:S(2)}, u32[]{:S(2)}) collective-permute-start(bf16[192,384]{1,0:T(8,128)(2,1)} %dynamic-slice_bitcast_fusion), channel_id=1, source_target_pairs={{0,6},{2,4},{4,2},{6,0},{1,7},{3,5},{5,3},{7,1},{8,14},{10,12},{12... | collective-permute-start | bytes 442376 | tf_op jit(solution)/shard_map/ppermute | solution.py:32
  43.4 11.1 %collective-permute-start.5 = (bf16[3,192,384]{2,1,0:T(8,128)(2,1)S(1)}, bf16[3,192,384]{2,1,0:T(8,128)(2,1)S(1)}, u32[]{:S(2)}, u32[]{:S(2)}) collective-permute-start(bf16[3,192,384]{2,1,0:T(8,128)(2,1)S(1)} %pad_maximum_fusion.8), channel_id=1, source_target_pairs={{0,8},{8,0},{16,24},{24,16},{1,9},{9,1},{17,25},{25,17},{2,10},{10... | collective-permute-start | bytes 1327112 | tf_op jit(solution)/shard_map/ppermute | solution.py:40
  45.1 9.2 %collective-permute-start.6 = (bf16[512,384]{1,0:T(8,128)(2,1)S(1)}, bf16[512,384]{1,0:T(8,128)(2,1)S(1)}, u32[]{:S(2)}, u32[]{:S(2)}) collective-permute-start(bf16[512,384]{1,0:T(8,128)(2,1)S(1)} %slice.250), channel_id=1, source_target_pairs={{0,4},{2,6},{4,0},{6,2},{1,5},{3,7},{5,1},{7,3},{8,12},{10,14},{12... | collective-permute-start | bytes 1179656 | tf_op jit(solution)/shard_map/ppermute | solution.py:32
  45.6 8.9 %collective-permute-start.7 = (bf16[512,384]{1,0:T(8,128)(2,1)S(1)}, bf16[512,384]{1,0:T(8,128)(2,1)S(1)}, u32[]{:S(2)}, u32[]{:S(2)}) collective-permute-start(bf16[512,384]{1,0:T(8,128)(2,1)S(1)} %slice.251), channel_id=1, source_target_pairs={{0,2},{2,0},{4,6},{6,4},{1,3},{3,1},{5,7},{7,5},{8,10},{10,8},{12,... | collective-permute-start | bytes 1179656 | tf_op jit(solution)/shard_map/ppermute | solution.py:32
  57.0 20.3 %collective-permute-start.10 = (bf16[192,1024]{1,0:T(8,128)(2,1)}, bf16[192,1024]{1,0:T(8,128)(2,1)}, u32[]{:S(2)}, u32[]{:S(2)}) collective-permute-start(bf16[192,1024]{1,0:T(8,128)(2,1)} %fusion.15), channel_id=1, source_target_pairs={{0,4},{2,6},{4,0},{6,2},{1,5},{3,7},{5,1},{7,3},{8,12},{10,14},{12... | collective-permute-start | bytes 1179656 | tf_op jit(solution)/shard_map/ppermute | solution.py:32
  58.5 18.7 %collective-permute-start.11 = (bf16[192,1024]{1,0:T(8,128)(2,1)}, bf16[192,1024]{1,0:T(8,128)(2,1)}, u32[]{:S(2)}, u32[]{:S(2)}) collective-permute-start(bf16[192,1024]{1,0:T(8,128)(2,1)} %fusion.14), channel_id=1, source_target_pairs={{0,6},{2,4},{4,2},{6,0},{1,7},{3,5},{5,3},{7,1},{8,14},{10,12},{12... | collective-permute-start | bytes 1179656 | tf_op jit(solution)/shard_map/ppermute | solution.py:32
  59.0 19.5 %collective-permute-start.9 = (bf16[192,1024]{1,0:T(8,128)(2,1)}, bf16[192,1024]{1,0:T(8,128)(2,1)}, u32[]{:S(2)}, u32[]{:S(2)}) collective-permute-start(bf16[192,1024]{1,0:T(8,128)(2,1)} %fusion.16), channel_id=1, source_target_pairs={{0,2},{2,0},{4,6},{6,4},{1,3},{3,1},{5,7},{7,5},{8,10},{10,8},{12,... | collective-permute-start | bytes 1179656 | tf_op jit(solution)/shard_map/ppermute | solution.py:32
  79.9 27.3 %collective-permute-start.13 = (bf16[3,192,1024]{2,1,0:T(8,128)(2,1)S(1)}, bf16[3,192,1024]{2,1,0:T(8,128)(2,1)S(1)}, u32[]{:S(2)}, u32[]{:S(2)}) collective-permute-start(bf16[3,192,1024]{2,1,0:T(8,128)(2,1)S(1)} %pad_maximum_fusion.3), channel_id=1, source_target_pairs={{0,8},{8,0},{16,24},{24,16},{1,9},{9,1},{17,25},{25,17},{2,10},{10... | collective-permute-start | bytes 3538952 | tf_op jit(solution)/shard_map/ppermute | solution.py:40
  81.1 17.0 %collective-permute-start.14 = (bf16[640,384]{1,0:T(8,128)(2,1)S(1)}, bf16[640,384]{1,0:T(8,128)(2,1)S(1)}, u32[]{:S(2)}, u32[]{:S(2)}) collective-permute-start(bf16[640,384]{1,0:T(8,128)(2,1)S(1)} %copy-done.79), channel_id=1, source_target_pairs={{0,2},{2,0},{4,6},{6,4},{1,3},{3,1},{5,7},{7,5},{8,10},{10,8},{12,... | collective-permute-start | bytes 1474568 | tf_op jit(solution)/shard_map/ppermute | solution.py:32
  81.6 16.5 %collective-permute-start.15 = (bf16[640,384]{1,0:T(8,128)(2,1)S(1)}, bf16[640,384]{1,0:T(8,128)(2,1)S(1)}, u32[]{:S(2)}, u32[]{:S(2)}) collective-permute-start(bf16[640,384]{1,0:T(8,128)(2,1)S(1)} %copy-done.78), channel_id=1, source_target_pairs={{0,4},{2,6},{4,0},{6,2},{1,5},{3,7},{5,1},{7,3},{8,12},{10,14},{12... | collective-permute-start | bytes 1474568 | tf_op jit(solution)/shard_map/ppermute | solution.py:32
  82.5 23.1 %collective-permute-start.16 = (bf16[640,384]{1,0:T(8,128)(2,1)S(1)}, bf16[640,384]{1,0:T(8,128)(2,1)S(1)}, u32[]{:S(2)}, u32[]{:S(2)}) collective-permute-start(bf16[640,384]{1,0:T(8,128)(2,1)S(1)} %copy-done.77), channel_id=1, source_target_pairs={{0,6},{2,4},{4,2},{6,0},{1,7},{3,5},{5,3},{7,1},{8,14},{10,12},{12... | collective-permute-start | bytes 1474568 | tf_op jit(solution)/shard_map/ppermute | solution.py:32
  109.5 37.7 %collective-permute-start.22 = (bf16[3,640,384]{2,1,0:T(8,128)(2,1)}, bf16[3,640,384]{2,1,0:T(8,128)(2,1)}, u32[]{:S(2)}, u32[]{:S(2)}) collective-permute-start(bf16[3,640,384]{2,1,0:T(8,128)(2,1)} %pad_maximum_fusion.2), channel_id=1, source_target_pairs={{0,8},{8,0},{16,24},{24,16},{1,9},{9,1},{17,25},{25,17},{2,10},{10... | collective-permute-start | bytes 4423688 | tf_op jit(solution)/shard_map/ppermute | solution.py:40
  110.7 20.4 %collective-permute-start.18 = (bf16[1024,384]{1,0:T(8,128)(2,1)S(1)}, bf16[1024,384]{1,0:T(8,128)(2,1)S(1)}, u32[]{:S(2)}, u32[]{:S(2)}) collective-permute-start(bf16[1024,384]{1,0:T(8,128)(2,1)S(1)} %copy-done.26), channel_id=1, source_target_pairs={{0,2},{2,0},{4,6},{6,4},{1,3},{3,1},{5,7},{7,5},{8,10},{10,8},{12,... | collective-permute-start | bytes 2359304 | tf_op jit(solution)/shard_map/ppermute | solution.py:32
  111.2 20.5 %collective-permute-start.19 = (bf16[1024,384]{1,0:T(8,128)(2,1)S(1)}, bf16[1024,384]{1,0:T(8,128)(2,1)S(1)}, u32[]{:S(2)}, u32[]{:S(2)}) collective-permute-start(bf16[1024,384]{1,0:T(8,128)(2,1)S(1)} %copy-done.26), channel_id=1, source_target_pairs={{0,4},{2,6},{4,0},{6,2},{1,5},{3,7},{5,1},{7,3},{8,12},{10,14},{12... | collective-permute-start | bytes 2359304 | tf_op jit(solution)/shard_map/ppermute | solution.py:32
  112.1 34.9 %collective-permute-start.20 = (bf16[1024,384]{1,0:T(8,128)(2,1)S(1)}, bf16[1024,384]{1,0:T(8,128)(2,1)}, u32[]{:S(2)}, u32[]{:S(2)}) collective-permute-start(bf16[1024,384]{1,0:T(8,128)(2,1)S(1)} %pad_maximum_fusion.7.refs_0_), channel_id=1, source_target_pairs={{0,2},{2,0},{4,6},{6,4},{1,3},{3,1},{5,7},{7,5},{8,10},{10,8},{12,... | collective-permute-start | bytes 2359304 | tf_op jit(solution)/shard_map/ppermute | solution.py:32
  113.6 33.6 %collective-permute-start.21 = (bf16[1024,384]{1,0:T(8,128)(2,1)S(1)}, bf16[1024,384]{1,0:T(8,128)(2,1)}, u32[]{:S(2)}, u32[]{:S(2)}) collective-permute-start(bf16[1024,384]{1,0:T(8,128)(2,1)S(1)} %pad_maximum_fusion.7.refs_0_), channel_id=1, source_target_pairs={{0,4},{2,6},{4,0},{6,2},{1,5},{3,7},{5,1},{7,3},{8,12},{10,14},{12... | collective-permute-start | bytes 2359304 | tf_op jit(solution)/shard_map/ppermute | solution.py:32
  153.2 15.4 %collective-permute-start.23 = (bf16[512,384]{1,0:T(8,128)(2,1)S(1)}, bf16[512,384]{1,0:T(8,128)(2,1)S(1)}, u32[]{:S(2)}, u32[]{:S(2)}) collective-permute-start(bf16[512,384]{1,0:T(8,128)(2,1)S(1)} %slice.254), channel_id=1, source_target_pairs={{0,4},{2,6},{4,0},{6,2},{1,5},{3,7},{5,1},{7,3},{8,12},{10,14},{12... | collective-permute-start | bytes 1179656 | tf_op jit(solution)/shard_map/ppermute | solution.py:32
  154.4 14.1 %collective-permute-start.24 = (bf16[512,384]{1,0:T(8,128)(2,1)S(1)}, bf16[512,384]{1,0:T(8,128)(2,1)S(1)}, u32[]{:S(2)}, u32[]{:S(2)}) collective-permute-start(bf16[512,384]{1,0:T(8,128)(2,1)S(1)} %slice.255), channel_id=1, source_target_pairs={{0,2},{2,0},{4,6},{6,4},{1,3},{3,1},{5,7},{7,5},{8,10},{10,8},{12,... | collective-permute-start | bytes 1179656 | tf_op jit(solution)/shard_map/ppermute | solution.py:32
  155.9 17.2 %collective-permute-start.26 = (bf16[512,384]{1,0:T(8,128)(2,1)S(1)}, bf16[512,384]{1,0:T(8,128)(2,1)S(1)}, u32[]{:S(2)}, u32[]{:S(2)}) collective-permute-start(bf16[512,384]{1,0:T(8,128)(2,1)S(1)} %slice.252), channel_id=1, source_target_pairs={{0,4},{2,6},{4,0},{6,2},{1,5},{3,7},{5,1},{7,3},{8,12},{10,14},{12... | collective-permute-start | bytes 1179656 | tf_op jit(solution)/shard_map/ppermute | solution.py:32
  156.7 17.3 %collective-permute-start.27 = (bf16[512,384]{1,0:T(8,128)(2,1)S(1)}, bf16[512,384]{1,0:T(8,128)(2,1)S(1)}, u32[]{:S(2)}, u32[]{:S(2)}) collective-permute-start(bf16[512,384]{1,0:T(8,128)(2,1)S(1)} %slice.253), channel_id=1, source_target_pairs={{0,2},{2,0},{4,6},{6,4},{1,3},{3,1},{5,7},{7,5},{8,10},{10,8},{12,... | collective-permute-start | bytes 1179656 | tf_op jit(solution)/shard_map/ppermute | solution.py:32
  174.1 13.2 %collective-permute-start.28 = (bf16[1536,1024]{1,0:T(8,128)(2,1)S(1)}, bf16[1536,1024]{1,0:T(8,128)(2,1)}, u32[]{:S(2)}, u32[]{:S(2)}) collective-permute-start(bf16[1536,1024]{1,0:T(8,128)(2,1)S(1)} %bitcast.101), channel_id=1, source_target_pairs={{0,1},{1,0},{2,3},{3,2},{4,5},{5,4},{6,7},{7,6},{8,9},{9,8},{10,11... | collective-permute-start | bytes 9437192 | tf_op jit(solution)/shard_map/ppermute | solution.py:36
  218.5 20.1 %collective-permute-start.29 = (bf16[512,768]{1,0:T(8,128)(2,1)S(1)}, bf16[512,768]{1,0:T(8,128)(2,1)S(1)}, u32[]{:S(2)}, u32[]{:S(2)}) collective-permute-start(bf16[512,768]{1,0:T(8,128)(2,1)S(1)} %get-tuple-element.824), channel_id=1, source_target_pairs={{0,2},{2,0},{4,6},{6,4},{1,3},{3,1},{5,7},{7,5},{8,10},{10,8},{12,... | collective-permute-start | bytes 2359304 | tf_op jit(solution)/shard_map/ppermute | solution.py:32
  220.1 18.8 %collective-permute-start.30 = (bf16[512,768]{1,0:T(8,128)(2,1)S(1)}, bf16[512,768]{1,0:T(8,128)(2,1)S(1)}, u32[]{:S(2)}, u32[]{:S(2)}) collective-permute-start(bf16[512,768]{1,0:T(8,128)(2,1)S(1)} %get-tuple-element.826), channel_id=1, source_target_pairs={{0,4},{2,6},{4,0},{6,2},{1,5},{3,7},{5,1},{7,3},{8,12},{10,14},{12... | collective-permute-start | bytes 2359304 | tf_op jit(solution)/shard_map/ppermute | solution.py:32
  220.9 17.7 %collective-permute-start.31 = (f32[8,128]{1,0:T(8,128)S(1)}, f32[8,128]{1,0:T(8,128)S(1)}, u32[]{:S(2)}, u32[]{:S(2)}) collective-permute-start(f32[8,128]{1,0:T(8,128)S(1)} %bitcast.123), channel_id=1, source_target_pairs={{0,2},{2,0},{4,6},{6,4},{1,3},{3,1},{5,7},{7,5},{8,10},{10,8},{12,... | collective-permute-start | bytes 12296 | tf_op jit(solution)/shard_map/ppermute | solution.py:32
  239.1 12.3 %collective-permute-start.32 = (bf16[4,4,96,1536]{3,2,1,0:T(8,128)(2,1)}, bf16[4,4,96,1536]{3,2,1,0:T(8,128)(2,1)S(1)}, u32[]{:S(2)}, u32[]{:S(2)}) collective-permute-start(bf16[4,4,96,1536]{3,2,1,0:T(8,128)(2,1)} %shard_map.211), channel_id=1, source_target_pairs={{0,1},{1,0},{2,3},{3,2},{4,5},{5,4},{6,7},{7,6},{8,9},{9,8},{10,11... | collective-permute-start | bytes 14155784 | tf_op jit(solution)/shard_map/ppermute | solution.py:36
  239.2 11.6 %collective-permute-start.33 = (bf16[512,384]{1,0:T(8,128)(2,1)S(1)}, bf16[512,384]{1,0:T(8,128)(2,1)S(1)}, u32[]{:S(2)}, u32[]{:S(2)}) collective-permute-start(bf16[512,384]{1,0:T(8,128)(2,1)S(1)} %add_convert_fusion.7), channel_id=1, source_target_pairs={{0,4},{2,6},{4,0},{6,2},{1,5},{3,7},{5,1},{7,3},{8,12},{10,14},{12... | collective-permute-start | bytes 1179656 | tf_op jit(solution)/shard_map/ppermute | solution.py:32
  240.2 11.2 %collective-permute-start.34 = (bf16[512,384]{1,0:T(8,128)(2,1)S(1)}, bf16[512,384]{1,0:T(8,128)(2,1)S(1)}, u32[]{:S(2)}, u32[]{:S(2)}) collective-permute-start(bf16[512,384]{1,0:T(8,128)(2,1)S(1)} %add_convert_fusion.6), channel_id=1, source_target_pairs={{0,2},{2,0},{4,6},{6,4},{1,3},{3,1},{5,7},{7,5},{8,10},{10,8},{12,... | collective-permute-start | bytes 1179656 | tf_op jit(solution)/shard_map/ppermute | solution.py:32
  241.7 9.1 %collective-permute-start.35 = (f32[8,128]{1,0:T(8,128)S(1)}, f32[8,128]{1,0:T(8,128)S(1)}, u32[]{:S(2)}, u32[]{:S(2)}) collective-permute-start(f32[8,128]{1,0:T(8,128)S(1)} %add.417), channel_id=1, source_target_pairs={{0,4},{2,6},{4,0},{6,2},{1,5},{3,7},{5,1},{7,3},{8,12},{10,14},{12... | collective-permute-start | bytes 12296 | tf_op jit(solution)/shard_map/ppermute | solution.py:32
  258.1 226.5 %all-gather.3.cloned.1.call-start = ((), (), s32[]{:S(2)}) async-start(), calls=%async_computation.2 | async-start | bytes 5898240 | tf_op jit(solution)/shard_map/all_gather | solution.py:1102
  263.0 18.8 %collective-permute-start.36 = (bf16[1024,384]{1,0:T(8,128)(2,1)S(1)}, bf16[1024,384]{1,0:T(8,128)(2,1)S(1)}, u32[]{:S(2)}, u32[]{:S(2)}) collective-permute-start(bf16[1024,384]{1,0:T(8,128)(2,1)S(1)} %get-tuple-element.941.x0), channel_id=1, source_target_pairs={{0,2},{2,0},{4,6},{6,4},{1,3},{3,1},{5,7},{7,5},{8,10},{10,8},{12,... | collective-permute-start | bytes 2359304 | tf_op jit(solution)/shard_map/ppermute | solution.py:32
  264.5 18.5 %collective-permute-start.37 = (bf16[1024,384]{1,0:T(8,128)(2,1)S(1)}, bf16[1024,384]{1,0:T(8,128)(2,1)S(1)}, u32[]{:S(2)}, u32[]{:S(2)}) collective-permute-start(bf16[1024,384]{1,0:T(8,128)(2,1)S(1)} %get-tuple-element.941.x0), channel_id=1, source_target_pairs={{0,4},{2,6},{4,0},{6,2},{1,5},{3,7},{5,1},{7,3},{8,12},{10,14},{12... | collective-permute-start | bytes 2359304 | tf_op jit(solution)/shard_map/ppermute | solution.py:32
  283.1 9.3 %collective-permute-start.38 = (bf16[512,384]{1,0:T(8,128)(2,1)S(1)}, bf16[512,384]{1,0:T(8,128)(2,1)S(1)}, u32[]{:S(2)}, u32[]{:S(2)}) collective-permute-start(bf16[512,384]{1,0:T(8,128)(2,1)S(1)} %slice.268), channel_id=1, source_target_pairs={{0,4},{2,6},{4,0},{6,2},{1,5},{3,7},{5,1},{7,3},{8,12},{10,14},{12... | collective-permute-start | bytes 1179656 | tf_op jit(solution)/shard_map/ppermute | solution.py:32
  284.0 9.0 %collective-permute-start.39 = (bf16[512,384]{1,0:T(8,128)(2,1)S(1)}, bf16[512,384]{1,0:T(8,128)(2,1)S(1)}, u32[]{:S(2)}, u32[]{:S(2)}) collective-permute-start(bf16[512,384]{1,0:T(8,128)(2,1)S(1)} %slice.269), channel_id=1, source_target_pairs={{0,2},{2,0},{4,6},{6,4},{1,3},{3,1},{5,7},{7,5},{8,10},{10,8},{12,... | collective-permute-start | bytes 1179656 | tf_op jit(solution)/shard_map/ppermute | solution.py:32
  297.7 23.6 %collective-permute-start.42 = (bf16[512,768]{1,0:T(8,128)(2,1)}, bf16[512,768]{1,0:T(8,128)(2,1)}, u32[]{:S(2)}, u32[]{:S(2)}) collective-permute-start(bf16[512,768]{1,0:T(8,128)(2,1)} %get-tuple-element.975), channel_id=1, source_target_pairs={{0,2},{2,0},{4,6},{6,4},{1,3},{3,1},{5,7},{7,5},{8,10},{10,8},{12,... | collective-permute-start | bytes 2359304 | tf_op jit(solution)/shard_map/ppermute | solution.py:32
  298.5 22.7 %collective-permute-start.43 = (bf16[512,768]{1,0:T(8,128)(2,1)}, bf16[512,768]{1,0:T(8,128)(2,1)}, u32[]{:S(2)}, u32[]{:S(2)}) collective-permute-start(bf16[512,768]{1,0:T(8,128)(2,1)} %get-tuple-element.977), channel_id=1, source_target_pairs={{0,4},{2,6},{4,0},{6,2},{1,5},{3,7},{5,1},{7,3},{8,12},{10,14},{12... | collective-permute-start | bytes 2359304 | tf_op jit(solution)/shard_map/ppermute | solution.py:32
  301.2 20.0 %collective-permute-start.44 = (bf16[4,48,384]{2,1,0:T(8,128)(2,1)}, bf16[4,48,384]{2,1,0:T(8,128)(2,1)S(1)}, u32[]{:S(2)}, u32[]{:S(2)}) collective-permute-start(bf16[4,48,384]{2,1,0:T(8,128)(2,1)} %broadcast_select_fusion.4), channel_id=1, source_target_pairs={{0,8},{24,16},{1,9},{25,17},{2,10},{26,18},{3,11},{27,19},{4,12},{... | collective-permute-start | bytes 442376 | tf_op jit(solution)/shard_map/ppermute | solution.py:163
  325.1 12.7 %collective-permute-start.46 = (bf16[512,384]{1,0:T(8,128)(2,1)S(1)}, bf16[512,384]{1,0:T(8,128)(2,1)S(1)}, u32[]{:S(2)}, u32[]{:S(2)}) collective-permute-start(bf16[512,384]{1,0:T(8,128)(2,1)S(1)} %add_convert_fusion.5), channel_id=1, source_target_pairs={{0,4},{2,6},{4,0},{6,2},{1,5},{3,7},{5,1},{7,3},{8,12},{10,14},{12... | collective-permute-start | bytes 1179656 | tf_op jit(solution)/shard_map/ppermute | solution.py:32
  326.2 11.6 %collective-permute-start.47 = (bf16[512,384]{1,0:T(8,128)(2,1)S(1)}, bf16[512,384]{1,0:T(8,128)(2,1)S(1)}, u32[]{:S(2)}, u32[]{:S(2)}) collective-permute-start(bf16[512,384]{1,0:T(8,128)(2,1)S(1)} %add_convert_fusion.4), channel_id=1, source_target_pairs={{0,2},{2,0},{4,6},{6,4},{1,3},{3,1},{5,7},{7,5},{8,10},{10,8},{12,... | collective-permute-start | bytes 1179656 | tf_op jit(solution)/shard_map/ppermute | solution.py:32
  327.5 10.3 %collective-permute-start.48 = (bf16[4,48,384]{2,1,0:T(8,128)(2,1)S(1)}, bf16[4,48,384]{2,1,0:T(8,128)(2,1)S(1)}, u32[]{:S(2)}, u32[]{:S(2)}) collective-permute-start(bf16[4,48,384]{2,1,0:T(8,128)(2,1)S(1)} %get-tuple-element.1007), channel_id=1, source_target_pairs={{0,8},{8,16},{1,9},{9,17},{2,10},{10,18},{3,11},{11,19},{4,12},{12... | collective-permute-start | bytes 442376 | tf_op jit(solution)/shard_map/ppermute | solution.py:165
  328.8 8.9 %collective-permute-start.49 = (bf16[4,48,384]{2,1,0:T(8,128)(2,1)S(1)}, bf16[4,48,384]{2,1,0:T(8,128)(2,1)S(1)}, u32[]{:S(2)}, u32[]{:S(2)}) collective-permute-start(bf16[4,48,384]{2,1,0:T(8,128)(2,1)S(1)} %get-tuple-element.1008), channel_id=1, source_target_pairs={{24,16},{16,8},{25,17},{17,9},{26,18},{18,10},{27,19},{19,11},{28,... | collective-permute-start | bytes 442376 | tf_op jit(solution)/shard_map/ppermute | solution.py:165
  345.1 14.2 %collective-permute-start.54 = (bf16[4,96,384]{2,1,0:T(8,128)(2,1)S(1)}, bf16[4,96,384]{2,1,0:T(8,128)(2,1)S(1)}, u32[]{:S(2)}, u32[]{:S(2)}) collective-permute-start(bf16[4,96,384]{2,1,0:T(8,128)(2,1)S(1)} %dynamic-slice_select_fusion), channel_id=1, source_target_pairs={{0,8},{24,16},{1,9},{25,17},{2,10},{26,18},{3,11},{27,19},{4,12},{... | collective-permute-start | bytes 884744 | tf_op jit(solution)/shard_map/ppermute | solution.py:163
  354.1 10.0 %collective-permute-start.50 = (bf16[96,1536]{1,0:T(8,128)(2,1)S(1)}, bf16[96,1536]{1,0:T(8,128)(2,1)S(1)}, u32[]{:S(2)}, u32[]{:S(2)}) collective-permute-start(bf16[96,1536]{1,0:T(8,128)(2,1)S(1)} %get-tuple-element.1173), channel_id=1, source_target_pairs={{0,2},{2,0},{4,6},{6,4},{1,3},{3,1},{5,7},{7,5},{8,10},{10,8},{12,... | collective-permute-start | bytes 884744 | tf_op jit(solution)/shard_map/ppermute | solution.py:32
  355.6 14.8 %collective-permute-start.51 = (bf16[96,1536]{1,0:T(8,128)(2,1)S(1)}, bf16[96,1536]{1,0:T(8,128)(2,1)S(1)}, u32[]{:S(2)}, u32[]{:S(2)}) collective-permute-start(bf16[96,1536]{1,0:T(8,128)(2,1)S(1)} %get-tuple-element.1172), channel_id=1, source_target_pairs={{0,4},{2,6},{4,0},{6,2},{1,5},{3,7},{5,1},{7,3},{8,12},{10,14},{12... | collective-permute-start | bytes 884744 | tf_op jit(solution)/shard_map/ppermute | solution.py:32
  357.1 13.3 %collective-permute-start.52 = (bf16[96,1536]{1,0:T(8,128)(2,1)S(1)}, bf16[96,1536]{1,0:T(8,128)(2,1)S(1)}, u32[]{:S(2)}, u32[]{:S(2)}) collective-permute-start(bf16[96,1536]{1,0:T(8,128)(2,1)S(1)} %get-tuple-element.1171), channel_id=1, source_target_pairs={{0,6},{2,4},{4,2},{6,0},{1,7},{3,5},{5,3},{7,1},{8,14},{10,12},{12... | collective-permute-start | bytes 884744 | tf_op jit(solution)/shard_map/ppermute | solution.py:32
  374.1 20.9 %collective-permute-start.55 = (bf16[4,96,384]{2,1,0:T(8,128)(2,1)S(1)}, bf16[4,96,384]{2,1,0:T(8,128)(2,1)S(1)}, u32[]{:S(2)}, u32[]{:S(2)}) collective-permute-start(bf16[4,96,384]{2,1,0:T(8,128)(2,1)S(1)} %get-tuple-element.1062), channel_id=1, source_target_pairs={{0,8},{8,16},{1,9},{9,17},{2,10},{10,18},{3,11},{11,19},{4,12},{12... | collective-permute-start | bytes 884744 | tf_op jit(solution)/shard_map/ppermute | solution.py:165
  375.7 19.3 %collective-permute-start.56 = (bf16[4,96,384]{2,1,0:T(8,128)(2,1)S(1)}, bf16[4,96,384]{2,1,0:T(8,128)(2,1)S(1)}, u32[]{:S(2)}, u32[]{:S(2)}) collective-permute-start(bf16[4,96,384]{2,1,0:T(8,128)(2,1)S(1)} %get-tuple-element.1063), channel_id=1, source_target_pairs={{24,16},{16,8},{25,17},{17,9},{26,18},{18,10},{27,19},{19,11},{28,... | collective-permute-start | bytes 884744 | tf_op jit(solution)/shard_map/ppermute | solution.py:165
  376.4 16.2 %collective-permute-start.57 = (bf16[4,48,384]{2,1,0:T(8,128)(2,1)S(1)}, bf16[4,48,384]{2,1,0:T(8,128)(2,1)S(1)}, u32[]{:S(2)}, u32[]{:S(2)}) collective-permute-start(bf16[4,48,384]{2,1,0:T(8,128)(2,1)S(1)} %get-tuple-element.1064), channel_id=1, source_target_pairs={{0,8},{8,16},{16,24},{1,9},{9,17},{17,25},{2,10},{10,18},{18,26},{... | collective-permute-start | bytes 442376 | tf_op jit(solution)/shard_map/ppermute | solution.py:165
  379.7 15.2 %collective-permute-start.58 = (bf16[4,48,384]{2,1,0:T(8,128)(2,1)S(1)}, bf16[4,48,384]{2,1,0:T(8,128)(2,1)S(1)}, u32[]{:S(2)}, u32[]{:S(2)}) collective-permute-start(bf16[4,48,384]{2,1,0:T(8,128)(2,1)S(1)} %get-tuple-element.1065), channel_id=1, source_target_pairs={{24,16},{16,8},{8,0},{25,17},{17,9},{9,1},{26,18},{18,10},{10,2},{... | collective-permute-start | bytes 442376 | tf_op jit(solution)/shard_map/ppermute | solution.py:165
  395.7 39.4 %collective-permute-start.59 = (bf16[512,768]{1,0:T(8,128)(2,1)}, bf16[512,768]{1,0:T(8,128)(2,1)S(1)}, u32[]{:S(2)}, u32[]{:S(2)}) collective-permute-start(bf16[512,768]{1,0:T(8,128)(2,1)} %get-tuple-element.1076), channel_id=1, source_target_pairs={{0,2},{2,0},{4,6},{6,4},{1,3},{3,1},{5,7},{7,5},{8,10},{10,8},{12,... | collective-permute-start | bytes 2359304 | tf_op jit(solution)/shard_map/ppermute | solution.py:32
  396.9 38.3 %collective-permute-start.60 = (bf16[512,768]{1,0:T(8,128)(2,1)}, bf16[512,768]{1,0:T(8,128)(2,1)}, u32[]{:S(2)}, u32[]{:S(2)}) collective-permute-start(bf16[512,768]{1,0:T(8,128)(2,1)} %get-tuple-element.1078), channel_id=1, source_target_pairs={{0,4},{2,6},{4,0},{6,2},{1,5},{3,7},{5,1},{7,3},{8,12},{10,14},{12... | collective-permute-start | bytes 2359304 | tf_op jit(solution)/shard_map/ppermute | solution.py:32
  399.8 25.6 %collective-permute-start.61 = (bf16[4,96,384]{2,1,0:T(8,128)(2,1)}, bf16[4,96,384]{2,1,0:T(8,128)(2,1)S(1)}, u32[]{:S(2)}, u32[]{:S(2)}) collective-permute-start(bf16[4,96,384]{2,1,0:T(8,128)(2,1)} %get-tuple-element.1085), channel_id=1, source_target_pairs={{0,8},{8,16},{16,24},{1,9},{9,17},{17,25},{2,10},{10,18},{18,26},{... | collective-permute-start | bytes 884744 | tf_op jit(solution)/shard_map/ppermute | solution.py:165
  414.7 20.5 %collective-permute-start.62 = (bf16[4,96,384]{2,1,0:T(8,128)(2,1)}, bf16[4,96,384]{2,1,0:T(8,128)(2,1)S(1)}, u32[]{:S(2)}, u32[]{:S(2)}) collective-permute-start(bf16[4,96,384]{2,1,0:T(8,128)(2,1)} %get-tuple-element.1086), channel_id=1, source_target_pairs={{24,16},{16,8},{8,0},{25,17},{17,9},{9,1},{26,18},{18,10},{10,2},{... | collective-permute-start | bytes 884744 | tf_op jit(solution)/shard_map/ppermute | solution.py:165
  437.5 15.5 %collective-permute-start.64 = (bf16[512,384]{1,0:T(8,128)(2,1)S(1)}, bf16[512,384]{1,0:T(8,128)(2,1)S(1)}, u32[]{:S(2)}, u32[]{:S(2)}) collective-permute-start(bf16[512,384]{1,0:T(8,128)(2,1)S(1)} %add_convert_fusion.3), channel_id=1, source_target_pairs={{0,4},{2,6},{4,0},{6,2},{1,5},{3,7},{5,1},{7,3},{8,12},{10,14},{12... | collective-permute-start | bytes 1179656 | tf_op jit(solution)/shard_map/ppermute | solution.py:32
  440.2 12.9 %collective-permute-start.65 = (bf16[512,384]{1,0:T(8,128)(2,1)S(1)}, bf16[512,384]{1,0:T(8,128)(2,1)S(1)}, u32[]{:S(2)}, u32[]{:S(2)}) collective-permute-start(bf16[512,384]{1,0:T(8,128)(2,1)S(1)} %add_convert_fusion.2), channel_id=1, source_target_pairs={{0,2},{2,0},{4,6},{6,4},{1,3},{3,1},{5,7},{7,5},{8,10},{10,8},{12,... | collective-permute-start | bytes 1179656 | tf_op jit(solution)/shard_map/ppermute | solution.py:32
  459.6 17.7 %collective-permute-start.71 = (bf16[4,160,384]{2,1,0:T(8,128)(2,1)S(1)}, bf16[4,160,384]{2,1,0:T(8,128)(2,1)S(1)}, u32[]{:S(2)}, u32[]{:S(2)}) collective-permute-start(bf16[4,160,384]{2,1,0:T(8,128)(2,1)S(1)} %fusion.10), channel_id=1, source_target_pairs={{0,8},{8,16},{16,24},{1,9},{9,17},{17,25},{2,10},{10,18},{18,26},{... | collective-permute-start | bytes 1474568 | tf_op jit(solution)/shard_map/ppermute | solution.py:192
  461.5 18.5 %collective-permute-start.72 = (bf16[4,160,384]{2,1,0:T(8,128)(2,1)S(1)}, bf16[4,160,384]{2,1,0:T(8,128)(2,1)}, u32[]{:S(2)}, u32[]{:S(2)}) collective-permute-start(bf16[4,160,384]{2,1,0:T(8,128)(2,1)S(1)} %fusion.10), channel_id=1, source_target_pairs={{24,16},{16,8},{8,0},{25,17},{17,9},{9,1},{26,18},{18,10},{10,2},{... | collective-permute-start | bytes 1474568 | tf_op jit(solution)/shard_map/ppermute | solution.py:193
  479.9 11.2 %collective-permute-start.73 = (bf16[4,160,384]{2,1,0:T(8,128)(2,1)S(1)}, bf16[4,160,384]{2,1,0:T(8,128)(2,1)S(1)}, u32[]{:S(2)}, u32[]{:S(2)}) collective-permute-start(bf16[4,160,384]{2,1,0:T(8,128)(2,1)S(1)} %collective-permute-done.71), channel_id=1, source_target_pairs={{8,16},{16,24},{9,17},{17,25},{10,18},{18,26},{11,19},{19,27},{12,... | collective-permute-start | bytes 1474568 | tf_op jit(solution)/shard_map/ppermute | solution.py:192
  480.6 16.2 %collective-permute-start.74 = (bf16[4,160,384]{2,1,0:T(8,128)(2,1)}, bf16[4,160,384]{2,1,0:T(8,128)(2,1)S(1)}, u32[]{:S(2)}, u32[]{:S(2)}) collective-permute-start(bf16[4,160,384]{2,1,0:T(8,128)(2,1)} %collective-permute-done.72), channel_id=1, source_target_pairs={{16,8},{8,0},{17,9},{9,1},{18,10},{10,2},{19,11},{11,3},{20,12},{1... | collective-permute-start | bytes 1474568 | tf_op jit(solution)/shard_map/ppermute | solution.py:193
  496.9 14.0 %collective-permute-start.75 = (bf16[4,160,384]{2,1,0:T(8,128)(2,1)S(1)}, bf16[4,160,384]{2,1,0:T(8,128)(2,1)S(1)}, u32[]{:S(2)}, u32[]{:S(2)}) collective-permute-start(bf16[4,160,384]{2,1,0:T(8,128)(2,1)S(1)} %broadcast_select_fusion), channel_id=1, source_target_pairs={{16,24},{8,0},{17,25},{9,1},{18,26},{10,2},{19,27},{11,3},{20,28},... | collective-permute-start | bytes 1474568 | tf_op jit(solution)/shard_map/ppermute | solution.py:187
  (110 other events, 977.7 us)
Sparse Core Ops, SparseCore 0:
  258.2 90.8 reduce-scatter.1
  371.7 102.7 all-gather.2

commit v7 on v6

--- a/solution.py
+++ b/solution.py
@@ -420,10 +420,6 @@
         step(number, True)
         return carry
 
-    def plain(number, carry):
-        step(number, False)
-        return carry
-
     lax.fori_loop(first, whole_from, masked, 0)
     def both(pair, carry):
         step(whole_from + 2 * pair, False)
@@ -432,8 +428,16 @@
 
     pairs = (block - whole_from) // 2
     lax.fori_loop(0, pairs, both, 0)
-    lax.fori_loop(whole_from + 2 * pairs, block, plain, 0)
-    step(block, True)
+    alone = (block - whole_from) % 2 == 1
+
+    @pl.when(alone)
+    def _():
+        step(block - 1, False)
+        step(block, True)
+
+    @pl.when(jnp.logical_not(alone))
+    def _():
+        step(block, True)
 
 
 def attend_kernel(info, own, oth, start_ref, keep, send, out, lse, full, values, top, total, acc):

time: 529 us -> 528 us (level)
  no operation moved by 1% of the time
where the time goes in v7:
time: 528 us; the launch traced here: 522 us
  waiting for transfers between devices  159 us (30%)
  Pallas kernels  134 us (25%)
  starting transfers between devices  101 us (19%)
  other arithmetic  55.9 us (11%)
  local copies, waits for them, and re-layouts  50.2 us (10%)
  between operations  18.2 us (3%)
    ppermute x47, waiting for transfers between devices, swap(): return lax.ppermute(value, 'row', [(i, i ^ step) for i in range(4)])  96.4 us
    ppermute x47, starting transfers between devices, swap(): return lax.ppermute(value, 'row', [(i, i ^ step) for i in range(4)])  52 us
    pallas_call x3, Pallas kernels, partial_sums(): call(functools.partial(partial_kernel, blocked), tuple(outs), specs, tupl...  27.4 us
    unnamed x192, local copies, waits for them, and re-layouts  22.5 us
    ppermute x4, starting transfers between devices, chain_sum(): lax.ppermute(up, 'dp', chain_up(count, 0, last))  21.1 us
    pallas_call x1, Pallas kernels, feed(): call(feed_kernel, outs, [whole(second), whole(cot), column(early), column...  17.2 us
    pallas_call x2, Pallas kernels, feed_grads(): call(feed_grads_kernel, out, [block, block, whole(back), whole(hidden)],...  17.1 us
    pallas_call x1, Pallas kernels, attend_back(): call(attend_back_kernel, outs, [whole(own), whole(oth), whole(g_own), who...  16.4 us
  transfers between devices with their start and end apart: 78, of which 38 were waited for; matrix products, arithmetic and copies ran while one was open for 13% of the time, Pallas kernels for 20%

profile of v7, /device:TPU:0, one launch (start us, length us, event | category | flops | bytes accessed | tf_op | source)
XLA Modules:
  0.0 522.1 jit_solution(12323750492183913196)
XLA Ops:
  7.2 3.0 collective-permute-start.3
  22.6 2.9 collective-permute-start.2
  25.6 3.5 multiply_convert_fusion.1
  31.5 2.1 pad_maximum_fusion.6
  35.7 2.3 fusion.11
  46.2 6.1 %fusion.7 = (f32[2048,128]{1,0:T(8,128)}, f32[2048,128]{1,0:T(8,128)}) fusion(f32[128]{0:T(128)S(1)} %get-tuple-element.1215, f32[128]{0:T(128)S(1)} %get-tuple-element.1216, f32[2048]{0:T(1024)S(1)} %get-tuple-element.1213, pred[128]{0:T(512)(128)(4,1)S(1)} %broadcast_compare_fusion), kind=kLoop, calls=%fused_computation.26 | loop fusion | flops 1048576 | bytes 2106496 | tf_op jit(solution)/shard_map/jit(_where)/select_n | solution.py:906
  52.3 2.0 collective-permute-done.6.top.refs_8_
  54.8 2.2 convolution_convert_fusion.w_own
  62.7 8.0 %shard_map.204 = (bf16[1024,1536]{1,0:T(8,128)(2,1)}, f32[1024,128]{1,0:T(8,128)S(1)}, bf16[1024,512]{1,0:T(8,128)(2,1)S(1)}, bf16[1024,512]{1,0:T(8,128)(2,1)}) custom-call(bf16[1024,384]{1,0:T(8,128)(2,1)S(1)} %copy-done.6, bf16[1024,384]{1,0:T(8,128)(2,1)S(1)} %collective-permute-done.3.x1.refs_6_, ...), custom_call_target="tpu_custom_call" | custom-call | flops 50331648 | bytes 188416 | tf_op jit(solution)/shard_map/pallas_call | solution.py:387
  70.8 6.5 %collective-permute-done.10 = bf16[192,1024]{1,0:T(8,128)(2,1)} collective-permute-done((bf16[192,1024]{1,0:T(8,128)(2,1)}, bf16[192,1024]{1,0:T(8,128)(2,1)}, u32[]{:S(2)}, u32[]{:S(2)}) %collective-permute-start.10) | collective-permute-done | bytes 393248 | tf_op jit(solution)/shard_map/ppermute | solution.py:32
  82.5 2.1 collective-permute-start.16
  84.6 13.4 %shard_map.205 = (bf16[1024,192]{1,0:T(8,128)(2,1)S(1)}, bf16[1024,192]{1,0:T(8,128)(2,1)S(1)}, bf16[2048,256]{1,0:T(8,128)(2,1)S(1)}, f32[1,4096]{1,0:T(1,128)S(1)}) custom-call(s32[17]{0:T(128)S(1)} %pad_add_fusion.info, bf16[1024,512]{1,0:T(8,128)(2,1)S(1)} %get-tuple-element.963.own, bf16[1024,512]{1,0:T(8,128)(2,1)S(1)} %collective-permute-done.12.oth, ...), custom_call_target="tpu_custom_call" | custom-call | flops 67108864 | bytes 61696 | tf_op jit(solution)/shard_map/pallas_call | solution.py:498
  98.0 7.6 %collective-permute-done.16 = bf16[640,384]{1,0:T(8,128)(2,1)S(1)} collective-permute-done((bf16[640,384]{1,0:T(8,128)(2,1)S(1)}, bf16[640,384]{1,0:T(8,128)(2,1)S(1)}, u32[]{:S(2)}, u32[]{:S(2)}) %collective-permute-start.16) | collective-permute-done | bytes 491552 | tf_op jit(solution)/shard_map/ppermute | solution.py:32
  105.5 1.7 collective-permute-done.13
  117.8 13.3 %collective-permute-done.18.x1 = bf16[1024,384]{1,0:T(8,128)(2,1)S(1)} collective-permute-done((bf16[1024,384]{1,0:T(8,128)(2,1)S(1)}, bf16[1024,384]{1,0:T(8,128)(2,1)S(1)}, u32[]{:S(2)}, u32[]{:S(2)}) %collective-permute-start.18) | collective-permute-done | bytes 786464 | tf_op jit(solution)/shard_map/ppermute | solution.py:32
  131.7 15.3 %collective-permute-done.20.refs_1_ = bf16[1024,384]{1,0:T(8,128)(2,1)} collective-permute-done((bf16[1024,384]{1,0:T(8,128)(2,1)S(1)}, bf16[1024,384]{1,0:T(8,128)(2,1)}, u32[]{:S(2)}, u32[]{:S(2)}) %collective-permute-start.20) | collective-permute-done | bytes 786464 | tf_op jit(solution)/shard_map/ppermute | solution.py:32
  149.2 1.7 constant_dynamic-update-slice_fusion
  157.7 2.0 copy-done.69
  161.4 4.2 shard_map.206
  166.8 1.7 slice.317.d_oth.w_oth
  168.6 4.6 collective-permute-done.26.refs_3_
  174.2 1.9 shard_map.208.cot
  177.1 10.4 %shard_map.207 = (bf16[1024,1536]{1,0:T(8,128)(2,1)}, f32[1024,384]{1,0:T(8,128)}, f32[1024,128]{1,0:T(8,128)S(1)}, bf16[1024,1536]{1,0:T(8,128)(2,1)}) custom-call(bf16[1024,384]{1,0:T(8,128)(2,1)S(1)} %copy-done.30, bf16[1024,384]{1,0:T(8,128)(2,1)} %collective-permute-done.20.refs_1_, bf16[1024,384]{1,0:T(8,128)(2,1)} %collective-permute-done.21.refs_2_, ...), custom_call_target="tpu_custom_call" | custom-call | flops 75497472 | bytes 303104 | tf_op jit(solution)/shard_map/pallas_call | solution.py:642
  187.5 17.2 %shard_map.209 = (bf16[1024,512]{1,0:T(8,128)(2,1)S(1)}, bf16[1024,512]{1,0:T(8,128)(2,1)S(1)}, bf16[1024,1024]{1,0:T(8,128)(2,1)}, bf16[1024,1024]{1,0:T(8,128)(2,1)}) custom-call(bf16[1024,1536]{1,0:T(8,128)(2,1)} %get-tuple-element.807.second.rest_0_, bf16[1024,1536]{1,0:T(8,128)(2,1)} %shard_map.208.cot, bf16[1536,1024]{1,0:T(8,128)(2,1)} %bitcast.102, ...), custom_call_target="tpu_custom_call" | custom-call | flops 150994944 | bytes 344064 | tf_op jit(solution)/shard_map/pallas_call | solution.py:692
  204.7 2.3 copy-done.4
  207.1 11.3 %shard_map.210 = (bf16[1024,384]{1,0:T(8,128)(2,1)S(1)}, bf16[512,768]{1,0:T(8,128)(2,1)S(1)}, bf16[512,384]{1,0:T(8,128)(2,1)S(1)}, bf16[512,768]{1,0:T(8,128)(...) custom-call(bf16[1024,1024]{1,0:T(8,128)(2,1)S(1)} %copy-done.4, ...), custom_call_target="tpu_custom_call" | custom-call | flops 100663296 | bytes 270336 | tf_op jit(solution)/shard_map/pallas_call | solution.py:764
  221.5 8.6 %shard_map.212 = bf16[4,4,96,1536]{3,2,1,0:T(8,128)(2,1)} custom-call(bf16[1024,1536]{1,0:T(8,128)(2,1)} %get-tuple-element.807.second.rest_0_, bf16[1024,1536]{1,0:T(8,128)(2,1)} %shard_map.208.cot, bf16[1024,1024]{1,0:T(8,128)(2,1)S(1)} %copy-done.5, bf16[1024,512]{1,0:T(8,128)(2,1)S(1)} %get-tuple-element.882.hidden.a_own), custom_call_target="tpu_custom_call" | custom-call | flops 75497472 | bytes 221184 | tf_op jit(solution)/shard_map/pallas_call | solution.py:789
  230.1 8.5 %shard_map.211 = bf16[4,4,96,1536]{3,2,1,0:T(8,128)(2,1)} custom-call(bf16[1024,1536]{1,0:T(8,128)(2,1)} %get-tuple-element.807.second.rest_0_, bf16[1024,1536]{1,0:T(8,128)(2,1)} %shard_map.208.cot, bf16[1024,1024]{1,0:T(8,128)(2,1)S(1)} %copy-done.3, bf16[1024,512]{1,0:T(8,128)(2,1)S(1)} %get-tuple-element.883.hidden.a_oth), custom_call_target="tpu_custom_call" | custom-call | flops 75497472 | bytes 221184 | tf_op jit(solution)/shard_map/pallas_call | solution.py:789
  242.6 8.3 %collective-permute-done.35 = f32[8,128]{1,0:T(8,128)S(1)} collective-permute-done((f32[8,128]{1,0:T(8,128)S(1)}, f32[8,128]{1,0:T(8,128)S(1)}, u32[]{:S(2)}, u32[]{:S(2)}) %collective-permute-start.35) | collective-permute-done | bytes 4128 | tf_op jit(solution)/shard_map/ppermute | solution.py:32
  252.2 6.0 %add_convert_fusion = bf16[4,4,96,1536]{3,2,1,0:T(8,128)(2,1)} fusion(bf16[4,4,96,1536]{3,2,1,0:T(8,128)(2,1)S(1)} %collective-permute-done.32, bf16[4,4,96,1536]{3,2,1,0:T(8,128)(2,1)} %shard_map.212), kind=kLoop, calls=%fused_computation | loop fusion | flops 9437184 | bytes 14155776 | tf_op jit(solution)/shard_map/convert_element_type | solution.py:1030
  266.0 8.2 %shard_map.213 = (bf16[1024,384]{1,0:T(8,128)(2,1)S(1)}, bf16[512,768]{1,0:T(8,128)(2,1)}, bf16[512,384]{1,0:T(8,128)(2,1)S(1)}, bf16[512,768]{1,0:T(8,128)(2,1)}, bf16[512,384]{1,0:T(8,128)(2,1)S(1)}) custom-call(bf16[1024,512]{1,0:T(8,128)(2,1)S(1)} %copy-done.15, bf16[1024,512]{1,0:T(8,128)(2,1)S(1)} %copy-done.17, bf16[4,512,384]{2,1,0:T(8,128)(2,1)} %copy-done.1, ...), custom_call_target="tpu_custom_call" | custom-call | flops 50331648 | bytes 131072 | tf_op jit(solution)/shard_map/pallas_call | solution.py:764
  274.3 7.6 %collective-permute-done.36.x1 = bf16[1024,384]{1,0:T(8,128)(2,1)S(1)} collective-permute-done((bf16[1024,384]{1,0:T(8,128)(2,1)S(1)}, bf16[1024,384]{1,0:T(8,128)(2,1)S(1)}, u32[]{:S(2)}, u32[]{:S(2)}) %collective-permute-start.36) | collective-permute-done | bytes 786464 | tf_op jit(solution)/shard_map/ppermute | solution.py:32
  284.9 1.9 convolution_convert_fusion.1
  286.8 5.8 %collective-permute-done.38.top = bf16[512,384]{1,0:T(8,128)(2,1)S(1)} collective-permute-done((bf16[512,384]{1,0:T(8,128)(2,1)S(1)}, bf16[512,384]{1,0:T(8,128)(2,1)S(1)}, u32[]{:S(2)}, u32[]{:S(2)}) %collective-permute-start.38) | collective-permute-done | bytes 393248 | tf_op jit(solution)/shard_map/ppermute | solution.py:32
  293.3 2.5 shard_map.214
  301.3 3.2 collective-permute-start.44
  304.5 16.4 %shard_map.215 = (bf16[1024,512]{1,0:T(8,128)(2,1)S(1)}, bf16[1024,512]{1,0:T(8,128)(2,1)S(1)}) custom-call(s32[17]{0:T(128)S(1)} %pad_add_fusion.info, bf16[1024,512]{1,0:T(8,128)(2,1)S(1)} %copy-done.19, bf16[1024,512]{1,0:T(8,128)(2,1)S(1)} %copy-done.21, bf16[1024,256]{1,0:T(8,128)(2,1)S(1)} %get-tuple-element.965.g_own, ...), custom_call_target="tpu_custom_call" | custom-call | flops 167772160 | bytes 98304 | tf_op jit(solution)/shard_map/pallas_call | solution.py:589
  329.6 3.5 shard_map.217
  333.2 4.3 shard_map.216
  339.0 3.1 collective-permute-done.53
  344.8 8.0 %collective-permute-start.54 = (bf16[4,96,384]{2,1,0:T(8,128)(2,1)S(1)}, bf16[4,96,384]{2,1,0:T(8,128)(2,1)S(1)}, u32[]{:S(2)}, u32[]{:S(2)}) collective-permute-start(bf16[4,96,384]{2,1,0:T(8,128)(2,1)S(1)} %dynamic-slice_select_fusion), channel_id=1, source_target_pairs={{0,8},{24,16},{1,9},{25,17},{2,10},{26,18},{3,11},{27,19},{4,12},{... | collective-permute-start | bytes 884744 | tf_op jit(solution)/shard_map/ppermute | solution.py:163
  360.1 4.0 collective-permute-done.50
  364.1 6.4 %collective-permute-done.51 = bf16[96,1536]{1,0:T(8,128)(2,1)S(1)} collective-permute-done((bf16[96,1536]{1,0:T(8,128)(2,1)S(1)}, bf16[96,1536]{1,0:T(8,128)(2,1)S(1)}, u32[]{:S(2)}, u32[]{:S(2)}) %collective-permute-start.51) | collective-permute-done | bytes 294944 | tf_op jit(solution)/shard_map/ppermute | solution.py:32
  376.5 3.4 collective-permute-start.57
  381.1 7.8 %shard_map.218 = (bf16[1024,384]{1,0:T(8,128)(2,1)S(1)}, bf16[512,768]{1,0:T(8,128)(2,1)}, bf16[512,384]{1,0:T(8,128)(2,1)S(1)}, bf16[512,768]{1,0:T(8,128)(2,1)...) custom-call(bf16[1024,512]{1,0:T(8,128)(2,1)S(1)} %copy-done.23, bf16[1024,512]{1,0:T(8,128)(2,1)S(1)} %copy-done.25, ...), custom_call_target="tpu_custom_call" | custom-call | flops 50331648 | bytes 188416 | tf_op jit(solution)/shard_map/pallas_call | solution.py:764
  390.5 2.2 collective-permute-done.57
  392.7 2.4 collective-permute-done.58
  397.7 2.2 add_convert_fusion.9
  399.9 14.8 %collective-permute-start.61 = (bf16[4,96,384]{2,1,0:T(8,128)(2,1)}, bf16[4,96,384]{2,1,0:T(8,128)(2,1)S(1)}, u32[]{:S(2)}, u32[]{:S(2)}) collective-permute-start(bf16[4,96,384]{2,1,0:T(8,128)(2,1)} %get-tuple-element.1085), channel_id=1, source_target_pairs={{0,8},{8,16},{16,24},{1,9},{9,17},{17,25},{2,10},{10,18},{18,26},{... | collective-permute-start | bytes 884744 | tf_op jit(solution)/shard_map/ppermute | solution.py:165
  417.9 1.7 collective-permute-done.63
  419.7 5.8 %collective-permute-done.61 = bf16[4,96,384]{2,1,0:T(8,128)(2,1)S(1)} collective-permute-done((bf16[4,96,384]{2,1,0:T(8,128)(2,1)}, bf16[4,96,384]{2,1,0:T(8,128)(2,1)S(1)}, u32[]{:S(2)}, u32[]{:S(2)}) %collective-permute-start.61) | collective-permute-done | bytes 294944 | tf_op jit(solution)/shard_map/ppermute | solution.py:165
  425.5 9.7 %collective-permute-done.62 = bf16[4,96,384]{2,1,0:T(8,128)(2,1)S(1)} collective-permute-done((bf16[4,96,384]{2,1,0:T(8,128)(2,1)}, bf16[4,96,384]{2,1,0:T(8,128)(2,1)S(1)}, u32[]{:S(2)}, u32[]{:S(2)}) %collective-permute-start.62) | collective-permute-done | bytes 294944 | tf_op jit(solution)/shard_map/ppermute | solution.py:165
  437.5 2.5 collective-permute-start.64
  442.2 2.3 collective-permute-start.68
  444.5 4.1 collective-permute-done.66
  448.9 3.3 collective-permute-done.69
  458.7 2.9 collective-permute-start.71
  463.2 14.3 %collective-permute-done.71 = bf16[4,160,384]{2,1,0:T(8,128)(2,1)S(1)} collective-permute-done((bf16[4,160,384]{2,1,0:T(8,128)(2,1)S(1)}, bf16[4,160,384]{2,1,0:T(8,128)(2,1)S(1)}, u32[]{:S(2)}, u32[]{:S(2)}) %collective-permute-start.71) | collective-permute-done | bytes 491552 | tf_op jit(solution)/shard_map/ppermute | solution.py:192
  477.4 2.6 collective-permute-done.72
  484.7 2.3 copy-done.12
  487.1 4.2 shard_map.219
  491.3 5.6 %collective-permute-done.74 = bf16[4,160,384]{2,1,0:T(8,128)(2,1)S(1)} collective-permute-done((bf16[4,160,384]{2,1,0:T(8,128)(2,1)}, bf16[4,160,384]{2,1,0:T(8,128)(2,1)S(1)}, u32[]{:S(2)}, u32[]{:S(2)}) %collective-permute-start.74) | collective-permute-done | bytes 491552 | tf_op jit(solution)/shard_map/ppermute | solution.py:193
  499.9 11.1 %collective-permute-done.75 = bf16[4,160,384]{2,1,0:T(8,128)(2,1)S(1)} collective-permute-done((bf16[4,160,384]{2,1,0:T(8,128)(2,1)S(1)}, bf16[4,160,384]{2,1,0:T(8,128)(2,1)S(1)}, u32[]{:S(2)}, u32[]{:S(2)}) %collective-permute-start.75) | collective-permute-done | bytes 491552 | tf_op jit(solution)/shard_map/ppermute | solution.py:187
  512.1 2.7 shard_map.220
  (426 shorter events, 140.7 us)
Async XLA Ops:
  7.2 345.7 %reduce-scatter.2.cloned.1.call-start = ((), (), s32[]{:S(2)}) async-start(), calls=%async_computation.1 | async-start | bytes 5898240 | tf_op jit(solution)/shard_map/reduce_scatter | solution.py:1056
  7.2 30.8 %collective-permute-start.3 = (bf16[1024,384]{1,0:T(8,128)(2,1)}, bf16[1024,384]{1,0:T(8,128)(2,1)S(1)}, u32[]{:S(2)}, u32[]{:S(2)}) collective-permute-start(bf16[1024,384]{1,0:T(8,128)(2,1)} %refs_5_), channel_id=1, source_target_pairs={{0,2},{2,0},{4,6},{6,4},{1,3},{3,1},{5,7},{7,5},{8,10},{10,8},{12,... | collective-permute-start | bytes 2359304 | tf_op jit(solution)/shard_map/ppermute | solution.py:32
  10.2 27.8 %collective-permute-start.4 = (bf16[1024,384]{1,0:T(8,128)(2,1)}, bf16[1024,384]{1,0:T(8,128)(2,1)S(1)}, u32[]{:S(2)}, u32[]{:S(2)}) collective-permute-start(bf16[1024,384]{1,0:T(8,128)(2,1)} %refs_5_), channel_id=1, source_target_pairs={{0,4},{2,6},{4,0},{6,2},{1,5},{3,7},{5,1},{7,3},{8,12},{10,14},{12... | collective-permute-start | bytes 2359304 | tf_op jit(solution)/shard_map/ppermute | solution.py:32
  22.0 16.0 %collective-permute-start = (bf16[192,384]{1,0:T(8,128)(2,1)}, bf16[192,384]{1,0:T(8,128)(2,1)S(1)}, u32[]{:S(2)}, u32[]{:S(2)}) collective-permute-start(bf16[192,384]{1,0:T(8,128)(2,1)} %dynamic-slice_bitcast_fusion.2), channel_id=1, source_target_pairs={{0,2},{2,0},{4,6},{6,4},{1,3},{3,1},{5,7},{7,5},{8,10},{10,8},{12,... | collective-permute-start | bytes 442376 | tf_op jit(solution)/shard_map/ppermute | solution.py:32
  22.5 15.4 %collective-permute-start.1 = (bf16[192,384]{1,0:T(8,128)(2,1)}, bf16[192,384]{1,0:T(8,128)(2,1)}, u32[]{:S(2)}, u32[]{:S(2)}) collective-permute-start(bf16[192,384]{1,0:T(8,128)(2,1)} %dynamic-slice_bitcast_fusion.1), channel_id=1, source_target_pairs={{0,4},{2,6},{4,0},{6,2},{1,5},{3,7},{5,1},{7,3},{8,12},{10,14},{12... | collective-permute-start | bytes 442376 | tf_op jit(solution)/shard_map/ppermute | solution.py:32
  22.6 15.4 %collective-permute-start.2 = (bf16[192,384]{1,0:T(8,128)(2,1)}, bf16[192,384]{1,0:T(8,128)(2,1)}, u32[]{:S(2)}, u32[]{:S(2)}) collective-permute-start(bf16[192,384]{1,0:T(8,128)(2,1)} %dynamic-slice_bitcast_fusion), channel_id=1, source_target_pairs={{0,6},{2,4},{4,2},{6,0},{1,7},{3,5},{5,3},{7,1},{8,14},{10,12},{12... | collective-permute-start | bytes 442376 | tf_op jit(solution)/shard_map/ppermute | solution.py:32
  43.4 11.1 %collective-permute-start.5 = (bf16[3,192,384]{2,1,0:T(8,128)(2,1)S(1)}, bf16[3,192,384]{2,1,0:T(8,128)(2,1)S(1)}, u32[]{:S(2)}, u32[]{:S(2)}) collective-permute-start(bf16[3,192,384]{2,1,0:T(8,128)(2,1)S(1)} %pad_maximum_fusion.8), channel_id=1, source_target_pairs={{0,8},{8,0},{16,24},{24,16},{1,9},{9,1},{17,25},{25,17},{2,10},{10... | collective-permute-start | bytes 1327112 | tf_op jit(solution)/shard_map/ppermute | solution.py:40
  45.1 9.2 %collective-permute-start.6 = (bf16[512,384]{1,0:T(8,128)(2,1)S(1)}, bf16[512,384]{1,0:T(8,128)(2,1)S(1)}, u32[]{:S(2)}, u32[]{:S(2)}) collective-permute-start(bf16[512,384]{1,0:T(8,128)(2,1)S(1)} %slice.250), channel_id=1, source_target_pairs={{0,4},{2,6},{4,0},{6,2},{1,5},{3,7},{5,1},{7,3},{8,12},{10,14},{12... | collective-permute-start | bytes 1179656 | tf_op jit(solution)/shard_map/ppermute | solution.py:32
  45.6 8.9 %collective-permute-start.7 = (bf16[512,384]{1,0:T(8,128)(2,1)S(1)}, bf16[512,384]{1,0:T(8,128)(2,1)S(1)}, u32[]{:S(2)}, u32[]{:S(2)}) collective-permute-start(bf16[512,384]{1,0:T(8,128)(2,1)S(1)} %slice.251), channel_id=1, source_target_pairs={{0,2},{2,0},{4,6},{6,4},{1,3},{3,1},{5,7},{7,5},{8,10},{10,8},{12,... | collective-permute-start | bytes 1179656 | tf_op jit(solution)/shard_map/ppermute | solution.py:32
  57.0 20.3 %collective-permute-start.10 = (bf16[192,1024]{1,0:T(8,128)(2,1)}, bf16[192,1024]{1,0:T(8,128)(2,1)}, u32[]{:S(2)}, u32[]{:S(2)}) collective-permute-start(bf16[192,1024]{1,0:T(8,128)(2,1)} %fusion.15), channel_id=1, source_target_pairs={{0,4},{2,6},{4,0},{6,2},{1,5},{3,7},{5,1},{7,3},{8,12},{10,14},{12... | collective-permute-start | bytes 1179656 | tf_op jit(solution)/shard_map/ppermute | solution.py:32
  58.5 18.7 %collective-permute-start.11 = (bf16[192,1024]{1,0:T(8,128)(2,1)}, bf16[192,1024]{1,0:T(8,128)(2,1)}, u32[]{:S(2)}, u32[]{:S(2)}) collective-permute-start(bf16[192,1024]{1,0:T(8,128)(2,1)} %fusion.14), channel_id=1, source_target_pairs={{0,6},{2,4},{4,2},{6,0},{1,7},{3,5},{5,3},{7,1},{8,14},{10,12},{12... | collective-permute-start | bytes 1179656 | tf_op jit(solution)/shard_map/ppermute | solution.py:32
  59.0 19.5 %collective-permute-start.9 = (bf16[192,1024]{1,0:T(8,128)(2,1)}, bf16[192,1024]{1,0:T(8,128)(2,1)}, u32[]{:S(2)}, u32[]{:S(2)}) collective-permute-start(bf16[192,1024]{1,0:T(8,128)(2,1)} %fusion.16), channel_id=1, source_target_pairs={{0,2},{2,0},{4,6},{6,4},{1,3},{3,1},{5,7},{7,5},{8,10},{10,8},{12,... | collective-permute-start | bytes 1179656 | tf_op jit(solution)/shard_map/ppermute | solution.py:32
  79.9 27.3 %collective-permute-start.13 = (bf16[3,192,1024]{2,1,0:T(8,128)(2,1)S(1)}, bf16[3,192,1024]{2,1,0:T(8,128)(2,1)S(1)}, u32[]{:S(2)}, u32[]{:S(2)}) collective-permute-start(bf16[3,192,1024]{2,1,0:T(8,128)(2,1)S(1)} %pad_maximum_fusion.3), channel_id=1, source_target_pairs={{0,8},{8,0},{16,24},{24,16},{1,9},{9,1},{17,25},{25,17},{2,10},{10... | collective-permute-start | bytes 3538952 | tf_op jit(solution)/shard_map/ppermute | solution.py:40
  81.1 16.9 %collective-permute-start.14 = (bf16[640,384]{1,0:T(8,128)(2,1)S(1)}, bf16[640,384]{1,0:T(8,128)(2,1)S(1)}, u32[]{:S(2)}, u32[]{:S(2)}) collective-permute-start(bf16[640,384]{1,0:T(8,128)(2,1)S(1)} %copy-done.79), channel_id=1, source_target_pairs={{0,2},{2,0},{4,6},{6,4},{1,3},{3,1},{5,7},{7,5},{8,10},{10,8},{12,... | collective-permute-start | bytes 1474568 | tf_op jit(solution)/shard_map/ppermute | solution.py:32
  81.6 16.4 %collective-permute-start.15 = (bf16[640,384]{1,0:T(8,128)(2,1)S(1)}, bf16[640,384]{1,0:T(8,128)(2,1)S(1)}, u32[]{:S(2)}, u32[]{:S(2)}) collective-permute-start(bf16[640,384]{1,0:T(8,128)(2,1)S(1)} %copy-done.78), channel_id=1, source_target_pairs={{0,4},{2,6},{4,0},{6,2},{1,5},{3,7},{5,1},{7,3},{8,12},{10,14},{12... | collective-permute-start | bytes 1474568 | tf_op jit(solution)/shard_map/ppermute | solution.py:32
  82.5 23.1 %collective-permute-start.16 = (bf16[640,384]{1,0:T(8,128)(2,1)S(1)}, bf16[640,384]{1,0:T(8,128)(2,1)S(1)}, u32[]{:S(2)}, u32[]{:S(2)}) collective-permute-start(bf16[640,384]{1,0:T(8,128)(2,1)S(1)} %copy-done.77), channel_id=1, source_target_pairs={{0,6},{2,4},{4,2},{6,0},{1,7},{3,5},{5,3},{7,1},{8,14},{10,12},{12... | collective-permute-start | bytes 1474568 | tf_op jit(solution)/shard_map/ppermute | solution.py:32
  109.5 37.7 %collective-permute-start.22 = (bf16[3,640,384]{2,1,0:T(8,128)(2,1)}, bf16[3,640,384]{2,1,0:T(8,128)(2,1)}, u32[]{:S(2)}, u32[]{:S(2)}) collective-permute-start(bf16[3,640,384]{2,1,0:T(8,128)(2,1)} %pad_maximum_fusion.2), channel_id=1, source_target_pairs={{0,8},{8,0},{16,24},{24,16},{1,9},{9,1},{17,25},{25,17},{2,10},{10... | collective-permute-start | bytes 4423688 | tf_op jit(solution)/shard_map/ppermute | solution.py:40
  110.7 20.4 %collective-permute-start.18 = (bf16[1024,384]{1,0:T(8,128)(2,1)S(1)}, bf16[1024,384]{1,0:T(8,128)(2,1)S(1)}, u32[]{:S(2)}, u32[]{:S(2)}) collective-permute-start(bf16[1024,384]{1,0:T(8,128)(2,1)S(1)} %copy-done.26), channel_id=1, source_target_pairs={{0,2},{2,0},{4,6},{6,4},{1,3},{3,1},{5,7},{7,5},{8,10},{10,8},{12,... | collective-permute-start | bytes 2359304 | tf_op jit(solution)/shard_map/ppermute | solution.py:32
  111.2 20.5 %collective-permute-start.19 = (bf16[1024,384]{1,0:T(8,128)(2,1)S(1)}, bf16[1024,384]{1,0:T(8,128)(2,1)S(1)}, u32[]{:S(2)}, u32[]{:S(2)}) collective-permute-start(bf16[1024,384]{1,0:T(8,128)(2,1)S(1)} %copy-done.26), channel_id=1, source_target_pairs={{0,4},{2,6},{4,0},{6,2},{1,5},{3,7},{5,1},{7,3},{8,12},{10,14},{12... | collective-permute-start | bytes 2359304 | tf_op jit(solution)/shard_map/ppermute | solution.py:32
  112.1 34.9 %collective-permute-start.20 = (bf16[1024,384]{1,0:T(8,128)(2,1)S(1)}, bf16[1024,384]{1,0:T(8,128)(2,1)}, u32[]{:S(2)}, u32[]{:S(2)}) collective-permute-start(bf16[1024,384]{1,0:T(8,128)(2,1)S(1)} %pad_maximum_fusion.7.refs_0_), channel_id=1, source_target_pairs={{0,2},{2,0},{4,6},{6,4},{1,3},{3,1},{5,7},{7,5},{8,10},{10,8},{12,... | collective-permute-start | bytes 2359304 | tf_op jit(solution)/shard_map/ppermute | solution.py:32
  113.6 33.6 %collective-permute-start.21 = (bf16[1024,384]{1,0:T(8,128)(2,1)S(1)}, bf16[1024,384]{1,0:T(8,128)(2,1)}, u32[]{:S(2)}, u32[]{:S(2)}) collective-permute-start(bf16[1024,384]{1,0:T(8,128)(2,1)S(1)} %pad_maximum_fusion.7.refs_0_), channel_id=1, source_target_pairs={{0,4},{2,6},{4,0},{6,2},{1,5},{3,7},{5,1},{7,3},{8,12},{10,14},{12... | collective-permute-start | bytes 2359304 | tf_op jit(solution)/shard_map/ppermute | solution.py:32
  153.2 15.4 %collective-permute-start.23 = (bf16[512,384]{1,0:T(8,128)(2,1)S(1)}, bf16[512,384]{1,0:T(8,128)(2,1)S(1)}, u32[]{:S(2)}, u32[]{:S(2)}) collective-permute-start(bf16[512,384]{1,0:T(8,128)(2,1)S(1)} %slice.254), channel_id=1, source_target_pairs={{0,4},{2,6},{4,0},{6,2},{1,5},{3,7},{5,1},{7,3},{8,12},{10,14},{12... | collective-permute-start | bytes 1179656 | tf_op jit(solution)/shard_map/ppermute | solution.py:32
  154.4 14.1 %collective-permute-start.24 = (bf16[512,384]{1,0:T(8,128)(2,1)S(1)}, bf16[512,384]{1,0:T(8,128)(2,1)S(1)}, u32[]{:S(2)}, u32[]{:S(2)}) collective-permute-start(bf16[512,384]{1,0:T(8,128)(2,1)S(1)} %slice.255), channel_id=1, source_target_pairs={{0,2},{2,0},{4,6},{6,4},{1,3},{3,1},{5,7},{7,5},{8,10},{10,8},{12,... | collective-permute-start | bytes 1179656 | tf_op jit(solution)/shard_map/ppermute | solution.py:32
  155.9 17.2 %collective-permute-start.26 = (bf16[512,384]{1,0:T(8,128)(2,1)S(1)}, bf16[512,384]{1,0:T(8,128)(2,1)S(1)}, u32[]{:S(2)}, u32[]{:S(2)}) collective-permute-start(bf16[512,384]{1,0:T(8,128)(2,1)S(1)} %slice.252), channel_id=1, source_target_pairs={{0,4},{2,6},{4,0},{6,2},{1,5},{3,7},{5,1},{7,3},{8,12},{10,14},{12... | collective-permute-start | bytes 1179656 | tf_op jit(solution)/shard_map/ppermute | solution.py:32
  156.7 17.3 %collective-permute-start.27 = (bf16[512,384]{1,0:T(8,128)(2,1)S(1)}, bf16[512,384]{1,0:T(8,128)(2,1)S(1)}, u32[]{:S(2)}, u32[]{:S(2)}) collective-permute-start(bf16[512,384]{1,0:T(8,128)(2,1)S(1)} %slice.253), channel_id=1, source_target_pairs={{0,2},{2,0},{4,6},{6,4},{1,3},{3,1},{5,7},{7,5},{8,10},{10,8},{12,... | collective-permute-start | bytes 1179656 | tf_op jit(solution)/shard_map/ppermute | solution.py:32
  174.1 13.4 %collective-permute-start.28 = (bf16[1536,1024]{1,0:T(8,128)(2,1)S(1)}, bf16[1536,1024]{1,0:T(8,128)(2,1)}, u32[]{:S(2)}, u32[]{:S(2)}) collective-permute-start(bf16[1536,1024]{1,0:T(8,128)(2,1)S(1)} %bitcast.101), channel_id=1, source_target_pairs={{0,1},{1,0},{2,3},{3,2},{4,5},{5,4},{6,7},{7,6},{8,9},{9,8},{10,11... | collective-permute-start | bytes 9437192 | tf_op jit(solution)/shard_map/ppermute | solution.py:36
  218.6 20.1 %collective-permute-start.29 = (bf16[512,768]{1,0:T(8,128)(2,1)S(1)}, bf16[512,768]{1,0:T(8,128)(2,1)S(1)}, u32[]{:S(2)}, u32[]{:S(2)}) collective-permute-start(bf16[512,768]{1,0:T(8,128)(2,1)S(1)} %get-tuple-element.824), channel_id=1, source_target_pairs={{0,2},{2,0},{4,6},{6,4},{1,3},{3,1},{5,7},{7,5},{8,10},{10,8},{12,... | collective-permute-start | bytes 2359304 | tf_op jit(solution)/shard_map/ppermute | solution.py:32
  220.1 18.8 %collective-permute-start.30 = (bf16[512,768]{1,0:T(8,128)(2,1)S(1)}, bf16[512,768]{1,0:T(8,128)(2,1)S(1)}, u32[]{:S(2)}, u32[]{:S(2)}) collective-permute-start(bf16[512,768]{1,0:T(8,128)(2,1)S(1)} %get-tuple-element.826), channel_id=1, source_target_pairs={{0,4},{2,6},{4,0},{6,2},{1,5},{3,7},{5,1},{7,3},{8,12},{10,14},{12... | collective-permute-start | bytes 2359304 | tf_op jit(solution)/shard_map/ppermute | solution.py:32
  221.0 17.7 %collective-permute-start.31 = (f32[8,128]{1,0:T(8,128)S(1)}, f32[8,128]{1,0:T(8,128)S(1)}, u32[]{:S(2)}, u32[]{:S(2)}) collective-permute-start(f32[8,128]{1,0:T(8,128)S(1)} %bitcast.123), channel_id=1, source_target_pairs={{0,2},{2,0},{4,6},{6,4},{1,3},{3,1},{5,7},{7,5},{8,10},{10,8},{12,... | collective-permute-start | bytes 12296 | tf_op jit(solution)/shard_map/ppermute | solution.py:32
  239.2 12.3 %collective-permute-start.32 = (bf16[4,4,96,1536]{3,2,1,0:T(8,128)(2,1)}, bf16[4,4,96,1536]{3,2,1,0:T(8,128)(2,1)S(1)}, u32[]{:S(2)}, u32[]{:S(2)}) collective-permute-start(bf16[4,4,96,1536]{3,2,1,0:T(8,128)(2,1)} %shard_map.211), channel_id=1, source_target_pairs={{0,1},{1,0},{2,3},{3,2},{4,5},{5,4},{6,7},{7,6},{8,9},{9,8},{10,11... | collective-permute-start | bytes 14155784 | tf_op jit(solution)/shard_map/ppermute | solution.py:36
  239.3 11.6 %collective-permute-start.33 = (bf16[512,384]{1,0:T(8,128)(2,1)S(1)}, bf16[512,384]{1,0:T(8,128)(2,1)S(1)}, u32[]{:S(2)}, u32[]{:S(2)}) collective-permute-start(bf16[512,384]{1,0:T(8,128)(2,1)S(1)} %add_convert_fusion.7), channel_id=1, source_target_pairs={{0,4},{2,6},{4,0},{6,2},{1,5},{3,7},{5,1},{7,3},{8,12},{10,14},{12... | collective-permute-start | bytes 1179656 | tf_op jit(solution)/shard_map/ppermute | solution.py:32
  240.3 11.2 %collective-permute-start.34 = (bf16[512,384]{1,0:T(8,128)(2,1)S(1)}, bf16[512,384]{1,0:T(8,128)(2,1)S(1)}, u32[]{:S(2)}, u32[]{:S(2)}) collective-permute-start(bf16[512,384]{1,0:T(8,128)(2,1)S(1)} %add_convert_fusion.6), channel_id=1, source_target_pairs={{0,2},{2,0},{4,6},{6,4},{1,3},{3,1},{5,7},{7,5},{8,10},{10,8},{12,... | collective-permute-start | bytes 1179656 | tf_op jit(solution)/shard_map/ppermute | solution.py:32
  241.8 9.1 %collective-permute-start.35 = (f32[8,128]{1,0:T(8,128)S(1)}, f32[8,128]{1,0:T(8,128)S(1)}, u32[]{:S(2)}, u32[]{:S(2)}) collective-permute-start(f32[8,128]{1,0:T(8,128)S(1)} %add.417), channel_id=1, source_target_pairs={{0,4},{2,6},{4,0},{6,2},{1,5},{3,7},{5,1},{7,3},{8,12},{10,14},{12... | collective-permute-start | bytes 12296 | tf_op jit(solution)/shard_map/ppermute | solution.py:32
  258.2 226.5 %all-gather.3.cloned.1.call-start = ((), (), s32[]{:S(2)}) async-start(), calls=%async_computation.2 | async-start | bytes 5898240 | tf_op jit(solution)/shard_map/all_gather | solution.py:1106
  263.1 18.8 %collective-permute-start.36 = (bf16[1024,384]{1,0:T(8,128)(2,1)S(1)}, bf16[1024,384]{1,0:T(8,128)(2,1)S(1)}, u32[]{:S(2)}, u32[]{:S(2)}) collective-permute-start(bf16[1024,384]{1,0:T(8,128)(2,1)S(1)} %get-tuple-element.941.x0), channel_id=1, source_target_pairs={{0,2},{2,0},{4,6},{6,4},{1,3},{3,1},{5,7},{7,5},{8,10},{10,8},{12,... | collective-permute-start | bytes 2359304 | tf_op jit(solution)/shard_map/ppermute | solution.py:32
  264.6 18.5 %collective-permute-start.37 = (bf16[1024,384]{1,0:T(8,128)(2,1)S(1)}, bf16[1024,384]{1,0:T(8,128)(2,1)S(1)}, u32[]{:S(2)}, u32[]{:S(2)}) collective-permute-start(bf16[1024,384]{1,0:T(8,128)(2,1)S(1)} %get-tuple-element.941.x0), channel_id=1, source_target_pairs={{0,4},{2,6},{4,0},{6,2},{1,5},{3,7},{5,1},{7,3},{8,12},{10,14},{12... | collective-permute-start | bytes 2359304 | tf_op jit(solution)/shard_map/ppermute | solution.py:32
  283.2 9.3 %collective-permute-start.38 = (bf16[512,384]{1,0:T(8,128)(2,1)S(1)}, bf16[512,384]{1,0:T(8,128)(2,1)S(1)}, u32[]{:S(2)}, u32[]{:S(2)}) collective-permute-start(bf16[512,384]{1,0:T(8,128)(2,1)S(1)} %slice.268), channel_id=1, source_target_pairs={{0,4},{2,6},{4,0},{6,2},{1,5},{3,7},{5,1},{7,3},{8,12},{10,14},{12... | collective-permute-start | bytes 1179656 | tf_op jit(solution)/shard_map/ppermute | solution.py:32
  284.1 9.0 %collective-permute-start.39 = (bf16[512,384]{1,0:T(8,128)(2,1)S(1)}, bf16[512,384]{1,0:T(8,128)(2,1)S(1)}, u32[]{:S(2)}, u32[]{:S(2)}) collective-permute-start(bf16[512,384]{1,0:T(8,128)(2,1)S(1)} %slice.269), channel_id=1, source_target_pairs={{0,2},{2,0},{4,6},{6,4},{1,3},{3,1},{5,7},{7,5},{8,10},{10,8},{12,... | collective-permute-start | bytes 1179656 | tf_op jit(solution)/shard_map/ppermute | solution.py:32
  297.8 23.2 %collective-permute-start.42 = (bf16[512,768]{1,0:T(8,128)(2,1)}, bf16[512,768]{1,0:T(8,128)(2,1)}, u32[]{:S(2)}, u32[]{:S(2)}) collective-permute-start(bf16[512,768]{1,0:T(8,128)(2,1)} %get-tuple-element.975), channel_id=1, source_target_pairs={{0,2},{2,0},{4,6},{6,4},{1,3},{3,1},{5,7},{7,5},{8,10},{10,8},{12,... | collective-permute-start | bytes 2359304 | tf_op jit(solution)/shard_map/ppermute | solution.py:32
  298.6 22.4 %collective-permute-start.43 = (bf16[512,768]{1,0:T(8,128)(2,1)}, bf16[512,768]{1,0:T(8,128)(2,1)}, u32[]{:S(2)}, u32[]{:S(2)}) collective-permute-start(bf16[512,768]{1,0:T(8,128)(2,1)} %get-tuple-element.977), channel_id=1, source_target_pairs={{0,4},{2,6},{4,0},{6,2},{1,5},{3,7},{5,1},{7,3},{8,12},{10,14},{12... | collective-permute-start | bytes 2359304 | tf_op jit(solution)/shard_map/ppermute | solution.py:32
  301.3 19.7 %collective-permute-start.44 = (bf16[4,48,384]{2,1,0:T(8,128)(2,1)}, bf16[4,48,384]{2,1,0:T(8,128)(2,1)S(1)}, u32[]{:S(2)}, u32[]{:S(2)}) collective-permute-start(bf16[4,48,384]{2,1,0:T(8,128)(2,1)} %broadcast_select_fusion.4), channel_id=1, source_target_pairs={{0,8},{24,16},{1,9},{25,17},{2,10},{26,18},{3,11},{27,19},{4,12},{... | collective-permute-start | bytes 442376 | tf_op jit(solution)/shard_map/ppermute | solution.py:163
  324.8 12.7 %collective-permute-start.46 = (bf16[512,384]{1,0:T(8,128)(2,1)S(1)}, bf16[512,384]{1,0:T(8,128)(2,1)S(1)}, u32[]{:S(2)}, u32[]{:S(2)}) collective-permute-start(bf16[512,384]{1,0:T(8,128)(2,1)S(1)} %add_convert_fusion.5), channel_id=1, source_target_pairs={{0,4},{2,6},{4,0},{6,2},{1,5},{3,7},{5,1},{7,3},{8,12},{10,14},{12... | collective-permute-start | bytes 1179656 | tf_op jit(solution)/shard_map/ppermute | solution.py:32
  325.9 11.6 %collective-permute-start.47 = (bf16[512,384]{1,0:T(8,128)(2,1)S(1)}, bf16[512,384]{1,0:T(8,128)(2,1)S(1)}, u32[]{:S(2)}, u32[]{:S(2)}) collective-permute-start(bf16[512,384]{1,0:T(8,128)(2,1)S(1)} %add_convert_fusion.4), channel_id=1, source_target_pairs={{0,2},{2,0},{4,6},{6,4},{1,3},{3,1},{5,7},{7,5},{8,10},{10,8},{12,... | collective-permute-start | bytes 1179656 | tf_op jit(solution)/shard_map/ppermute | solution.py:32
  327.2 10.3 %collective-permute-start.48 = (bf16[4,48,384]{2,1,0:T(8,128)(2,1)S(1)}, bf16[4,48,384]{2,1,0:T(8,128)(2,1)S(1)}, u32[]{:S(2)}, u32[]{:S(2)}) collective-permute-start(bf16[4,48,384]{2,1,0:T(8,128)(2,1)S(1)} %get-tuple-element.1007), channel_id=1, source_target_pairs={{0,8},{8,16},{1,9},{9,17},{2,10},{10,18},{3,11},{11,19},{4,12},{12... | collective-permute-start | bytes 442376 | tf_op jit(solution)/shard_map/ppermute | solution.py:165
  328.5 8.9 %collective-permute-start.49 = (bf16[4,48,384]{2,1,0:T(8,128)(2,1)S(1)}, bf16[4,48,384]{2,1,0:T(8,128)(2,1)S(1)}, u32[]{:S(2)}, u32[]{:S(2)}) collective-permute-start(bf16[4,48,384]{2,1,0:T(8,128)(2,1)S(1)} %get-tuple-element.1008), channel_id=1, source_target_pairs={{24,16},{16,8},{25,17},{17,9},{26,18},{18,10},{27,19},{19,11},{28,... | collective-permute-start | bytes 442376 | tf_op jit(solution)/shard_map/ppermute | solution.py:165
  344.8 14.6 %collective-permute-start.54 = (bf16[4,96,384]{2,1,0:T(8,128)(2,1)S(1)}, bf16[4,96,384]{2,1,0:T(8,128)(2,1)S(1)}, u32[]{:S(2)}, u32[]{:S(2)}) collective-permute-start(bf16[4,96,384]{2,1,0:T(8,128)(2,1)S(1)} %dynamic-slice_select_fusion), channel_id=1, source_target_pairs={{0,8},{24,16},{1,9},{25,17},{2,10},{26,18},{3,11},{27,19},{4,12},{... | collective-permute-start | bytes 884744 | tf_op jit(solution)/shard_map/ppermute | solution.py:163
  354.2 10.0 %collective-permute-start.50 = (bf16[96,1536]{1,0:T(8,128)(2,1)S(1)}, bf16[96,1536]{1,0:T(8,128)(2,1)S(1)}, u32[]{:S(2)}, u32[]{:S(2)}) collective-permute-start(bf16[96,1536]{1,0:T(8,128)(2,1)S(1)} %get-tuple-element.1173), channel_id=1, source_target_pairs={{0,2},{2,0},{4,6},{6,4},{1,3},{3,1},{5,7},{7,5},{8,10},{10,8},{12,... | collective-permute-start | bytes 884744 | tf_op jit(solution)/shard_map/ppermute | solution.py:32
  355.7 14.8 %collective-permute-start.51 = (bf16[96,1536]{1,0:T(8,128)(2,1)S(1)}, bf16[96,1536]{1,0:T(8,128)(2,1)S(1)}, u32[]{:S(2)}, u32[]{:S(2)}) collective-permute-start(bf16[96,1536]{1,0:T(8,128)(2,1)S(1)} %get-tuple-element.1172), channel_id=1, source_target_pairs={{0,4},{2,6},{4,0},{6,2},{1,5},{3,7},{5,1},{7,3},{8,12},{10,14},{12... | collective-permute-start | bytes 884744 | tf_op jit(solution)/shard_map/ppermute | solution.py:32
  357.1 13.4 %collective-permute-start.52 = (bf16[96,1536]{1,0:T(8,128)(2,1)S(1)}, bf16[96,1536]{1,0:T(8,128)(2,1)S(1)}, u32[]{:S(2)}, u32[]{:S(2)}) collective-permute-start(bf16[96,1536]{1,0:T(8,128)(2,1)S(1)} %get-tuple-element.1171), channel_id=1, source_target_pairs={{0,6},{2,4},{4,2},{6,0},{1,7},{3,5},{5,3},{7,1},{8,14},{10,12},{12... | collective-permute-start | bytes 884744 | tf_op jit(solution)/shard_map/ppermute | solution.py:32
  374.2 20.8 %collective-permute-start.55 = (bf16[4,96,384]{2,1,0:T(8,128)(2,1)S(1)}, bf16[4,96,384]{2,1,0:T(8,128)(2,1)S(1)}, u32[]{:S(2)}, u32[]{:S(2)}) collective-permute-start(bf16[4,96,384]{2,1,0:T(8,128)(2,1)S(1)} %get-tuple-element.1062), channel_id=1, source_target_pairs={{0,8},{8,16},{1,9},{9,17},{2,10},{10,18},{3,11},{11,19},{4,12},{12... | collective-permute-start | bytes 884744 | tf_op jit(solution)/shard_map/ppermute | solution.py:165
  375.8 19.3 %collective-permute-start.56 = (bf16[4,96,384]{2,1,0:T(8,128)(2,1)S(1)}, bf16[4,96,384]{2,1,0:T(8,128)(2,1)S(1)}, u32[]{:S(2)}, u32[]{:S(2)}) collective-permute-start(bf16[4,96,384]{2,1,0:T(8,128)(2,1)S(1)} %get-tuple-element.1063), channel_id=1, source_target_pairs={{24,16},{16,8},{25,17},{17,9},{26,18},{18,10},{27,19},{19,11},{28,... | collective-permute-start | bytes 884744 | tf_op jit(solution)/shard_map/ppermute | solution.py:165
  376.5 16.2 %collective-permute-start.57 = (bf16[4,48,384]{2,1,0:T(8,128)(2,1)S(1)}, bf16[4,48,384]{2,1,0:T(8,128)(2,1)S(1)}, u32[]{:S(2)}, u32[]{:S(2)}) collective-permute-start(bf16[4,48,384]{2,1,0:T(8,128)(2,1)S(1)} %get-tuple-element.1064), channel_id=1, source_target_pairs={{0,8},{8,16},{16,24},{1,9},{9,17},{17,25},{2,10},{10,18},{18,26},{... | collective-permute-start | bytes 442376 | tf_op jit(solution)/shard_map/ppermute | solution.py:165
  379.8 15.2 %collective-permute-start.58 = (bf16[4,48,384]{2,1,0:T(8,128)(2,1)S(1)}, bf16[4,48,384]{2,1,0:T(8,128)(2,1)S(1)}, u32[]{:S(2)}, u32[]{:S(2)}) collective-permute-start(bf16[4,48,384]{2,1,0:T(8,128)(2,1)S(1)} %get-tuple-element.1065), channel_id=1, source_target_pairs={{24,16},{16,8},{8,0},{25,17},{17,9},{9,1},{26,18},{18,10},{10,2},{... | collective-permute-start | bytes 442376 | tf_op jit(solution)/shard_map/ppermute | solution.py:165
  395.8 39.4 %collective-permute-start.59 = (bf16[512,768]{1,0:T(8,128)(2,1)}, bf16[512,768]{1,0:T(8,128)(2,1)S(1)}, u32[]{:S(2)}, u32[]{:S(2)}) collective-permute-start(bf16[512,768]{1,0:T(8,128)(2,1)} %get-tuple-element.1076), channel_id=1, source_target_pairs={{0,2},{2,0},{4,6},{6,4},{1,3},{3,1},{5,7},{7,5},{8,10},{10,8},{12,... | collective-permute-start | bytes 2359304 | tf_op jit(solution)/shard_map/ppermute | solution.py:32
  397.0 38.2 %collective-permute-start.60 = (bf16[512,768]{1,0:T(8,128)(2,1)}, bf16[512,768]{1,0:T(8,128)(2,1)}, u32[]{:S(2)}, u32[]{:S(2)}) collective-permute-start(bf16[512,768]{1,0:T(8,128)(2,1)} %get-tuple-element.1078), channel_id=1, source_target_pairs={{0,4},{2,6},{4,0},{6,2},{1,5},{3,7},{5,1},{7,3},{8,12},{10,14},{12... | collective-permute-start | bytes 2359304 | tf_op jit(solution)/shard_map/ppermute | solution.py:32
  399.9 25.6 %collective-permute-start.61 = (bf16[4,96,384]{2,1,0:T(8,128)(2,1)}, bf16[4,96,384]{2,1,0:T(8,128)(2,1)S(1)}, u32[]{:S(2)}, u32[]{:S(2)}) collective-permute-start(bf16[4,96,384]{2,1,0:T(8,128)(2,1)} %get-tuple-element.1085), channel_id=1, source_target_pairs={{0,8},{8,16},{16,24},{1,9},{9,17},{17,25},{2,10},{10,18},{18,26},{... | collective-permute-start | bytes 884744 | tf_op jit(solution)/shard_map/ppermute | solution.py:165
  414.7 20.5 %collective-permute-start.62 = (bf16[4,96,384]{2,1,0:T(8,128)(2,1)}, bf16[4,96,384]{2,1,0:T(8,128)(2,1)S(1)}, u32[]{:S(2)}, u32[]{:S(2)}) collective-permute-start(bf16[4,96,384]{2,1,0:T(8,128)(2,1)} %get-tuple-element.1086), channel_id=1, source_target_pairs={{24,16},{16,8},{8,0},{25,17},{17,9},{9,1},{26,18},{18,10},{10,2},{... | collective-permute-start | bytes 884744 | tf_op jit(solution)/shard_map/ppermute | solution.py:165
  437.5 14.7 %collective-permute-start.64 = (bf16[512,384]{1,0:T(8,128)(2,1)S(1)}, bf16[512,384]{1,0:T(8,128)(2,1)S(1)}, u32[]{:S(2)}, u32[]{:S(2)}) collective-permute-start(bf16[512,384]{1,0:T(8,128)(2,1)S(1)} %add_convert_fusion.3), channel_id=1, source_target_pairs={{0,4},{2,6},{4,0},{6,2},{1,5},{3,7},{5,1},{7,3},{8,12},{10,14},{12... | collective-permute-start | bytes 1179656 | tf_op jit(solution)/shard_map/ppermute | solution.py:32
  440.0 12.2 %collective-permute-start.65 = (bf16[512,384]{1,0:T(8,128)(2,1)S(1)}, bf16[512,384]{1,0:T(8,128)(2,1)S(1)}, u32[]{:S(2)}, u32[]{:S(2)}) collective-permute-start(bf16[512,384]{1,0:T(8,128)(2,1)S(1)} %add_convert_fusion.2), channel_id=1, source_target_pairs={{0,2},{2,0},{4,6},{6,4},{1,3},{3,1},{5,7},{7,5},{8,10},{10,8},{12,... | collective-permute-start | bytes 1179656 | tf_op jit(solution)/shard_map/ppermute | solution.py:32
  458.7 18.7 %collective-permute-start.71 = (bf16[4,160,384]{2,1,0:T(8,128)(2,1)S(1)}, bf16[4,160,384]{2,1,0:T(8,128)(2,1)S(1)}, u32[]{:S(2)}, u32[]{:S(2)}) collective-permute-start(bf16[4,160,384]{2,1,0:T(8,128)(2,1)S(1)} %fusion.10), channel_id=1, source_target_pairs={{0,8},{8,16},{16,24},{1,9},{9,17},{17,25},{2,10},{10,18},{18,26},{... | collective-permute-start | bytes 1474568 | tf_op jit(solution)/shard_map/ppermute | solution.py:192
  461.6 18.4 %collective-permute-start.72 = (bf16[4,160,384]{2,1,0:T(8,128)(2,1)S(1)}, bf16[4,160,384]{2,1,0:T(8,128)(2,1)}, u32[]{:S(2)}, u32[]{:S(2)}) collective-permute-start(bf16[4,160,384]{2,1,0:T(8,128)(2,1)S(1)} %fusion.10), channel_id=1, source_target_pairs={{24,16},{16,8},{8,0},{25,17},{17,9},{9,1},{26,18},{18,10},{10,2},{... | collective-permute-start | bytes 1474568 | tf_op jit(solution)/shard_map/ppermute | solution.py:193
  480.1 11.2 %collective-permute-start.73 = (bf16[4,160,384]{2,1,0:T(8,128)(2,1)S(1)}, bf16[4,160,384]{2,1,0:T(8,128)(2,1)S(1)}, u32[]{:S(2)}, u32[]{:S(2)}) collective-permute-start(bf16[4,160,384]{2,1,0:T(8,128)(2,1)S(1)} %collective-permute-done.71), channel_id=1, source_target_pairs={{8,16},{16,24},{9,17},{17,25},{10,18},{18,26},{11,19},{19,27},{12,... | collective-permute-start | bytes 1474568 | tf_op jit(solution)/shard_map/ppermute | solution.py:192
  480.8 16.2 %collective-permute-start.74 = (bf16[4,160,384]{2,1,0:T(8,128)(2,1)}, bf16[4,160,384]{2,1,0:T(8,128)(2,1)S(1)}, u32[]{:S(2)}, u32[]{:S(2)}) collective-permute-start(bf16[4,160,384]{2,1,0:T(8,128)(2,1)} %collective-permute-done.72), channel_id=1, source_target_pairs={{16,8},{8,0},{17,9},{9,1},{18,10},{10,2},{19,11},{11,3},{20,12},{1... | collective-permute-start | bytes 1474568 | tf_op jit(solution)/shard_map/ppermute | solution.py:193
  497.0 14.0 %collective-permute-start.75 = (bf16[4,160,384]{2,1,0:T(8,128)(2,1)S(1)}, bf16[4,160,384]{2,1,0:T(8,128)(2,1)S(1)}, u32[]{:S(2)}, u32[]{:S(2)}) collective-permute-start(bf16[4,160,384]{2,1,0:T(8,128)(2,1)S(1)} %broadcast_select_fusion), channel_id=1, source_target_pairs={{16,24},{8,0},{17,25},{9,1},{18,26},{10,2},{19,27},{11,3},{20,28},... | collective-permute-start | bytes 1474568 | tf_op jit(solution)/shard_map/ppermute | solution.py:187
  (110 other events, 979.7 us)
Sparse Core Ops, SparseCore 0:
  258.3 90.8 reduce-scatter.1
  371.8 102.7 all-gather.2
